TPU v7x, 32 devices: a whole 2x2x4 slice. The times are simulated.
32 devices in a mesh: ja: 8 (over z, core), ka: 4 (over y, x).
Axes of the slice: x: 2, y: 2, z: 4, core: 2. Of those that a mesh axis runs over, the one named last changes fastest.
Arguments:
- tensor: float32 [16, 1024, 1024], P('ka', 'ja'), may hold values from -6 to 6
- factor_one: float32 [1024, 256], replicated, may hold values from -0.1875 to 0.1875
- factor_two: bfloat16 [1024, 256], P('ja'), may hold values from -0.1875 to 0.1875
Outputs:
- gram_one: float32 [1024, 1024], P(('ja', 'ka'))
- gram_two: float32 [1024, 1024], P(('ja', 'ka'))
- reduced: float32 [16, 256, 256], P('ka', 'ja')
All inputs are finite; a program needn't handle non-finite values.
Results may differ from a plain program's by a relative error of at most 0.0029.
Values may be sent and summed in bfloat16 or wider, within the bound.
No kernel may reach another device: no remote copies, remote signals or barrier semaphores. Data moves between devices by JAX's collectives and lax.ppermute only.
A program may use at most 64 MiB of HBM per device.

v0:
```python
import math

import jax
import jax.numpy as jnp
from jax import lax
from jax.sharding import PartitionSpec as P


def shards(tensor, factor_one, factor_two):
    slices, owned, width = tensor.shape
    count_ja = lax.axis_size("ja")
    count_ka = lax.axis_size("ka")
    flat = tensor.reshape(slices * owned, width)
    halfway = lax.psum_scatter(
        jnp.dot(flat.T, flat, precision=lax.Precision.HIGHEST, preferred_element_type=jnp.float32),
        "ja",
        scatter_dimension=0,
        tiled=True,
    )
    summed = lax.psum_scatter(halfway, "ka", scatter_dimension=0, tiled=True)
    gram_one = summed * (1.0 / math.sqrt(owned * count_ja * slices * count_ka))
    rank_one = factor_one.shape[1]
    core = jnp.dot(
        flat, factor_one, precision=lax.Precision.HIGHEST, preferred_element_type=jnp.float32
    )
    core = core.astype(jnp.bfloat16).reshape(slices, owned, rank_one)
    norm_two = 1.0 / math.sqrt(slices * count_ka * rank_one)
    blocks = jnp.einsum(
        "kjr,klr->jl",
        core,
        lax.all_gather(core, "ja", axis=1, tiled=True),
        preferred_element_type=jnp.float32,
    )
    gram_two = lax.psum_scatter(blocks, "ka", scatter_dimension=0, tiled=True)
    partial_value = jnp.einsum("kjr,js->ksr", core, factor_two, preferred_element_type=jnp.float32)
    reduced = lax.psum_scatter(partial_value, "ja", scatter_dimension=1, tiled=True)
    return (gram_one, gram_two * norm_two, reduced)


def solution(mesh):
    in_specs = (P("ka", "ja", None), P(), P("ja", None))
    out_specs = (P(("ja", "ka"), None), P(("ja", "ka"), None), P("ka", "ja", None))
    return jax.shard_map(shards, mesh=mesh, in_specs=in_specs, out_specs=out_specs, check_vma=False)
```

profile of v0, /device:TPU:0, one launch (start us, length us, event | category | flops | bytes accessed | tf_op | source)
XLA Modules:
  0.0 217.9 jit_solution(12870789567627791411)
XLA Ops:
  7.2 0.0 copy-start
  7.2 0.0 all-gather.2.cloned.1.call-start
  7.2 1.5 copy-done
  8.8 3.7 %convolution_convert_fusion = bf16[512,256]{1,0:T(8,128)(2,1)} fusion(f32[512,1024]{1,0:T(8,128)S(1)} %bitcast.19, f32[1024,256]{1,0:T(8,128)} %param.4), kind=kOutput, calls=%fused_computation.3 | convolution fusion | flops 1610743808 | bytes 3407872 | tf_op jit(solution)/shard_map/dot_general | solution.py:23
  12.5 0.0 all-gather.2.cloned.1.call-update
  12.5 0.0 reduce-scatter.4.cloned.1.call-start
  12.6 8.3 %convolution_bitcast_fusion = f32[1024,1024]{1,0:T(8,128)} fusion(f32[4,128,1024]{2,1,0:T(8,128)S(1)} %copy-done), kind=kOutput, calls=%fused_computation | convolution fusion | flops 6442450944 | bytes 6291456 | tf_op jit(solution)/shard_map/dot_general | solution.py:15
  20.9 0.0 copy-start.1
  20.9 0.0 copy-start.2
  20.9 0.0 reduce-scatter.4.cloned.1.call-update
  20.9 0.0 all-reduce.3.cloned.1.call-start
  20.9 0.9 copy-done.1
  21.8 0.0 copy-done.2
  21.8 0.3 convolution_bitcast_fusion.1
  22.2 1.3 copy.11
  23.5 0.0 all-reduce.3.cloned.1.call-update
  23.5 0.0 copy-start.3
  23.5 0.0 reduce-scatter.8.cloned.1.call-start
  23.6 20.9 %all-gather.2.cloned.1.call-done = bf16[4,1024,256]{2,1,0:T(8,128)(2,1)} async-done(((bf16[4,128,256]{2,1,0:T(8,128)(2,1)}), bf16[4,1024,256]{2,1,0:T(8,128)(2,1)}) %all-gather.2.cloned.1.call-update) | async-done | bytes 2097168 | tf_op jit(solution)/shard_map/all_gather | solution.py:31
  44.5 3.2 %convolution_bitcast_fusion.2 = f32[128,1024]{1,0:T(8,128)} fusion(bf16[4,128,256]{2,1,0:T(8,128)(2,1)S(1)} %bitcast.22, bf16[4,1024,256]{2,1,0:T(8,128)(2,1)} %all-gather.2.cloned.1.call-done), kind=kOutput, calls=%fused_computation.2 | convolution fusion | flops 268435456 | bytes 2883584 | tf_op jit(solution)/shard_map/kjr,klr->jl/dot_general | solution.py:28
  47.7 0.0 reduce-scatter.8.cloned.1.call-update
  47.7 0.0 reduce-scatter.6.cloned.1.call-start
  47.8 48.5 %reduce-scatter.4.cloned.1.call-done = f32[128,1024]{1,0:T(8,128)} async-done(((f32[1024,1024]{1,0:T(8,128)}), f32[128,1024]{1,0:T(8,128)}) %reduce-scatter.4.cloned.1.call-update) | async-done | bytes 524304 | tf_op jit(solution)/shard_map/reduce_scatter | solution.py:14
  96.3 0.0 reduce-scatter.6.cloned.1.call-update
  96.4 0.0 copy-done.3
  96.4 0.6 dynamic-slice
  97.6 58.1 %all-reduce.3.cloned.1.call-done = f32[4,256,256]{2,0,1:T(4,128)} async-done(((f32[4,256,256]{2,0,1:T(4,128)}), f32[4,256,256]{2,0,1:T(4,128)}) %all-reduce.3.cloned.1.call-update) | async-done | bytes 1048592
  155.7 0.9 constant_dynamic-slice_fusion
  156.6 0.7 copy.12
  157.3 24.9 %reduce-scatter.8.cloned.1.call-done = f32[32,1024]{1,0:T(8,128)} async-done(((f32[128,1024]{1,0:T(8,128)}), f32[32,1024]{1,0:T(8,128)}) %reduce-scatter.8.cloned.1.call-update) | async-done | bytes 131088 | tf_op jit(solution)/shard_map/reduce_scatter | solution.py:34
  182.1 1.6 broadcast_multiply_fusion
  183.7 26.1 %reduce-scatter.6.cloned.1.call-done = f32[32,1024]{1,0:T(8,128)} async-done(((f32[128,1024]{1,0:T(8,128)}), f32[32,1024]{1,0:T(8,128)}) %reduce-scatter.6.cloned.1.call-update) | async-done | bytes 131088 | tf_op jit(solution)/shard_map/reduce_scatter | solution.py:20
  209.8 1.6 broadcast_multiply_fusion.1
Async XLA Ops:
  7.2 1.6 copy-start
  7.2 37.3 %all-gather.2.cloned.1.call-start = ((), (), s32[]{:S(2)}) async-start(), calls=%async_computation.5 | async-start | bytes 2359296 | tf_op jit(solution)/shard_map/all_gather | solution.py:31
  12.5 83.8 %reduce-scatter.4.cloned.1.call-start = ((), (), s32[]{:S(2)}) async-start(), calls=%async_computation.3 | async-start | bytes 4718592 | tf_op jit(solution)/shard_map/reduce_scatter | solution.py:14
  20.9 1.0 copy-start.1
  20.9 1.0 copy-start.2
  20.9 134.8 %all-reduce.3.cloned.1.call-start = ((), (), s32[]{:S(2)}) async-start(), calls=%async_computation.7 | async-start | bytes 2097152
  23.5 72.8 %copy-start.3 = (u32[32]{0:T(128)S(1)}, u32[32]{0:T(128)}, u32[]{:S(2)}) copy-start(u32[32]{0:T(128)} %constant.6) | copy-start | bytes 388
  23.5 158.6 %reduce-scatter.8.cloned.1.call-start = ((), (), s32[]{:S(2)}) async-start(), calls=%async_computation.6 | async-start | bytes 655360 | tf_op jit(solution)/shard_map/reduce_scatter | solution.py:34
  47.7 162.1 %reduce-scatter.6.cloned.1.call-start = ((), (), s32[]{:S(2)}) async-start(), calls=%async_computation.4 | async-start | bytes 655360 | tf_op jit(solution)/shard_map/reduce_scatter | solution.py:20
Sparse Core Ops, SparseCore 0:
  12.7 31.7 all-gather.1
  46.8 49.4 reduce-scatter.3
  98.7 56.9 all-reduce.2
  158.4 23.7 reduce-scatter.7
  185.0 24.7 reduce-scatter.5
where the time goes:
time: 218 us
  waiting for transfers between devices  179 us (82%)
  matrix products  15.6 us (7%)
  between operations  14.5 us (7%)
  local copies, waits for them, and re-layouts  5.95 us (3%)
  other arithmetic  3.14 us (1%)
    unnamed x6, waiting for transfers between devices  58.2 us
    reduce_scatter x1, waiting for transfers between devices, shards(): lax.psum_scatter(jnp.dot(flat.T, flat, precision=lax.Precision.HIGHEST, p...  48.5 us
    reduce_scatter x1, waiting for transfers between devices, shards(): summed = lax.psum_scatter(halfway, 'ka', scatter_dimension=0, tiled=True)  26.1 us
    reduce_scatter x1, waiting for transfers between devices, shards(): gram_two = lax.psum_scatter(blocks, 'ka', scatter_dimension=0, tiled=True)  24.9 us
    all_gather x1, waiting for transfers between devices, shards(): lax.all_gather(core, 'ja', axis=1, tiled=True)  20.9 us
    dot_general x1, matrix products, shards(): jnp.dot(flat.T, flat, precision=lax.Precision.HIGHEST, preferred_element_...  8.29 us
    unnamed x11, local copies, waits for them, and re-layouts  4.61 us
  transfers between devices with their start and end apart: 5, of which 5 were waited for; matrix products, arithmetic and copies ran while one was open for 8% of the time, Pallas kernels for 0%

commit v1 on v0

v1 whole, which is shorter than its diff:
```python
import functools
import math

import jax
import jax.numpy as jnp
from jax import lax
from jax.experimental import pallas as pl
from jax.experimental.pallas import tpu as pltpu
from jax.sharding import PartitionSpec as P

F32 = jnp.float32
BF16 = jnp.bfloat16
NT = (((1,), (1,)), ((), ()))
TN = (((0,), (0,)), ((), ()))
VMEM = pl.BlockSpec(memory_space=pltpu.VMEM)
SMEM = pl.BlockSpec(memory_space=pltpu.SMEM)


def halves(x):
    high = x.astype(BF16)
    return high, (x - high.astype(F32)).astype(BF16)


def dot3(a, b, dims):
    ah, al = a
    bh, bl = b
    dot = functools.partial(lax.dot_general, dimension_numbers=dims, preferred_element_type=F32)
    return dot(ah, bh) + (dot(ah, bl) + dot(al, bh))


def params():
    return pltpu.CompilerParams(vmem_limit_bytes=24 * 1024 * 1024)


def cost(flops, *arrays):
    moved = sum(a.size * a.dtype.itemsize for a in arrays)
    return pl.CostEstimate(flops=flops, bytes_accessed=moved, transcendentals=0)


def core_kernel(x_ref, f_ref, u_ref):
    slices, owned, width = x_ref.shape
    rank = f_ref.shape[1]
    x = halves(x_ref[...].reshape(slices * owned, width))
    core = dot3(x, halves(f_ref[...]), (((1,), (0,)), ((), ()))).astype(BF16)
    for k in range(slices):
        u_ref[:, k * rank : (k + 1) * rank] = core[k * owned : (k + 1) * owned]


def core_of(tensor, factor_one):
    slices, owned, _ = tensor.shape
    rank = factor_one.shape[1]
    out = jax.ShapeDtypeStruct((owned, slices * rank), BF16)
    return pl.pallas_call(
        core_kernel,
        out_shape=out,
        in_specs=[VMEM, VMEM],
        out_specs=VMEM,
        compiler_params=params(),
        cost_estimate=cost(6 * tensor.size * rank, tensor, factor_one, out),
        name="core",
    )(tensor, factor_one)


def gram_rows(x_ref, lhs_at, count, step):
    slices, owned, width = x_ref.shape
    right = halves(x_ref[...].reshape(slices * owned, width))
    for g in range(count):
        left = halves(x_ref[:, :, pl.ds(lhs_at(g), step)].reshape(slices * owned, step))
        yield g, dot3(left, right, TN)


def gram_away_kernel(c_ref, x_ref, away_ref):
    groups, step, _ = away_ref.shape
    other = 1 - c_ref[0]
    at = lambda g: pl.multiple_of((2 * g + other) * step, step)
    for g, rows in gram_rows(x_ref, at, groups, step):
        away_ref[g] = rows.astype(BF16)


def gram_home_kernel(c_ref, x_ref, came_ref, *outs):
    groups, step, _ = came_ref.shape
    block = step // len(outs)
    core, ka = c_ref[0], c_ref[1]
    at = lambda g: pl.multiple_of((2 * g + core) * step, step)
    total = outs[0]
    for g, rows in gram_rows(x_ref, at, groups, step):
        rows = rows + came_ref[g].astype(F32)
        for t in range(len(outs)):
            for b in range(len(outs)):
                @pl.when(ka == (b ^ t))
                def _():
                    outs[t][g] = rows[b * block : (b + 1) * block].astype(outs[t].dtype)


def gram_away(place, tensor, groups):
    width = tensor.shape[2]
    out = jax.ShapeDtypeStruct((groups, width // (2 * groups), width), BF16)
    return pl.pallas_call(
        gram_away_kernel,
        out_shape=out,
        in_specs=[SMEM, VMEM],
        out_specs=VMEM,
        compiler_params=params(),
        cost_estimate=cost(3 * tensor.size * width, tensor, out),
        name="gram_away",
    )(place, tensor)


def gram_home(place, tensor, came, count_ka):
    groups, step, width = came.shape
    shape = (groups, step // count_ka, width)
    outs = [jax.ShapeDtypeStruct(shape, F32 if t == 0 else BF16) for t in range(count_ka)]
    return pl.pallas_call(
        gram_home_kernel,
        out_shape=outs,
        in_specs=[SMEM, VMEM, VMEM],
        out_specs=[VMEM] * count_ka,
        compiler_params=params(),
        cost_estimate=cost(3 * tensor.size * width, tensor, came, *outs),
        name="gram_home",
    )(place, tensor, came)


def xor_permute(x, axis, bits):
    return lax.ppermute(x, axis, [(i, i ^ bits) for i in range(lax.axis_size(axis))])


def shards(tensor, factor_one, factor_two):
    slices, owned, width = tensor.shape
    count_ja = lax.axis_size("ja")
    count_ka = lax.axis_size("ka")
    count_z = count_ja // 2
    rank_one = factor_one.shape[1]
    rank_two = factor_two.shape[1]
    ja = lax.axis_index("ja")
    ka = lax.axis_index("ka")
    core_at, z = lax.rem(ja, 2), lax.div(ja, 2)
    place = jnp.stack([core_at, ka, z]).astype(jnp.int32)

    part = rank_two // count_ja
    cut = factor_two.reshape(owned, count_z, 2, part)
    mine = lax.dynamic_index_in_dim(cut, core_at, 2, keepdims=False)
    away = lax.dynamic_index_in_dim(cut, 1 - core_at, 2, keepdims=False)
    f2 = jnp.stack([mine, xor_permute(away, "ja", 1)])
    f2 = f2.transpose(2, 0, 1, 3)

    u = core_of(tensor, factor_one)

    got = {0: u}
    f2got = {0: lax.dynamic_index_in_dim(f2, z, 0, keepdims=False)}
    for t in range(1, count_z):
        low = t & -t
        got[t] = xor_permute(got[t ^ low], "ja", 2 * low)
        f2got[t] = xor_permute(lax.dynamic_index_in_dim(f2, z ^ t, 0, keepdims=False), "ja", 2 * t)

    step = width // count_ja
    norm_one = 1.0 / math.sqrt(owned * count_ja * slices * count_ka)
    if step % 128 == 0 and (step // count_ka) % 16 == 0:
        sent = gram_away(place, tensor, count_z)
        came = xor_permute(sent, "ja", 1)
        pieces = gram_home(place, tensor, came, count_ka)
    else:
        flat = tensor.reshape(slices * owned, width)
        local = jnp.dot(flat.T, flat, precision=lax.Precision.HIGH, preferred_element_type=F32)
        local = local.reshape(count_z, 2, step, width)
        sent = lax.dynamic_index_in_dim(local, 1 - core_at, 1, keepdims=False).astype(BF16)
        came = xor_permute(sent, "ja", 1)
        home = lax.dynamic_index_in_dim(local, core_at, 1, keepdims=False) + came.astype(F32)
        home = home.reshape(count_z, count_ka, step // count_ka, width)
        pieces = [
            lax.dynamic_index_in_dim(home, ka ^ t, 1, keepdims=False).astype(F32 if t == 0 else BF16)
            for t in range(count_ka)
        ]
    slab = pieces[0]
    for t in range(1, count_ka):
        slab = slab + xor_permute(pieces[t], "ka", t).astype(F32)
    gram_one = lax.dynamic_index_in_dim(slab, z, 0, keepdims=False)
    for t in range(1, count_z):
        piece = lax.dynamic_index_in_dim(slab, z ^ t, 0, keepdims=False).astype(BF16)
        gram_one = gram_one + xor_permute(piece, "ja", 2 * t).astype(F32)
    gram_one = gram_one * norm_one

    blocks = []
    for t in range(count_z):
        blocks += [got[t], xor_permute(got[t], "ja", 1)]
    gathered = jnp.concatenate(blocks, axis=0)
    columns = jnp.concatenate([f2got[t].reshape(2 * owned, part) for t in range(count_z)], axis=0)
    norm_two = 1.0 / math.sqrt(slices * count_ka * rank_one)
    partial_two = lax.dot_general(u, gathered, NT, preferred_element_type=F32)
    partial_two = partial_two.reshape(count_ka, owned // count_ka, count_ja * owned)
    gram_two = lax.dynamic_index_in_dim(partial_two, ka, 0, keepdims=False)
    for t in range(1, count_ka):
        piece = lax.dynamic_index_in_dim(partial_two, ka ^ t, 0, keepdims=False).astype(BF16)
        gram_two = gram_two + xor_permute(piece, "ka", t).astype(F32)
    gram_two = (gram_two * norm_two).reshape(owned // count_ka, count_ja, owned)
    order = jnp.arange(count_ja) ^ ja
    gram_two = jnp.take(gram_two, order, axis=1).reshape(owned // count_ka, count_ja * owned)
    reduced = lax.dot_general(columns, gathered, TN, preferred_element_type=F32)
    reduced = reduced.reshape(part, slices, rank_one).transpose(1, 0, 2)
    return (gram_one, gram_two, reduced)


def solution(mesh):
    in_specs = (P("ka", "ja", None), P(), P("ja", None))
    out_specs = (P(("ja", "ka"), None), P(("ja", "ka"), None), P("ka", "ja", None))
    return jax.shard_map(shards, mesh=mesh, in_specs=in_specs, out_specs=out_specs, check_vma=False)
```

time: 218 us -> 76 us (0.35)
  waiting for transfers between devices: 179 us -> 29.6 us
  starting transfers between devices: 0.21 us -> 22.1 us
  between operations: 14.5 us -> 0.84 us
  matrix products: 15.6 us -> 2.88 us
  Pallas kernels: 0 us -> 8.55 us
  local copies, waits for them, and re-layouts: 5.95 us -> 10.2 us
    reduce_scatter x3 -> x0, waiting for transfers between devices: 99.5 us -> none  [the longest x1 48.5 us: shards(): lax.psum_scatter(jnp.dot(flat.T, flat, precision=lax.Precision.HIGHEST, p...]
    unnamed x6 -> x0, waiting for transfers between devices: 58.2 us -> none
    ppermute x0 -> x21, waiting for transfers between devices: none -> 29.6 us  [xor_permute(): lax.ppermute(x, axis, [(i, i ^ bits) for i in range(lax.axis_size(axis))])]
    ppermute x0 -> x21, starting transfers between devices: none -> 22.1 us  [xor_permute(): lax.ppermute(x, axis, [(i, i ^ bits) for i in range(lax.axis_size(axis))])]
    all_gather x1 -> x0, waiting for transfers between devices: 20.9 us -> none  [shards(): lax.all_gather(core, 'ja', axis=1, tiled=True)]
    dot_general x4 -> x2, matrix products: 15.6 us -> 2.88 us  [the longest x1 2.42 us: shards(): partial_two = lax.dot_general(u, gathered, NT, preferred_element_type=F32)]
    pallas_call x0 -> x3, Pallas kernels: none -> 8.55 us  [the longest x1 4.11 us: gram_home(): pl.pallas_call(gram_home_kernel, out_shape=outs, in_specs=[SMEM, VMEM, VM...]
    unnamed x11 -> x19, local copies, waits for them, and re-layouts: 4.61 us -> 8.08 us
  transfers between devices with their start and end apart: 5 -> 21, of which waited for: 5 -> 8; matrix products, arithmetic and copies ran while one was open for 8% -> 15% of each run, Pallas kernels for 0% -> 10%
where the time goes in v1:
time: 76 us; the launch traced here: 75.8 us
  waiting for transfers between devices  29.6 us (39%)
  starting transfers between devices  22.1 us (29%)
  local copies, waits for them, and re-layouts  10.2 us (13%)
  Pallas kernels  8.55 us (11%)
  matrix products  2.88 us (4%)
  other arithmetic  1.65 us (2%)
  between operations  0.84 us (1%)
    ppermute x21, waiting for transfers between devices, xor_permute(): lax.ppermute(x, axis, [(i, i ^ bits) for i in range(lax.axis_size(axis))])  29.6 us
    ppermute x21, starting transfers between devices, xor_permute(): lax.ppermute(x, axis, [(i, i ^ bits) for i in range(lax.axis_size(axis))])  22.1 us
    unnamed x19, local copies, waits for them, and re-layouts  8.08 us
    pallas_call x1, Pallas kernels, gram_home(): pl.pallas_call(gram_home_kernel, out_shape=outs, in_specs=[SMEM, VMEM, VM...  4.11 us
    pallas_call x1, Pallas kernels, gram_away(): pl.pallas_call(gram_away_kernel, out_shape=out, in_specs=[SMEM, VMEM], ou...  3.43 us
    dot_general x1, matrix products, shards(): partial_two = lax.dot_general(u, gathered, NT, preferred_element_type=F32)  2.42 us
  transfers between devices with their start and end apart: 21, of which 8 were waited for; matrix products, arithmetic and copies ran while one was open for 15% of the time, Pallas kernels for 10%

profile of v1, /device:TPU:0, one launch (start us, length us, event | category | flops | bytes accessed | tf_op | source)
XLA Modules:
  0.0 75.8 jit_solution(13674534226033140194)
XLA Ops:
  0.6 1.6 %copy-done = f32[4,128,1024]{2,1,0:T(8,128)S(1)} copy-done((f32[4,128,1024]{2,1,0:T(8,128)S(1)}, f32[4,128,1024]{2,1,0:T(8,128)}, u32[]{:S(2)}) %copy-start) | copy-done | bytes 2097176
  2.2 1.2 %copy-done.2 = f32[1024,256]{1,0:T(8,128)S(1)} copy-done((f32[1024,256]{1,0:T(8,128)S(1)}, f32[1024,256]{1,0:T(8,128)}, u32[]{:S(2)}) %copy-start.2) | copy-done | bytes 1048600
  3.5 1.0 %core.1 = bf16[128,1024]{1,0:T(8,128)(2,1)S(1)} custom-call(f32[4,128,1024]{2,1,0:T(8,128)S(1)} %copy-done, f32[1024,256]{1,0:T(8,128)S(1)} %copy-done.2), custom_call_target="tpu_custom_call" | custom-call | flops 805306368 | bytes 3407872 | tf_op jit(solution)/shard_map/core/pallas_call | solution.py:53
  4.5 0.5 collective-permute-start.7
  5.0 2.7 %collective-permute-start.8 = (bf16[128,1024]{1,0:T(8,128)(2,1)S(1)}, bf16[128,1024]{1,0:T(8,128)(2,1)S(1)}, u32[]{:S(2)}, u32[]{:S(2)}) collective-permute-start(bf16[128,1024]{1,0:T(8,128)(2,1)S(1)} %core.1), channel_id=1, source_target_pairs={{0,8},{4,12},{8,0},{12,4},{16,24},{20,28},{24,16},{28,20},{1,9},{5... | collective-permute-start | bytes 786440 | tf_op jit(solution)/shard_map/ppermute | solution.py:125
  7.6 2.6 %collective-permute-start.10 = (bf16[128,1024]{1,0:T(8,128)(2,1)S(1)}, bf16[128,1024]{1,0:T(8,128)(2,1)S(1)}, u32[]{:S(2)}, u32[]{:S(2)}) collective-permute-start(bf16[128,1024]{1,0:T(8,128)(2,1)S(1)} %core.1), channel_id=1, source_target_pairs={{0,16},{4,20},{8,24},{12,28},{16,0},{20,4},{24,8},{28,12},{1,17},{... | collective-permute-start | bytes 786440 | tf_op jit(solution)/shard_map/ppermute | solution.py:125
  10.2 0.1 copy.15
  10.5 0.1 pad_add_fusion.c_ref
  10.6 3.4 %gram_away.1 = bf16[4,128,1024]{2,1,0:T(8,128)(2,1)} custom-call(s32[3]{0:T(128)S(1)} %pad_add_fusion.c_ref, f32[4,128,1024]{2,1,0:T(8,128)S(1)} %copy-done.1), custom_call_target="tpu_custom_call" | custom-call | flops 1610612736 | bytes 3145728 | tf_op jit(solution)/shard_map/gram_away/pallas_call | solution.py:98
  14.0 0.5 collective-permute-start
  14.4 0.7 constant_dynamic-update-slice_fusion.7
  15.2 0.1 broadcast_bitcast_fusion
  15.3 0.1 collective-permute-start.20
  15.4 7.4 %collective-permute-done.20 = bf16[2,128,32]{1,2,0:T(8,128)(2,1)S(1)} collective-permute-done((bf16[2,128,32]{1,2,0:T(8,128)(2,1)S(1)}, bf16[2,128,32]{1,2,0:T(8,128)(2,1)S(1)}, u32[]{:S(2)}, u32[]{:S(2)}) %collective-permute-start.20) | collective-permute-done | bytes 16416 | tf_op jit(solution)/shard_map/ppermute | solution.py:125
  22.8 2.0 %collective-permute-start.19 = (bf16[2,128,32]{1,2,0:T(8,128)(2,1)S(1)}, bf16[2,128,32]{1,2,0:T(8,128)(2,1)S(1)}, u32[]{:S(2)}, u32[]{:S(2)}) collective-permute-start(bf16[2,128,32]{1,2,0:T(8,128)(2,1)S(1)} %get-tuple-element.19), channel_id=1, source_target_pairs={{0,16},{4,20},{8,24},{12,28},{16,0},{20,4},{24,8},{28,12},{1,17},{... | collective-permute-start | bytes 49160 | tf_op jit(solution)/shard_map/ppermute | solution.py:125
  24.9 2.6 %collective-permute-done.19 = bf16[2,128,32]{1,2,0:T(8,128)(2,1)S(1)} collective-permute-done((bf16[2,128,32]{1,2,0:T(8,128)(2,1)S(1)}, bf16[2,128,32]{1,2,0:T(8,128)(2,1)S(1)}, u32[]{:S(2)}, u32[]{:S(2)}) %collective-permute-start.19) | collective-permute-done | bytes 16416 | tf_op jit(solution)/shard_map/ppermute | solution.py:125
  27.5 1.0 %collective-permute-start.18 = (bf16[2,128,32]{1,2,0:T(8,128)(2,1)S(1)}, bf16[2,128,32]{1,2,0:T(8,128)(2,1)S(1)}, u32[]{:S(2)}, u32[]{:S(2)}) collective-permute-start(bf16[2,128,32]{1,2,0:T(8,128)(2,1)S(1)} %get-tuple-element.18), channel_id=1, source_target_pairs={{0,8},{4,12},{8,0},{12,4},{16,24},{20,28},{24,16},{28,20},{1,9},{5... | collective-permute-start | bytes 49160 | tf_op jit(solution)/shard_map/ppermute | solution.py:125
  28.5 1.1 %collective-permute-start.12 = (bf16[128,1024]{1,0:T(8,128)(2,1)S(1)}, bf16[128,1024]{1,0:T(8,128)(2,1)S(1)}, u32[]{:S(2)}, u32[]{:S(2)}) collective-permute-start(bf16[128,1024]{1,0:T(8,128)(2,1)S(1)} %collective-permute-done.10), channel_id=1, source_target_pairs={{0,8},{4,12},{8,0},{12,4},{16,24},{20,28},{24,16},{28,20},{1,9},{5... | collective-permute-start | bytes 786440 | tf_op jit(solution)/shard_map/ppermute | solution.py:125
  29.6 1.6 %collective-permute-done.18 = bf16[2,128,32]{1,2,0:T(8,128)(2,1)S(1)} collective-permute-done((bf16[2,128,32]{1,2,0:T(8,128)(2,1)S(1)}, bf16[2,128,32]{1,2,0:T(8,128)(2,1)S(1)}, u32[]{:S(2)}, u32[]{:S(2)}) %collective-permute-start.18) | collective-permute-done | bytes 16416 | tf_op jit(solution)/shard_map/ppermute | solution.py:125
  31.2 0.7 constant_dynamic-update-slice_fusion.6
  32.0 0.7 constant_dynamic-update-slice_fusion.5
  32.7 4.5 %collective-permute-done.12 = bf16[128,1024]{1,0:T(8,128)(2,1)S(1)} collective-permute-done((bf16[128,1024]{1,0:T(8,128)(2,1)S(1)}, bf16[128,1024]{1,0:T(8,128)(2,1)S(1)}, u32[]{:S(2)}, u32[]{:S(2)}) %collective-permute-start.12) | collective-permute-done | bytes 262176 | tf_op jit(solution)/shard_map/ppermute | solution.py:125
  37.2 0.7 constant_dynamic-update-slice_fusion.4
  38.0 0.7 constant_dynamic-update-slice_fusion.3
  38.7 0.7 constant_dynamic-update-slice_fusion.2
  39.5 0.7 constant_dynamic-update-slice_fusion.1
  40.2 0.7 constant_dynamic-update-slice_fusion
  40.9 2.4 %fusion.30 = f32[128,1024]{1,0:T(8,128)S(1)} fusion(bf16[128,1024]{1,0:T(8,128)(2,1)S(1)} %core.1, bf16[1024,1024]{1,0:T(8,128)(2,1)} %constant_dynamic-update-slice_fusion), kind=kOutput, calls=%fused_computation.71 | convolution fusion | flops 268435456 | bytes 2883584 | tf_op jit(solution)/shard_map/dot_general | solution.py:189
  43.4 1.6 %collective-permute-start.14 = (bf16[32,1024]{1,0:T(8,128)(2,1)S(1)}, bf16[32,1024]{1,0:T(8,128)(2,1)S(1)}, u32[]{:S(2)}, u32[]{:S(2)}) collective-permute-start(bf16[32,1024]{1,0:T(8,128)(2,1)S(1)} %get-tuple-element.11), channel_id=1, source_target_pairs={{0,1},{1,0},{2,3},{3,2},{4,5},{5,4},{6,7},{7,6},{8,9},{9,8},{10,11... | collective-permute-start | bytes 196616 | tf_op jit(solution)/shard_map/ppermute | solution.py:125
  44.9 1.5 %collective-permute-start.15 = (bf16[32,1024]{1,0:T(8,128)(2,1)S(1)}, bf16[32,1024]{1,0:T(8,128)(2,1)S(1)}, u32[]{:S(2)}, u32[]{:S(2)}) collective-permute-start(bf16[32,1024]{1,0:T(8,128)(2,1)S(1)} %get-tuple-element.13), channel_id=1, source_target_pairs={{0,2},{1,3},{2,0},{3,1},{4,6},{5,7},{6,4},{7,5},{8,10},{9,11},{10,... | collective-permute-start | bytes 196616 | tf_op jit(solution)/shard_map/ppermute | solution.py:125
  46.5 0.5 collective-permute-start.16
  47.0 4.1 %gram_home.1 = (f32[4,32,1024]{2,1,0:T(8,128)S(1)}, bf16[4,32,1024]{2,1,0:T(8,128)(2,1)S(1)}, bf16[4,32,1024]{2,1,0:T(8,128)(2,1)S(1)}, bf16[4,32,1024]{2,1,0:T(8,128)(2,1)S(1)}) custom-call(s32[3]{0:T(128)S(1)} %pad_add_fusion.c_ref, f32[4,128,1024]{2,1,0:T(8,128)S(1)} %copy-done.1, bf16[4,128,1024]{2,1,0:T(8,128)(2,1)} %collective-permute-done.came_ref), custom_call_target="tpu_custom_call" | custom-call | flops 1610612736 | bytes 4456448 | tf_op jit(solution)/shard_map/gram_home/pallas_call | solution.py:113
  51.1 1.4 %collective-permute-start.1 = (bf16[4,32,1024]{2,1,0:T(8,128)(2,1)S(1)}, bf16[4,32,1024]{2,1,0:T(8,128)(2,1)S(1)}, u32[]{:S(2)}, u32[]{:S(2)}) collective-permute-start(bf16[4,32,1024]{2,1,0:T(8,128)(2,1)S(1)} %get-tuple-element.8), channel_id=1, source_target_pairs={{0,1},{1,0},{2,3},{3,2},{4,5},{5,4},{6,7},{7,6},{8,9},{9,8},{10,11... | collective-permute-start | bytes 786440 | tf_op jit(solution)/shard_map/ppermute | solution.py:125
  52.5 1.5 %collective-permute-start.2 = (bf16[4,32,1024]{2,1,0:T(8,128)(2,1)S(1)}, bf16[4,32,1024]{2,1,0:T(8,128)(2,1)S(1)}, u32[]{:S(2)}, u32[]{:S(2)}) collective-permute-start(bf16[4,32,1024]{2,1,0:T(8,128)(2,1)S(1)} %get-tuple-element.9), channel_id=1, source_target_pairs={{0,2},{1,3},{2,0},{3,1},{4,6},{5,7},{6,4},{7,5},{8,10},{9,11},{10,... | collective-permute-start | bytes 786440 | tf_op jit(solution)/shard_map/ppermute | solution.py:125
  54.0 0.6 collective-permute-start.3
  54.6 0.5 fusion.13
  55.1 0.7 copy.35
  55.8 0.6 gather_fusion
  56.4 4.0 %collective-permute-done.1 = bf16[4,32,1024]{2,1,0:T(8,128)(2,1)S(1)} collective-permute-done((bf16[4,32,1024]{2,1,0:T(8,128)(2,1)S(1)}, bf16[4,32,1024]{2,1,0:T(8,128)(2,1)S(1)}, u32[]{:S(2)}, u32[]{:S(2)}) %collective-permute-start.1) | collective-permute-done | bytes 262176 | tf_op jit(solution)/shard_map/ppermute | solution.py:125
  60.4 5.4 %collective-permute-done.2 = bf16[4,32,1024]{2,1,0:T(8,128)(2,1)S(1)} collective-permute-done((bf16[4,32,1024]{2,1,0:T(8,128)(2,1)S(1)}, bf16[4,32,1024]{2,1,0:T(8,128)(2,1)S(1)}, u32[]{:S(2)}, u32[]{:S(2)}) %collective-permute-start.2) | collective-permute-done | bytes 262176 | tf_op jit(solution)/shard_map/ppermute | solution.py:125
  65.7 0.1 convert_add_fusion
  65.9 1.1 %collective-permute-start.4 = (bf16[32,1024]{1,0:T(8,128)(2,1)S(1)}, bf16[32,1024]{1,0:T(8,128)(2,1)S(1)}, u32[]{:S(2)}, u32[]{:S(2)}) collective-permute-start(bf16[32,1024]{1,0:T(8,128)(2,1)S(1)} %get-tuple-element.14), channel_id=1, source_target_pairs={{0,8},{4,12},{8,0},{12,4},{16,24},{20,28},{24,16},{28,20},{1,9},{5... | collective-permute-start | bytes 196616 | tf_op jit(solution)/shard_map/ppermute | solution.py:125
  67.0 2.0 %collective-permute-start.5 = (bf16[32,1024]{1,0:T(8,128)(2,1)S(1)}, bf16[32,1024]{1,0:T(8,128)(2,1)S(1)}, u32[]{:S(2)}, u32[]{:S(2)}) collective-permute-start(bf16[32,1024]{1,0:T(8,128)(2,1)S(1)} %get-tuple-element.16), channel_id=1, source_target_pairs={{0,16},{4,20},{8,24},{12,28},{16,0},{20,4},{24,8},{28,12},{1,17},{... | collective-permute-start | bytes 196616 | tf_op jit(solution)/shard_map/ppermute | solution.py:125
  69.0 1.4 %collective-permute-start.6 = (bf16[32,1024]{1,0:T(8,128)(2,1)S(1)}, bf16[32,1024]{1,0:T(8,128)(2,1)S(1)}, u32[]{:S(2)}, u32[]{:S(2)}) collective-permute-start(bf16[32,1024]{1,0:T(8,128)(2,1)S(1)} %get-tuple-element.15), channel_id=1, source_target_pairs={{0,24},{4,28},{8,16},{12,20},{16,8},{20,12},{24,0},{28,4},{1,25},{... | collective-permute-start | bytes 196616 | tf_op jit(solution)/shard_map/ppermute | solution.py:125
  70.4 0.7 bitcast_select_fusion
  71.1 2.5 %collective-permute-done.5 = bf16[32,1024]{1,0:T(8,128)(2,1)S(1)} collective-permute-done((bf16[32,1024]{1,0:T(8,128)(2,1)S(1)}, bf16[32,1024]{1,0:T(8,128)(2,1)S(1)}, u32[]{:S(2)}, u32[]{:S(2)}) %collective-permute-start.5) | collective-permute-done | bytes 65568 | tf_op jit(solution)/shard_map/ppermute | solution.py:125
  73.5 1.6 %collective-permute-done.6 = bf16[32,1024]{1,0:T(8,128)(2,1)S(1)} collective-permute-done((bf16[32,1024]{1,0:T(8,128)(2,1)S(1)}, bf16[32,1024]{1,0:T(8,128)(2,1)S(1)}, u32[]{:S(2)}, u32[]{:S(2)}) %collective-permute-start.6) | collective-permute-done | bytes 65568 | tf_op jit(solution)/shard_map/ppermute | solution.py:125
  75.1 0.7 fusion.6
  (38 shorter events, 0.3 us)
Async XLA Ops:
  0.6 1.6 %copy-start = (f32[4,128,1024]{2,1,0:T(8,128)S(1)}, f32[4,128,1024]{2,1,0:T(8,128)}, u32[]{:S(2)}) copy-start(f32[4,128,1024]{2,1,0:T(8,128)} %x_ref.5) | copy-start | bytes 6291460
  2.2 1.2 %copy-start.2 = (f32[1024,256]{1,0:T(8,128)S(1)}, f32[1024,256]{1,0:T(8,128)}, u32[]{:S(2)}) copy-start(f32[1024,256]{1,0:T(8,128)} %f_ref.1) | copy-start | bytes 3145732
  3.4 6.8 %copy-start.4 = (bf16[128,256]{1,0:T(8,128)(2,1)S(1)}, bf16[128,256]{1,0:T(8,128)(2,1)}, u32[]{:S(2)}) copy-start(bf16[128,256]{1,0:T(8,128)(2,1)} %param.5) | copy-start | bytes 196612
  3.5 7.1 %copy-start.1 = (f32[4,128,1024]{2,1,0:T(8,128)S(1)}, f32[4,128,1024]{2,1,0:T(8,128)}, u32[]{:S(2)}) copy-start(f32[4,128,1024]{2,1,0:T(8,128)} %x_ref.5) | copy-start | bytes 6291460
  4.5 26.7 %collective-permute-start.7 = (bf16[128,1024]{1,0:T(8,128)(2,1)S(1)}, bf16[128,1024]{1,0:T(8,128)(2,1)S(1)}, u32[]{:S(2)}, u32[]{:S(2)}) collective-permute-start(bf16[128,1024]{1,0:T(8,128)(2,1)S(1)} %core.1), channel_id=1, source_target_pairs={{0,4},{4,0},{8,12},{12,8},{16,20},{20,16},{24,28},{28,24},{1,5},{5... | collective-permute-start | bytes 786440 | tf_op jit(solution)/shard_map/ppermute | solution.py:125
  5.0 23.5 %collective-permute-start.8 = (bf16[128,1024]{1,0:T(8,128)(2,1)S(1)}, bf16[128,1024]{1,0:T(8,128)(2,1)S(1)}, u32[]{:S(2)}, u32[]{:S(2)}) collective-permute-start(bf16[128,1024]{1,0:T(8,128)(2,1)S(1)} %core.1), channel_id=1, source_target_pairs={{0,8},{4,12},{8,0},{12,4},{16,24},{20,28},{24,16},{28,20},{1,9},{5... | collective-permute-start | bytes 786440 | tf_op jit(solution)/shard_map/ppermute | solution.py:125
  7.6 20.9 %collective-permute-start.10 = (bf16[128,1024]{1,0:T(8,128)(2,1)S(1)}, bf16[128,1024]{1,0:T(8,128)(2,1)S(1)}, u32[]{:S(2)}, u32[]{:S(2)}) collective-permute-start(bf16[128,1024]{1,0:T(8,128)(2,1)S(1)} %core.1), channel_id=1, source_target_pairs={{0,16},{4,20},{8,24},{12,28},{16,0},{20,4},{24,8},{28,12},{1,17},{... | collective-permute-start | bytes 786440 | tf_op jit(solution)/shard_map/ppermute | solution.py:125
  10.4 4.9 %collective-permute-start.17 = (bf16[128,4,32]{0,2,1:T(8,128)(2,1)S(1)}, bf16[128,4,32]{0,2,1:T(8,128)(2,1)S(1)}, u32[]{:S(2)}, u32[]{:S(2)}) collective-permute-start(bf16[128,4,32]{0,2,1:T(8,128)(2,1)S(1)} %get-tuple-element.21), channel_id=1, source_target_pairs={{0,4},{4,0},{8,12},{12,8},{16,20},{20,16},{24,28},{28,24},{1,5},{5... | collective-permute-start | bytes 98312 | tf_op jit(solution)/shard_map/ppermute | solution.py:125
  14.0 33.0 %collective-permute-start = (bf16[4,128,1024]{2,1,0:T(8,128)(2,1)}, bf16[4,128,1024]{2,1,0:T(8,128)(2,1)}, u32[]{:S(2)}, u32[]{:S(2)}) collective-permute-start(bf16[4,128,1024]{2,1,0:T(8,128)(2,1)} %gram_away.1), channel_id=1, source_target_pairs={{0,4},{4,0},{8,12},{12,8},{16,20},{20,16},{24,28},{28,24},{1,5},{5... | collective-permute-start | bytes 3145736 | tf_op jit(solution)/shard_map/ppermute | solution.py:125
  15.3 7.5 %collective-permute-start.20 = (bf16[2,128,32]{1,2,0:T(8,128)(2,1)S(1)}, bf16[2,128,32]{1,2,0:T(8,128)(2,1)S(1)}, u32[]{:S(2)}, u32[]{:S(2)}) collective-permute-start(bf16[2,128,32]{1,2,0:T(8,128)(2,1)S(1)} %get-tuple-element.20), channel_id=1, source_target_pairs={{0,24},{4,28},{8,16},{12,20},{16,8},{20,12},{24,0},{28,4},{1,25},{... | collective-permute-start | bytes 49160 | tf_op jit(solution)/shard_map/ppermute | solution.py:125
  22.8 4.6 %collective-permute-start.19 = (bf16[2,128,32]{1,2,0:T(8,128)(2,1)S(1)}, bf16[2,128,32]{1,2,0:T(8,128)(2,1)S(1)}, u32[]{:S(2)}, u32[]{:S(2)}) collective-permute-start(bf16[2,128,32]{1,2,0:T(8,128)(2,1)S(1)} %get-tuple-element.19), channel_id=1, source_target_pairs={{0,16},{4,20},{8,24},{12,28},{16,0},{20,4},{24,8},{28,12},{1,17},{... | collective-permute-start | bytes 49160 | tf_op jit(solution)/shard_map/ppermute | solution.py:125
  27.5 3.7 %collective-permute-start.18 = (bf16[2,128,32]{1,2,0:T(8,128)(2,1)S(1)}, bf16[2,128,32]{1,2,0:T(8,128)(2,1)S(1)}, u32[]{:S(2)}, u32[]{:S(2)}) collective-permute-start(bf16[2,128,32]{1,2,0:T(8,128)(2,1)S(1)} %get-tuple-element.18), channel_id=1, source_target_pairs={{0,8},{4,12},{8,0},{12,4},{16,24},{20,28},{24,16},{28,20},{1,9},{5... | collective-permute-start | bytes 49160 | tf_op jit(solution)/shard_map/ppermute | solution.py:125
  28.5 8.7 %collective-permute-start.9 = (bf16[128,1024]{1,0:T(8,128)(2,1)S(1)}, bf16[128,1024]{1,0:T(8,128)(2,1)S(1)}, u32[]{:S(2)}, u32[]{:S(2)}) collective-permute-start(bf16[128,1024]{1,0:T(8,128)(2,1)S(1)} %collective-permute-done.8), channel_id=1, source_target_pairs={{0,4},{4,0},{8,12},{12,8},{16,20},{20,16},{24,28},{28,24},{1,5},{5... | collective-permute-start | bytes 786440 | tf_op jit(solution)/shard_map/ppermute | solution.py:125
  28.5 8.7 %collective-permute-start.12 = (bf16[128,1024]{1,0:T(8,128)(2,1)S(1)}, bf16[128,1024]{1,0:T(8,128)(2,1)S(1)}, u32[]{:S(2)}, u32[]{:S(2)}) collective-permute-start(bf16[128,1024]{1,0:T(8,128)(2,1)S(1)} %collective-permute-done.10), channel_id=1, source_target_pairs={{0,8},{4,12},{8,0},{12,4},{16,24},{20,28},{24,16},{28,20},{1,9},{5... | collective-permute-start | bytes 786440 | tf_op jit(solution)/shard_map/ppermute | solution.py:125
  31.2 7.5 %collective-permute-start.11 = (bf16[128,1024]{1,0:T(8,128)(2,1)S(1)}, bf16[128,1024]{1,0:T(8,128)(2,1)S(1)}, u32[]{:S(2)}, u32[]{:S(2)}) collective-permute-start(bf16[128,1024]{1,0:T(8,128)(2,1)S(1)} %collective-permute-done.10), channel_id=1, source_target_pairs={{0,4},{4,0},{8,12},{12,8},{16,20},{20,16},{24,28},{28,24},{1,5},{5... | collective-permute-start | bytes 786440 | tf_op jit(solution)/shard_map/ppermute | solution.py:125
  37.2 3.0 %collective-permute-start.13 = (bf16[128,1024]{1,0:T(8,128)(2,1)S(1)}, bf16[128,1024]{1,0:T(8,128)(2,1)S(1)}, u32[]{:S(2)}, u32[]{:S(2)}) collective-permute-start(bf16[128,1024]{1,0:T(8,128)(2,1)S(1)} %collective-permute-done.12), channel_id=1, source_target_pairs={{0,4},{4,0},{8,12},{12,8},{16,20},{20,16},{24,28},{28,24},{1,5},{5... | collective-permute-start | bytes 786440 | tf_op jit(solution)/shard_map/ppermute | solution.py:125
  43.4 10.6 %collective-permute-start.14 = (bf16[32,1024]{1,0:T(8,128)(2,1)S(1)}, bf16[32,1024]{1,0:T(8,128)(2,1)S(1)}, u32[]{:S(2)}, u32[]{:S(2)}) collective-permute-start(bf16[32,1024]{1,0:T(8,128)(2,1)S(1)} %get-tuple-element.11), channel_id=1, source_target_pairs={{0,1},{1,0},{2,3},{3,2},{4,5},{5,4},{6,7},{7,6},{8,9},{9,8},{10,11... | collective-permute-start | bytes 196616 | tf_op jit(solution)/shard_map/ppermute | solution.py:125
  44.9 10.8 %collective-permute-start.15 = (bf16[32,1024]{1,0:T(8,128)(2,1)S(1)}, bf16[32,1024]{1,0:T(8,128)(2,1)S(1)}, u32[]{:S(2)}, u32[]{:S(2)}) collective-permute-start(bf16[32,1024]{1,0:T(8,128)(2,1)S(1)} %get-tuple-element.13), channel_id=1, source_target_pairs={{0,2},{1,3},{2,0},{3,1},{4,6},{5,7},{6,4},{7,5},{8,10},{9,11},{10,... | collective-permute-start | bytes 196616 | tf_op jit(solution)/shard_map/ppermute | solution.py:125
  46.5 8.2 %copy-start.3 = (bf16[1024,1024]{1,0:T(8,128)(2,1)S(1)}, bf16[1024,1024]{1,0:T(8,128)(2,1)}, u32[]{:S(2)}) copy-start(bf16[1024,1024]{1,0:T(8,128)(2,1)} %constant_dynamic-update-slice_fusion) | copy-start | bytes 6291460
  46.5 9.3 %collective-permute-start.16 = (bf16[32,1024]{1,0:T(8,128)(2,1)S(1)}, bf16[32,1024]{1,0:T(8,128)(2,1)S(1)}, u32[]{:S(2)}, u32[]{:S(2)}) collective-permute-start(bf16[32,1024]{1,0:T(8,128)(2,1)S(1)} %get-tuple-element.12), channel_id=1, source_target_pairs={{0,3},{1,2},{2,1},{3,0},{4,7},{5,6},{6,5},{7,4},{8,11},{9,10},{10,... | collective-permute-start | bytes 196616 | tf_op jit(solution)/shard_map/ppermute | solution.py:125
  51.1 9.3 %collective-permute-start.1 = (bf16[4,32,1024]{2,1,0:T(8,128)(2,1)S(1)}, bf16[4,32,1024]{2,1,0:T(8,128)(2,1)S(1)}, u32[]{:S(2)}, u32[]{:S(2)}) collective-permute-start(bf16[4,32,1024]{2,1,0:T(8,128)(2,1)S(1)} %get-tuple-element.8), channel_id=1, source_target_pairs={{0,1},{1,0},{2,3},{3,2},{4,5},{5,4},{6,7},{7,6},{8,9},{9,8},{10,11... | collective-permute-start | bytes 786440 | tf_op jit(solution)/shard_map/ppermute | solution.py:125
  52.5 13.2 %collective-permute-start.2 = (bf16[4,32,1024]{2,1,0:T(8,128)(2,1)S(1)}, bf16[4,32,1024]{2,1,0:T(8,128)(2,1)S(1)}, u32[]{:S(2)}, u32[]{:S(2)}) collective-permute-start(bf16[4,32,1024]{2,1,0:T(8,128)(2,1)S(1)} %get-tuple-element.9), channel_id=1, source_target_pairs={{0,2},{1,3},{2,0},{3,1},{4,6},{5,7},{6,4},{7,5},{8,10},{9,11},{10,... | collective-permute-start | bytes 786440 | tf_op jit(solution)/shard_map/ppermute | solution.py:125
  54.0 11.7 %collective-permute-start.3 = (bf16[4,32,1024]{2,1,0:T(8,128)(2,1)S(1)}, bf16[4,32,1024]{2,1,0:T(8,128)(2,1)S(1)}, u32[]{:S(2)}, u32[]{:S(2)}) collective-permute-start(bf16[4,32,1024]{2,1,0:T(8,128)(2,1)S(1)} %get-tuple-element.10), channel_id=1, source_target_pairs={{0,3},{1,2},{2,1},{3,0},{4,7},{5,6},{6,5},{7,4},{8,11},{9,10},{10,... | collective-permute-start | bytes 786440 | tf_op jit(solution)/shard_map/ppermute | solution.py:125
  65.9 5.1 %collective-permute-start.4 = (bf16[32,1024]{1,0:T(8,128)(2,1)S(1)}, bf16[32,1024]{1,0:T(8,128)(2,1)S(1)}, u32[]{:S(2)}, u32[]{:S(2)}) collective-permute-start(bf16[32,1024]{1,0:T(8,128)(2,1)S(1)} %get-tuple-element.14), channel_id=1, source_target_pairs={{0,8},{4,12},{8,0},{12,4},{16,24},{20,28},{24,16},{28,20},{1,9},{5... | collective-permute-start | bytes 196616 | tf_op jit(solution)/shard_map/ppermute | solution.py:125
  67.0 6.6 %collective-permute-start.5 = (bf16[32,1024]{1,0:T(8,128)(2,1)S(1)}, bf16[32,1024]{1,0:T(8,128)(2,1)S(1)}, u32[]{:S(2)}, u32[]{:S(2)}) collective-permute-start(bf16[32,1024]{1,0:T(8,128)(2,1)S(1)} %get-tuple-element.16), channel_id=1, source_target_pairs={{0,16},{4,20},{8,24},{12,28},{16,0},{20,4},{24,8},{28,12},{1,17},{... | collective-permute-start | bytes 196616 | tf_op jit(solution)/shard_map/ppermute | solution.py:125
  69.0 6.1 %collective-permute-start.6 = (bf16[32,1024]{1,0:T(8,128)(2,1)S(1)}, bf16[32,1024]{1,0:T(8,128)(2,1)S(1)}, u32[]{:S(2)}, u32[]{:S(2)}) collective-permute-start(bf16[32,1024]{1,0:T(8,128)(2,1)S(1)} %get-tuple-element.15), channel_id=1, source_target_pairs={{0,24},{4,28},{8,16},{12,20},{16,8},{20,12},{24,0},{28,4},{1,25},{... | collective-permute-start | bytes 196616 | tf_op jit(solution)/shard_map/ppermute | solution.py:125

commit v2 on v0

v2 whole, which is shorter than its diff:
```python
import functools
import math

import jax
import jax.numpy as jnp
from jax import lax
from jax.experimental import pallas as pl
from jax.experimental.pallas import tpu as pltpu
from jax.sharding import PartitionSpec as P

F32 = jnp.float32
BF16 = jnp.bfloat16
NN = (((1,), (0,)), ((), ()))
NT = (((1,), (1,)), ((), ()))
TN = (((0,), (0,)), ((), ()))
VMEM = pl.BlockSpec(memory_space=pltpu.VMEM)
SMEM = pl.BlockSpec(memory_space=pltpu.SMEM)
ANY = pl.BlockSpec(memory_space=pl.ANY)


def halves(x):
    high = x.astype(BF16)
    return high, (x - high.astype(F32)).astype(BF16)


def dot1(a, b, dims):
    return lax.dot_general(a, b, dims, preferred_element_type=F32)


def dot3(a, b, dims):
    return dot1(a[0], b[0], dims) + (dot1(a[0], b[1], dims) + dot1(a[1], b[0], dims))


def call(kernel, name, flops, outs, in_specs, *args, scratch=()):
    out_shape = [jax.ShapeDtypeStruct(s, d) for s, d in outs]
    moved = sum(a.size * a.dtype.itemsize for a in (*args, *out_shape))
    return pl.pallas_call(
        kernel,
        out_shape=out_shape,
        in_specs=in_specs,
        out_specs=[VMEM] * len(outs),
        scratch_shapes=list(scratch),
        compiler_params=pltpu.CompilerParams(vmem_limit_bytes=20 * 1024 * 1024),
        cost_estimate=pl.CostEstimate(flops=flops, bytes_accessed=moved, transcendentals=0),
        name=name,
    )(*args)


def core_kernel(x_hbm, f_hbm, u_ref, high_ref, low_ref, x_ref, f_ref, x_sem, f_sem):
    slices, owned, _ = x_ref.shape
    rank = f_ref.shape[1]
    f_copy = pltpu.make_async_copy(f_hbm, f_ref, f_sem)
    f_copy.start()
    copies = []
    for k in range(slices):
        copies.append(pltpu.make_async_copy(x_hbm.at[k], x_ref.at[k], x_sem.at[k]))
        copies[k].start()
    f_copy.wait()
    f = halves(f_ref[...])
    for k in range(slices):
        copies[k].wait()
        x = halves(x_ref[k])
        high_ref[k * owned : (k + 1) * owned] = x[0]
        low_ref[k * owned : (k + 1) * owned] = x[1]
        u_ref[:, k * rank : (k + 1) * rank] = dot3(x, f, NN).astype(BF16)


def own_columns(ref, core, groups, step):
    at = [pl.multiple_of((2 * g + core) * step, step) for g in range(groups)]
    return jnp.concatenate([ref[:, pl.ds(a, step)] for a in at], axis=1)


def gram_rows(core, high_ref, low_ref, groups, step):
    left = [own_columns(ref, core, groups, step) for ref in (high_ref, low_ref)]
    return dot3(left, (high_ref[...], low_ref[...]), TN)


def gram_away_kernel(place_ref, high_ref, low_ref, away_ref):
    groups, step, width = away_ref.shape
    rows = gram_rows(1 - place_ref[0], high_ref, low_ref, groups, step)
    away_ref[...] = rows.astype(BF16).reshape(groups, step, width)


def gram_home_kernel(place_ref, high_ref, low_ref, came_ref, *outs):
    *outs, rows_ref = outs
    groups, step, width = came_ref.shape
    block = step // len(outs)
    rows = gram_rows(place_ref[0], high_ref, low_ref, groups, step)
    rows_ref[...] = rows.reshape(groups, step, width) + came_ref[...].astype(F32)
    for t, out in enumerate(outs):
        at = pl.multiple_of((place_ref[1] ^ t) * block, block)
        out[...] = rows_ref[:, pl.ds(at, block)].astype(out.dtype)


def early_kernel(pairs, u_ref, *refs):
    blocks, columns, (gram_ref, sum_ref) = refs[: 2 * pairs], refs[2 * pairs : -2], refs[-2:]
    owned = u_ref.shape[0]
    total = None
    for i, block in enumerate(blocks):
        gram_ref[:, i * owned : (i + 1) * owned] = dot1(u_ref[...], block[...], NT)
        part = dot1(columns[i // 2][i % 2], block[...], TN)
        total = part if total is None else total + part
    sum_ref[...] = total


def late_kernel(pairs, scale, place_ref, u_ref, *refs):
    blocks, columns = refs[: 2 * pairs], refs[2 * pairs : 3 * pairs]
    gram_ref, sum_ref, *outs, reduced_ref, rows_ref = refs[3 * pairs :]
    owned = u_ref.shape[0]
    before = gram_ref.shape[1]
    slices, _, rank = reduced_ref.shape
    rows_ref[:, :before] = gram_ref[...]
    total = sum_ref[...]
    for i, block in enumerate(blocks):
        at = before + i * owned
        rows_ref[:, at : at + owned] = dot1(u_ref[...], block[...], NT)
    height = owned // len(outs)
    for t, out in enumerate(outs):
        at = pl.multiple_of((place_ref[1] ^ t) * height, height)
        out[...] = (rows_ref[pl.ds(at, height)] * scale).astype(out.dtype)
    for i, block in enumerate(blocks):
        total = total + dot1(columns[i // 2][i % 2], block[...], TN)
    for k in range(slices):
        reduced_ref[k] = total[:, k * rank : (k + 1) * rank]


def settle_kernel(order, place_ref, *refs):
    *parts, out_ref = refs
    width = out_ref.shape[1] // len(order)
    for i, b in enumerate(order):
        block = parts[0][:, i * width : (i + 1) * width]
        for part in parts[1:]:
            block = block + part[:, i * width : (i + 1) * width].astype(F32)
        at = pl.multiple_of((place_ref[2] ^ b) * width, width)
        out_ref[:, pl.ds(at, width)] = block


def xor_permute(x, axis, bits):
    return lax.ppermute(x, axis, [(i, i ^ bits) for i in range(lax.axis_size(axis))])


def pick(x, index, axis):
    return lax.dynamic_index_in_dim(x, index, axis, keepdims=False)


def after(x, *others):
    return lax.optimization_barrier((x, *others))[0]


def shards(tensor, factor_one, factor_two):
    slices, owned, width = tensor.shape
    count_ja = lax.axis_size("ja")
    count_ka = lax.axis_size("ka")
    count_z = count_ja // 2
    rank_one = factor_one.shape[1]
    rank_two = factor_two.shape[1]
    ja = lax.axis_index("ja")
    ka = lax.axis_index("ka")
    core_at, z = lax.rem(ja, 2), lax.div(ja, 2)
    place = jnp.stack([core_at, ka, ja]).astype(jnp.int32)
    step = width // count_ja
    tiled = step % 128 == 0 and owned % 128 == 0
    tiled = tiled and (step // count_ka) % 16 == 0 and (owned // count_ka) % 16 == 0
    norm_one = 1.0 / math.sqrt(owned * count_ja * slices * count_ka)
    norm_two = 1.0 / math.sqrt(slices * count_ka * rank_one)

    part = rank_two // count_ja
    cut = factor_two.reshape(owned, count_z, 2, part)
    f2 = [pick(cut, core_at, 2), xor_permute(pick(cut, 1 - core_at, 2), "ja", 1)]
    f2 = jnp.stack(f2).transpose(2, 0, 1, 3)
    f2 = [pick(f2, z ^ t, 0) for t in range(count_z)]

    u, high, low = call(
        core_kernel,
        "core",
        6 * tensor.size * rank_one,
        [
            ((owned, slices * rank_one), BF16),
            ((slices * owned, width), BF16),
            ((slices * owned, width), BF16),
        ],
        [ANY, ANY],
        tensor,
        factor_one,
        scratch=[
            pltpu.VMEM(tensor.shape, F32),
            pltpu.VMEM(factor_one.shape, F32),
            pltpu.SemaphoreType.DMA((slices,)),
            pltpu.SemaphoreType.DMA,
        ],
    )
    f2 = list(after(tuple(f2), u))

    got = {0: u}
    bits = [1 << b for b in range(count_z.bit_length() - 1)]
    for t in bits:
        got[t] = xor_permute(u, "ja", 2 * t)

    if tiled:
        (sent,) = call(
            gram_away_kernel,
            "gram_away",
            3 * tensor.size * width,
            [((count_z, step, width), BF16)],
            [SMEM, VMEM, VMEM],
            place,
            high,
            low,
        )
        came = xor_permute(sent, "ja", 1)
        shape = (count_z, step // count_ka, width)
        pieces = call(
            gram_home_kernel,
            "gram_home",
            3 * tensor.size * width,
            [(shape, F32 if t == 0 else BF16) for t in range(count_ka)],
            [SMEM, VMEM, VMEM, VMEM],
            place,
            high,
            low,
            came,
            scratch=[pltpu.VMEM(came.shape, F32)],
        )
    else:
        local = dot3((high, low), (high, low), TN).reshape(count_z, 2, step, width)
        came = xor_permute(pick(local, 1 - core_at, 1).astype(BF16), "ja", 1)
        home = pick(local, core_at, 1) + came.astype(F32)
        home = home.reshape(count_z, count_ka, step // count_ka, width)
        pieces = [pick(home, ka ^ t, 1) for t in range(count_ka)]
        pieces = [p if t == 0 else p.astype(BF16) for t, p in enumerate(pieces)]
    arrived = [xor_permute(pieces[t], "ka", t) for t in range(1, count_ka)]

    blocks = {0: (u, xor_permute(u, "ja", 1))}
    for t in bits:
        blocks[t] = (got[t], xor_permute(got[t], "ja", 1))
    for bit in reversed(bits):
        ahead = [t for t in range(count_z) if t & bit]
        moved = xor_permute(jnp.stack([f2[t] for t in ahead]), "ja", 2 * bit)
        for i, t in enumerate(ahead):
            f2[t] = moved[i]
    late = [t for t in range(count_z) if t not in blocks]
    for t in late:
        low_bit = t & -t
        got[t] = xor_permute(after(got[t ^ low_bit], pieces[0]), "ja", 2 * low_bit)
        blocks[t] = (got[t], xor_permute(got[t], "ja", 1))
    early = [t for t in blocks if t not in late]

    slab = pieces[0]
    for a in arrived:
        slab = slab + a.astype(F32)
    gram_one = pick(slab, z, 0)
    for t in range(1, count_z):
        gram_one = gram_one + xor_permute(pick(slab, z ^ t, 0).astype(BF16), "ja", 2 * t).astype(F32)
    gram_one = gram_one * norm_one

    order = [2 * t + c for t in early + late for c in range(2)]
    height = owned // count_ka
    if tiled:
        columns = slices * rank_one
        gram_part, sum_part = call(
            functools.partial(early_kernel, len(early)),
            "two_early",
            4 * len(early) * owned * columns * (owned + part),
            [((owned, 2 * len(early) * owned), F32), ((part, columns), F32)],
            [VMEM] * (1 + 3 * len(early)),
            u,
            *[b for t in early for b in blocks[t]],
            *[f2[t] for t in early],
        )
        shape = (height, count_ja * owned)
        *rows, reduced = call(
            functools.partial(late_kernel, len(late), norm_two),
            "two_late",
            4 * len(late) * owned * columns * (owned + part),
            [(shape, F32 if t == 0 else BF16) for t in range(count_ka)]
            + [((slices, part, rank_one), F32)],
            [SMEM] + [VMEM] * (3 + 3 * len(late)),
            place,
            u,
            *[b for t in late for b in blocks[t]],
            *[f2[t] for t in late],
            gram_part,
            sum_part,
            scratch=[pltpu.VMEM((owned, count_ja * owned), F32)],
        )
        rows = [rows[0]] + [xor_permute(rows[t], "ka", t) for t in range(1, count_ka)]
        (gram_two,) = call(
            functools.partial(settle_kernel, order),
            "settle",
            count_ka * rows[0].size,
            [(shape, F32)],
            [SMEM] + [VMEM] * count_ka,
            place,
            *rows,
        )
    else:
        gathered = jnp.concatenate([b for t in early + late for b in blocks[t]])
        columns = jnp.concatenate([f2[t].reshape(2 * owned, part) for t in early + late])
        rows = dot1(u, gathered, NT).reshape(count_ka, height, count_ja * owned) * norm_two
        gram_two = pick(rows, ka, 0)
        for t in range(1, count_ka):
            gram_two = gram_two + xor_permute(pick(rows, ka ^ t, 0).astype(BF16), "ka", t).astype(F32)
        places = jnp.zeros(count_ja, jnp.int32).at[jnp.array(order) ^ ja].set(jnp.arange(count_ja))
        gram_two = jnp.take(gram_two.reshape(height, count_ja, owned), places, axis=1)
        gram_two = gram_two.reshape(height, count_ja * owned)
        reduced = dot1(columns, gathered, TN).reshape(part, slices, rank_one).transpose(1, 0, 2)
    return (gram_one, gram_two, reduced)


def solution(mesh):
    in_specs = (P("ka", "ja", None), P(), P("ja", None))
    out_specs = (P(("ja", "ka"), None), P(("ja", "ka"), None), P("ka", "ja", None))
    return jax.shard_map(shards, mesh=mesh, in_specs=in_specs, out_specs=out_specs, check_vma=False)
```

time: 218 us -> 59.4 us (0.27)
  waiting for transfers between devices: 179 us -> 18.6 us
  starting transfers between devices: 0.21 us -> 22.5 us
  matrix products: 15.6 us -> 0 us
  between operations: 14.5 us -> 0.8 us
  Pallas kernels: 0 us -> 12.9 us
  local copies, waits for them, and re-layouts: 5.95 us -> 3.36 us
  other arithmetic: 3.14 us -> 0.96 us
    reduce_scatter x3 -> x0, waiting for transfers between devices: 99.5 us -> none  [the longest x1 48.5 us: shards(): lax.psum_scatter(jnp.dot(flat.T, flat, precision=lax.Precision.HIGHEST, p...]
    unnamed x6 -> x0, waiting for transfers between devices: 58.2 us -> none
    ppermute x0 -> x20, starting transfers between devices: none -> 22.5 us  [xor_permute(): lax.ppermute(x, axis, [(i, i ^ bits) for i in range(lax.axis_size(axis))])]
    all_gather x1 -> x0, waiting for transfers between devices: 20.9 us -> none  [shards(): lax.all_gather(core, 'ja', axis=1, tiled=True)]
    ppermute x0 -> x20, waiting for transfers between devices: none -> 18.6 us  [xor_permute(): lax.ppermute(x, axis, [(i, i ^ bits) for i in range(lax.axis_size(axis))])]
    dot_general x4 -> x0, matrix products: 15.6 us -> none  [the longest x1 8.29 us: shards(): jnp.dot(flat.T, flat, precision=lax.Precision.HIGHEST, preferred_element_...]
    pallas_call x0 -> x6, Pallas kernels: none -> 12.9 us  [call(): pl.pallas_call(kernel, out_shape=out_shape, in_specs=in_specs, out_specs=...]
    mul x2 -> x1, other arithmetic: 3.14 us -> 0.69 us  [shards(): gram_one = gram_one * norm_one]
  transfers between devices with their start and end apart: 5 -> 20, of which waited for: 5 -> 9; matrix products, arithmetic and copies ran while one was open for 8% -> 2% of each run, Pallas kernels for 0% -> 9%
where the time goes in v2:
time: 59.4 us; the launch traced here: 59.2 us
  starting transfers between devices  22.5 us (38%)
  waiting for transfers between devices  18.6 us (31%)
  Pallas kernels  12.9 us (22%)
  local copies, waits for them, and re-layouts  3.36 us (6%)
  other arithmetic  0.96 us (2%)
  between operations  0.8 us (1%)
    ppermute x20, starting transfers between devices, xor_permute(): lax.ppermute(x, axis, [(i, i ^ bits) for i in range(lax.axis_size(axis))])  22.5 us
    ppermute x20, waiting for transfers between devices, xor_permute(): lax.ppermute(x, axis, [(i, i ^ bits) for i in range(lax.axis_size(axis))])  18.6 us
    pallas_call x6, Pallas kernels, call(): pl.pallas_call(kernel, out_shape=out_shape, in_specs=in_specs, out_specs=...  12.9 us
    unnamed x7, local copies, waits for them, and re-layouts  2.92 us
  transfers between devices with their start and end apart: 20, of which 9 were waited for; matrix products, arithmetic and copies ran while one was open for 2% of the time, Pallas kernels for 9%

profile of v2, /device:TPU:0, one launch (start us, length us, event | category | flops | bytes accessed | tf_op | source)
XLA Modules:
  0.0 59.2 jit_solution(9589560208038844670)
XLA Ops:
  0.6 1.6 %copy-done = f32[4,128,1024]{2,1,0:T(8,128)S(1)} copy-done((f32[4,128,1024]{2,1,0:T(8,128)S(1)}, f32[4,128,1024]{2,1,0:T(8,128)}, u32[]{:S(2)}) %copy-start) | copy-done | bytes 2097176
  2.2 1.2 %copy-done.1 = f32[1024,256]{1,0:T(8,128)S(1)} copy-done((f32[1024,256]{1,0:T(8,128)S(1)}, f32[1024,256]{1,0:T(8,128)}, u32[]{:S(2)}) %copy-start.1) | copy-done | bytes 1048600
  3.5 2.7 %core.1 = (bf16[128,1024]{1,0:T(8,128)(2,1)S(1)}, bf16[512,1024]{1,0:T(8,128)(2,1)S(1)}, bf16[512,1024]{1,0:T(8,128)(2,1)S(1)}) custom-call(f32[4,128,1024]{2,1,0:T(8,128)S(1)} %copy-done, f32[1024,256]{1,0:T(8,128)S(1)} %copy-done.1), custom_call_target="tpu_custom_call" | custom-call | flops 805306368 | bytes 5505024 | tf_op jit(solution)/shard_map/core/pallas_call | solution.py:37
  6.2 0.1 pad_add_fusion.place_ref
  6.2 3.4 %gram_away.1 = bf16[4,128,1024]{2,1,0:T(8,128)(2,1)} custom-call(s32[3]{0:T(128)S(1)} %pad_add_fusion.place_ref, bf16[512,1024]{1,0:T(8,128)(2,1)S(1)} %get-tuple-element.22.high_ref, bf16[512,1024]{1,0:T(8,128)(2,1)S(1)} %get-tuple-element.23.low_ref), custom_call_target="tpu_custom_call" | custom-call | flops 1610612736 | bytes 3145740 | tf_op jit(solution)/shard_map/gram_away/pallas_call | solution.py:37
  9.6 0.5 collective-permute-start
  10.1 0.1 copy.19
  10.2 0.1 collective-permute-start.10
  10.3 4.0 %collective-permute-start.7 = (bf16[128,1024]{1,0:T(8,128)(2,1)S(1)}, bf16[128,1024]{1,0:T(8,128)(2,1)S(1)}, u32[]{:S(2)}, u32[]{:S(2)}) collective-permute-start(bf16[128,1024]{1,0:T(8,128)(2,1)S(1)} %get-tuple-element.28.u_ref.refs_0_), channel_id=1, source_target_pairs={{0,16},{4,20},{8,24},{12,28},{16,0},{20,4},{24,8},{28,12},{1,17},{... | collective-permute-start | bytes 786440 | tf_op jit(solution)/shard_map/ppermute | solution.py:139
  14.4 1.6 %collective-permute-start.14 = (bf16[128,1024]{1,0:T(8,128)(2,1)S(1)}, bf16[128,1024]{1,0:T(8,128)(2,1)S(1)}, u32[]{:S(2)}, u32[]{:S(2)}) collective-permute-start(bf16[128,1024]{1,0:T(8,128)(2,1)S(1)} %get-tuple-element.28.u_ref.refs_0_), channel_id=1, source_target_pairs={{0,8},{4,12},{8,0},{12,4},{16,24},{20,28},{24,16},{28,20},{1,9},{5... | collective-permute-start | bytes 786440 | tf_op jit(solution)/shard_map/ppermute | solution.py:139
  16.0 0.0 collective-permute-done.10
  16.0 0.1 copy.20
  16.1 0.1 copy.21
  16.2 0.1 copy.22
  16.4 0.5 collective-permute-start.11
  16.9 3.2 %gram_home.1 = (f32[4,32,1024]{2,1,0:T(8,128)S(1)}, bf16[4,32,1024]{2,1,0:T(8,128)(2,1)S(1)}, bf16[4,32,1024]{2,1,0:T(8,128)(2,1)S(1)}, bf16[4,32,1024]{2,1,0:T(8,128)(2,1)S(1)}) custom-call(s32[3]{0:T(128)S(1)} %pad_add_fusion.place_ref, bf16[512,1024]{1,0:T(8,128)(2,1)S(1)} %get-tuple-element.22.high_ref, bf16[512,1024]{1,0:T(8,128)(2,1)S(1)} %get-tuple-element.23.low_ref, ...), custom_call_target="tpu_custom_call" | custom-call | flops 1610612736 | bytes 4456460 | tf_op jit(solution)/shard_map/gram_home/pallas_call | solution.py:37
  20.1 2.5 %collective-permute-start.3 = (bf16[4,32,1024]{2,1,0:T(8,128)(2,1)S(1)}, bf16[4,32,1024]{2,1,0:T(8,128)(2,1)S(1)}, u32[]{:S(2)}, u32[]{:S(2)}) collective-permute-start(bf16[4,32,1024]{2,1,0:T(8,128)(2,1)S(1)} %get-tuple-element.27), channel_id=1, source_target_pairs={{0,3},{1,2},{2,1},{3,0},{4,7},{5,6},{6,5},{7,4},{8,11},{9,10},{10,... | collective-permute-start | bytes 786440 | tf_op jit(solution)/shard_map/ppermute | solution.py:139
  22.6 0.5 collective-permute-start.2
  23.1 4.4 %collective-permute-done.7.refs_4_ = bf16[128,1024]{1,0:T(8,128)(2,1)S(1)} collective-permute-done((bf16[128,1024]{1,0:T(8,128)(2,1)S(1)}, bf16[128,1024]{1,0:T(8,128)(2,1)S(1)}, u32[]{:S(2)}, u32[]{:S(2)}) %collective-permute-start.7) | collective-permute-done | bytes 262176 | tf_op jit(solution)/shard_map/ppermute | solution.py:139
  27.5 2.2 %collective-permute-start.1 = (bf16[4,32,1024]{2,1,0:T(8,128)(2,1)S(1)}, bf16[4,32,1024]{2,1,0:T(8,128)(2,1)S(1)}, u32[]{:S(2)}, u32[]{:S(2)}) collective-permute-start(bf16[4,32,1024]{2,1,0:T(8,128)(2,1)S(1)} %get-tuple-element.25), channel_id=1, source_target_pairs={{0,1},{1,0},{2,3},{3,2},{4,5},{5,4},{6,7},{7,6},{8,9},{9,8},{10,11... | collective-permute-start | bytes 786440 | tf_op jit(solution)/shard_map/ppermute | solution.py:139
  29.7 2.5 %collective-permute-done.11 = bf16[2,2,128,32]{3,2,1,0:T(8,128)(2,1)S(1)} collective-permute-done((bf16[2,2,128,32]{3,2,1,0:T(8,128)(2,1)S(1)}, bf16[2,2,128,32]{3,2,1,0:T(8,128)(2,1)S(1)}, u32[]{:S(2)}, u32[]{:S(2)}) %collective-permute-start.11) | collective-permute-done | bytes 32800 | tf_op jit(solution)/shard_map/ppermute | solution.py:139
  32.2 0.7 %collective-permute-start.8 = (bf16[128,1024]{1,0:T(8,128)(2,1)S(1)}, bf16[128,1024]{1,0:T(8,128)(2,1)S(1)}, u32[]{:S(2)}, u32[]{:S(2)}) collective-permute-start(bf16[128,1024]{1,0:T(8,128)(2,1)S(1)} %collective-permute-done.7.refs_4_), channel_id=1, source_target_pairs={{0,8},{4,12},{8,0},{12,4},{16,24},{20,28},{24,16},{28,20},{1,9},{5... | collective-permute-start | bytes 786440 | tf_op jit(solution)/shard_map/ppermute | solution.py:139
  32.9 0.0 collective-permute-done.14.refs_2_
  33.0 0.1 collective-permute-start.13
  33.0 0.0 collective-permute-done.3
  33.0 1.4 %collective-permute-start.12 = (bf16[2,2,128,32]{3,2,1,0:T(8,128)(2,1)S(1)}, bf16[2,2,128,32]{3,2,1,0:T(8,128)(2,1)S(1)}, u32[]{:S(2)}, u32[]{:S(2)}) collective-permute-start(bf16[2,2,128,32]{3,2,1,0:T(8,128)(2,1)S(1)} %pad_maximum_fusion), channel_id=1, source_target_pairs={{0,8},{4,12},{8,0},{12,4},{16,24},{20,28},{24,16},{28,20},{1,9},{5... | collective-permute-start | bytes 98312 | tf_op jit(solution)/shard_map/ppermute | solution.py:139
  34.5 0.2 collective-permute-done.2
  34.7 0.0 collective-permute-start.16
  34.7 0.1 collective-permute-done.1
  34.8 0.4 collective-permute-start.15
  35.2 6.2 %collective-permute-done.8.refs_0_ = bf16[128,1024]{1,0:T(8,128)(2,1)S(1)} collective-permute-done((bf16[128,1024]{1,0:T(8,128)(2,1)S(1)}, bf16[128,1024]{1,0:T(8,128)(2,1)S(1)}, u32[]{:S(2)}, u32[]{:S(2)}) %collective-permute-start.8) | collective-permute-done | bytes 262176 | tf_op jit(solution)/shard_map/ppermute | solution.py:139
  41.4 0.1 convert_add_fusion
  41.6 1.2 %collective-permute-done.12 = bf16[2,2,128,32]{3,2,1,0:T(8,128)(2,1)S(1)} collective-permute-done((bf16[2,2,128,32]{3,2,1,0:T(8,128)(2,1)S(1)}, bf16[2,2,128,32]{3,2,1,0:T(8,128)(2,1)S(1)}, u32[]{:S(2)}, u32[]{:S(2)}) %collective-permute-start.12) | collective-permute-done | bytes 32800 | tf_op jit(solution)/shard_map/ppermute | solution.py:139
  42.8 4.0 %collective-permute-start.6 = (bf16[32,1024]{1,0:T(8,128)(2,1)S(1)}, bf16[32,1024]{1,0:T(8,128)(2,1)S(1)}, u32[]{:S(2)}, u32[]{:S(2)}) collective-permute-start(bf16[32,1024]{1,0:T(8,128)(2,1)S(1)} %get-tuple-element.42), channel_id=1, source_target_pairs={{0,24},{4,28},{8,16},{12,20},{16,8},{20,12},{24,0},{28,4},{1,25},{... | collective-permute-start | bytes 196616 | tf_op jit(solution)/shard_map/ppermute | solution.py:139
  46.8 0.0 collective-permute-start.5
  46.8 0.0 collective-permute-done.15.refs_3_
  46.8 0.6 collective-permute-start.4
  47.4 0.8 %two_early.1 = (f32[128,768]{1,0:T(8,128)S(1)}, f32[32,1024]{1,0:T(8,128)S(1)}) custom-call(bf16[128,1024]{1,0:T(8,128)(2,1)S(1)} %get-tuple-element.28.u_ref.refs_0_, bf16[128,1024]{1,0:T(8,128)(2,1)S(1)} %get-tuple-element.28.u_ref.refs_0_, bf16[128,1024]{1,0:T(8,128)(2,1)S(1)} %collective-permute-done.13.refs_1_, ...), custom_call_target="tpu_custom_call" | custom-call | flops 251658240 | bytes 2408448 | tf_op jit(solution)/shard_map/two_early/pallas_call | solution.py:37
  48.2 0.0 collective-permute-done.9.refs_1_
  48.2 1.6 %two_late.1 = (f32[32,1024]{1,0:T(8,128)S(1)}, bf16[32,1024]{1,0:T(8,128)(2,1)S(1)}, bf16[32,1024]{1,0:T(8,128)(2,1)S(1)}, bf16[32,1024]{1,0:T(8,128)(2,1)S(1)}, f32[4,32,256]{2,1,0:T(8,128)}) custom-call(s32[3]{0:T(128)S(1)} %pad_add_fusion.place_ref, bf16[128,1024]{1,0:T(8,128)(2,1)S(1)} %get-tuple-element.28.u_ref.refs_0_, ...), custom_call_target="tpu_custom_call" | custom-call | flops 83886080 | bytes 1785868 | tf_op jit(solution)/shard_map/two_late/pallas_call | solution.py:37
  49.8 1.5 %collective-permute-start.17 = (bf16[32,1024]{1,0:T(8,128)(2,1)S(1)}, bf16[32,1024]{1,0:T(8,128)(2,1)S(1)}, u32[]{:S(2)}, u32[]{:S(2)}) collective-permute-start(bf16[32,1024]{1,0:T(8,128)(2,1)S(1)} %get-tuple-element.37), channel_id=1, source_target_pairs={{0,1},{1,0},{2,3},{3,2},{4,5},{5,4},{6,7},{7,6},{8,9},{9,8},{10,11... | collective-permute-start | bytes 196616 | tf_op jit(solution)/shard_map/ppermute | solution.py:139
  51.3 1.5 %collective-permute-start.18 = (bf16[32,1024]{1,0:T(8,128)(2,1)S(1)}, bf16[32,1024]{1,0:T(8,128)(2,1)S(1)}, u32[]{:S(2)}, u32[]{:S(2)}) collective-permute-start(bf16[32,1024]{1,0:T(8,128)(2,1)S(1)} %get-tuple-element.38), channel_id=1, source_target_pairs={{0,2},{1,3},{2,0},{3,1},{4,6},{5,7},{6,4},{7,5},{8,10},{9,11},{10,... | collective-permute-start | bytes 196616 | tf_op jit(solution)/shard_map/ppermute | solution.py:139
  52.8 0.5 collective-permute-start.19
  53.3 0.7 %fusion.2 = f32[32,1024]{1,0:T(8,128)} fusion(bf16[32,1024]{1,0:T(8,128)(2,1)S(1)} %collective-permute-done.6, bf16[32,1024]{1,0:T(8,128)(2,1)S(1)} %collective-permute-done.5, bf16[32,1024]{1,0:T(8,128)(2,1)S(1)} %collective-permute-done.4, f32[4,32,1024]{2,1,0:T(8,128)S(1)} %convert_add_fusion, s32[]{:T(128)S(6)} %select_n.25), kind=kLoop, calls=%fused_computation.5 | loop fusion | flops 229376 | bytes 458756 | tf_op jit(solution)/shard_map/mul | solution.py:254
  54.0 0.7 %collective-permute-done.17.refs_1_ = bf16[32,1024]{1,0:T(8,128)(2,1)S(1)} collective-permute-done((bf16[32,1024]{1,0:T(8,128)(2,1)S(1)}, bf16[32,1024]{1,0:T(8,128)(2,1)S(1)}, u32[]{:S(2)}, u32[]{:S(2)}) %collective-permute-start.17) | collective-permute-done | bytes 65568 | tf_op jit(solution)/shard_map/ppermute | solution.py:139
  54.7 1.3 %collective-permute-done.18.refs_2_ = bf16[32,1024]{1,0:T(8,128)(2,1)S(1)} collective-permute-done((bf16[32,1024]{1,0:T(8,128)(2,1)S(1)}, bf16[32,1024]{1,0:T(8,128)(2,1)S(1)}, u32[]{:S(2)}, u32[]{:S(2)}) %collective-permute-start.18) | collective-permute-done | bytes 65568 | tf_op jit(solution)/shard_map/ppermute | solution.py:139
  56.0 2.0 %collective-permute-done.19.refs_3_ = bf16[32,1024]{1,0:T(8,128)(2,1)S(1)} collective-permute-done((bf16[32,1024]{1,0:T(8,128)(2,1)S(1)}, bf16[32,1024]{1,0:T(8,128)(2,1)S(1)}, u32[]{:S(2)}, u32[]{:S(2)}) %collective-permute-start.19) | collective-permute-done | bytes 65568 | tf_op jit(solution)/shard_map/ppermute | solution.py:139
  58.0 1.2 %settle.1 = f32[32,1024]{1,0:T(8,128)} custom-call(s32[3]{0:T(128)S(1)} %pad_add_fusion.place_ref, f32[32,1024]{1,0:T(8,128)S(1)} %get-tuple-element.36.refs_0_, bf16[32,1024]{1,0:T(8,128)(2,1)S(1)} %collective-permute-done.17.refs_1_, bf16[32,1024]{1,0:T(8,128)(2,1)S(1)} %collective-permute-done.18.refs_2_, bf16[32,1024]{1,0:T(8,128)(2,1)S(1)} %collective-permute-done.19.refs_3_), custom_call_target="tpu_custom_call" | custom-call | flops 131072 | bytes 458764 | tf_op jit(solution)/shard_map/settle/pallas_call | solution.py:37
  (18 shorter events, 0.1 us)
Async XLA Ops:
  0.6 1.6 %copy-start = (f32[4,128,1024]{2,1,0:T(8,128)S(1)}, f32[4,128,1024]{2,1,0:T(8,128)}, u32[]{:S(2)}) copy-start(f32[4,128,1024]{2,1,0:T(8,128)} %x_hbm.1) | copy-start | bytes 6291460
  2.2 1.2 %copy-start.1 = (f32[1024,256]{1,0:T(8,128)S(1)}, f32[1024,256]{1,0:T(8,128)}, u32[]{:S(2)}) copy-start(f32[1024,256]{1,0:T(8,128)} %f_hbm.1) | copy-start | bytes 3145732
  6.2 3.8 %copy-start.2 = (bf16[128,256]{1,0:T(8,128)(2,1)S(1)}, bf16[128,256]{1,0:T(8,128)(2,1)}, u32[]{:S(2)}) copy-start(bf16[128,256]{1,0:T(8,128)(2,1)} %param.5) | copy-start | bytes 196612
  9.6 7.2 %collective-permute-start = (bf16[4,128,1024]{2,1,0:T(8,128)(2,1)}, bf16[4,128,1024]{2,1,0:T(8,128)(2,1)}, u32[]{:S(2)}, u32[]{:S(2)}) collective-permute-start(bf16[4,128,1024]{2,1,0:T(8,128)(2,1)} %gram_away.1), channel_id=1, source_target_pairs={{0,4},{4,0},{8,12},{12,8},{16,20},{20,16},{24,28},{28,24},{1,5},{5... | collective-permute-start | bytes 3145736 | tf_op jit(solution)/shard_map/ppermute | solution.py:139
  10.2 5.7 %collective-permute-start.10 = (bf16[128,4,32]{0,2,1:T(8,128)(2,1)S(1)}, bf16[128,4,32]{0,2,1:T(8,128)(2,1)S(1)}, u32[]{:S(2)}, u32[]{:S(2)}) collective-permute-start(bf16[128,4,32]{0,2,1:T(8,128)(2,1)S(1)} %get-tuple-element.52), channel_id=1, source_target_pairs={{0,4},{4,0},{8,12},{12,8},{16,20},{20,16},{24,28},{28,24},{1,5},{5... | collective-permute-start | bytes 98312 | tf_op jit(solution)/shard_map/ppermute | solution.py:139
  10.3 17.1 %collective-permute-start.7 = (bf16[128,1024]{1,0:T(8,128)(2,1)S(1)}, bf16[128,1024]{1,0:T(8,128)(2,1)S(1)}, u32[]{:S(2)}, u32[]{:S(2)}) collective-permute-start(bf16[128,1024]{1,0:T(8,128)(2,1)S(1)} %get-tuple-element.28.u_ref.refs_0_), channel_id=1, source_target_pairs={{0,16},{4,20},{8,24},{12,28},{16,0},{20,4},{24,8},{28,12},{1,17},{... | collective-permute-start | bytes 786440 | tf_op jit(solution)/shard_map/ppermute | solution.py:139
  14.4 18.6 %collective-permute-start.14 = (bf16[128,1024]{1,0:T(8,128)(2,1)S(1)}, bf16[128,1024]{1,0:T(8,128)(2,1)S(1)}, u32[]{:S(2)}, u32[]{:S(2)}) collective-permute-start(bf16[128,1024]{1,0:T(8,128)(2,1)S(1)} %get-tuple-element.28.u_ref.refs_0_), channel_id=1, source_target_pairs={{0,8},{4,12},{8,0},{12,4},{16,24},{20,28},{24,16},{28,20},{1,9},{5... | collective-permute-start | bytes 786440 | tf_op jit(solution)/shard_map/ppermute | solution.py:139
  16.4 15.8 %collective-permute-start.11 = (bf16[2,2,128,32]{3,2,1,0:T(8,128)(2,1)S(1)}, bf16[2,2,128,32]{3,2,1,0:T(8,128)(2,1)S(1)}, u32[]{:S(2)}, u32[]{:S(2)}) collective-permute-start(bf16[2,2,128,32]{3,2,1,0:T(8,128)(2,1)S(1)} %copy.22), channel_id=1, source_target_pairs={{0,16},{4,20},{8,24},{12,28},{16,0},{20,4},{24,8},{28,12},{1,17},{... | collective-permute-start | bytes 98312 | tf_op jit(solution)/shard_map/ppermute | solution.py:139
  20.1 13.0 %collective-permute-start.3 = (bf16[4,32,1024]{2,1,0:T(8,128)(2,1)S(1)}, bf16[4,32,1024]{2,1,0:T(8,128)(2,1)S(1)}, u32[]{:S(2)}, u32[]{:S(2)}) collective-permute-start(bf16[4,32,1024]{2,1,0:T(8,128)(2,1)S(1)} %get-tuple-element.27), channel_id=1, source_target_pairs={{0,3},{1,2},{2,1},{3,0},{4,7},{5,6},{6,5},{7,4},{8,11},{9,10},{10,... | collective-permute-start | bytes 786440 | tf_op jit(solution)/shard_map/ppermute | solution.py:139
  22.6 12.1 %collective-permute-start.2 = (bf16[4,32,1024]{2,1,0:T(8,128)(2,1)S(1)}, bf16[4,32,1024]{2,1,0:T(8,128)(2,1)S(1)}, u32[]{:S(2)}, u32[]{:S(2)}) collective-permute-start(bf16[4,32,1024]{2,1,0:T(8,128)(2,1)S(1)} %get-tuple-element.26), channel_id=1, source_target_pairs={{0,2},{1,3},{2,0},{3,1},{4,6},{5,7},{6,4},{7,5},{8,10},{9,11},{10,... | collective-permute-start | bytes 786440 | tf_op jit(solution)/shard_map/ppermute | solution.py:139
  27.5 7.3 %collective-permute-start.1 = (bf16[4,32,1024]{2,1,0:T(8,128)(2,1)S(1)}, bf16[4,32,1024]{2,1,0:T(8,128)(2,1)S(1)}, u32[]{:S(2)}, u32[]{:S(2)}) collective-permute-start(bf16[4,32,1024]{2,1,0:T(8,128)(2,1)S(1)} %get-tuple-element.25), channel_id=1, source_target_pairs={{0,1},{1,0},{2,3},{3,2},{4,5},{5,4},{6,7},{7,6},{8,9},{9,8},{10,11... | collective-permute-start | bytes 786440 | tf_op jit(solution)/shard_map/ppermute | solution.py:139
  32.2 9.2 %collective-permute-start.8 = (bf16[128,1024]{1,0:T(8,128)(2,1)S(1)}, bf16[128,1024]{1,0:T(8,128)(2,1)S(1)}, u32[]{:S(2)}, u32[]{:S(2)}) collective-permute-start(bf16[128,1024]{1,0:T(8,128)(2,1)S(1)} %collective-permute-done.7.refs_4_), channel_id=1, source_target_pairs={{0,8},{4,12},{8,0},{12,4},{16,24},{20,28},{24,16},{28,20},{1,9},{5... | collective-permute-start | bytes 786440 | tf_op jit(solution)/shard_map/ppermute | solution.py:139
  33.0 13.8 %collective-permute-start.13 = (bf16[128,1024]{1,0:T(8,128)(2,1)S(1)}, bf16[128,1024]{1,0:T(8,128)(2,1)S(1)}, u32[]{:S(2)}, u32[]{:S(2)}) collective-permute-start(bf16[128,1024]{1,0:T(8,128)(2,1)S(1)} %get-tuple-element.28.u_ref.refs_0_), channel_id=1, source_target_pairs={{0,4},{4,0},{8,12},{12,8},{16,20},{20,16},{24,28},{28,24},{1,5},{5... | collective-permute-start | bytes 786440 | tf_op jit(solution)/shard_map/ppermute | solution.py:139
  33.0 9.8 %collective-permute-start.12 = (bf16[2,2,128,32]{3,2,1,0:T(8,128)(2,1)S(1)}, bf16[2,2,128,32]{3,2,1,0:T(8,128)(2,1)S(1)}, u32[]{:S(2)}, u32[]{:S(2)}) collective-permute-start(bf16[2,2,128,32]{3,2,1,0:T(8,128)(2,1)S(1)} %pad_maximum_fusion), channel_id=1, source_target_pairs={{0,8},{4,12},{8,0},{12,4},{16,24},{20,28},{24,16},{28,20},{1,9},{5... | collective-permute-start | bytes 98312 | tf_op jit(solution)/shard_map/ppermute | solution.py:139
  34.7 12.7 %collective-permute-start.16 = (bf16[128,1024]{1,0:T(8,128)(2,1)S(1)}, bf16[128,1024]{1,0:T(8,128)(2,1)S(1)}, u32[]{:S(2)}, u32[]{:S(2)}) collective-permute-start(bf16[128,1024]{1,0:T(8,128)(2,1)S(1)} %collective-permute-done.7.refs_4_), channel_id=1, source_target_pairs={{0,4},{4,0},{8,12},{12,8},{16,20},{20,16},{24,28},{28,24},{1,5},{5... | collective-permute-start | bytes 786440 | tf_op jit(solution)/shard_map/ppermute | solution.py:139
  34.8 12.0 %collective-permute-start.15 = (bf16[128,1024]{1,0:T(8,128)(2,1)S(1)}, bf16[128,1024]{1,0:T(8,128)(2,1)S(1)}, u32[]{:S(2)}, u32[]{:S(2)}) collective-permute-start(bf16[128,1024]{1,0:T(8,128)(2,1)S(1)} %collective-permute-done.14.refs_2_), channel_id=1, source_target_pairs={{0,4},{4,0},{8,12},{12,8},{16,20},{20,16},{24,28},{28,24},{1,5},{5... | collective-permute-start | bytes 786440 | tf_op jit(solution)/shard_map/ppermute | solution.py:139
  41.4 6.8 %collective-permute-start.9 = (bf16[128,1024]{1,0:T(8,128)(2,1)S(1)}, bf16[128,1024]{1,0:T(8,128)(2,1)S(1)}, u32[]{:S(2)}, u32[]{:S(2)}) collective-permute-start(bf16[128,1024]{1,0:T(8,128)(2,1)S(1)} %collective-permute-done.8.refs_0_), channel_id=1, source_target_pairs={{0,4},{4,0},{8,12},{12,8},{16,20},{20,16},{24,28},{28,24},{1,5},{5... | collective-permute-start | bytes 786440 | tf_op jit(solution)/shard_map/ppermute | solution.py:139
  42.8 10.0 %collective-permute-start.6 = (bf16[32,1024]{1,0:T(8,128)(2,1)S(1)}, bf16[32,1024]{1,0:T(8,128)(2,1)S(1)}, u32[]{:S(2)}, u32[]{:S(2)}) collective-permute-start(bf16[32,1024]{1,0:T(8,128)(2,1)S(1)} %get-tuple-element.42), channel_id=1, source_target_pairs={{0,24},{4,28},{8,16},{12,20},{16,8},{20,12},{24,0},{28,4},{1,25},{... | collective-permute-start | bytes 196616 | tf_op jit(solution)/shard_map/ppermute | solution.py:139
  46.8 6.5 %collective-permute-start.5 = (bf16[32,1024]{1,0:T(8,128)(2,1)S(1)}, bf16[32,1024]{1,0:T(8,128)(2,1)S(1)}, u32[]{:S(2)}, u32[]{:S(2)}) collective-permute-start(bf16[32,1024]{1,0:T(8,128)(2,1)S(1)} %get-tuple-element.43), channel_id=1, source_target_pairs={{0,16},{4,20},{8,24},{12,28},{16,0},{20,4},{24,8},{28,12},{1,17},{... | collective-permute-start | bytes 196616 | tf_op jit(solution)/shard_map/ppermute | solution.py:139
  46.8 6.5 %collective-permute-start.4 = (bf16[32,1024]{1,0:T(8,128)(2,1)S(1)}, bf16[32,1024]{1,0:T(8,128)(2,1)S(1)}, u32[]{:S(2)}, u32[]{:S(2)}) collective-permute-start(bf16[32,1024]{1,0:T(8,128)(2,1)S(1)} %get-tuple-element.41), channel_id=1, source_target_pairs={{0,8},{4,12},{8,0},{12,4},{16,24},{20,28},{24,16},{28,20},{1,9},{5... | collective-permute-start | bytes 196616 | tf_op jit(solution)/shard_map/ppermute | solution.py:139
  49.8 4.9 %collective-permute-start.17 = (bf16[32,1024]{1,0:T(8,128)(2,1)S(1)}, bf16[32,1024]{1,0:T(8,128)(2,1)S(1)}, u32[]{:S(2)}, u32[]{:S(2)}) collective-permute-start(bf16[32,1024]{1,0:T(8,128)(2,1)S(1)} %get-tuple-element.37), channel_id=1, source_target_pairs={{0,1},{1,0},{2,3},{3,2},{4,5},{5,4},{6,7},{7,6},{8,9},{9,8},{10,11... | collective-permute-start | bytes 196616 | tf_op jit(solution)/shard_map/ppermute | solution.py:139
  51.3 4.7 %collective-permute-start.18 = (bf16[32,1024]{1,0:T(8,128)(2,1)S(1)}, bf16[32,1024]{1,0:T(8,128)(2,1)S(1)}, u32[]{:S(2)}, u32[]{:S(2)}) collective-permute-start(bf16[32,1024]{1,0:T(8,128)(2,1)S(1)} %get-tuple-element.38), channel_id=1, source_target_pairs={{0,2},{1,3},{2,0},{3,1},{4,6},{5,7},{6,4},{7,5},{8,10},{9,11},{10,... | collective-permute-start | bytes 196616 | tf_op jit(solution)/shard_map/ppermute | solution.py:139
  52.8 5.2 %collective-permute-start.19 = (bf16[32,1024]{1,0:T(8,128)(2,1)S(1)}, bf16[32,1024]{1,0:T(8,128)(2,1)S(1)}, u32[]{:S(2)}, u32[]{:S(2)}) collective-permute-start(bf16[32,1024]{1,0:T(8,128)(2,1)S(1)} %get-tuple-element.39), channel_id=1, source_target_pairs={{0,3},{1,2},{2,1},{3,0},{4,7},{5,6},{6,5},{7,4},{8,11},{9,10},{10,... | collective-permute-start | bytes 196616 | tf_op jit(solution)/shard_map/ppermute | solution.py:139

commit v3 on v0

v3 whole, which is shorter than its diff:
```python
import functools
import math

import jax
import jax.numpy as jnp
from jax import lax
from jax.experimental import pallas as pl
from jax.experimental.pallas import tpu as pltpu
from jax.sharding import PartitionSpec as P

F32 = jnp.float32
BF16 = jnp.bfloat16
NN = (((1,), (0,)), ((), ()))
NT = (((1,), (1,)), ((), ()))
TN = (((0,), (0,)), ((), ()))
VMEM = pl.BlockSpec(memory_space=pltpu.VMEM)
SMEM = pl.BlockSpec(memory_space=pltpu.SMEM)
ANY = pl.BlockSpec(memory_space=pl.ANY)


def halves(x):
    high = x.astype(BF16)
    return high, (x - high.astype(F32)).astype(BF16)


def dot1(a, b, dims):
    return lax.dot_general(a, b, dims, preferred_element_type=F32)


def dot3(a, b, dims):
    return dot1(a[0], b[0], dims) + (dot1(a[0], b[1], dims) + dot1(a[1], b[0], dims))


def call(kernel, name, outs, in_specs, *args, scratch=(), vmem=4, flops=0):
    return pl.pallas_call(
        kernel,
        out_shape=[jax.ShapeDtypeStruct(s, d) for s, d in outs],
        in_specs=in_specs,
        out_specs=[VMEM] * len(outs),
        scratch_shapes=list(scratch),
        compiler_params=pltpu.CompilerParams(vmem_limit_bytes=vmem * 1024 * 1024),
        cost_estimate=pl.CostEstimate(flops=flops, bytes_accessed=0, transcendentals=0),
        name=name,
    )(*args)


def gram_rows(core, x_ref, groups, step, keep):
    slices, owned, width = x_ref.shape
    at = [pl.multiple_of((2 * g + core) * step, step) for g in range(groups)]
    left = [x_ref[:, :, pl.ds(a, step)].reshape(slices * owned, step) for a in at]
    left = halves(jnp.concatenate(left, axis=1))
    wide = min(256, width)
    for n in range(0, width, wide):
        right = halves(x_ref[:, :, n : n + wide].reshape(slices * owned, wide))
        keep(slice(n, n + wide), dot3(left, right, TN).reshape(groups, step, wide))


def away_kernel(place_ref, x_ref, away_ref):
    groups, step, _ = away_ref.shape

    def keep(at, rows):
        away_ref[:, :, at] = rows.astype(BF16)

    gram_rows(1 - place_ref[0], x_ref, groups, step, keep)


def core_kernel(place_ref, x_ref, f_ref, two_ref, _, near_ref, far_ref):
    slices, owned, _ = x_ref.shape
    rank = f_ref.shape[1]
    high = near_ref.shape[0] - owned
    side = lax.div(place_ref[2], 4)
    for out, here in ((near_ref, side), (far_ref, 1 - side)):
        chunk = two_ref[:, pl.ds(pl.multiple_of(here * 128, 128), 128)]
        for q in range(owned // high):
            out[owned:, q * 128 : (q + 1) * 128] = chunk[q * high : (q + 1) * high]
    f = halves(f_ref[...])
    for k in range(slices):
        core = dot3(halves(x_ref[k]), f, NN).astype(BF16)
        at = slice(k * rank, (k + 1) * rank)
        near_ref[:owned, at] = core
        far_ref[:owned, at] = core


def home_kernel(place_ref, x_ref, came_ref, _, own_ref, keep1_ref, keep2_ref, to1_ref, to2_ref, rows_ref):
    groups, step, _ = came_ref.shape
    block = own_ref.shape[1]
    lower, upper = slice(0, groups // 2), slice(groups // 2, groups)

    def keep(at, rows):
        rows_ref[...] = rows + came_ref[:, :, at].astype(F32)

        def part(chips, t):
            return rows_ref[chips, pl.ds(pl.multiple_of((place_ref[1] ^ t) * block, block), block)]

        own_ref[:, :, at] = part(slice(0, groups), 0)
        keep1_ref[:, :, at] = part(upper, 1)
        keep2_ref[:, :, at] = part(lower, 2)
        for i, t in enumerate((1, 3)):
            to1_ref[i, :, :, at] = part(lower, t).astype(BF16)
        for i, t in enumerate((2, 3)):
            to2_ref[i, :, :, at] = part(upper, t).astype(BF16)

    gram_rows(place_ref[0], x_ref, groups, step, keep)


def middle_kernel(own_ref, keep1_ref, keep2_ref, from1_ref, from2_ref, far_ref, sum_ref, to1_ref, to2_ref, on_ref):
    half = from1_ref.shape[1]
    to1_ref[...] = (keep1_ref[...] + from2_ref[1].astype(F32)).astype(BF16)
    to2_ref[...] = (keep2_ref[...] + from1_ref[1].astype(F32)).astype(BF16)
    on_ref[...] = far_ref[...]
    sum_ref[:half] = own_ref[:half] + from1_ref[0].astype(F32)
    sum_ref[half:] = own_ref[half:] + from2_ref[0].astype(F32)


def slab_kernel(place_ref, sum_ref, from1_ref, from2_ref, _, *outs):
    *outs, rows_ref = outs
    half = from1_ref.shape[0]
    rows_ref[:half] = sum_ref[:half] + from2_ref[...].astype(F32)
    rows_ref[half:] = sum_ref[half:] + from1_ref[...].astype(F32)
    for t, out in enumerate(outs):
        out[...] = rows_ref[lax.div(place_ref[2], 2) ^ t].astype(out.dtype)


def sum_kernel(scale, *refs):
    *parts, out_ref = refs
    total = parts[0][...]
    for part in parts[1:]:
        total = total + part[...].astype(F32)
    out_ref[...] = total * scale


def early_kernel(near, paired, got, far, mine_ref, other_ref):
    owned = mine_ref.shape[0]
    left = jnp.concatenate([near[:owned], paired[:owned]], axis=0)
    for t, block in enumerate((near, got, far)):
        rows = dot1(left, block[:owned], NT)
        at = slice(t * owned, (t + 1) * owned)
        mine_ref[:, at] = rows[:owned]
        other_ref[:, at] = rows[owned:].astype(BF16)


def late_kernel(near, paired, far, mine_early, other_early, mine_ref, other_ref):
    owned, before = mine_early.shape
    mine_ref[:, :before] = mine_early[...]
    other_ref[:, :before] = other_early[...]
    left = jnp.concatenate([near[:owned], paired[:owned]], axis=0)
    rows = dot1(left, far[:owned], NT)
    mine_ref[:, before:] = rows[:owned]
    other_ref[:, before:] = rows[owned:].astype(BF16)


def place_kernel(place_ref, mine, came, *outs):
    *outs, rows_ref = outs
    owned = mine.shape[0]
    for t in range(mine.shape[1] // owned):
        for core, part in enumerate((mine, came)):
            at = pl.multiple_of((place_ref[2] ^ (2 * t + core)) * owned, owned)
            rows_ref[:, pl.ds(at, owned)] = part[:, t * owned : (t + 1) * owned].astype(F32)
    height = owned // len(outs)
    for t, out in enumerate(outs):
        at = pl.multiple_of((place_ref[1] ^ t) * height, height)
        out[...] = rows_ref[pl.ds(at, height)].astype(out.dtype)


def reduced_kernel(place_ref, *refs):
    *blocks, _, mine_ref, other_ref, sum_ref = refs
    part = mine_ref.shape[0]
    high = blocks[0].shape[0] * 128 // (blocks[0].shape[1] + 128)
    owned = blocks[0].shape[0] - high
    total = None
    for block in blocks:
        chunk = [block[owned:, q * 128 : (q + 1) * 128] for q in range(owned // high)]
        value = dot1(jnp.concatenate(chunk, axis=0), block[:owned], TN)
        total = value if total is None else total + value
    sum_ref[...] = total
    for out, ja in ((mine_ref, place_ref[2]), (other_ref, place_ref[2] ^ 1)):
        out[...] = sum_ref[pl.ds(pl.multiple_of(lax.rem(ja, 4) * part, part), part)]


def add_kernel(mine, came, out_ref):
    slices, _, rank = out_ref.shape
    for k in range(slices):
        at = slice(k * rank, (k + 1) * rank)
        out_ref[k] = mine[:, at] + came[:, at]


def xor_permute(x, axis, bits):
    return lax.ppermute(x, axis, [(i, i ^ bits) for i in range(lax.axis_size(axis))])


def pick(x, index, axis):
    return lax.dynamic_index_in_dim(x, index, axis, keepdims=False)


def tiled_shards(tensor, factor_one, factor_two):
    slices, owned, width = tensor.shape
    count_ja = lax.axis_size("ja")
    count_ka = lax.axis_size("ka")
    count_z = count_ja // 2
    rank_one = factor_one.shape[1]
    part = factor_two.shape[1] // count_ja
    ja = lax.axis_index("ja")
    ka = lax.axis_index("ka")
    place = jnp.stack([lax.rem(ja, 2), ka, ja]).astype(jnp.int32)
    step = width // count_ja
    columns = slices * rank_one
    high = owned * 128 // columns
    norm_one = 1.0 / math.sqrt(owned * count_ja * slices * count_ka)
    norm_two = 1.0 / math.sqrt(slices * count_ka * rank_one)

    (away,) = call(
        away_kernel, "away", [((count_z, step, width), BF16)], [SMEM, VMEM], place, tensor, vmem=4
    )
    near, far = call(
        core_kernel,
        "core",
        [((owned + high, columns), BF16)] * 2,
        [SMEM, VMEM, VMEM, VMEM, ANY],
        place,
        tensor,
        factor_one,
        factor_two,
        away,
        vmem=4,
    )

    far2 = xor_permute(far, "ja", 4)
    got1 = xor_permute(near, "ja", 2)
    paired = xor_permute(near, "ja", 1)
    came = xor_permute(away, "ja", 1)

    shape = (count_z, step // count_ka, width)
    half = (count_z // 2, *shape[1:])
    own, keep1, keep2, to1, to2 = call(
        home_kernel,
        "home",
        [(shape, F32), (half, F32), (half, F32), ((2, *half), BF16), ((2, *half), BF16)],
        [SMEM, VMEM, VMEM, ANY],
        place,
        tensor,
        came,
        paired,
        scratch=[pltpu.VMEM((count_z, step, min(256, width)), F32)],
        vmem=6,
    )
    from1 = xor_permute(to1, "ka", 1)
    from2 = xor_permute(to2, "ka", 2)
    total, to1, to2, far2 = call(
        middle_kernel,
        "middle",
        [(shape, F32), (half, BF16), (half, BF16), (far2.shape, BF16)],
        [VMEM] * 6,
        own,
        keep1,
        keep2,
        from1,
        from2,
        far2,
    )
    from1 = xor_permute(to1, "ka", 1)
    from2 = xor_permute(to2, "ka", 2)
    far3 = xor_permute(far2, "ja", 2)
    begun = call(
        early_kernel,
        "two_early",
        [((owned, 3 * owned), F32), ((owned, 3 * owned), BF16)],
        [VMEM] * 4,
        near,
        paired,
        got1,
        far2,
    )
    sums = call(
        slab_kernel,
        "slab",
        [(shape[1:], F32 if t == 0 else BF16) for t in range(count_z)],
        [SMEM] + [VMEM] * 3 + [ANY],
        place,
        total,
        from1,
        from2,
        begun[0],
        scratch=[pltpu.VMEM(shape, F32)],
    )
    sums = [p if t == 0 else xor_permute(p, "ja", 2 * t) for t, p in enumerate(sums)]
    (gram_one,) = call(
        functools.partial(sum_kernel, norm_one), "one", [(shape[1:], F32)], [VMEM] * count_z, *sums
    )

    mine, other = call(
        late_kernel,
        "two_late",
        [((owned, 4 * owned), F32), ((owned, 4 * owned), BF16)],
        [VMEM] * 5,
        near,
        paired,
        far3,
        *begun,
    )
    other = xor_permute(other, "ja", 1)
    shape = (owned // count_ka, count_ja * owned)
    rows = call(
        place_kernel,
        "two_place",
        [(shape, F32 if t == 0 else BF16) for t in range(count_ka)],
        [SMEM] + [VMEM] * 2,
        place,
        mine,
        other,
        scratch=[pltpu.VMEM((owned, count_ja * owned), F32)],
    )
    mine, other = call(
        reduced_kernel,
        "reduced",
        [((part, columns), F32)] * 2,
        [SMEM] + [VMEM] * 4 + [ANY],
        place,
        near,
        got1,
        far2,
        far3,
        rows[0],
        scratch=[pltpu.VMEM((128, columns), F32)],
    )
    other = xor_permute(other, "ja", 1)
    (reduced,) = call(add_kernel, "add", [((slices, part, rank_one), F32)], [VMEM] * 2, mine, other)
    rows = [p if t == 0 else xor_permute(p, "ka", t) for t, p in enumerate(rows)]
    (gram_two,) = call(
        functools.partial(sum_kernel, norm_two), "two", [(shape, F32)], [VMEM] * count_ka, *rows
    )
    return (gram_one, gram_two, reduced)


def plain_shards(tensor, factor_one, factor_two):
    slices, owned, width = tensor.shape
    count_ja = lax.axis_size("ja")
    count_ka = lax.axis_size("ka")
    count_z = count_ja // 2
    rank_one = factor_one.shape[1]
    ja = lax.axis_index("ja")
    ka = lax.axis_index("ka")
    core_at, z = lax.rem(ja, 2), lax.div(ja, 2)
    step = width // count_ja
    x = halves(tensor.reshape(slices * owned, width))
    core = dot3(x, halves(factor_one), NN).astype(BF16).reshape(slices, owned, rank_one)
    u = core.transpose(1, 0, 2).reshape(owned, slices * rank_one)
    local = dot3(x, x, TN).reshape(count_z, 2, step, width)
    home = pick(local, core_at, 1)
    home = home + xor_permute(pick(local, 1 - core_at, 1).astype(BF16), "ja", 1).astype(F32)
    home = home.reshape(count_z, count_ka, step // count_ka, width)
    slab = pick(home, ka, 1)
    for t in range(1, count_ka):
        slab = slab + xor_permute(pick(home, ka ^ t, 1).astype(BF16), "ka", t).astype(F32)
    gram_one = pick(slab, z, 0)
    for t in range(1, count_z):
        gram_one = gram_one + xor_permute(pick(slab, z ^ t, 0).astype(BF16), "ja", 2 * t).astype(F32)
    gram_one = gram_one * (1.0 / math.sqrt(owned * count_ja * slices * count_ka))

    blocks = [u, xor_permute(u, "ja", 1)]
    for t in range(1, count_z):
        block = xor_permute(u, "ja", 2 * t)
        blocks += [block, xor_permute(block, "ja", 1)]
    places = jnp.arange(count_ja) ^ ja
    gathered = jnp.take(jnp.stack(blocks), places, axis=0).reshape(count_ja * owned, -1)
    rows = dot1(u, gathered, NT).reshape(count_ka, owned // count_ka, count_ja * owned)
    gram_two = pick(rows, ka, 0)
    for t in range(1, count_ka):
        gram_two = gram_two + xor_permute(pick(rows, ka ^ t, 0).astype(BF16), "ka", t).astype(F32)
    gram_two = gram_two * (1.0 / math.sqrt(slices * count_ka * rank_one))

    cut = factor_two.reshape(owned, count_ja, -1)
    two = [pick(cut, ja, 1)]
    two += [xor_permute(pick(cut, ja ^ b, 1), "ja", b) for b in range(1, count_ja)]
    two = jnp.take(jnp.stack(two), places, axis=0).reshape(count_ja * owned, -1)
    reduced = dot1(two, gathered, TN).reshape(-1, slices, rank_one).transpose(1, 0, 2)
    return (gram_one, gram_two, reduced)


def shards(tensor, factor_one, factor_two):
    slices, owned, width = tensor.shape
    count_ja = lax.axis_size("ja")
    count_ka = lax.axis_size("ka")
    step = width // count_ja
    columns = slices * factor_one.shape[1]
    tiled = count_ja == 8 and count_ka == 4 and factor_two.shape[1] == 256
    tiled = tiled and step % 128 == 0 and owned % 128 == 0
    tiled = tiled and step % (16 * count_ka) == 0 and owned % (16 * count_ka) == 0
    tiled = tiled and owned * 128 % (16 * columns) == 0 and columns % 128 == 0
    tiled = tiled and owned * 128 // columns * (columns // 128) == owned
    return (tiled_shards if tiled else plain_shards)(tensor, factor_one, factor_two)


def solution(mesh):
    in_specs = (P("ka", "ja", None), P(), P("ja", None))
    out_specs = (P(("ja", "ka"), None), P(("ja", "ka"), None), P("ka", "ja", None))
    return jax.shard_map(shards, mesh=mesh, in_specs=in_specs, out_specs=out_specs, check_vma=False)
```

time: 218 us -> 52.4 us (0.24)
  waiting for transfers between devices: 179 us -> 17 us
  starting transfers between devices: 0.21 us -> 20.8 us
  matrix products: 15.6 us -> 0 us
  between operations: 14.5 us -> 0.76 us
  Pallas kernels: 0 us -> 12 us
  local copies, waits for them, and re-layouts: 5.95 us -> 1.61 us
  other arithmetic: 3.14 us -> 0.08 us
    reduce_scatter x3 -> x0, waiting for transfers between devices: 99.5 us -> none  [the longest x1 48.5 us: shards(): lax.psum_scatter(jnp.dot(flat.T, flat, precision=lax.Precision.HIGHEST, p...]
    unnamed x6 -> x0, waiting for transfers between devices: 58.2 us -> none
    all_gather x1 -> x0, waiting for transfers between devices: 20.9 us -> none  [shards(): lax.all_gather(core, 'ja', axis=1, tiled=True)]
    ppermute x0 -> x17, starting transfers between devices: none -> 20.8 us  [xor_permute(): lax.ppermute(x, axis, [(i, i ^ bits) for i in range(lax.axis_size(axis))])]
    ppermute x0 -> x17, waiting for transfers between devices: none -> 17 us  [xor_permute(): lax.ppermute(x, axis, [(i, i ^ bits) for i in range(lax.axis_size(axis))])]
    dot_general x4 -> x0, matrix products: 15.6 us -> none  [the longest x1 8.29 us: shards(): jnp.dot(flat.T, flat, precision=lax.Precision.HIGHEST, preferred_element_...]
    pallas_call x0 -> x12, Pallas kernels: none -> 12 us  [call(): pl.pallas_call(kernel, out_shape=[jax.ShapeDtypeStruct(s, d) for s, d in...]
    mul x2 -> x0, other arithmetic: 3.14 us -> none  [the longest x1 1.57 us: shards(): return (gram_one, gram_two * norm_two, reduced)]
  transfers between devices with their start and end apart: 5 -> 17, of which waited for: 5 -> 7; matrix products, arithmetic and copies ran while one was open for 8% -> 0% of each run, Pallas kernels for 0% -> 17%
where the time goes in v3:
time: 52.4 us; the launch traced here: 52.2 us
  starting transfers between devices  20.8 us (40%)
  waiting for transfers between devices  17 us (32%)
  Pallas kernels  12 us (23%)
  local copies, waits for them, and re-layouts  1.61 us (3%)
  between operations  0.76 us (1%)
    ppermute x17, starting transfers between devices, xor_permute(): lax.ppermute(x, axis, [(i, i ^ bits) for i in range(lax.axis_size(axis))])  20.8 us
    ppermute x17, waiting for transfers between devices, xor_permute(): lax.ppermute(x, axis, [(i, i ^ bits) for i in range(lax.axis_size(axis))])  17 us
    pallas_call x12, Pallas kernels, call(): pl.pallas_call(kernel, out_shape=[jax.ShapeDtypeStruct(s, d) for s, d in...  12 us
    unnamed x8, local copies, waits for them, and re-layouts  1.61 us
  transfers between devices with their start and end apart: 17, of which 7 were waited for; matrix products, arithmetic and copies ran while one was open for 0% of the time, Pallas kernels for 17%

profile of v3, /device:TPU:0, one launch (start us, length us, event | category | flops | bytes accessed | tf_op | source)
XLA Modules:
  0.0 52.2 jit_solution(15585914923239273598)
XLA Ops:
  0.6 0.1 pad_add_fusion.place_ref
  0.7 1.6 %copy-done = f32[4,128,1024]{2,1,0:T(8,128)S(1)} copy-done((f32[4,128,1024]{2,1,0:T(8,128)S(1)}, f32[4,128,1024]{2,1,0:T(8,128)}, u32[]{:S(2)}) %copy-start) | copy-done | bytes 2097176
  2.3 2.5 %away.1._ = bf16[4,128,1024]{2,1,0:T(8,128)(2,1)S(1)} custom-call(s32[3]{0:T(128)S(1)} %pad_add_fusion.place_ref, f32[4,128,1024]{2,1,0:T(8,128)S(1)} %copy-done), custom_call_target="tpu_custom_call" | custom-call | tf_op jit(solution)/shard_map/away/pallas_call | solution.py:35
  4.8 0.0 copy-start.1
  4.8 0.5 collective-permute-start
  5.3 1.6 %core.1 = (bf16[144,1024]{1,0:T(8,128)(2,1)S(1)}, bf16[144,1024]{1,0:T(8,128)(2,1)S(1)}) custom-call(s32[3]{0:T(128)S(1)} %pad_add_fusion.place_ref, f32[4,128,1024]{2,1,0:T(8,128)S(1)} %copy-done, f32[1024,256]{1,0:T(8,128)S(1)} %copy-done.2, bf16[128,256]{1,0:T(8,128)(2,1)S(1)} %copy-done.3, bf16[4,128,1024]{2,1,0:T(8,128)(2,1)S(1)} %away.1._), custom_call_target="tpu_custom_call" | custom-call | tf_op jit(solution)/shard_map/core/pallas_call | solution.py:35
  6.9 0.1 collective-permute-start.1
  7.0 4.0 %collective-permute-start.4 = (bf16[144,1024]{1,0:T(8,128)(2,1)S(1)}, bf16[144,1024]{1,0:T(8,128)(2,1)S(1)}, u32[]{:S(2)}, u32[]{:S(2)}) collective-permute-start(bf16[144,1024]{1,0:T(8,128)(2,1)S(1)} %get-tuple-element.34), channel_id=1, source_target_pairs={{0,16},{4,20},{8,24},{12,28},{16,0},{20,4},{24,8},{28,12},{1,17},{... | collective-permute-start | bytes 884744 | tf_op jit(solution)/shard_map/ppermute | solution.py:188
  11.0 0.0 collective-permute-done.1._.paired
  11.0 0.0 collective-permute-done.came_ref
  11.1 2.7 %home.1 = (f32[4,32,1024]{2,1,0:T(8,128)S(1)}, f32[2,32,1024]{2,1,0:T(8,128)S(1)}, f32[2,32,1024]{2,1,0:T(8,128)S(1)}, bf16[2,2,32,1024]{3,2,1,0:T(8,128)(2,1)S(1)}, bf16[2,2,32,1024]{3,2,1,0:T(8,128)(2,1)S(1)}) custom-call(s32[3]{0:T(128)S(1)} %pad_add_fusion.place_ref, f32[4,128,1024]{2,1,0:T(8,128)S(1)} %copy-done.1, ...), custom_call_target="tpu_custom_call" | custom-call | tf_op jit(solution)/shard_map/home/pallas_call | solution.py:35
  13.8 1.6 %collective-permute-start.2 = (bf16[2,2,32,1024]{3,2,1,0:T(8,128)(2,1)S(1)}, bf16[2,2,32,1024]{3,2,1,0:T(8,128)(2,1)S(1)}, u32[]{:S(2)}, u32[]{:S(2)}) collective-permute-start(bf16[2,2,32,1024]{3,2,1,0:T(8,128)(2,1)S(1)} %get-tuple-element.32), channel_id=1, source_target_pairs={{0,1},{1,0},{2,3},{3,2},{4,5},{5,4},{6,7},{7,6},{8,9},{9,8},{10,11... | collective-permute-start | bytes 786440 | tf_op jit(solution)/shard_map/ppermute | solution.py:188
  15.3 1.5 %collective-permute-start.3 = (bf16[2,2,32,1024]{3,2,1,0:T(8,128)(2,1)S(1)}, bf16[2,2,32,1024]{3,2,1,0:T(8,128)(2,1)S(1)}, u32[]{:S(2)}, u32[]{:S(2)}) collective-permute-start(bf16[2,2,32,1024]{3,2,1,0:T(8,128)(2,1)S(1)} %get-tuple-element.33), channel_id=1, source_target_pairs={{0,2},{1,3},{2,0},{3,1},{4,6},{5,7},{6,4},{7,5},{8,10},{9,11},{10,... | collective-permute-start | bytes 786440 | tf_op jit(solution)/shard_map/ppermute | solution.py:188
  16.9 1.6 %collective-permute-start.7 = (bf16[144,1024]{1,0:T(8,128)(2,1)S(1)}, bf16[144,1024]{1,0:T(8,128)(2,1)S(1)}, u32[]{:S(2)}, u32[]{:S(2)}) collective-permute-start(bf16[144,1024]{1,0:T(8,128)(2,1)S(1)} %get-tuple-element.28.near.refs_0_), channel_id=1, source_target_pairs={{0,8},{4,12},{8,0},{12,4},{16,24},{20,28},{24,16},{28,20},{1,9},{5... | collective-permute-start | bytes 884744 | tf_op jit(solution)/shard_map/ppermute | solution.py:188
  18.4 6.3 %collective-permute-done.4.far_ref = bf16[144,1024]{1,0:T(8,128)(2,1)S(1)} collective-permute-done((bf16[144,1024]{1,0:T(8,128)(2,1)S(1)}, bf16[144,1024]{1,0:T(8,128)(2,1)S(1)}, u32[]{:S(2)}, u32[]{:S(2)}) %collective-permute-start.4) | collective-permute-done | bytes 294944 | tf_op jit(solution)/shard_map/ppermute | solution.py:188
  24.7 0.0 collective-permute-done.2.from1_ref
  24.7 0.0 collective-permute-done.3.from2_ref
  24.7 0.1 middle.1
  24.8 0.7 %collective-permute-start.11 = (bf16[144,1024]{1,0:T(8,128)(2,1)S(1)}, bf16[144,1024]{1,0:T(8,128)(2,1)S(1)}, u32[]{:S(2)}, u32[]{:S(2)}) collective-permute-start(bf16[144,1024]{1,0:T(8,128)(2,1)S(1)} %get-tuple-element.38.far.refs_2_), channel_id=1, source_target_pairs={{0,8},{4,12},{8,0},{12,4},{16,24},{20,28},{24,16},{28,20},{1,9},{5... | collective-permute-start | bytes 884744 | tf_op jit(solution)/shard_map/ppermute | solution.py:188
  25.6 1.5 %collective-permute-start.5 = (bf16[2,32,1024]{2,1,0:T(8,128)(2,1)S(1)}, bf16[2,32,1024]{2,1,0:T(8,128)(2,1)S(1)}, u32[]{:S(2)}, u32[]{:S(2)}) collective-permute-start(bf16[2,32,1024]{2,1,0:T(8,128)(2,1)S(1)} %get-tuple-element.36), channel_id=1, source_target_pairs={{0,1},{1,0},{2,3},{3,2},{4,5},{5,4},{6,7},{7,6},{8,9},{9,8},{10,11... | collective-permute-start | bytes 393224 | tf_op jit(solution)/shard_map/ppermute | solution.py:188
  27.1 1.5 %collective-permute-start.6 = (bf16[2,32,1024]{2,1,0:T(8,128)(2,1)S(1)}, bf16[2,32,1024]{2,1,0:T(8,128)(2,1)S(1)}, u32[]{:S(2)}, u32[]{:S(2)}) collective-permute-start(bf16[2,32,1024]{2,1,0:T(8,128)(2,1)S(1)} %get-tuple-element.37), channel_id=1, source_target_pairs={{0,2},{1,3},{2,0},{3,1},{4,6},{5,7},{6,4},{7,5},{8,10},{9,11},{10,... | collective-permute-start | bytes 393224 | tf_op jit(solution)/shard_map/ppermute | solution.py:188
  28.6 2.5 %collective-permute-done.7.got.refs_1_ = bf16[144,1024]{1,0:T(8,128)(2,1)S(1)} collective-permute-done((bf16[144,1024]{1,0:T(8,128)(2,1)S(1)}, bf16[144,1024]{1,0:T(8,128)(2,1)S(1)}, u32[]{:S(2)}, u32[]{:S(2)}) %collective-permute-start.7) | collective-permute-done | bytes 294944 | tf_op jit(solution)/shard_map/ppermute | solution.py:188
  31.1 0.6 %two_early.1 = (f32[128,384]{1,0:T(8,128)S(1)}, bf16[128,384]{1,0:T(8,128)(2,1)S(1)}) custom-call(bf16[144,1024]{1,0:T(8,128)(2,1)S(1)} %get-tuple-element.28.near.refs_0_, bf16[144,1024]{1,0:T(8,128)(2,1)S(1)} %collective-permute-done.1._.paired, bf16[144,1024]{1,0:T(8,128)(2,1)S(1)} %collective-permute-done.7.got.refs_1_, ...), custom_call_target="tpu_custom_call" | custom-call | tf_op jit(solution)/shard_map/two_early/pallas_call | solution.py:35
  31.7 4.8 %collective-permute-done.11.far.refs_3_ = bf16[144,1024]{1,0:T(8,128)(2,1)S(1)} collective-permute-done((bf16[144,1024]{1,0:T(8,128)(2,1)S(1)}, bf16[144,1024]{1,0:T(8,128)(2,1)S(1)}, u32[]{:S(2)}, u32[]{:S(2)}) %collective-permute-start.11) | collective-permute-done | bytes 294944 | tf_op jit(solution)/shard_map/ppermute | solution.py:188
  36.5 0.3 two_late.1
  36.8 0.1 collective-permute-start.12
  36.9 0.0 collective-permute-done.5.from1_ref
  36.9 0.0 collective-permute-done.6.from2_ref
  36.9 0.6 %slab.1 = (f32[32,1024]{1,0:T(8,128)S(1)}, bf16[32,1024]{1,0:T(8,128)(2,1)S(1)}, bf16[32,1024]{1,0:T(8,128)(2,1)S(1)}, bf16[32,1024]{1,0:T(8,128)(2,1)S(1)}) custom-call(s32[3]{0:T(128)S(1)} %pad_add_fusion.place_ref, f32[4,32,1024]{2,1,0:T(8,128)S(1)} %get-tuple-element.35.sum_ref, bf16[2,32,1024]{2,1,0:T(8,128)(2,1)S(1)} %collective-permute-done.5.from1_ref, ...), custom_call_target="tpu_custom_call" | custom-call | tf_op jit(solution)/shard_map/slab/pallas_call | solution.py:35
  37.5 3.9 %collective-permute-start.10 = (bf16[32,1024]{1,0:T(8,128)(2,1)S(1)}, bf16[32,1024]{1,0:T(8,128)(2,1)S(1)}, u32[]{:S(2)}, u32[]{:S(2)}) collective-permute-start(bf16[32,1024]{1,0:T(8,128)(2,1)S(1)} %get-tuple-element.43), channel_id=1, source_target_pairs={{0,24},{4,28},{8,16},{12,20},{16,8},{20,12},{24,0},{28,4},{1,25},{... | collective-permute-start | bytes 196616 | tf_op jit(solution)/shard_map/ppermute | solution.py:188
  41.4 0.0 collective-permute-start.8
  41.4 0.0 collective-permute-done.12.came
  41.4 0.6 %two_place.1 = (f32[32,1024]{1,0:T(8,128)S(1)}, bf16[32,1024]{1,0:T(8,128)(2,1)S(1)}, bf16[32,1024]{1,0:T(8,128)(2,1)S(1)}, bf16[32,1024]{1,0:T(8,128)(2,1)S(1)}) custom-call(s32[3]{0:T(128)S(1)} %pad_add_fusion.place_ref, f32[128,512]{1,0:T(8,128)S(1)} %get-tuple-element.45.mine, bf16[128,512]{1,0:T(8,128)(2,1)S(1)} %collective-permute-done.12.came), custom_call_target="tpu_custom_call" | custom-call | tf_op jit(solution)/shard_map/two_place/pallas_call | solution.py:35
  42.1 1.0 %reduced.1 = (f32[32,1024]{1,0:T(8,128)S(1)}, f32[32,1024]{1,0:T(8,128)S(1)}) custom-call(s32[3]{0:T(128)S(1)} %pad_add_fusion.place_ref, bf16[144,1024]{1,0:T(8,128)(2,1)S(1)} %get-tuple-element.28.near.refs_0_, bf16[144,1024]{1,0:T(8,128)(2,1)S(1)} %collective-permute-done.7.got.refs_1_, bf16[144,1024]{1,0:T(8,128)(2,1)S(1)} %get-tuple-element.38.far.refs_2_, ...), custom_call_target="tpu_custom_call" | custom-call | tf_op jit(solution)/shard_map/reduced/pallas_call | solution.py:35
  43.1 0.3 collective-permute-start.16
  43.4 0.6 %collective-permute-start.9 = (bf16[32,1024]{1,0:T(8,128)(2,1)S(1)}, bf16[32,1024]{1,0:T(8,128)(2,1)S(1)}, u32[]{:S(2)}, u32[]{:S(2)}) collective-permute-start(bf16[32,1024]{1,0:T(8,128)(2,1)S(1)} %get-tuple-element.42), channel_id=1, source_target_pairs={{0,16},{4,20},{8,24},{12,28},{16,0},{20,4},{24,8},{28,12},{1,17},{... | collective-permute-start | bytes 196616 | tf_op jit(solution)/shard_map/ppermute | solution.py:188
  44.0 0.5 %collective-permute-start.13 = (bf16[32,1024]{1,0:T(8,128)(2,1)S(1)}, bf16[32,1024]{1,0:T(8,128)(2,1)S(1)}, u32[]{:S(2)}, u32[]{:S(2)}) collective-permute-start(bf16[32,1024]{1,0:T(8,128)(2,1)S(1)} %get-tuple-element.48), channel_id=1, source_target_pairs={{0,1},{1,0},{2,3},{3,2},{4,5},{5,4},{6,7},{7,6},{8,9},{9,8},{10,11... | collective-permute-start | bytes 196616 | tf_op jit(solution)/shard_map/ppermute | solution.py:188
  44.6 0.0 collective-permute-done.10.refs_3_
  44.6 0.5 collective-permute-start.14
  45.1 0.7 %collective-permute-done.8.refs_1_ = bf16[32,1024]{1,0:T(8,128)(2,1)S(1)} collective-permute-done((bf16[32,1024]{1,0:T(8,128)(2,1)S(1)}, bf16[32,1024]{1,0:T(8,128)(2,1)S(1)}, u32[]{:S(2)}, u32[]{:S(2)}) %collective-permute-start.8) | collective-permute-done | bytes 65568 | tf_op jit(solution)/shard_map/ppermute | solution.py:188
  45.7 1.8 %collective-permute-start.15 = (bf16[32,1024]{1,0:T(8,128)(2,1)S(1)}, bf16[32,1024]{1,0:T(8,128)(2,1)S(1)}, u32[]{:S(2)}, u32[]{:S(2)}) collective-permute-start(bf16[32,1024]{1,0:T(8,128)(2,1)S(1)} %get-tuple-element.50), channel_id=1, source_target_pairs={{0,3},{1,2},{2,1},{3,0},{4,7},{5,6},{6,5},{7,4},{8,11},{9,10},{10,... | collective-permute-start | bytes 196616 | tf_op jit(solution)/shard_map/ppermute | solution.py:188
  47.5 1.1 %collective-permute-done.9.refs_2_ = bf16[32,1024]{1,0:T(8,128)(2,1)S(1)} collective-permute-done((bf16[32,1024]{1,0:T(8,128)(2,1)S(1)}, bf16[32,1024]{1,0:T(8,128)(2,1)S(1)}, u32[]{:S(2)}, u32[]{:S(2)}) %collective-permute-start.9) | collective-permute-done | bytes 65568 | tf_op jit(solution)/shard_map/ppermute | solution.py:188
  48.6 0.7 %one.1 = f32[32,1024]{1,0:T(8,128)} custom-call(f32[32,1024]{1,0:T(8,128)S(1)} %get-tuple-element.40.refs_0_, bf16[32,1024]{1,0:T(8,128)(2,1)S(1)} %collective-permute-done.8.refs_1_, bf16[32,1024]{1,0:T(8,128)(2,1)S(1)} %collective-permute-done.9.refs_2_, bf16[32,1024]{1,0:T(8,128)(2,1)S(1)} %collective-permute-done.10.refs_3_), custom_call_target="tpu_custom_call" | custom-call | tf_op jit(solution)/shard_map/one/pallas_call | solution.py:35
  49.3 0.0 collective-permute-done.13.refs_1_
  49.3 0.2 collective-permute-done.14.refs_2_
  49.5 1.4 %collective-permute-done.15.refs_3_ = bf16[32,1024]{1,0:T(8,128)(2,1)S(1)} collective-permute-done((bf16[32,1024]{1,0:T(8,128)(2,1)S(1)}, bf16[32,1024]{1,0:T(8,128)(2,1)S(1)}, u32[]{:S(2)}, u32[]{:S(2)}) %collective-permute-start.15) | collective-permute-done | bytes 65568 | tf_op jit(solution)/shard_map/ppermute | solution.py:188
  50.9 0.7 %two.1 = f32[32,1024]{1,0:T(8,128)} custom-call(f32[32,1024]{1,0:T(8,128)S(1)} %get-tuple-element.47.refs_0_.refs_4_, bf16[32,1024]{1,0:T(8,128)(2,1)S(1)} %collective-permute-done.13.refs_1_, bf16[32,1024]{1,0:T(8,128)(2,1)S(1)} %collective-permute-done.14.refs_2_, bf16[32,1024]{1,0:T(8,128)(2,1)S(1)} %collective-permute-done.15.refs_3_), custom_call_target="tpu_custom_call" | custom-call | tf_op jit(solution)/shard_map/two/pallas_call | solution.py:35
  51.6 0.7 %add.5 = f32[4,32,256]{2,1,0:T(8,128)} custom-call(f32[32,1024]{1,0:T(8,128)S(1)} %get-tuple-element.51.mine, f32[32,1024]{1,0:T(8,128)S(1)} %collective-permute-done.16.came), custom_call_target="tpu_custom_call" | custom-call | tf_op jit(solution)/shard_map/add/pallas_call | solution.py:35
  (7 shorter events, 0.0 us)
Async XLA Ops:
  0.7 1.6 %copy-start = (f32[4,128,1024]{2,1,0:T(8,128)S(1)}, f32[4,128,1024]{2,1,0:T(8,128)}, u32[]{:S(2)}) copy-start(f32[4,128,1024]{2,1,0:T(8,128)} %x_ref.5) | copy-start | bytes 6291460
  2.3 3.0 %copy-start.2 = (f32[1024,256]{1,0:T(8,128)S(1)}, f32[1024,256]{1,0:T(8,128)}, u32[]{:S(2)}) copy-start(f32[1024,256]{1,0:T(8,128)} %f_ref.1) | copy-start | bytes 3145732
  2.3 3.0 %copy-start.3 = (bf16[128,256]{1,0:T(8,128)(2,1)S(1)}, bf16[128,256]{1,0:T(8,128)(2,1)}, u32[]{:S(2)}) copy-start(bf16[128,256]{1,0:T(8,128)(2,1)} %two_ref.1) | copy-start | bytes 196612
  4.8 6.3 %copy-start.1 = (f32[4,128,1024]{2,1,0:T(8,128)S(1)}, f32[4,128,1024]{2,1,0:T(8,128)}, u32[]{:S(2)}) copy-start(f32[4,128,1024]{2,1,0:T(8,128)} %x_ref.5) | copy-start | bytes 6291460
  4.8 6.3 %collective-permute-start = (bf16[4,128,1024]{2,1,0:T(8,128)(2,1)S(1)}, bf16[4,128,1024]{2,1,0:T(8,128)(2,1)S(1)}, u32[]{:S(2)}, u32[]{:S(2)}) collective-permute-start(bf16[4,128,1024]{2,1,0:T(8,128)(2,1)S(1)} %away.1._), channel_id=1, source_target_pairs={{0,4},{4,0},{8,12},{12,8},{16,20},{20,16},{24,28},{28,24},{1,5},{5... | collective-permute-start | bytes 3145736 | tf_op jit(solution)/shard_map/ppermute | solution.py:188
  6.9 4.2 %collective-permute-start.1 = (bf16[144,1024]{1,0:T(8,128)(2,1)S(1)}, bf16[144,1024]{1,0:T(8,128)(2,1)S(1)}, u32[]{:S(2)}, u32[]{:S(2)}) collective-permute-start(bf16[144,1024]{1,0:T(8,128)(2,1)S(1)} %get-tuple-element.28.near.refs_0_), channel_id=1, source_target_pairs={{0,4},{4,0},{8,12},{12,8},{16,20},{20,16},{24,28},{28,24},{1,5},{5... | collective-permute-start | bytes 884744 | tf_op jit(solution)/shard_map/ppermute | solution.py:188
  7.0 17.7 %collective-permute-start.4 = (bf16[144,1024]{1,0:T(8,128)(2,1)S(1)}, bf16[144,1024]{1,0:T(8,128)(2,1)S(1)}, u32[]{:S(2)}, u32[]{:S(2)}) collective-permute-start(bf16[144,1024]{1,0:T(8,128)(2,1)S(1)} %get-tuple-element.34), channel_id=1, source_target_pairs={{0,16},{4,20},{8,24},{12,28},{16,0},{20,4},{24,8},{28,12},{1,17},{... | collective-permute-start | bytes 884744 | tf_op jit(solution)/shard_map/ppermute | solution.py:188
  13.8 10.9 %collective-permute-start.2 = (bf16[2,2,32,1024]{3,2,1,0:T(8,128)(2,1)S(1)}, bf16[2,2,32,1024]{3,2,1,0:T(8,128)(2,1)S(1)}, u32[]{:S(2)}, u32[]{:S(2)}) collective-permute-start(bf16[2,2,32,1024]{3,2,1,0:T(8,128)(2,1)S(1)} %get-tuple-element.32), channel_id=1, source_target_pairs={{0,1},{1,0},{2,3},{3,2},{4,5},{5,4},{6,7},{7,6},{8,9},{9,8},{10,11... | collective-permute-start | bytes 786440 | tf_op jit(solution)/shard_map/ppermute | solution.py:188
  15.3 9.4 %collective-permute-start.3 = (bf16[2,2,32,1024]{3,2,1,0:T(8,128)(2,1)S(1)}, bf16[2,2,32,1024]{3,2,1,0:T(8,128)(2,1)S(1)}, u32[]{:S(2)}, u32[]{:S(2)}) collective-permute-start(bf16[2,2,32,1024]{3,2,1,0:T(8,128)(2,1)S(1)} %get-tuple-element.33), channel_id=1, source_target_pairs={{0,2},{1,3},{2,0},{3,1},{4,6},{5,7},{6,4},{7,5},{8,10},{9,11},{10,... | collective-permute-start | bytes 786440 | tf_op jit(solution)/shard_map/ppermute | solution.py:188
  16.9 14.2 %collective-permute-start.7 = (bf16[144,1024]{1,0:T(8,128)(2,1)S(1)}, bf16[144,1024]{1,0:T(8,128)(2,1)S(1)}, u32[]{:S(2)}, u32[]{:S(2)}) collective-permute-start(bf16[144,1024]{1,0:T(8,128)(2,1)S(1)} %get-tuple-element.28.near.refs_0_), channel_id=1, source_target_pairs={{0,8},{4,12},{8,0},{12,4},{16,24},{20,28},{24,16},{28,20},{1,9},{5... | collective-permute-start | bytes 884744 | tf_op jit(solution)/shard_map/ppermute | solution.py:188
  24.8 11.6 %collective-permute-start.11 = (bf16[144,1024]{1,0:T(8,128)(2,1)S(1)}, bf16[144,1024]{1,0:T(8,128)(2,1)S(1)}, u32[]{:S(2)}, u32[]{:S(2)}) collective-permute-start(bf16[144,1024]{1,0:T(8,128)(2,1)S(1)} %get-tuple-element.38.far.refs_2_), channel_id=1, source_target_pairs={{0,8},{4,12},{8,0},{12,4},{16,24},{20,28},{24,16},{28,20},{1,9},{5... | collective-permute-start | bytes 884744 | tf_op jit(solution)/shard_map/ppermute | solution.py:188
  25.6 11.3 %collective-permute-start.5 = (bf16[2,32,1024]{2,1,0:T(8,128)(2,1)S(1)}, bf16[2,32,1024]{2,1,0:T(8,128)(2,1)S(1)}, u32[]{:S(2)}, u32[]{:S(2)}) collective-permute-start(bf16[2,32,1024]{2,1,0:T(8,128)(2,1)S(1)} %get-tuple-element.36), channel_id=1, source_target_pairs={{0,1},{1,0},{2,3},{3,2},{4,5},{5,4},{6,7},{7,6},{8,9},{9,8},{10,11... | collective-permute-start | bytes 393224 | tf_op jit(solution)/shard_map/ppermute | solution.py:188
  27.1 9.8 %collective-permute-start.6 = (bf16[2,32,1024]{2,1,0:T(8,128)(2,1)S(1)}, bf16[2,32,1024]{2,1,0:T(8,128)(2,1)S(1)}, u32[]{:S(2)}, u32[]{:S(2)}) collective-permute-start(bf16[2,32,1024]{2,1,0:T(8,128)(2,1)S(1)} %get-tuple-element.37), channel_id=1, source_target_pairs={{0,2},{1,3},{2,0},{3,1},{4,6},{5,7},{6,4},{7,5},{8,10},{9,11},{10,... | collective-permute-start | bytes 393224 | tf_op jit(solution)/shard_map/ppermute | solution.py:188
  36.8 4.6 %collective-permute-start.12 = (bf16[128,512]{1,0:T(8,128)(2,1)S(1)}, bf16[128,512]{1,0:T(8,128)(2,1)S(1)}, u32[]{:S(2)}, u32[]{:S(2)}) collective-permute-start(bf16[128,512]{1,0:T(8,128)(2,1)S(1)} %get-tuple-element.46), channel_id=1, source_target_pairs={{0,4},{4,0},{8,12},{12,8},{16,20},{20,16},{24,28},{28,24},{1,5},{5... | collective-permute-start | bytes 393224 | tf_op jit(solution)/shard_map/ppermute | solution.py:188
  37.5 7.0 %collective-permute-start.10 = (bf16[32,1024]{1,0:T(8,128)(2,1)S(1)}, bf16[32,1024]{1,0:T(8,128)(2,1)S(1)}, u32[]{:S(2)}, u32[]{:S(2)}) collective-permute-start(bf16[32,1024]{1,0:T(8,128)(2,1)S(1)} %get-tuple-element.43), channel_id=1, source_target_pairs={{0,24},{4,28},{8,16},{12,20},{16,8},{20,12},{24,0},{28,4},{1,25},{... | collective-permute-start | bytes 196616 | tf_op jit(solution)/shard_map/ppermute | solution.py:188
  41.4 4.3 %collective-permute-start.8 = (bf16[32,1024]{1,0:T(8,128)(2,1)S(1)}, bf16[32,1024]{1,0:T(8,128)(2,1)S(1)}, u32[]{:S(2)}, u32[]{:S(2)}) collective-permute-start(bf16[32,1024]{1,0:T(8,128)(2,1)S(1)} %get-tuple-element.41), channel_id=1, source_target_pairs={{0,8},{4,12},{8,0},{12,4},{16,24},{20,28},{24,16},{28,20},{1,9},{5... | collective-permute-start | bytes 196616 | tf_op jit(solution)/shard_map/ppermute | solution.py:188
  43.1 8.5 %collective-permute-start.16 = (f32[32,1024]{1,0:T(8,128)S(1)}, f32[32,1024]{1,0:T(8,128)S(1)}, u32[]{:S(2)}, u32[]{:S(2)}) collective-permute-start(f32[32,1024]{1,0:T(8,128)S(1)} %get-tuple-element.52), channel_id=1, source_target_pairs={{0,4},{4,0},{8,12},{12,8},{16,20},{20,16},{24,28},{28,24},{1,5},{5... | collective-permute-start | bytes 393224 | tf_op jit(solution)/shard_map/ppermute | solution.py:188
  43.4 5.2 %collective-permute-start.9 = (bf16[32,1024]{1,0:T(8,128)(2,1)S(1)}, bf16[32,1024]{1,0:T(8,128)(2,1)S(1)}, u32[]{:S(2)}, u32[]{:S(2)}) collective-permute-start(bf16[32,1024]{1,0:T(8,128)(2,1)S(1)} %get-tuple-element.42), channel_id=1, source_target_pairs={{0,16},{4,20},{8,24},{12,28},{16,0},{20,4},{24,8},{28,12},{1,17},{... | collective-permute-start | bytes 196616 | tf_op jit(solution)/shard_map/ppermute | solution.py:188
  44.0 5.3 %collective-permute-start.13 = (bf16[32,1024]{1,0:T(8,128)(2,1)S(1)}, bf16[32,1024]{1,0:T(8,128)(2,1)S(1)}, u32[]{:S(2)}, u32[]{:S(2)}) collective-permute-start(bf16[32,1024]{1,0:T(8,128)(2,1)S(1)} %get-tuple-element.48), channel_id=1, source_target_pairs={{0,1},{1,0},{2,3},{3,2},{4,5},{5,4},{6,7},{7,6},{8,9},{9,8},{10,11... | collective-permute-start | bytes 196616 | tf_op jit(solution)/shard_map/ppermute | solution.py:188
  44.6 5.0 %collective-permute-start.14 = (bf16[32,1024]{1,0:T(8,128)(2,1)S(1)}, bf16[32,1024]{1,0:T(8,128)(2,1)S(1)}, u32[]{:S(2)}, u32[]{:S(2)}) collective-permute-start(bf16[32,1024]{1,0:T(8,128)(2,1)S(1)} %get-tuple-element.49), channel_id=1, source_target_pairs={{0,2},{1,3},{2,0},{3,1},{4,6},{5,7},{6,4},{7,5},{8,10},{9,11},{10,... | collective-permute-start | bytes 196616 | tf_op jit(solution)/shard_map/ppermute | solution.py:188
  45.7 5.2 %collective-permute-start.15 = (bf16[32,1024]{1,0:T(8,128)(2,1)S(1)}, bf16[32,1024]{1,0:T(8,128)(2,1)S(1)}, u32[]{:S(2)}, u32[]{:S(2)}) collective-permute-start(bf16[32,1024]{1,0:T(8,128)(2,1)S(1)} %get-tuple-element.50), channel_id=1, source_target_pairs={{0,3},{1,2},{2,1},{3,0},{4,7},{5,6},{6,5},{7,4},{8,11},{9,10},{10,... | collective-permute-start | bytes 196616 | tf_op jit(solution)/shard_map/ppermute | solution.py:188

commit v4 on v3

--- a/solution.py
+++ b/solution.py
@@ -103,11 +103,10 @@
     gram_rows(place_ref[0], x_ref, groups, step, keep)
 
 
-def middle_kernel(own_ref, keep1_ref, keep2_ref, from1_ref, from2_ref, far_ref, sum_ref, to1_ref, to2_ref, on_ref):
+def middle_kernel(own_ref, keep1_ref, keep2_ref, from1_ref, from2_ref, _, __, sum_ref, to1_ref, to2_ref):
     half = from1_ref.shape[1]
     to1_ref[...] = (keep1_ref[...] + from2_ref[1].astype(F32)).astype(BF16)
     to2_ref[...] = (keep2_ref[...] + from1_ref[1].astype(F32)).astype(BF16)
-    on_ref[...] = far_ref[...]
     sum_ref[:half] = own_ref[:half] + from1_ref[0].astype(F32)
     sum_ref[half:] = own_ref[half:] + from2_ref[0].astype(F32)
 
@@ -121,67 +120,82 @@
         out[...] = rows_ref[lax.div(place_ref[2], 2) ^ t].astype(out.dtype)
 
 
-def sum_kernel(scale, *refs):
-    *parts, out_ref = refs
-    total = parts[0][...]
-    for part in parts[1:]:
-        total = total + part[...].astype(F32)
-    out_ref[...] = total * scale
-
-
-def early_kernel(near, paired, got, far, mine_ref, other_ref):
+def relay_kernel(x_ref, _, *outs):
+    for i, out in enumerate(outs):
+        out[...] = x_ref[i * out.shape[0] : (i + 1) * out.shape[0]]
+
+
+def columns_of(ref, start, owned):
+    high = ref.shape[0] - start
+    chunk = [ref[start:, q * 128 : (q + 1) * 128] for q in range(owned // high)]
+    return jnp.concatenate(chunk, axis=0)
+
+
+def early_kernel(near, paired, got, far, mine_ref, other_ref, sum_ref):
     owned = mine_ref.shape[0]
     left = jnp.concatenate([near[:owned], paired[:owned]], axis=0)
-    for t, block in enumerate((near, got, far)):
-        rows = dot1(left, block[:owned], NT)
+    total = None
+    for t, ref in enumerate((near, got, far)):
+        rows = dot1(left, ref[:owned], NT)
         at = slice(t * owned, (t + 1) * owned)
         mine_ref[:, at] = rows[:owned]
         other_ref[:, at] = rows[owned:].astype(BF16)
-
-
-def late_kernel(near, paired, far, mine_early, other_early, mine_ref, other_ref):
+        value = dot1(columns_of(ref, owned, owned), ref[:owned], TN)
+        total = value if total is None else total + value
+    sum_ref[...] = total
+
+
+def late_kernel(count, place_ref, near, paired, mine_early, other_early, sum_early, *refs):
+    far = jnp.concatenate([ref[...] for ref in refs[:1]], axis=0)
+    mine_ref, part_ref, other_ref, sum_ref = refs[1 + count :]
     owned, before = mine_early.shape
+    half = owned // 2
+    wide = mine_ref.shape[1]
+    part = part_ref.shape[0]
     mine_ref[:, :before] = mine_early[...]
-    other_ref[:, :before] = other_early[...]
     left = jnp.concatenate([near[:owned], paired[:owned]], axis=0)
     rows = dot1(left, far[:owned], NT)
     mine_ref[:, before:] = rows[:owned]
-    other_ref[:, before:] = rows[owned:].astype(BF16)
+    for i in range(2):
+        at = slice(i * half, (i + 1) * half)
+        other_ref[:half, i * wide : i * wide + before] = other_early[at]
+        other_ref[:half, i * wide + before : (i + 1) * wide] = rows[owned:][at].astype(BF16)
+    sum_ref[...] = sum_early[...] + dot1(columns_of(far, owned, owned), far[:owned], TN)
+    part_ref[...] = sum_ref[pl.ds(pl.multiple_of(lax.rem(place_ref[2], 4) * part, part), part)]
+    away = sum_ref[pl.ds(pl.multiple_of(lax.rem(place_ref[2] ^ 1, 4) * part, part), part)]
+    other_ref[half : half + part], other_ref[half + part :] = halves(away)
 
 
 def place_kernel(place_ref, mine, came, *outs):
     *outs, rows_ref = outs
-    owned = mine.shape[0]
-    for t in range(mine.shape[1] // owned):
-        for core, part in enumerate((mine, came)):
-            at = pl.multiple_of((place_ref[2] ^ (2 * t + core)) * owned, owned)
-            rows_ref[:, pl.ds(at, owned)] = part[:, t * owned : (t + 1) * owned].astype(F32)
+    owned, wide = mine.shape
+    half = owned // 2
+    for t in range(wide // owned):
+        at = pl.multiple_of((place_ref[2] ^ (2 * t)) * owned, owned)
+        rows_ref[:, pl.ds(at, owned)] = mine[:, t * owned : (t + 1) * owned]
+        at = pl.multiple_of((place_ref[2] ^ (2 * t + 1)) * owned, owned)
+        for i in range(2):
+            part = came[:half, i * wide + t * owned : i * wide + (t + 1) * owned]
+            rows_ref[i * half : (i + 1) * half, pl.ds(at, owned)] = part.astype(F32)
     height = owned // len(outs)
     for t, out in enumerate(outs):
         at = pl.multiple_of((place_ref[1] ^ t) * height, height)
         out[...] = rows_ref[pl.ds(at, height)].astype(out.dtype)
 
 
-def reduced_kernel(place_ref, *refs):
-    *blocks, _, mine_ref, other_ref, sum_ref = refs
-    part = mine_ref.shape[0]
-    high = blocks[0].shape[0] * 128 // (blocks[0].shape[1] + 128)
-    owned = blocks[0].shape[0] - high
-    total = None
-    for block in blocks:
-        chunk = [block[owned:, q * 128 : (q + 1) * 128] for q in range(owned // high)]
-        value = dot1(jnp.concatenate(chunk, axis=0), block[:owned], TN)
-        total = value if total is None else total + value
-    sum_ref[...] = total
-    for out, ja in ((mine_ref, place_ref[2]), (other_ref, place_ref[2] ^ 1)):
-        out[...] = sum_ref[pl.ds(pl.multiple_of(lax.rem(ja, 4) * part, part), part)]
-
-
-def add_kernel(mine, came, out_ref):
-    slices, _, rank = out_ref.shape
+def last_kernel(scales, count, mine, came, *refs):
+    parts, outs = refs[: 2 * count], refs[2 * count :]
+    for i, scale in enumerate(scales):
+        total = parts[i * count][...]
+        for part in parts[i * count + 1 : (i + 1) * count]:
+            total = total + part[...].astype(F32)
+        outs[i][...] = total * scale
+    slices, part, rank = outs[2].shape
     for k in range(slices):
         at = slice(k * rank, (k + 1) * rank)
-        out_ref[k] = mine[:, at] + came[:, at]
+        low = came[came.shape[0] - part :, at].astype(F32)
+        high = came[came.shape[0] - 2 * part : came.shape[0] - part, at].astype(F32)
+        outs[2][k] = mine[:, at] + (high + low)
 
 
 def xor_permute(x, axis, bits):
@@ -245,25 +259,27 @@
     )
     from1 = xor_permute(to1, "ka", 1)
     from2 = xor_permute(to2, "ka", 2)
-    total, to1, to2, far2 = call(
+    total, to1, to2 = call(
         middle_kernel,
         "middle",
-        [(shape, F32), (half, BF16), (half, BF16), (far2.shape, BF16)],
-        [VMEM] * 6,
+        [(shape, F32), (half, BF16), (half, BF16)],
+        [VMEM] * 5 + [ANY] * 2,
         own,
         keep1,
         keep2,
         from1,
         from2,
+        got1,
         far2,
     )
     from1 = xor_permute(to1, "ka", 1)
     from2 = xor_permute(to2, "ka", 2)
-    far3 = xor_permute(far2, "ja", 2)
+    far3 = call(relay_kernel, "relay", [(far.shape, BF16)], [VMEM, ANY], far2, total)
+    far3 = [xor_permute(p, "ja", 2) for p in far3]
     begun = call(
         early_kernel,
         "two_early",
-        [((owned, 3 * owned), F32), ((owned, 3 * owned), BF16)],
+        [((owned, 3 * owned), F32), ((owned, 3 * owned), BF16), ((128, columns), F32)],
         [VMEM] * 4,
         near,
         paired,
@@ -283,52 +299,44 @@
         scratch=[pltpu.VMEM(shape, F32)],
     )
     sums = [p if t == 0 else xor_permute(p, "ja", 2 * t) for t, p in enumerate(sums)]
-    (gram_one,) = call(
-        functools.partial(sum_kernel, norm_one), "one", [(shape[1:], F32)], [VMEM] * count_z, *sums
-    )
-
-    mine, other = call(
-        late_kernel,
+
+    waits = sums[:1]
+    mine, mine_part, other = call(
+        functools.partial(late_kernel, len(waits)),
         "two_late",
-        [((owned, 4 * owned), F32), ((owned, 4 * owned), BF16)],
-        [VMEM] * 5,
+        [((owned, 4 * owned), F32), ((part, columns), F32), ((owned // 2 + 2 * part, columns), BF16)],
+        [SMEM] + [VMEM] * 6 + [ANY] * len(waits),
+        place,
         near,
         paired,
-        far3,
         *begun,
+        *far3,
+        *waits,
+        scratch=[pltpu.VMEM((128, columns), F32)],
     )
     other = xor_permute(other, "ja", 1)
-    shape = (owned // count_ka, count_ja * owned)
+    final = (owned // count_ka, count_ja * owned)
     rows = call(
         place_kernel,
         "two_place",
-        [(shape, F32 if t == 0 else BF16) for t in range(count_ka)],
+        [(final, F32 if t == 0 else BF16) for t in range(count_ka)],
         [SMEM] + [VMEM] * 2,
         place,
         mine,
         other,
         scratch=[pltpu.VMEM((owned, count_ja * owned), F32)],
     )
-    mine, other = call(
-        reduced_kernel,
-        "reduced",
-        [((part, columns), F32)] * 2,
-        [SMEM] + [VMEM] * 4 + [ANY],
-        place,
-        near,
-        got1,
-        far2,
-        far3,
-        rows[0],
-        scratch=[pltpu.VMEM((128, columns), F32)],
-    )
-    other = xor_permute(other, "ja", 1)
-    (reduced,) = call(add_kernel, "add", [((slices, part, rank_one), F32)], [VMEM] * 2, mine, other)
     rows = [p if t == 0 else xor_permute(p, "ka", t) for t, p in enumerate(rows)]
-    (gram_two,) = call(
-        functools.partial(sum_kernel, norm_two), "two", [(shape, F32)], [VMEM] * count_ka, *rows
-    )
-    return (gram_one, gram_two, reduced)
+    return call(
+        functools.partial(last_kernel, (norm_one, norm_two), count_z),
+        "last",
+        [(shape[1:], F32), (final, F32), ((slices, part, rank_one), F32)],
+        [VMEM] * (2 + count_z + count_ka),
+        mine_part,
+        other,
+        *sums,
+        *rows,
+    )
 
 
 def plain_shards(tensor, factor_one, factor_two):
@@ -386,7 +394,7 @@
     tiled = tiled and step % 128 == 0 and owned % 128 == 0
     tiled = tiled and step % (16 * count_ka) == 0 and owned % (16 * count_ka) == 0
     tiled = tiled and owned * 128 % (16 * columns) == 0 and columns % 128 == 0
-    tiled = tiled and owned * 128 // columns * (columns // 128) == owned
+    tiled = tiled and columns == 8 * owned and owned == 128
     return (tiled_shards if tiled else plain_shards)(tensor, factor_one, factor_two)
 
 

time: 52.4 us -> 48.3 us (0.922)
  waiting for transfers between devices: 17 us -> 14.2 us
  Pallas kernels: 12 us -> 10.6 us
    ppermute x17 -> x16, waiting for transfers between devices: 17 us -> 14.2 us  [xor_permute(): lax.ppermute(x, axis, [(i, i ^ bits) for i in range(lax.axis_size(axis))])]
    pallas_call x12 -> x10, Pallas kernels: 12 us -> 10.6 us  [call(): pl.pallas_call(kernel, out_shape=[jax.ShapeDtypeStruct(s, d) for s, d in...]
    ppermute x17 -> x16, starting transfers between devices: 20.8 us -> 20.9 us  [xor_permute(): lax.ppermute(x, axis, [(i, i ^ bits) for i in range(lax.axis_size(axis))])]
  transfers between devices with their start and end apart: 17 -> 16, of which waited for: 7 -> 7; matrix products, arithmetic and copies ran while one was open for 0% -> 0% of each run, Pallas kernels for 17% -> 13%
where the time goes in v4:
time: 48.3 us; the launch traced here: 48.2 us
  starting transfers between devices  20.9 us (43%)
  waiting for transfers between devices  14.2 us (29%)
  Pallas kernels  10.6 us (22%)
  local copies, waits for them, and re-layouts  1.61 us (3%)
  between operations  0.74 us (2%)
    ppermute x16, starting transfers between devices, xor_permute(): lax.ppermute(x, axis, [(i, i ^ bits) for i in range(lax.axis_size(axis))])  20.9 us
    ppermute x16, waiting for transfers between devices, xor_permute(): lax.ppermute(x, axis, [(i, i ^ bits) for i in range(lax.axis_size(axis))])  14.2 us
    pallas_call x10, Pallas kernels, call(): pl.pallas_call(kernel, out_shape=[jax.ShapeDtypeStruct(s, d) for s, d in...  10.6 us
    unnamed x8, local copies, waits for them, and re-layouts  1.61 us
  transfers between devices with their start and end apart: 16, of which 7 were waited for; matrix products, arithmetic and copies ran while one was open for 0% of the time, Pallas kernels for 13%

profile of v4, /device:TPU:0, one launch (start us, length us, event | category | flops | bytes accessed | tf_op | source)
XLA Modules:
  0.0 48.2 jit_solution(17142617730171080516)
XLA Ops:
  0.6 0.1 pad_add_fusion.place_ref
  0.7 0.0 copy-start
  0.7 1.6 %copy-done = f32[4,128,1024]{2,1,0:T(8,128)S(1)} copy-done((f32[4,128,1024]{2,1,0:T(8,128)S(1)}, f32[4,128,1024]{2,1,0:T(8,128)}, u32[]{:S(2)}) %copy-start) | copy-done | bytes 2097176
  2.3 2.5 %away.1._ = bf16[4,128,1024]{2,1,0:T(8,128)(2,1)S(1)} custom-call(s32[3]{0:T(128)S(1)} %pad_add_fusion.place_ref, f32[4,128,1024]{2,1,0:T(8,128)S(1)} %copy-done), custom_call_target="tpu_custom_call" | custom-call | tf_op jit(solution)/shard_map/away/pallas_call | solution.py:35
  4.8 0.0 copy-start.1
  4.8 0.5 %collective-permute-start.3 = (bf16[4,128,1024]{2,1,0:T(8,128)(2,1)S(1)}, bf16[4,128,1024]{2,1,0:T(8,128)(2,1)S(1)}, u32[]{:S(2)}, u32[]{:S(2)}) collective-permute-start(bf16[4,128,1024]{2,1,0:T(8,128)(2,1)S(1)} %away.1._), channel_id=1, source_target_pairs={{0,4},{4,0},{8,12},{12,8},{16,20},{20,16},{24,28},{28,24},{1,5},{5... | collective-permute-start | bytes 3145736 | tf_op jit(solution)/shard_map/ppermute | solution.py:202
  5.3 0.0 copy-done.2
  5.3 0.0 copy-done.3
  5.3 1.6 %core.1 = (bf16[144,1024]{1,0:T(8,128)(2,1)S(1)}, bf16[144,1024]{1,0:T(8,128)(2,1)S(1)}) custom-call(s32[3]{0:T(128)S(1)} %pad_add_fusion.place_ref, f32[4,128,1024]{2,1,0:T(8,128)S(1)} %copy-done, f32[1024,256]{1,0:T(8,128)S(1)} %copy-done.2, bf16[128,256]{1,0:T(8,128)(2,1)S(1)} %copy-done.3, bf16[4,128,1024]{2,1,0:T(8,128)(2,1)S(1)} %away.1._), custom_call_target="tpu_custom_call" | custom-call | tf_op jit(solution)/shard_map/core/pallas_call | solution.py:35
  6.9 0.1 collective-permute-start
  7.0 3.0 %collective-permute-start.1 = (bf16[144,1024]{1,0:T(8,128)(2,1)S(1)}, bf16[144,1024]{1,0:T(8,128)(2,1)S(1)}, u32[]{:S(2)}, u32[]{:S(2)}) collective-permute-start(bf16[144,1024]{1,0:T(8,128)(2,1)S(1)} %get-tuple-element.27.near), channel_id=1, source_target_pairs={{0,8},{4,12},{8,0},{12,4},{16,24},{20,28},{24,16},{28,20},{1,9},{5... | collective-permute-start | bytes 884744 | tf_op jit(solution)/shard_map/ppermute | solution.py:202
  10.0 2.6 %collective-permute-start.2 = (bf16[144,1024]{1,0:T(8,128)(2,1)S(1)}, bf16[144,1024]{1,0:T(8,128)(2,1)S(1)}, u32[]{:S(2)}, u32[]{:S(2)}) collective-permute-start(bf16[144,1024]{1,0:T(8,128)(2,1)S(1)} %get-tuple-element.28), channel_id=1, source_target_pairs={{0,16},{4,20},{8,24},{12,28},{16,0},{20,4},{24,8},{28,12},{1,17},{... | collective-permute-start | bytes 884744 | tf_op jit(solution)/shard_map/ppermute | solution.py:202
  12.6 0.0 collective-permute-done.paired._
  12.6 0.0 collective-permute-done.3.came_ref
  12.6 0.0 copy-done.1
  12.6 2.7 %home.1 = (f32[4,32,1024]{2,1,0:T(8,128)S(1)}, f32[2,32,1024]{2,1,0:T(8,128)S(1)}, f32[2,32,1024]{2,1,0:T(8,128)S(1)}, bf16[2,2,32,1024]{3,2,1,0:T(8,128)(2,1)S(1)}, bf16[2,2,32,1024]{3,2,1,0:T(8,128)(2,1)S(1)}) custom-call(s32[3]{0:T(128)S(1)} %pad_add_fusion.place_ref, f32[4,128,1024]{2,1,0:T(8,128)S(1)} %copy-done.1, ...), custom_call_target="tpu_custom_call" | custom-call | tf_op jit(solution)/shard_map/home/pallas_call | solution.py:35
  15.4 1.6 %collective-permute-start.4 = (bf16[2,2,32,1024]{3,2,1,0:T(8,128)(2,1)S(1)}, bf16[2,2,32,1024]{3,2,1,0:T(8,128)(2,1)S(1)}, u32[]{:S(2)}, u32[]{:S(2)}) collective-permute-start(bf16[2,2,32,1024]{3,2,1,0:T(8,128)(2,1)S(1)} %get-tuple-element.35), channel_id=1, source_target_pairs={{0,1},{1,0},{2,3},{3,2},{4,5},{5,4},{6,7},{7,6},{8,9},{9,8},{10,11... | collective-permute-start | bytes 786440 | tf_op jit(solution)/shard_map/ppermute | solution.py:202
  16.9 1.5 %collective-permute-start.5 = (bf16[2,2,32,1024]{3,2,1,0:T(8,128)(2,1)S(1)}, bf16[2,2,32,1024]{3,2,1,0:T(8,128)(2,1)S(1)}, u32[]{:S(2)}, u32[]{:S(2)}) collective-permute-start(bf16[2,2,32,1024]{3,2,1,0:T(8,128)(2,1)S(1)} %get-tuple-element.36), channel_id=1, source_target_pairs={{0,2},{1,3},{2,0},{3,1},{4,6},{5,7},{6,4},{7,5},{8,10},{9,11},{10,... | collective-permute-start | bytes 786440 | tf_op jit(solution)/shard_map/ppermute | solution.py:202
  18.4 5.0 %collective-permute-done.1.got._ = bf16[144,1024]{1,0:T(8,128)(2,1)S(1)} collective-permute-done((bf16[144,1024]{1,0:T(8,128)(2,1)S(1)}, bf16[144,1024]{1,0:T(8,128)(2,1)S(1)}, u32[]{:S(2)}, u32[]{:S(2)}) %collective-permute-start.1) | collective-permute-done | bytes 294944 | tf_op jit(solution)/shard_map/ppermute | solution.py:202
  23.5 2.5 %collective-permute-done.2.far.__.x_ref = bf16[144,1024]{1,0:T(8,128)(2,1)S(1)} collective-permute-done((bf16[144,1024]{1,0:T(8,128)(2,1)S(1)}, bf16[144,1024]{1,0:T(8,128)(2,1)S(1)}, u32[]{:S(2)}, u32[]{:S(2)}) %collective-permute-start.2) | collective-permute-done | bytes 294944 | tf_op jit(solution)/shard_map/ppermute | solution.py:202
  26.0 0.0 collective-permute-done.4.from1_ref
  26.0 0.0 collective-permute-done.5.from2_ref
  26.0 0.1 middle.1
  26.1 0.5 %collective-permute-start.6 = (bf16[144,1024]{1,0:T(8,128)(2,1)S(1)}, bf16[144,1024]{1,0:T(8,128)(2,1)S(1)}, u32[]{:S(2)}, u32[]{:S(2)}) collective-permute-start(bf16[144,1024]{1,0:T(8,128)(2,1)S(1)} %relay.1), channel_id=1, source_target_pairs={{0,8},{4,12},{8,0},{12,4},{16,24},{20,28},{24,16},{28,20},{1,9},{5... | collective-permute-start | bytes 884744 | tf_op jit(solution)/shard_map/ppermute | solution.py:202
  26.7 1.5 %collective-permute-start.7 = (bf16[2,32,1024]{2,1,0:T(8,128)(2,1)S(1)}, bf16[2,32,1024]{2,1,0:T(8,128)(2,1)S(1)}, u32[]{:S(2)}, u32[]{:S(2)}) collective-permute-start(bf16[2,32,1024]{2,1,0:T(8,128)(2,1)S(1)} %get-tuple-element.38), channel_id=1, source_target_pairs={{0,1},{1,0},{2,3},{3,2},{4,5},{5,4},{6,7},{7,6},{8,9},{9,8},{10,11... | collective-permute-start | bytes 393224 | tf_op jit(solution)/shard_map/ppermute | solution.py:202
  28.1 1.5 %collective-permute-start.8 = (bf16[2,32,1024]{2,1,0:T(8,128)(2,1)S(1)}, bf16[2,32,1024]{2,1,0:T(8,128)(2,1)S(1)}, u32[]{:S(2)}, u32[]{:S(2)}) collective-permute-start(bf16[2,32,1024]{2,1,0:T(8,128)(2,1)S(1)} %get-tuple-element.39), channel_id=1, source_target_pairs={{0,2},{1,3},{2,0},{3,1},{4,6},{5,7},{6,4},{7,5},{8,10},{9,11},{10,... | collective-permute-start | bytes 393224 | tf_op jit(solution)/shard_map/ppermute | solution.py:202
  29.7 0.8 %two_early.1 = (f32[128,384]{1,0:T(8,128)S(1)}, bf16[128,384]{1,0:T(8,128)(2,1)S(1)}, f32[128,1024]{1,0:T(8,128)S(1)}) custom-call(bf16[144,1024]{1,0:T(8,128)(2,1)S(1)} %get-tuple-element.27.near, bf16[144,1024]{1,0:T(8,128)(2,1)S(1)} %collective-permute-done.paired._, bf16[144,1024]{1,0:T(8,128)(2,1)S(1)} %collective-permute-done.1.got._, ...), custom_call_target="tpu_custom_call" | custom-call | tf_op jit(solution)/shard_map/two_early/pallas_call | solution.py:35
  30.4 1.2 %collective-permute-done.7.from1_ref = bf16[2,32,1024]{2,1,0:T(8,128)(2,1)S(1)} collective-permute-done((bf16[2,32,1024]{2,1,0:T(8,128)(2,1)S(1)}, bf16[2,32,1024]{2,1,0:T(8,128)(2,1)S(1)}, u32[]{:S(2)}, u32[]{:S(2)}) %collective-permute-start.7) | collective-permute-done | bytes 131104 | tf_op jit(solution)/shard_map/ppermute | solution.py:202
  31.6 1.5 %collective-permute-done.8.from2_ref = bf16[2,32,1024]{2,1,0:T(8,128)(2,1)S(1)} collective-permute-done((bf16[2,32,1024]{2,1,0:T(8,128)(2,1)S(1)}, bf16[2,32,1024]{2,1,0:T(8,128)(2,1)S(1)}, u32[]{:S(2)}, u32[]{:S(2)}) %collective-permute-start.8) | collective-permute-done | bytes 131104 | tf_op jit(solution)/shard_map/ppermute | solution.py:202
  33.1 0.6 %slab.1 = (f32[32,1024]{1,0:T(8,128)S(1)}, bf16[32,1024]{1,0:T(8,128)(2,1)S(1)}, bf16[32,1024]{1,0:T(8,128)(2,1)S(1)}, bf16[32,1024]{1,0:T(8,128)(2,1)S(1)}) custom-call(s32[3]{0:T(128)S(1)} %pad_add_fusion.place_ref, f32[4,32,1024]{2,1,0:T(8,128)S(1)} %get-tuple-element.37._.sum_ref, bf16[2,32,1024]{2,1,0:T(8,128)(2,1)S(1)} %collective-permute-done.7.from1_ref, ...), custom_call_target="tpu_custom_call" | custom-call | tf_op jit(solution)/shard_map/slab/pallas_call | solution.py:35
  33.7 0.0 collective-permute-done.6.refs_0_
  33.7 0.9 %two_late.1 = (f32[128,512]{1,0:T(8,128)S(1)}, f32[32,1024]{1,0:T(8,128)S(1)}, bf16[128,1024]{1,0:T(8,128)(2,1)S(1)}) custom-call(s32[3]{0:T(128)S(1)} %pad_add_fusion.place_ref, bf16[144,1024]{1,0:T(8,128)(2,1)S(1)} %get-tuple-element.27.near, bf16[144,1024]{1,0:T(8,128)(2,1)S(1)} %collective-permute-done.paired._, ...), custom_call_target="tpu_custom_call" | custom-call | tf_op jit(solution)/shard_map/two_late/pallas_call | solution.py:35
  34.7 0.1 collective-permute-start.9
  34.8 1.6 %collective-permute-start.10 = (bf16[32,1024]{1,0:T(8,128)(2,1)S(1)}, bf16[32,1024]{1,0:T(8,128)(2,1)S(1)}, u32[]{:S(2)}, u32[]{:S(2)}) collective-permute-start(bf16[32,1024]{1,0:T(8,128)(2,1)S(1)} %get-tuple-element.43), channel_id=1, source_target_pairs={{0,8},{4,12},{8,0},{12,4},{16,24},{20,28},{24,16},{28,20},{1,9},{5... | collective-permute-start | bytes 196616 | tf_op jit(solution)/shard_map/ppermute | solution.py:202
  36.4 1.8 %collective-permute-start.11 = (bf16[32,1024]{1,0:T(8,128)(2,1)S(1)}, bf16[32,1024]{1,0:T(8,128)(2,1)S(1)}, u32[]{:S(2)}, u32[]{:S(2)}) collective-permute-start(bf16[32,1024]{1,0:T(8,128)(2,1)S(1)} %get-tuple-element.44), channel_id=1, source_target_pairs={{0,16},{4,20},{8,24},{12,28},{16,0},{20,4},{24,8},{28,12},{1,17},{... | collective-permute-start | bytes 196616 | tf_op jit(solution)/shard_map/ppermute | solution.py:202
  38.2 1.0 %collective-permute-start.12 = (bf16[32,1024]{1,0:T(8,128)(2,1)S(1)}, bf16[32,1024]{1,0:T(8,128)(2,1)S(1)}, u32[]{:S(2)}, u32[]{:S(2)}) collective-permute-start(bf16[32,1024]{1,0:T(8,128)(2,1)S(1)} %get-tuple-element.45), channel_id=1, source_target_pairs={{0,24},{4,28},{8,16},{12,20},{16,8},{20,12},{24,0},{28,4},{1,25},{... | collective-permute-start | bytes 196616 | tf_op jit(solution)/shard_map/ppermute | solution.py:202
  39.2 0.0 collective-permute-done.9.came
  39.2 0.6 %two_place.1 = (f32[32,1024]{1,0:T(8,128)S(1)}, bf16[32,1024]{1,0:T(8,128)(2,1)S(1)}, bf16[32,1024]{1,0:T(8,128)(2,1)S(1)}, bf16[32,1024]{1,0:T(8,128)(2,1)S(1)}) custom-call(s32[3]{0:T(128)S(1)} %pad_add_fusion.place_ref, f32[128,512]{1,0:T(8,128)S(1)} %get-tuple-element.46.mine, bf16[128,1024]{1,0:T(8,128)(2,1)S(1)} %collective-permute-done.9.came), custom_call_target="tpu_custom_call" | custom-call | tf_op jit(solution)/shard_map/two_place/pallas_call | solution.py:35
  39.9 0.8 %collective-permute-start.13 = (bf16[32,1024]{1,0:T(8,128)(2,1)S(1)}, bf16[32,1024]{1,0:T(8,128)(2,1)S(1)}, u32[]{:S(2)}, u32[]{:S(2)}) collective-permute-start(bf16[32,1024]{1,0:T(8,128)(2,1)S(1)} %get-tuple-element.48), channel_id=1, source_target_pairs={{0,1},{1,0},{2,3},{3,2},{4,5},{5,4},{6,7},{7,6},{8,9},{9,8},{10,11... | collective-permute-start | bytes 196616 | tf_op jit(solution)/shard_map/ppermute | solution.py:202
  40.7 1.5 %collective-permute-start.14 = (bf16[32,1024]{1,0:T(8,128)(2,1)S(1)}, bf16[32,1024]{1,0:T(8,128)(2,1)S(1)}, u32[]{:S(2)}, u32[]{:S(2)}) collective-permute-start(bf16[32,1024]{1,0:T(8,128)(2,1)S(1)} %get-tuple-element.49), channel_id=1, source_target_pairs={{0,2},{1,3},{2,0},{3,1},{4,6},{5,7},{6,4},{7,5},{8,10},{9,11},{10,... | collective-permute-start | bytes 196616 | tf_op jit(solution)/shard_map/ppermute | solution.py:202
  42.2 0.0 collective-permute-done.10.refs_1_
  42.2 1.2 %collective-permute-start.15 = (bf16[32,1024]{1,0:T(8,128)(2,1)S(1)}, bf16[32,1024]{1,0:T(8,128)(2,1)S(1)}, u32[]{:S(2)}, u32[]{:S(2)}) collective-permute-start(bf16[32,1024]{1,0:T(8,128)(2,1)S(1)} %get-tuple-element.50), channel_id=1, source_target_pairs={{0,3},{1,2},{2,1},{3,0},{4,7},{5,6},{6,5},{7,4},{8,11},{9,10},{10,... | collective-permute-start | bytes 196616 | tf_op jit(solution)/shard_map/ppermute | solution.py:202
  43.4 1.4 %collective-permute-done.11.refs_2_ = bf16[32,1024]{1,0:T(8,128)(2,1)S(1)} collective-permute-done((bf16[32,1024]{1,0:T(8,128)(2,1)S(1)}, bf16[32,1024]{1,0:T(8,128)(2,1)S(1)}, u32[]{:S(2)}, u32[]{:S(2)}) %collective-permute-start.11) | collective-permute-done | bytes 65568 | tf_op jit(solution)/shard_map/ppermute | solution.py:202
  44.8 0.0 collective-permute-done.12.refs_3_
  44.8 0.0 collective-permute-done.13.refs_5_
  44.8 0.3 collective-permute-done.14.refs_6_
  45.1 2.3 %collective-permute-done.15.refs_7_ = bf16[32,1024]{1,0:T(8,128)(2,1)S(1)} collective-permute-done((bf16[32,1024]{1,0:T(8,128)(2,1)S(1)}, bf16[32,1024]{1,0:T(8,128)(2,1)S(1)}, u32[]{:S(2)}, u32[]{:S(2)}) %collective-permute-start.15) | collective-permute-done | bytes 65568 | tf_op jit(solution)/shard_map/ppermute | solution.py:202
  47.4 0.8 %last.1 = (f32[32,1024]{1,0:T(8,128)}, f32[32,1024]{1,0:T(8,128)}, f32[4,32,256]{2,1,0:T(8,128)}) custom-call(f32[32,1024]{1,0:T(8,128)S(1)} %get-tuple-element.41.mine, bf16[128,1024]{1,0:T(8,128)(2,1)S(1)} %collective-permute-done.9.came, f32[32,1024]{1,0:T(8,128)S(1)} %get-tuple-element.40.refs_1_.refs_0_, ...), custom_call_target="tpu_custom_call" | custom-call | tf_op jit(solution)/shard_map/last/pallas_call | solution.py:35
  (3 shorter events, 0.0 us)
Async XLA Ops:
  0.7 1.6 %copy-start = (f32[4,128,1024]{2,1,0:T(8,128)S(1)}, f32[4,128,1024]{2,1,0:T(8,128)}, u32[]{:S(2)}) copy-start(f32[4,128,1024]{2,1,0:T(8,128)} %x_ref.5) | copy-start | bytes 6291460
  2.3 3.0 %copy-start.2 = (f32[1024,256]{1,0:T(8,128)S(1)}, f32[1024,256]{1,0:T(8,128)}, u32[]{:S(2)}) copy-start(f32[1024,256]{1,0:T(8,128)} %f_ref.1) | copy-start | bytes 3145732
  2.3 3.0 %copy-start.3 = (bf16[128,256]{1,0:T(8,128)(2,1)S(1)}, bf16[128,256]{1,0:T(8,128)(2,1)}, u32[]{:S(2)}) copy-start(bf16[128,256]{1,0:T(8,128)(2,1)} %two_ref.1) | copy-start | bytes 196612
  4.8 7.9 %copy-start.1 = (f32[4,128,1024]{2,1,0:T(8,128)S(1)}, f32[4,128,1024]{2,1,0:T(8,128)}, u32[]{:S(2)}) copy-start(f32[4,128,1024]{2,1,0:T(8,128)} %x_ref.5) | copy-start | bytes 6291460
  4.8 7.8 %collective-permute-start.3 = (bf16[4,128,1024]{2,1,0:T(8,128)(2,1)S(1)}, bf16[4,128,1024]{2,1,0:T(8,128)(2,1)S(1)}, u32[]{:S(2)}, u32[]{:S(2)}) collective-permute-start(bf16[4,128,1024]{2,1,0:T(8,128)(2,1)S(1)} %away.1._), channel_id=1, source_target_pairs={{0,4},{4,0},{8,12},{12,8},{16,20},{20,16},{24,28},{28,24},{1,5},{5... | collective-permute-start | bytes 3145736 | tf_op jit(solution)/shard_map/ppermute | solution.py:202
  6.9 5.7 %collective-permute-start = (bf16[144,1024]{1,0:T(8,128)(2,1)S(1)}, bf16[144,1024]{1,0:T(8,128)(2,1)S(1)}, u32[]{:S(2)}, u32[]{:S(2)}) collective-permute-start(bf16[144,1024]{1,0:T(8,128)(2,1)S(1)} %get-tuple-element.27.near), channel_id=1, source_target_pairs={{0,4},{4,0},{8,12},{12,8},{16,20},{20,16},{24,28},{28,24},{1,5},{5... | collective-permute-start | bytes 884744 | tf_op jit(solution)/shard_map/ppermute | solution.py:202
  7.0 16.5 %collective-permute-start.1 = (bf16[144,1024]{1,0:T(8,128)(2,1)S(1)}, bf16[144,1024]{1,0:T(8,128)(2,1)S(1)}, u32[]{:S(2)}, u32[]{:S(2)}) collective-permute-start(bf16[144,1024]{1,0:T(8,128)(2,1)S(1)} %get-tuple-element.27.near), channel_id=1, source_target_pairs={{0,8},{4,12},{8,0},{12,4},{16,24},{20,28},{24,16},{28,20},{1,9},{5... | collective-permute-start | bytes 884744 | tf_op jit(solution)/shard_map/ppermute | solution.py:202
  10.0 16.0 %collective-permute-start.2 = (bf16[144,1024]{1,0:T(8,128)(2,1)S(1)}, bf16[144,1024]{1,0:T(8,128)(2,1)S(1)}, u32[]{:S(2)}, u32[]{:S(2)}) collective-permute-start(bf16[144,1024]{1,0:T(8,128)(2,1)S(1)} %get-tuple-element.28), channel_id=1, source_target_pairs={{0,16},{4,20},{8,24},{12,28},{16,0},{20,4},{24,8},{28,12},{1,17},{... | collective-permute-start | bytes 884744 | tf_op jit(solution)/shard_map/ppermute | solution.py:202
  15.4 10.7 %collective-permute-start.4 = (bf16[2,2,32,1024]{3,2,1,0:T(8,128)(2,1)S(1)}, bf16[2,2,32,1024]{3,2,1,0:T(8,128)(2,1)S(1)}, u32[]{:S(2)}, u32[]{:S(2)}) collective-permute-start(bf16[2,2,32,1024]{3,2,1,0:T(8,128)(2,1)S(1)} %get-tuple-element.35), channel_id=1, source_target_pairs={{0,1},{1,0},{2,3},{3,2},{4,5},{5,4},{6,7},{7,6},{8,9},{9,8},{10,11... | collective-permute-start | bytes 786440 | tf_op jit(solution)/shard_map/ppermute | solution.py:202
  16.9 9.1 %collective-permute-start.5 = (bf16[2,2,32,1024]{3,2,1,0:T(8,128)(2,1)S(1)}, bf16[2,2,32,1024]{3,2,1,0:T(8,128)(2,1)S(1)}, u32[]{:S(2)}, u32[]{:S(2)}) collective-permute-start(bf16[2,2,32,1024]{3,2,1,0:T(8,128)(2,1)S(1)} %get-tuple-element.36), channel_id=1, source_target_pairs={{0,2},{1,3},{2,0},{3,1},{4,6},{5,7},{6,4},{7,5},{8,10},{9,11},{10,... | collective-permute-start | bytes 786440 | tf_op jit(solution)/shard_map/ppermute | solution.py:202
  26.1 7.6 %collective-permute-start.6 = (bf16[144,1024]{1,0:T(8,128)(2,1)S(1)}, bf16[144,1024]{1,0:T(8,128)(2,1)S(1)}, u32[]{:S(2)}, u32[]{:S(2)}) collective-permute-start(bf16[144,1024]{1,0:T(8,128)(2,1)S(1)} %relay.1), channel_id=1, source_target_pairs={{0,8},{4,12},{8,0},{12,4},{16,24},{20,28},{24,16},{28,20},{1,9},{5... | collective-permute-start | bytes 884744 | tf_op jit(solution)/shard_map/ppermute | solution.py:202
  26.7 5.0 %collective-permute-start.7 = (bf16[2,32,1024]{2,1,0:T(8,128)(2,1)S(1)}, bf16[2,32,1024]{2,1,0:T(8,128)(2,1)S(1)}, u32[]{:S(2)}, u32[]{:S(2)}) collective-permute-start(bf16[2,32,1024]{2,1,0:T(8,128)(2,1)S(1)} %get-tuple-element.38), channel_id=1, source_target_pairs={{0,1},{1,0},{2,3},{3,2},{4,5},{5,4},{6,7},{7,6},{8,9},{9,8},{10,11... | collective-permute-start | bytes 393224 | tf_op jit(solution)/shard_map/ppermute | solution.py:202
  28.1 5.0 %collective-permute-start.8 = (bf16[2,32,1024]{2,1,0:T(8,128)(2,1)S(1)}, bf16[2,32,1024]{2,1,0:T(8,128)(2,1)S(1)}, u32[]{:S(2)}, u32[]{:S(2)}) collective-permute-start(bf16[2,32,1024]{2,1,0:T(8,128)(2,1)S(1)} %get-tuple-element.39), channel_id=1, source_target_pairs={{0,2},{1,3},{2,0},{3,1},{4,6},{5,7},{6,4},{7,5},{8,10},{9,11},{10,... | collective-permute-start | bytes 393224 | tf_op jit(solution)/shard_map/ppermute | solution.py:202
  34.7 4.5 %collective-permute-start.9 = (bf16[128,1024]{1,0:T(8,128)(2,1)S(1)}, bf16[128,1024]{1,0:T(8,128)(2,1)S(1)}, u32[]{:S(2)}, u32[]{:S(2)}) collective-permute-start(bf16[128,1024]{1,0:T(8,128)(2,1)S(1)} %get-tuple-element.42), channel_id=1, source_target_pairs={{0,4},{4,0},{8,12},{12,8},{16,20},{20,16},{24,28},{28,24},{1,5},{5... | collective-permute-start | bytes 786440 | tf_op jit(solution)/shard_map/ppermute | solution.py:202
  34.8 7.4 %collective-permute-start.10 = (bf16[32,1024]{1,0:T(8,128)(2,1)S(1)}, bf16[32,1024]{1,0:T(8,128)(2,1)S(1)}, u32[]{:S(2)}, u32[]{:S(2)}) collective-permute-start(bf16[32,1024]{1,0:T(8,128)(2,1)S(1)} %get-tuple-element.43), channel_id=1, source_target_pairs={{0,8},{4,12},{8,0},{12,4},{16,24},{20,28},{24,16},{28,20},{1,9},{5... | collective-permute-start | bytes 196616 | tf_op jit(solution)/shard_map/ppermute | solution.py:202
  36.4 8.4 %collective-permute-start.11 = (bf16[32,1024]{1,0:T(8,128)(2,1)S(1)}, bf16[32,1024]{1,0:T(8,128)(2,1)S(1)}, u32[]{:S(2)}, u32[]{:S(2)}) collective-permute-start(bf16[32,1024]{1,0:T(8,128)(2,1)S(1)} %get-tuple-element.44), channel_id=1, source_target_pairs={{0,16},{4,20},{8,24},{12,28},{16,0},{20,4},{24,8},{28,12},{1,17},{... | collective-permute-start | bytes 196616 | tf_op jit(solution)/shard_map/ppermute | solution.py:202
  38.2 6.6 %collective-permute-start.12 = (bf16[32,1024]{1,0:T(8,128)(2,1)S(1)}, bf16[32,1024]{1,0:T(8,128)(2,1)S(1)}, u32[]{:S(2)}, u32[]{:S(2)}) collective-permute-start(bf16[32,1024]{1,0:T(8,128)(2,1)S(1)} %get-tuple-element.45), channel_id=1, source_target_pairs={{0,24},{4,28},{8,16},{12,20},{16,8},{20,12},{24,0},{28,4},{1,25},{... | collective-permute-start | bytes 196616 | tf_op jit(solution)/shard_map/ppermute | solution.py:202
  39.9 5.0 %collective-permute-start.13 = (bf16[32,1024]{1,0:T(8,128)(2,1)S(1)}, bf16[32,1024]{1,0:T(8,128)(2,1)S(1)}, u32[]{:S(2)}, u32[]{:S(2)}) collective-permute-start(bf16[32,1024]{1,0:T(8,128)(2,1)S(1)} %get-tuple-element.48), channel_id=1, source_target_pairs={{0,1},{1,0},{2,3},{3,2},{4,5},{5,4},{6,7},{7,6},{8,9},{9,8},{10,11... | collective-permute-start | bytes 196616 | tf_op jit(solution)/shard_map/ppermute | solution.py:202
  40.7 4.4 %collective-permute-start.14 = (bf16[32,1024]{1,0:T(8,128)(2,1)S(1)}, bf16[32,1024]{1,0:T(8,128)(2,1)S(1)}, u32[]{:S(2)}, u32[]{:S(2)}) collective-permute-start(bf16[32,1024]{1,0:T(8,128)(2,1)S(1)} %get-tuple-element.49), channel_id=1, source_target_pairs={{0,2},{1,3},{2,0},{3,1},{4,6},{5,7},{6,4},{7,5},{8,10},{9,11},{10,... | collective-permute-start | bytes 196616 | tf_op jit(solution)/shard_map/ppermute | solution.py:202
  42.2 5.2 %collective-permute-start.15 = (bf16[32,1024]{1,0:T(8,128)(2,1)S(1)}, bf16[32,1024]{1,0:T(8,128)(2,1)S(1)}, u32[]{:S(2)}, u32[]{:S(2)}) collective-permute-start(bf16[32,1024]{1,0:T(8,128)(2,1)S(1)} %get-tuple-element.50), channel_id=1, source_target_pairs={{0,3},{1,2},{2,1},{3,0},{4,7},{5,6},{6,5},{7,4},{8,11},{9,10},{10,... | collective-permute-start | bytes 196616 | tf_op jit(solution)/shard_map/ppermute | solution.py:202

commit v5 on v4

--- a/solution.py
+++ b/solution.py
@@ -14,7 +14,6 @@
 NT = (((1,), (1,)), ((), ()))
 TN = (((0,), (0,)), ((), ()))
 VMEM = pl.BlockSpec(memory_space=pltpu.VMEM)
-SMEM = pl.BlockSpec(memory_space=pltpu.SMEM)
 ANY = pl.BlockSpec(memory_space=pl.ANY)
 
 
@@ -44,31 +43,36 @@
     )(*args)
 
 
+def position():
+    ja = lax.axis_index("ja")
+    return lax.rem(ja, 2), lax.div(ja, 2), lax.axis_index("ka"), ja
+
+
 def gram_rows(core, x_ref, groups, step, keep):
     slices, owned, width = x_ref.shape
     at = [pl.multiple_of((2 * g + core) * step, step) for g in range(groups)]
     left = [x_ref[:, :, pl.ds(a, step)].reshape(slices * owned, step) for a in at]
-    left = halves(jnp.concatenate(left, axis=1))
+    left = halves(jnp.concatenate(left, axis=1).T)
     wide = min(256, width)
     for n in range(0, width, wide):
         right = halves(x_ref[:, :, n : n + wide].reshape(slices * owned, wide))
-        keep(slice(n, n + wide), dot3(left, right, TN).reshape(groups, step, wide))
-
-
-def away_kernel(place_ref, x_ref, away_ref):
+        keep(slice(n, n + wide), dot3(left, right, NN).reshape(groups, step, wide))
+
+
+def away_kernel(x_ref, away_ref):
     groups, step, _ = away_ref.shape
 
     def keep(at, rows):
         away_ref[:, :, at] = rows.astype(BF16)
 
-    gram_rows(1 - place_ref[0], x_ref, groups, step, keep)
-
-
-def core_kernel(place_ref, x_ref, f_ref, two_ref, _, near_ref, far_ref):
+    gram_rows(1 - position()[0], x_ref, groups, step, keep)
+
+
+def core_kernel(x_ref, f_ref, two_ref, _, near_ref, far_ref):
     slices, owned, _ = x_ref.shape
     rank = f_ref.shape[1]
     high = near_ref.shape[0] - owned
-    side = lax.div(place_ref[2], 4)
+    side = lax.div(position()[1], 2)
     for out, here in ((near_ref, side), (far_ref, 1 - side)):
         chunk = two_ref[:, pl.ds(pl.multiple_of(here * 128, 128), 128)]
         for q in range(owned // high):
@@ -81,7 +85,7 @@
         far_ref[:owned, at] = core
 
 
-def home_kernel(place_ref, x_ref, came_ref, _, own_ref, keep1_ref, keep2_ref, to1_ref, to2_ref, rows_ref):
+def home_kernel(x_ref, came_ref, _, own_ref, keep1_ref, keep2_ref, to1_ref, to2_ref, rows_ref):
     groups, step, _ = came_ref.shape
     block = own_ref.shape[1]
     lower, upper = slice(0, groups // 2), slice(groups // 2, groups)
@@ -90,7 +94,7 @@
         rows_ref[...] = rows + came_ref[:, :, at].astype(F32)
 
         def part(chips, t):
-            return rows_ref[chips, pl.ds(pl.multiple_of((place_ref[1] ^ t) * block, block), block)]
+            return rows_ref[chips, pl.ds(pl.multiple_of((position()[2] ^ t) * block, block), block)]
 
         own_ref[:, :, at] = part(slice(0, groups), 0)
         keep1_ref[:, :, at] = part(upper, 1)
@@ -100,7 +104,7 @@
         for i, t in enumerate((2, 3)):
             to2_ref[i, :, :, at] = part(upper, t).astype(BF16)
 
-    gram_rows(place_ref[0], x_ref, groups, step, keep)
+    gram_rows(position()[0], x_ref, groups, step, keep)
 
 
 def middle_kernel(own_ref, keep1_ref, keep2_ref, from1_ref, from2_ref, _, __, sum_ref, to1_ref, to2_ref):
@@ -111,13 +115,13 @@
     sum_ref[half:] = own_ref[half:] + from2_ref[0].astype(F32)
 
 
-def slab_kernel(place_ref, sum_ref, from1_ref, from2_ref, _, *outs):
+def slab_kernel(sum_ref, from1_ref, from2_ref, _, *outs):
     *outs, rows_ref = outs
     half = from1_ref.shape[0]
     rows_ref[:half] = sum_ref[:half] + from2_ref[...].astype(F32)
     rows_ref[half:] = sum_ref[half:] + from1_ref[...].astype(F32)
     for t, out in enumerate(outs):
-        out[...] = rows_ref[lax.div(place_ref[2], 2) ^ t].astype(out.dtype)
+        out[...] = rows_ref[position()[1] ^ t].astype(out.dtype)
 
 
 def relay_kernel(x_ref, _, *outs):
@@ -145,7 +149,7 @@
     sum_ref[...] = total
 
 
-def late_kernel(count, place_ref, near, paired, mine_early, other_early, sum_early, *refs):
+def late_kernel(count, near, paired, mine_early, other_early, sum_early, *refs):
     far = jnp.concatenate([ref[...] for ref in refs[:1]], axis=0)
     mine_ref, part_ref, other_ref, sum_ref = refs[1 + count :]
     owned, before = mine_early.shape
@@ -161,25 +165,25 @@
         other_ref[:half, i * wide : i * wide + before] = other_early[at]
         other_ref[:half, i * wide + before : (i + 1) * wide] = rows[owned:][at].astype(BF16)
     sum_ref[...] = sum_early[...] + dot1(columns_of(far, owned, owned), far[:owned], TN)
-    part_ref[...] = sum_ref[pl.ds(pl.multiple_of(lax.rem(place_ref[2], 4) * part, part), part)]
-    away = sum_ref[pl.ds(pl.multiple_of(lax.rem(place_ref[2] ^ 1, 4) * part, part), part)]
+    part_ref[...] = sum_ref[pl.ds(pl.multiple_of(lax.rem(position()[3], 4) * part, part), part)]
+    away = sum_ref[pl.ds(pl.multiple_of(lax.rem(position()[3] ^ 1, 4) * part, part), part)]
     other_ref[half : half + part], other_ref[half + part :] = halves(away)
 
 
-def place_kernel(place_ref, mine, came, *outs):
+def place_kernel(mine, came, *outs):
     *outs, rows_ref = outs
     owned, wide = mine.shape
     half = owned // 2
     for t in range(wide // owned):
-        at = pl.multiple_of((place_ref[2] ^ (2 * t)) * owned, owned)
+        at = pl.multiple_of((position()[3] ^ (2 * t)) * owned, owned)
         rows_ref[:, pl.ds(at, owned)] = mine[:, t * owned : (t + 1) * owned]
-        at = pl.multiple_of((place_ref[2] ^ (2 * t + 1)) * owned, owned)
+        at = pl.multiple_of((position()[3] ^ (2 * t + 1)) * owned, owned)
         for i in range(2):
             part = came[:half, i * wide + t * owned : i * wide + (t + 1) * owned]
             rows_ref[i * half : (i + 1) * half, pl.ds(at, owned)] = part.astype(F32)
     height = owned // len(outs)
     for t, out in enumerate(outs):
-        at = pl.multiple_of((place_ref[1] ^ t) * height, height)
+        at = pl.multiple_of((position()[2] ^ t) * height, height)
         out[...] = rows_ref[pl.ds(at, height)].astype(out.dtype)
 
 
@@ -213,9 +217,6 @@
     count_z = count_ja // 2
     rank_one = factor_one.shape[1]
     part = factor_two.shape[1] // count_ja
-    ja = lax.axis_index("ja")
-    ka = lax.axis_index("ka")
-    place = jnp.stack([lax.rem(ja, 2), ka, ja]).astype(jnp.int32)
     step = width // count_ja
     columns = slices * rank_one
     high = owned * 128 // columns
@@ -223,14 +224,13 @@
     norm_two = 1.0 / math.sqrt(slices * count_ka * rank_one)
 
     (away,) = call(
-        away_kernel, "away", [((count_z, step, width), BF16)], [SMEM, VMEM], place, tensor, vmem=4
+        away_kernel, "away", [((count_z, step, width), BF16)], [VMEM], tensor, vmem=4
     )
     near, far = call(
         core_kernel,
         "core",
         [((owned + high, columns), BF16)] * 2,
-        [SMEM, VMEM, VMEM, VMEM, ANY],
-        place,
+        [VMEM, VMEM, VMEM, ANY],
         tensor,
         factor_one,
         factor_two,
@@ -249,8 +249,7 @@
         home_kernel,
         "home",
         [(shape, F32), (half, F32), (half, F32), ((2, *half), BF16), ((2, *half), BF16)],
-        [SMEM, VMEM, VMEM, ANY],
-        place,
+        [VMEM, VMEM, ANY],
         tensor,
         came,
         paired,
@@ -290,8 +289,7 @@
         slab_kernel,
         "slab",
         [(shape[1:], F32 if t == 0 else BF16) for t in range(count_z)],
-        [SMEM] + [VMEM] * 3 + [ANY],
-        place,
+        [VMEM] * 3 + [ANY],
         total,
         from1,
         from2,
@@ -305,8 +303,7 @@
         functools.partial(late_kernel, len(waits)),
         "two_late",
         [((owned, 4 * owned), F32), ((part, columns), F32), ((owned // 2 + 2 * part, columns), BF16)],
-        [SMEM] + [VMEM] * 6 + [ANY] * len(waits),
-        place,
+        [VMEM] * 6 + [ANY] * len(waits),
         near,
         paired,
         *begun,
@@ -320,8 +317,7 @@
         place_kernel,
         "two_place",
         [(final, F32 if t == 0 else BF16) for t in range(count_ka)],
-        [SMEM] + [VMEM] * 2,
-        place,
+        [VMEM] * 2,
         mine,
         other,
         scratch=[pltpu.VMEM((owned, count_ja * owned), F32)],

time: 48.3 us -> 46 us (0.952)
  Pallas kernels: 10.6 us -> 7.24 us
  waiting for transfers between devices: 14.2 us -> 15.3 us
    pallas_call x10, Pallas kernels: 10.6 us -> 7.24 us  [call(): pl.pallas_call(kernel, out_shape=[jax.ShapeDtypeStruct(s, d) for s, d in...]
    ppermute x16, waiting for transfers between devices: 14.2 us -> 15.3 us  [xor_permute(): lax.ppermute(x, axis, [(i, i ^ bits) for i in range(lax.axis_size(axis))])]
  transfers between devices with their start and end apart: 16 -> 16, of which waited for: 7 -> 7; matrix products, arithmetic and copies ran while one was open for 0% -> 0% of each run, Pallas kernels for 13% -> 9%
where the time goes in v5:
time: 46 us; the launch traced here: 45.8 us
  starting transfers between devices  20.9 us (45%)
  waiting for transfers between devices  15.3 us (33%)
  Pallas kernels  7.24 us (16%)
  local copies, waits for them, and re-layouts  1.6 us (3%)
  between operations  0.74 us (2%)
    ppermute x16, starting transfers between devices, xor_permute(): lax.ppermute(x, axis, [(i, i ^ bits) for i in range(lax.axis_size(axis))])  20.9 us
    ppermute x16, waiting for transfers between devices, xor_permute(): lax.ppermute(x, axis, [(i, i ^ bits) for i in range(lax.axis_size(axis))])  15.3 us
    pallas_call x10, Pallas kernels, call(): pl.pallas_call(kernel, out_shape=[jax.ShapeDtypeStruct(s, d) for s, d in...  7.24 us
    unnamed x8, local copies, waits for them, and re-layouts  1.6 us
  transfers between devices with their start and end apart: 16, of which 7 were waited for; matrix products, arithmetic and copies ran while one was open for 0% of the time, Pallas kernels for 9%

profile of v5, /device:TPU:0, one launch (start us, length us, event | category | flops | bytes accessed | tf_op | source)
XLA Modules:
  0.0 45.8 jit_solution(4452152290472220104)
XLA Ops:
  0.6 0.0 copy-start
  0.6 1.6 %copy-done = f32[4,128,1024]{2,1,0:T(8,128)S(1)} copy-done((f32[4,128,1024]{2,1,0:T(8,128)S(1)}, f32[4,128,1024]{2,1,0:T(8,128)}, u32[]{:S(2)}) %copy-start) | copy-done | bytes 2097176
  2.2 0.0 copy-start.2
  2.2 1.9 %away.1._ = bf16[4,128,1024]{2,1,0:T(8,128)(2,1)S(1)} custom-call(f32[4,128,1024]{2,1,0:T(8,128)S(1)} %copy-done), custom_call_target="tpu_custom_call" | custom-call | tf_op jit(solution)/shard_map/away/pallas_call | solution.py:34
  4.1 0.0 copy-start.1
  4.1 0.5 %collective-permute-start.3 = (bf16[4,128,1024]{2,1,0:T(8,128)(2,1)S(1)}, bf16[4,128,1024]{2,1,0:T(8,128)(2,1)S(1)}, u32[]{:S(2)}, u32[]{:S(2)}) collective-permute-start(bf16[4,128,1024]{2,1,0:T(8,128)(2,1)S(1)} %away.1._), channel_id=1, source_target_pairs={{0,4},{4,0},{8,12},{12,8},{16,20},{20,16},{24,28},{28,24},{1,5},{5... | collective-permute-start | bytes 3145736 | tf_op jit(solution)/shard_map/ppermute | solution.py:206
  4.6 0.0 copy-done.2
  4.6 0.0 copy-done.3
  4.6 1.0 %core.1 = (bf16[144,1024]{1,0:T(8,128)(2,1)S(1)}, bf16[144,1024]{1,0:T(8,128)(2,1)S(1)}) custom-call(f32[4,128,1024]{2,1,0:T(8,128)S(1)} %copy-done, f32[1024,256]{1,0:T(8,128)S(1)} %copy-done.2, bf16[128,256]{1,0:T(8,128)(2,1)S(1)} %copy-done.3, bf16[4,128,1024]{2,1,0:T(8,128)(2,1)S(1)} %away.1._), custom_call_target="tpu_custom_call" | custom-call | tf_op jit(solution)/shard_map/core/pallas_call | solution.py:34
  5.6 0.2 collective-permute-start
  5.8 3.0 %collective-permute-start.1 = (bf16[144,1024]{1,0:T(8,128)(2,1)S(1)}, bf16[144,1024]{1,0:T(8,128)(2,1)S(1)}, u32[]{:S(2)}, u32[]{:S(2)}) collective-permute-start(bf16[144,1024]{1,0:T(8,128)(2,1)S(1)} %get-tuple-element.27.near), channel_id=1, source_target_pairs={{0,8},{4,12},{8,0},{12,4},{16,24},{20,28},{24,16},{28,20},{1,9},{5... | collective-permute-start | bytes 884744 | tf_op jit(solution)/shard_map/ppermute | solution.py:206
  8.8 2.6 %collective-permute-start.2 = (bf16[144,1024]{1,0:T(8,128)(2,1)S(1)}, bf16[144,1024]{1,0:T(8,128)(2,1)S(1)}, u32[]{:S(2)}, u32[]{:S(2)}) collective-permute-start(bf16[144,1024]{1,0:T(8,128)(2,1)S(1)} %get-tuple-element.28), channel_id=1, source_target_pairs={{0,16},{4,20},{8,24},{12,28},{16,0},{20,4},{24,8},{28,12},{1,17},{... | collective-permute-start | bytes 884744 | tf_op jit(solution)/shard_map/ppermute | solution.py:206
  11.4 0.0 collective-permute-done.paired._
  11.4 0.0 collective-permute-done.3.came_ref
  11.4 0.0 copy-done.1
  11.4 2.1 %home.1 = (f32[4,32,1024]{2,1,0:T(8,128)S(1)}, f32[2,32,1024]{2,1,0:T(8,128)S(1)}, f32[2,32,1024]{2,1,0:T(8,128)S(1)}, bf16[2,2,32,1024]{3,2,1,0:T(8,128)(2,1)S(1)}, bf16[2,2,32,1024]{3,2,1,0:T(8,128)(2,1)S(1)}) custom-call(f32[4,128,1024]{2,1,0:T(8,128)S(1)} %copy-done.1, bf16[4,128,1024]{2,1,0:T(8,128)(2,1)S(1)} %collective-permute-done.3.came_ref, ...), custom_call_target="tpu_custom_call" | custom-call | tf_op jit(solution)/shard_map/home/pallas_call | solution.py:34
  13.6 1.6 %collective-permute-start.4 = (bf16[2,2,32,1024]{3,2,1,0:T(8,128)(2,1)S(1)}, bf16[2,2,32,1024]{3,2,1,0:T(8,128)(2,1)S(1)}, u32[]{:S(2)}, u32[]{:S(2)}) collective-permute-start(bf16[2,2,32,1024]{3,2,1,0:T(8,128)(2,1)S(1)} %get-tuple-element.35), channel_id=1, source_target_pairs={{0,1},{1,0},{2,3},{3,2},{4,5},{5,4},{6,7},{7,6},{8,9},{9,8},{10,11... | collective-permute-start | bytes 786440 | tf_op jit(solution)/shard_map/ppermute | solution.py:206
  15.1 1.5 %collective-permute-start.5 = (bf16[2,2,32,1024]{3,2,1,0:T(8,128)(2,1)S(1)}, bf16[2,2,32,1024]{3,2,1,0:T(8,128)(2,1)S(1)}, u32[]{:S(2)}, u32[]{:S(2)}) collective-permute-start(bf16[2,2,32,1024]{3,2,1,0:T(8,128)(2,1)S(1)} %get-tuple-element.36), channel_id=1, source_target_pairs={{0,2},{1,3},{2,0},{3,1},{4,6},{5,7},{6,4},{7,5},{8,10},{9,11},{10,... | collective-permute-start | bytes 786440 | tf_op jit(solution)/shard_map/ppermute | solution.py:206
  16.6 5.6 %collective-permute-done.1.got._ = bf16[144,1024]{1,0:T(8,128)(2,1)S(1)} collective-permute-done((bf16[144,1024]{1,0:T(8,128)(2,1)S(1)}, bf16[144,1024]{1,0:T(8,128)(2,1)S(1)}, u32[]{:S(2)}, u32[]{:S(2)}) %collective-permute-start.1) | collective-permute-done | bytes 294944 | tf_op jit(solution)/shard_map/ppermute | solution.py:206
  22.2 2.5 %collective-permute-done.2.far.__.x_ref = bf16[144,1024]{1,0:T(8,128)(2,1)S(1)} collective-permute-done((bf16[144,1024]{1,0:T(8,128)(2,1)S(1)}, bf16[144,1024]{1,0:T(8,128)(2,1)S(1)}, u32[]{:S(2)}, u32[]{:S(2)}) %collective-permute-start.2) | collective-permute-done | bytes 294944 | tf_op jit(solution)/shard_map/ppermute | solution.py:206
  24.8 0.0 collective-permute-done.4.from1_ref
  24.8 0.0 collective-permute-done.5.from2_ref
  24.8 0.1 middle.1
  24.9 0.5 %collective-permute-start.6 = (bf16[144,1024]{1,0:T(8,128)(2,1)S(1)}, bf16[144,1024]{1,0:T(8,128)(2,1)S(1)}, u32[]{:S(2)}, u32[]{:S(2)}) collective-permute-start(bf16[144,1024]{1,0:T(8,128)(2,1)S(1)} %relay.1), channel_id=1, source_target_pairs={{0,8},{4,12},{8,0},{12,4},{16,24},{20,28},{24,16},{28,20},{1,9},{5... | collective-permute-start | bytes 884744 | tf_op jit(solution)/shard_map/ppermute | solution.py:206
  25.4 1.5 %collective-permute-start.7 = (bf16[2,32,1024]{2,1,0:T(8,128)(2,1)S(1)}, bf16[2,32,1024]{2,1,0:T(8,128)(2,1)S(1)}, u32[]{:S(2)}, u32[]{:S(2)}) collective-permute-start(bf16[2,32,1024]{2,1,0:T(8,128)(2,1)S(1)} %get-tuple-element.38), channel_id=1, source_target_pairs={{0,1},{1,0},{2,3},{3,2},{4,5},{5,4},{6,7},{7,6},{8,9},{9,8},{10,11... | collective-permute-start | bytes 393224 | tf_op jit(solution)/shard_map/ppermute | solution.py:206
  26.9 1.5 %collective-permute-start.8 = (bf16[2,32,1024]{2,1,0:T(8,128)(2,1)S(1)}, bf16[2,32,1024]{2,1,0:T(8,128)(2,1)S(1)}, u32[]{:S(2)}, u32[]{:S(2)}) collective-permute-start(bf16[2,32,1024]{2,1,0:T(8,128)(2,1)S(1)} %get-tuple-element.39), channel_id=1, source_target_pairs={{0,2},{1,3},{2,0},{3,1},{4,6},{5,7},{6,4},{7,5},{8,10},{9,11},{10,... | collective-permute-start | bytes 393224 | tf_op jit(solution)/shard_map/ppermute | solution.py:206
  28.4 0.8 %two_early.1 = (f32[128,384]{1,0:T(8,128)S(1)}, bf16[128,384]{1,0:T(8,128)(2,1)S(1)}, f32[128,1024]{1,0:T(8,128)S(1)}) custom-call(bf16[144,1024]{1,0:T(8,128)(2,1)S(1)} %get-tuple-element.27.near, bf16[144,1024]{1,0:T(8,128)(2,1)S(1)} %collective-permute-done.paired._, bf16[144,1024]{1,0:T(8,128)(2,1)S(1)} %collective-permute-done.1.got._, ...), custom_call_target="tpu_custom_call" | custom-call | tf_op jit(solution)/shard_map/two_early/pallas_call | solution.py:34
  29.2 1.2 %collective-permute-done.7.from1_ref = bf16[2,32,1024]{2,1,0:T(8,128)(2,1)S(1)} collective-permute-done((bf16[2,32,1024]{2,1,0:T(8,128)(2,1)S(1)}, bf16[2,32,1024]{2,1,0:T(8,128)(2,1)S(1)}, u32[]{:S(2)}, u32[]{:S(2)}) %collective-permute-start.7) | collective-permute-done | bytes 131104 | tf_op jit(solution)/shard_map/ppermute | solution.py:206
  30.4 1.5 %collective-permute-done.8.from2_ref = bf16[2,32,1024]{2,1,0:T(8,128)(2,1)S(1)} collective-permute-done((bf16[2,32,1024]{2,1,0:T(8,128)(2,1)S(1)}, bf16[2,32,1024]{2,1,0:T(8,128)(2,1)S(1)}, u32[]{:S(2)}, u32[]{:S(2)}) %collective-permute-start.8) | collective-permute-done | bytes 131104 | tf_op jit(solution)/shard_map/ppermute | solution.py:206
  31.9 0.1 slab.1
  32.0 0.0 collective-permute-done.6.refs_0_
  32.0 0.4 two_late.1
  32.4 0.1 collective-permute-start.9
  32.4 1.6 %collective-permute-start.10 = (bf16[32,1024]{1,0:T(8,128)(2,1)S(1)}, bf16[32,1024]{1,0:T(8,128)(2,1)S(1)}, u32[]{:S(2)}, u32[]{:S(2)}) collective-permute-start(bf16[32,1024]{1,0:T(8,128)(2,1)S(1)} %get-tuple-element.43), channel_id=1, source_target_pairs={{0,8},{4,12},{8,0},{12,4},{16,24},{20,28},{24,16},{28,20},{1,9},{5... | collective-permute-start | bytes 196616 | tf_op jit(solution)/shard_map/ppermute | solution.py:206
  34.1 2.3 %collective-permute-start.11 = (bf16[32,1024]{1,0:T(8,128)(2,1)S(1)}, bf16[32,1024]{1,0:T(8,128)(2,1)S(1)}, u32[]{:S(2)}, u32[]{:S(2)}) collective-permute-start(bf16[32,1024]{1,0:T(8,128)(2,1)S(1)} %get-tuple-element.44), channel_id=1, source_target_pairs={{0,16},{4,20},{8,24},{12,28},{16,0},{20,4},{24,8},{28,12},{1,17},{... | collective-permute-start | bytes 196616 | tf_op jit(solution)/shard_map/ppermute | solution.py:206
  36.4 0.5 %collective-permute-start.12 = (bf16[32,1024]{1,0:T(8,128)(2,1)S(1)}, bf16[32,1024]{1,0:T(8,128)(2,1)S(1)}, u32[]{:S(2)}, u32[]{:S(2)}) collective-permute-start(bf16[32,1024]{1,0:T(8,128)(2,1)S(1)} %get-tuple-element.45), channel_id=1, source_target_pairs={{0,24},{4,28},{8,16},{12,20},{16,8},{20,12},{24,0},{28,4},{1,25},{... | collective-permute-start | bytes 196616 | tf_op jit(solution)/shard_map/ppermute | solution.py:206
  36.9 0.0 collective-permute-done.9.came
  36.9 0.1 two_place.1
  37.0 1.4 %collective-permute-start.13 = (bf16[32,1024]{1,0:T(8,128)(2,1)S(1)}, bf16[32,1024]{1,0:T(8,128)(2,1)S(1)}, u32[]{:S(2)}, u32[]{:S(2)}) collective-permute-start(bf16[32,1024]{1,0:T(8,128)(2,1)S(1)} %get-tuple-element.48), channel_id=1, source_target_pairs={{0,1},{1,0},{2,3},{3,2},{4,5},{5,4},{6,7},{7,6},{8,9},{9,8},{10,11... | collective-permute-start | bytes 196616 | tf_op jit(solution)/shard_map/ppermute | solution.py:206
  38.4 1.5 %collective-permute-start.14 = (bf16[32,1024]{1,0:T(8,128)(2,1)S(1)}, bf16[32,1024]{1,0:T(8,128)(2,1)S(1)}, u32[]{:S(2)}, u32[]{:S(2)}) collective-permute-start(bf16[32,1024]{1,0:T(8,128)(2,1)S(1)} %get-tuple-element.49), channel_id=1, source_target_pairs={{0,2},{1,3},{2,0},{3,1},{4,6},{5,7},{6,4},{7,5},{8,10},{9,11},{10,... | collective-permute-start | bytes 196616 | tf_op jit(solution)/shard_map/ppermute | solution.py:206
  39.9 0.0 collective-permute-done.10.refs_1_
  39.9 0.7 %collective-permute-start.15 = (bf16[32,1024]{1,0:T(8,128)(2,1)S(1)}, bf16[32,1024]{1,0:T(8,128)(2,1)S(1)}, u32[]{:S(2)}, u32[]{:S(2)}) collective-permute-start(bf16[32,1024]{1,0:T(8,128)(2,1)S(1)} %get-tuple-element.50), channel_id=1, source_target_pairs={{0,3},{1,2},{2,1},{3,0},{4,7},{5,6},{6,5},{7,4},{8,11},{9,10},{10,... | collective-permute-start | bytes 196616 | tf_op jit(solution)/shard_map/ppermute | solution.py:206
  40.6 2.0 %collective-permute-done.11.refs_2_ = bf16[32,1024]{1,0:T(8,128)(2,1)S(1)} collective-permute-done((bf16[32,1024]{1,0:T(8,128)(2,1)S(1)}, bf16[32,1024]{1,0:T(8,128)(2,1)S(1)}, u32[]{:S(2)}, u32[]{:S(2)}) %collective-permute-start.11) | collective-permute-done | bytes 65568 | tf_op jit(solution)/shard_map/ppermute | solution.py:206
  42.5 0.0 collective-permute-done.12.refs_3_
  42.5 0.0 collective-permute-done.13.refs_5_
  42.5 0.8 %collective-permute-done.14.refs_6_ = bf16[32,1024]{1,0:T(8,128)(2,1)S(1)} collective-permute-done((bf16[32,1024]{1,0:T(8,128)(2,1)S(1)}, bf16[32,1024]{1,0:T(8,128)(2,1)S(1)}, u32[]{:S(2)}, u32[]{:S(2)}) %collective-permute-start.14) | collective-permute-done | bytes 65568 | tf_op jit(solution)/shard_map/ppermute | solution.py:206
  43.3 1.7 %collective-permute-done.15.refs_7_ = bf16[32,1024]{1,0:T(8,128)(2,1)S(1)} collective-permute-done((bf16[32,1024]{1,0:T(8,128)(2,1)S(1)}, bf16[32,1024]{1,0:T(8,128)(2,1)S(1)}, u32[]{:S(2)}, u32[]{:S(2)}) %collective-permute-start.15) | collective-permute-done | bytes 65568 | tf_op jit(solution)/shard_map/ppermute | solution.py:206
  45.1 0.8 %last.1 = (f32[32,1024]{1,0:T(8,128)}, f32[32,1024]{1,0:T(8,128)}, f32[4,32,256]{2,1,0:T(8,128)}) custom-call(f32[32,1024]{1,0:T(8,128)S(1)} %get-tuple-element.41.mine, bf16[128,1024]{1,0:T(8,128)(2,1)S(1)} %collective-permute-done.9.came, f32[32,1024]{1,0:T(8,128)S(1)} %get-tuple-element.40.refs_1_.refs_0_, ...), custom_call_target="tpu_custom_call" | custom-call | tf_op jit(solution)/shard_map/last/pallas_call | solution.py:34
  (2 shorter events, 0.0 us)
Async XLA Ops:
  0.6 1.6 %copy-start = (f32[4,128,1024]{2,1,0:T(8,128)S(1)}, f32[4,128,1024]{2,1,0:T(8,128)}, u32[]{:S(2)}) copy-start(f32[4,128,1024]{2,1,0:T(8,128)} %x_ref.5) | copy-start | bytes 6291460
  2.2 2.4 %copy-start.2 = (f32[1024,256]{1,0:T(8,128)S(1)}, f32[1024,256]{1,0:T(8,128)}, u32[]{:S(2)}) copy-start(f32[1024,256]{1,0:T(8,128)} %f_ref.1) | copy-start | bytes 3145732
  2.2 2.4 %copy-start.3 = (bf16[128,256]{1,0:T(8,128)(2,1)S(1)}, bf16[128,256]{1,0:T(8,128)(2,1)}, u32[]{:S(2)}) copy-start(bf16[128,256]{1,0:T(8,128)(2,1)} %two_ref.1) | copy-start | bytes 196612
  4.1 7.3 %copy-start.1 = (f32[4,128,1024]{2,1,0:T(8,128)S(1)}, f32[4,128,1024]{2,1,0:T(8,128)}, u32[]{:S(2)}) copy-start(f32[4,128,1024]{2,1,0:T(8,128)} %x_ref.5) | copy-start | bytes 6291460
  4.1 7.3 %collective-permute-start.3 = (bf16[4,128,1024]{2,1,0:T(8,128)(2,1)S(1)}, bf16[4,128,1024]{2,1,0:T(8,128)(2,1)S(1)}, u32[]{:S(2)}, u32[]{:S(2)}) collective-permute-start(bf16[4,128,1024]{2,1,0:T(8,128)(2,1)S(1)} %away.1._), channel_id=1, source_target_pairs={{0,4},{4,0},{8,12},{12,8},{16,20},{20,16},{24,28},{28,24},{1,5},{5... | collective-permute-start | bytes 3145736 | tf_op jit(solution)/shard_map/ppermute | solution.py:206
  5.6 5.8 %collective-permute-start = (bf16[144,1024]{1,0:T(8,128)(2,1)S(1)}, bf16[144,1024]{1,0:T(8,128)(2,1)S(1)}, u32[]{:S(2)}, u32[]{:S(2)}) collective-permute-start(bf16[144,1024]{1,0:T(8,128)(2,1)S(1)} %get-tuple-element.27.near), channel_id=1, source_target_pairs={{0,4},{4,0},{8,12},{12,8},{16,20},{20,16},{24,28},{28,24},{1,5},{5... | collective-permute-start | bytes 884744 | tf_op jit(solution)/shard_map/ppermute | solution.py:206
  5.8 16.5 %collective-permute-start.1 = (bf16[144,1024]{1,0:T(8,128)(2,1)S(1)}, bf16[144,1024]{1,0:T(8,128)(2,1)S(1)}, u32[]{:S(2)}, u32[]{:S(2)}) collective-permute-start(bf16[144,1024]{1,0:T(8,128)(2,1)S(1)} %get-tuple-element.27.near), channel_id=1, source_target_pairs={{0,8},{4,12},{8,0},{12,4},{16,24},{20,28},{24,16},{28,20},{1,9},{5... | collective-permute-start | bytes 884744 | tf_op jit(solution)/shard_map/ppermute | solution.py:206
  8.8 16.0 %collective-permute-start.2 = (bf16[144,1024]{1,0:T(8,128)(2,1)S(1)}, bf16[144,1024]{1,0:T(8,128)(2,1)S(1)}, u32[]{:S(2)}, u32[]{:S(2)}) collective-permute-start(bf16[144,1024]{1,0:T(8,128)(2,1)S(1)} %get-tuple-element.28), channel_id=1, source_target_pairs={{0,16},{4,20},{8,24},{12,28},{16,0},{20,4},{24,8},{28,12},{1,17},{... | collective-permute-start | bytes 884744 | tf_op jit(solution)/shard_map/ppermute | solution.py:206
  13.6 11.2 %collective-permute-start.4 = (bf16[2,2,32,1024]{3,2,1,0:T(8,128)(2,1)S(1)}, bf16[2,2,32,1024]{3,2,1,0:T(8,128)(2,1)S(1)}, u32[]{:S(2)}, u32[]{:S(2)}) collective-permute-start(bf16[2,2,32,1024]{3,2,1,0:T(8,128)(2,1)S(1)} %get-tuple-element.35), channel_id=1, source_target_pairs={{0,1},{1,0},{2,3},{3,2},{4,5},{5,4},{6,7},{7,6},{8,9},{9,8},{10,11... | collective-permute-start | bytes 786440 | tf_op jit(solution)/shard_map/ppermute | solution.py:206
  15.1 9.7 %collective-permute-start.5 = (bf16[2,2,32,1024]{3,2,1,0:T(8,128)(2,1)S(1)}, bf16[2,2,32,1024]{3,2,1,0:T(8,128)(2,1)S(1)}, u32[]{:S(2)}, u32[]{:S(2)}) collective-permute-start(bf16[2,2,32,1024]{3,2,1,0:T(8,128)(2,1)S(1)} %get-tuple-element.36), channel_id=1, source_target_pairs={{0,2},{1,3},{2,0},{3,1},{4,6},{5,7},{6,4},{7,5},{8,10},{9,11},{10,... | collective-permute-start | bytes 786440 | tf_op jit(solution)/shard_map/ppermute | solution.py:206
  24.9 7.1 %collective-permute-start.6 = (bf16[144,1024]{1,0:T(8,128)(2,1)S(1)}, bf16[144,1024]{1,0:T(8,128)(2,1)S(1)}, u32[]{:S(2)}, u32[]{:S(2)}) collective-permute-start(bf16[144,1024]{1,0:T(8,128)(2,1)S(1)} %relay.1), channel_id=1, source_target_pairs={{0,8},{4,12},{8,0},{12,4},{16,24},{20,28},{24,16},{28,20},{1,9},{5... | collective-permute-start | bytes 884744 | tf_op jit(solution)/shard_map/ppermute | solution.py:206
  25.4 5.0 %collective-permute-start.7 = (bf16[2,32,1024]{2,1,0:T(8,128)(2,1)S(1)}, bf16[2,32,1024]{2,1,0:T(8,128)(2,1)S(1)}, u32[]{:S(2)}, u32[]{:S(2)}) collective-permute-start(bf16[2,32,1024]{2,1,0:T(8,128)(2,1)S(1)} %get-tuple-element.38), channel_id=1, source_target_pairs={{0,1},{1,0},{2,3},{3,2},{4,5},{5,4},{6,7},{7,6},{8,9},{9,8},{10,11... | collective-permute-start | bytes 393224 | tf_op jit(solution)/shard_map/ppermute | solution.py:206
  26.9 5.0 %collective-permute-start.8 = (bf16[2,32,1024]{2,1,0:T(8,128)(2,1)S(1)}, bf16[2,32,1024]{2,1,0:T(8,128)(2,1)S(1)}, u32[]{:S(2)}, u32[]{:S(2)}) collective-permute-start(bf16[2,32,1024]{2,1,0:T(8,128)(2,1)S(1)} %get-tuple-element.39), channel_id=1, source_target_pairs={{0,2},{1,3},{2,0},{3,1},{4,6},{5,7},{6,4},{7,5},{8,10},{9,11},{10,... | collective-permute-start | bytes 393224 | tf_op jit(solution)/shard_map/ppermute | solution.py:206
  32.4 4.5 %collective-permute-start.9 = (bf16[128,1024]{1,0:T(8,128)(2,1)S(1)}, bf16[128,1024]{1,0:T(8,128)(2,1)S(1)}, u32[]{:S(2)}, u32[]{:S(2)}) collective-permute-start(bf16[128,1024]{1,0:T(8,128)(2,1)S(1)} %get-tuple-element.42), channel_id=1, source_target_pairs={{0,4},{4,0},{8,12},{12,8},{16,20},{20,16},{24,28},{28,24},{1,5},{5... | collective-permute-start | bytes 786440 | tf_op jit(solution)/shard_map/ppermute | solution.py:206
  32.4 7.4 %collective-permute-start.10 = (bf16[32,1024]{1,0:T(8,128)(2,1)S(1)}, bf16[32,1024]{1,0:T(8,128)(2,1)S(1)}, u32[]{:S(2)}, u32[]{:S(2)}) collective-permute-start(bf16[32,1024]{1,0:T(8,128)(2,1)S(1)} %get-tuple-element.43), channel_id=1, source_target_pairs={{0,8},{4,12},{8,0},{12,4},{16,24},{20,28},{24,16},{28,20},{1,9},{5... | collective-permute-start | bytes 196616 | tf_op jit(solution)/shard_map/ppermute | solution.py:206
  34.1 8.4 %collective-permute-start.11 = (bf16[32,1024]{1,0:T(8,128)(2,1)S(1)}, bf16[32,1024]{1,0:T(8,128)(2,1)S(1)}, u32[]{:S(2)}, u32[]{:S(2)}) collective-permute-start(bf16[32,1024]{1,0:T(8,128)(2,1)S(1)} %get-tuple-element.44), channel_id=1, source_target_pairs={{0,16},{4,20},{8,24},{12,28},{16,0},{20,4},{24,8},{28,12},{1,17},{... | collective-permute-start | bytes 196616 | tf_op jit(solution)/shard_map/ppermute | solution.py:206
  36.4 6.1 %collective-permute-start.12 = (bf16[32,1024]{1,0:T(8,128)(2,1)S(1)}, bf16[32,1024]{1,0:T(8,128)(2,1)S(1)}, u32[]{:S(2)}, u32[]{:S(2)}) collective-permute-start(bf16[32,1024]{1,0:T(8,128)(2,1)S(1)} %get-tuple-element.45), channel_id=1, source_target_pairs={{0,24},{4,28},{8,16},{12,20},{16,8},{20,12},{24,0},{28,4},{1,25},{... | collective-permute-start | bytes 196616 | tf_op jit(solution)/shard_map/ppermute | solution.py:206
  37.0 5.5 %collective-permute-start.13 = (bf16[32,1024]{1,0:T(8,128)(2,1)S(1)}, bf16[32,1024]{1,0:T(8,128)(2,1)S(1)}, u32[]{:S(2)}, u32[]{:S(2)}) collective-permute-start(bf16[32,1024]{1,0:T(8,128)(2,1)S(1)} %get-tuple-element.48), channel_id=1, source_target_pairs={{0,1},{1,0},{2,3},{3,2},{4,5},{5,4},{6,7},{7,6},{8,9},{9,8},{10,11... | collective-permute-start | bytes 196616 | tf_op jit(solution)/shard_map/ppermute | solution.py:206
  38.4 5.0 %collective-permute-start.14 = (bf16[32,1024]{1,0:T(8,128)(2,1)S(1)}, bf16[32,1024]{1,0:T(8,128)(2,1)S(1)}, u32[]{:S(2)}, u32[]{:S(2)}) collective-permute-start(bf16[32,1024]{1,0:T(8,128)(2,1)S(1)} %get-tuple-element.49), channel_id=1, source_target_pairs={{0,2},{1,3},{2,0},{3,1},{4,6},{5,7},{6,4},{7,5},{8,10},{9,11},{10,... | collective-permute-start | bytes 196616 | tf_op jit(solution)/shard_map/ppermute | solution.py:206
  39.9 5.2 %collective-permute-start.15 = (bf16[32,1024]{1,0:T(8,128)(2,1)S(1)}, bf16[32,1024]{1,0:T(8,128)(2,1)S(1)}, u32[]{:S(2)}, u32[]{:S(2)}) collective-permute-start(bf16[32,1024]{1,0:T(8,128)(2,1)S(1)} %get-tuple-element.50), channel_id=1, source_target_pairs={{0,3},{1,2},{2,1},{3,0},{4,7},{5,6},{6,5},{7,4},{8,11},{9,10},{10,... | collective-permute-start | bytes 196616 | tf_op jit(solution)/shard_map/ppermute | solution.py:206

commit v6 on v5

--- a/solution.py
+++ b/solution.py
@@ -71,12 +71,11 @@
 def core_kernel(x_ref, f_ref, two_ref, _, near_ref, far_ref):
     slices, owned, _ = x_ref.shape
     rank = f_ref.shape[1]
-    high = near_ref.shape[0] - owned
-    side = lax.div(position()[1], 2)
-    for out, here in ((near_ref, side), (far_ref, 1 - side)):
-        chunk = two_ref[:, pl.ds(pl.multiple_of(here * 128, 128), 128)]
-        for q in range(owned // high):
-            out[owned:, q * 128 : (q + 1) * 128] = chunk[q * high : (q + 1) * high]
+    high = far_ref.shape[0] - owned
+    other = 1 - lax.div(position()[1], 2)
+    chunk = two_ref[:, pl.ds(pl.multiple_of(other * 128, 128), 128)]
+    for q in range(owned // high):
+        far_ref[owned:, q * 128 : (q + 1) * 128] = chunk[q * high : (q + 1) * high]
     f = halves(f_ref[...])
     for k in range(slices):
         core = dot3(halves(x_ref[k]), f, NN).astype(BF16)
@@ -107,67 +106,74 @@
     gram_rows(position()[0], x_ref, groups, step, keep)
 
 
-def middle_kernel(own_ref, keep1_ref, keep2_ref, from1_ref, from2_ref, _, __, sum_ref, to1_ref, to2_ref):
+def middle_kernel(own_ref, keep1_ref, keep2_ref, from1_ref, from2_ref, sum_ref, to1_ref, to2_ref):
     half = from1_ref.shape[1]
-    to1_ref[...] = (keep1_ref[...] + from2_ref[1].astype(F32)).astype(BF16)
-    to2_ref[...] = (keep2_ref[...] + from1_ref[1].astype(F32)).astype(BF16)
+    count = half * from1_ref.shape[2]
+    for out, keep, came in ((to1_ref, keep1_ref, from2_ref), (to2_ref, keep2_ref, from1_ref)):
+        out[:count] = (keep[...] + came[1].astype(F32)).astype(BF16).reshape(count, out.shape[1])
+        out[count:] = jnp.zeros((out.shape[0] - count, out.shape[1]), BF16)
     sum_ref[:half] = own_ref[:half] + from1_ref[0].astype(F32)
     sum_ref[half:] = own_ref[half:] + from2_ref[0].astype(F32)
 
 
-def slab_kernel(sum_ref, from1_ref, from2_ref, _, *outs):
-    *outs, rows_ref = outs
-    half = from1_ref.shape[0]
-    rows_ref[:half] = sum_ref[:half] + from2_ref[...].astype(F32)
-    rows_ref[half:] = sum_ref[half:] + from1_ref[...].astype(F32)
+def slab_kernel(sum_ref, from1_ref, from2_ref, mine_ref, came_ref, *refs):
+    *outs, part_ref, rows_ref = refs[1:]
+    half, height = sum_ref.shape[0] // 2, sum_ref.shape[1]
+    count = half * height
+    part = part_ref.shape[0]
+    came = [ref[:count].astype(F32).reshape(half, height, ref.shape[1]) for ref in (from1_ref, from2_ref)]
+    rows_ref[:half] = sum_ref[:half] + came[1]
+    rows_ref[half:] = sum_ref[half:] + came[0]
     for t, out in enumerate(outs):
-        out[...] = rows_ref[position()[1] ^ t].astype(out.dtype)
-
-
-def relay_kernel(x_ref, _, *outs):
-    for i, out in enumerate(outs):
-        out[...] = x_ref[i * out.shape[0] : (i + 1) * out.shape[0]]
-
-
-def columns_of(ref, start, owned):
-    high = ref.shape[0] - start
-    chunk = [ref[start:, q * 128 : (q + 1) * 128] for q in range(owned // high)]
-    return jnp.concatenate(chunk, axis=0)
-
-
-def early_kernel(near, paired, got, far, mine_ref, other_ref, sum_ref):
+        out[:height] = rows_ref[position()[1] ^ t].astype(out.dtype)
+    part_ref[...] = mine_ref[:part] + came_ref[:part].astype(F32)
+    outs[1][height:] = (mine_ref[part:] + came_ref[part:].astype(F32)).astype(BF16)
+
+
+def near_kernel(u, paired, got, mine_ref, other_ref):
     owned = mine_ref.shape[0]
-    left = jnp.concatenate([near[:owned], paired[:owned]], axis=0)
-    total = None
-    for t, ref in enumerate((near, got, far)):
-        rows = dot1(left, ref[:owned], NT)
+    left = jnp.concatenate([u[:owned], paired[:owned]], axis=0)
+    for t, block in enumerate((u, got)):
+        rows = dot1(left, block[:owned], NT)
         at = slice(t * owned, (t + 1) * owned)
         mine_ref[:, at] = rows[:owned]
         other_ref[:, at] = rows[owned:].astype(BF16)
-        value = dot1(columns_of(ref, owned, owned), ref[:owned], TN)
-        total = value if total is None else total + value
-    sum_ref[...] = total
-
-
-def late_kernel(count, near, paired, mine_early, other_early, sum_early, *refs):
-    far = jnp.concatenate([ref[...] for ref in refs[:1]], axis=0)
-    mine_ref, part_ref, other_ref, sum_ref = refs[1 + count :]
-    owned, before = mine_early.shape
-    half = owned // 2
-    wide = mine_ref.shape[1]
-    part = part_ref.shape[0]
-    mine_ref[:, :before] = mine_early[...]
-    left = jnp.concatenate([near[:owned], paired[:owned]], axis=0)
-    rows = dot1(left, far[:owned], NT)
-    mine_ref[:, before:] = rows[:owned]
+
+
+def cross_kernel(u, paired, got, got_paired, far, _, mine_ref, other_ref, send_ref):
+    owned = mine_ref.shape[0]
+    left = [ref[:owned] for ref in (u, paired, got, got_paired)]
+    rows = dot1(jnp.concatenate(left, axis=0), far[:owned], NT)
+    mine_ref[...] = rows[:owned]
+    other_ref[...] = rows[owned : 2 * owned].astype(BF16)
+    send_ref[...] = rows[2 * owned :].astype(BF16)
+
+
+def merge_kernel(mine_near, other_near, mine_far, other_far, came, _, mine_ref, other_ref):
+    owned, before = mine_near.shape
+    half, wide = owned // 2, mine_ref.shape[1]
+    mine_ref[:, :before] = mine_near[...]
+    mine_ref[:, before : before + owned] = mine_far[...]
+    mine_ref[:, before + owned :] = came[:owned].astype(F32)
     for i in range(2):
-        at = slice(i * half, (i + 1) * half)
-        other_ref[:half, i * wide : i * wide + before] = other_early[at]
-        other_ref[:half, i * wide + before : (i + 1) * wide] = rows[owned:][at].astype(BF16)
-    sum_ref[...] = sum_early[...] + dot1(columns_of(far, owned, owned), far[:owned], TN)
-    part_ref[...] = sum_ref[pl.ds(pl.multiple_of(lax.rem(position()[3], 4) * part, part), part)]
-    away = sum_ref[pl.ds(pl.multiple_of(lax.rem(position()[3] ^ 1, 4) * part, part), part)]
-    other_ref[half : half + part], other_ref[half + part :] = halves(away)
+        at, start = slice(i * half, (i + 1) * half), i * wide
+        other_ref[:, start : start + before] = other_near[at]
+        other_ref[:, start + before : start + before + owned] = other_far[at]
+        other_ref[:, start + before + owned : start + wide] = came[owned + i * half : owned + (i + 1) * half]
+
+
+def parts_kernel(u, far, two_ref, _, mine_ref, other_ref, sum_ref):
+    owned = two_ref.shape[0]
+    part = mine_ref.shape[0] // 2
+    high = far.shape[0] - owned
+    _, z, _, ja = position()
+    own = two_ref[:, pl.ds(pl.multiple_of(lax.div(z, 2) * 128, 128), 128)]
+    chunk = [far[owned:, q * 128 : (q + 1) * 128] for q in range(owned // high)]
+    sum_ref[...] = dot1(own, u[:owned], TN) + dot1(jnp.concatenate(chunk, axis=0), far[:owned], TN)
+    for t in range(4):
+        start = pl.multiple_of(lax.rem(ja ^ t, 4) * part, part)
+        out = (mine_ref, other_ref)[t % 2]
+        out[t // 2 * part : (t // 2 + 1) * part] = sum_ref[pl.ds(start, part)].astype(out.dtype)
 
 
 def place_kernel(mine, came, *outs):
@@ -179,7 +185,7 @@
         rows_ref[:, pl.ds(at, owned)] = mine[:, t * owned : (t + 1) * owned]
         at = pl.multiple_of((position()[3] ^ (2 * t + 1)) * owned, owned)
         for i in range(2):
-            part = came[:half, i * wide + t * owned : i * wide + (t + 1) * owned]
+            part = came[:, i * wide + t * owned : i * wide + (t + 1) * owned]
             rows_ref[i * half : (i + 1) * half, pl.ds(at, owned)] = part.astype(F32)
     height = owned // len(outs)
     for t, out in enumerate(outs):
@@ -187,19 +193,17 @@
         out[...] = rows_ref[pl.ds(at, height)].astype(out.dtype)
 
 
-def last_kernel(scales, count, mine, came, *refs):
+def last_kernel(scales, count, mine, *refs):
     parts, outs = refs[: 2 * count], refs[2 * count :]
     for i, scale in enumerate(scales):
         total = parts[i * count][...]
         for part in parts[i * count + 1 : (i + 1) * count]:
-            total = total + part[...].astype(F32)
+            total = total + part[: total.shape[0]].astype(F32)
         outs[i][...] = total * scale
-    slices, part, rank = outs[2].shape
+    slices, _, rank = outs[2].shape
     for k in range(slices):
         at = slice(k * rank, (k + 1) * rank)
-        low = came[came.shape[0] - part :, at].astype(F32)
-        high = came[came.shape[0] - 2 * part : came.shape[0] - part, at].astype(F32)
-        outs[2][k] = mine[:, at] + (high + low)
+        outs[2][k] = mine[:, at] + parts[1][parts[0].shape[0] :, at].astype(F32)
 
 
 def xor_permute(x, axis, bits):
@@ -229,7 +233,7 @@
     near, far = call(
         core_kernel,
         "core",
-        [((owned + high, columns), BF16)] * 2,
+        [((owned, columns), BF16), ((owned + high, columns), BF16)],
         [VMEM, VMEM, VMEM, ANY],
         tensor,
         factor_one,
@@ -261,55 +265,80 @@
     total, to1, to2 = call(
         middle_kernel,
         "middle",
-        [(shape, F32), (half, BF16), (half, BF16)],
-        [VMEM] * 5 + [ANY] * 2,
+        [(shape, F32)] + [((half[0] * half[1] + 16, width), BF16)] * 2,
+        [VMEM] * 5,
         own,
         keep1,
         keep2,
         from1,
         from2,
-        got1,
-        far2,
     )
     from1 = xor_permute(to1, "ka", 1)
     from2 = xor_permute(to2, "ka", 2)
-    far3 = call(relay_kernel, "relay", [(far.shape, BF16)], [VMEM, ANY], far2, total)
-    far3 = [xor_permute(p, "ja", 2) for p in far3]
-    begun = call(
-        early_kernel,
-        "two_early",
-        [((owned, 3 * owned), F32), ((owned, 3 * owned), BF16), ((128, columns), F32)],
-        [VMEM] * 4,
+    got_paired = xor_permute(got1, "ja", 1)
+    first = call(
+        near_kernel,
+        "two_near",
+        [((owned, 2 * owned), F32), ((owned, 2 * owned), BF16)],
+        [VMEM] * 3,
         near,
         paired,
         got1,
+    )
+    *second, send = call(
+        cross_kernel,
+        "two_cross",
+        [((owned, owned), F32), ((owned, owned), BF16), ((2 * owned, owned), BF16)],
+        [VMEM] * 5 + [ANY],
+        near,
+        paired,
+        got1,
+        got_paired,
         far2,
-    )
-    sums = call(
+        total,
+    )
+    crossed = xor_permute(send, "ja", 2)
+    mine_part, other_part = call(
+        parts_kernel,
+        "parts",
+        [((2 * part, columns), F32), ((2 * part, columns), BF16)],
+        [VMEM] * 3 + [ANY],
+        near,
+        far2,
+        factor_two,
+        send,
+        scratch=[pltpu.VMEM((128, columns), F32)],
+    )
+    height = step // count_ka
+    *sums, mine_part = call(
         slab_kernel,
         "slab",
-        [(shape[1:], F32 if t == 0 else BF16) for t in range(count_z)],
-        [VMEM] * 3 + [ANY],
+        [
+            ((height + (part if t == 1 else 0), width), F32 if t == 0 else BF16)
+            for t in range(count_z)
+        ]
+        + [((part, columns), F32)],
+        [VMEM] * 5 + [ANY],
         total,
         from1,
         from2,
-        begun[0],
+        mine_part,
+        xor_permute(other_part, "ja", 1),
+        crossed,
         scratch=[pltpu.VMEM(shape, F32)],
     )
-    sums = [p if t == 0 else xor_permute(p, "ja", 2 * t) for t, p in enumerate(sums)]
-
-    waits = sums[:1]
-    mine, mine_part, other = call(
-        functools.partial(late_kernel, len(waits)),
-        "two_late",
-        [((owned, 4 * owned), F32), ((part, columns), F32), ((owned // 2 + 2 * part, columns), BF16)],
-        [VMEM] * 6 + [ANY] * len(waits),
-        near,
-        paired,
-        *begun,
-        *far3,
-        *waits,
-        scratch=[pltpu.VMEM((128, columns), F32)],
+    sums = list(sums)
+    for t in reversed(range(1, count_z)):
+        sums[t] = xor_permute(sums[t], "ja", 2 * t)
+    mine, other = call(
+        merge_kernel,
+        "two_merge",
+        [((owned, 4 * owned), F32), ((owned // 2, 8 * owned), BF16)],
+        [VMEM] * 5 + [ANY],
+        *first,
+        *second,
+        crossed,
+        sums[0],
     )
     other = xor_permute(other, "ja", 1)
     final = (owned // count_ka, count_ja * owned)
@@ -322,14 +351,15 @@
         other,
         scratch=[pltpu.VMEM((owned, count_ja * owned), F32)],
     )
-    rows = [p if t == 0 else xor_permute(p, "ka", t) for t, p in enumerate(rows)]
+    rows = list(rows)
+    for t in reversed(range(1, count_ka)):
+        rows[t] = xor_permute(rows[t], "ka", t)
     return call(
         functools.partial(last_kernel, (norm_one, norm_two), count_z),
         "last",
-        [(shape[1:], F32), (final, F32), ((slices, part, rank_one), F32)],
-        [VMEM] * (2 + count_z + count_ka),
+        [((height, width), F32), (final, F32), ((slices, part, rank_one), F32)],
+        [VMEM] * (1 + count_z + count_ka),
         mine_part,
-        other,
         *sums,
         *rows,
     )

time: 46 us -> 44.2 us (0.961)
  waiting for transfers between devices: 15.3 us -> 13.9 us
  starting transfers between devices: 20.9 us -> 20.4 us
    ppermute x16 -> x18, waiting for transfers between devices: 15.3 us -> 13.9 us  [xor_permute(): lax.ppermute(x, axis, [(i, i ^ bits) for i in range(lax.axis_size(axis))])]
    ppermute x16 -> x18, starting transfers between devices: 20.9 us -> 20.4 us  [xor_permute(): lax.ppermute(x, axis, [(i, i ^ bits) for i in range(lax.axis_size(axis))])]
    pallas_call x10 -> x11, Pallas kernels: 7.24 us -> 7.36 us  [call(): pl.pallas_call(kernel, out_shape=[jax.ShapeDtypeStruct(s, d) for s, d in...]
  transfers between devices with their start and end apart: 16 -> 18, of which waited for: 7 -> 7; matrix products, arithmetic and copies ran while one was open for 0% -> 0% of each run, Pallas kernels for 9% -> 10%
where the time goes in v6:
time: 44.2 us; the launch traced here: 44 us
  starting transfers between devices  20.4 us (46%)
  waiting for transfers between devices  13.9 us (31%)
  Pallas kernels  7.36 us (17%)
  local copies, waits for them, and re-layouts  1.6 us (4%)
  between operations  0.76 us (2%)
    ppermute x18, starting transfers between devices, xor_permute(): lax.ppermute(x, axis, [(i, i ^ bits) for i in range(lax.axis_size(axis))])  20.4 us
    ppermute x18, waiting for transfers between devices, xor_permute(): lax.ppermute(x, axis, [(i, i ^ bits) for i in range(lax.axis_size(axis))])  13.9 us
    pallas_call x11, Pallas kernels, call(): pl.pallas_call(kernel, out_shape=[jax.ShapeDtypeStruct(s, d) for s, d in...  7.36 us
    unnamed x8, local copies, waits for them, and re-layouts  1.6 us
  transfers between devices with their start and end apart: 18, of which 7 were waited for; matrix products, arithmetic and copies ran while one was open for 0% of the time, Pallas kernels for 10%

profile of v6, /device:TPU:0, one launch (start us, length us, event | category | flops | bytes accessed | tf_op | source)
XLA Modules:
  0.0 44.0 jit_solution(5579548846655720494)
XLA Ops:
  0.6 0.0 copy-start
  0.6 1.6 %copy-done = f32[4,128,1024]{2,1,0:T(8,128)S(1)} copy-done((f32[4,128,1024]{2,1,0:T(8,128)S(1)}, f32[4,128,1024]{2,1,0:T(8,128)}, u32[]{:S(2)}) %copy-start) | copy-done | bytes 2097176
  2.2 1.9 %away.1._ = bf16[4,128,1024]{2,1,0:T(8,128)(2,1)S(1)} custom-call(f32[4,128,1024]{2,1,0:T(8,128)S(1)} %copy-done), custom_call_target="tpu_custom_call" | custom-call | tf_op jit(solution)/shard_map/away/pallas_call | solution.py:34
  4.1 0.0 copy-start.1
  4.1 0.5 %collective-permute-start = (bf16[4,128,1024]{2,1,0:T(8,128)(2,1)S(1)}, bf16[4,128,1024]{2,1,0:T(8,128)(2,1)S(1)}, u32[]{:S(2)}, u32[]{:S(2)}) collective-permute-start(bf16[4,128,1024]{2,1,0:T(8,128)(2,1)S(1)} %away.1._), channel_id=1, source_target_pairs={{0,4},{4,0},{8,12},{12,8},{16,20},{20,16},{24,28},{28,24},{1,5},{5... | collective-permute-start | bytes 3145736 | tf_op jit(solution)/shard_map/ppermute | solution.py:210
  4.6 1.0 %core.1 = (bf16[128,1024]{1,0:T(8,128)(2,1)S(1)}, bf16[144,1024]{1,0:T(8,128)(2,1)S(1)}) custom-call(f32[4,128,1024]{2,1,0:T(8,128)S(1)} %copy-done, f32[1024,256]{1,0:T(8,128)S(1)} %copy-done.2, bf16[128,256]{1,0:T(8,128)(2,1)S(1)} %copy-done.3, bf16[4,128,1024]{2,1,0:T(8,128)(2,1)S(1)} %away.1._), custom_call_target="tpu_custom_call" | custom-call | tf_op jit(solution)/shard_map/core/pallas_call | solution.py:34
  5.6 0.1 collective-permute-start.1
  5.8 3.0 %collective-permute-start.7 = (bf16[128,1024]{1,0:T(8,128)(2,1)S(1)}, bf16[128,1024]{1,0:T(8,128)(2,1)S(1)}, u32[]{:S(2)}, u32[]{:S(2)}) collective-permute-start(bf16[128,1024]{1,0:T(8,128)(2,1)S(1)} %get-tuple-element.31.u), channel_id=1, source_target_pairs={{0,8},{4,12},{8,0},{12,4},{16,24},{20,28},{24,16},{28,20},{1,9},{5... | collective-permute-start | bytes 786440 | tf_op jit(solution)/shard_map/ppermute | solution.py:210
  8.8 2.6 %collective-permute-start.6 = (bf16[144,1024]{1,0:T(8,128)(2,1)S(1)}, bf16[144,1024]{1,0:T(8,128)(2,1)S(1)}, u32[]{:S(2)}, u32[]{:S(2)}) collective-permute-start(bf16[144,1024]{1,0:T(8,128)(2,1)S(1)} %get-tuple-element.40), channel_id=1, source_target_pairs={{0,16},{4,20},{8,24},{12,28},{16,0},{20,4},{24,8},{28,12},{1,17},{... | collective-permute-start | bytes 884744 | tf_op jit(solution)/shard_map/ppermute | solution.py:210
  11.4 0.0 collective-permute-done.1._.paired
  11.4 0.0 collective-permute-done.came_ref
  11.4 2.1 %home.1 = (f32[4,32,1024]{2,1,0:T(8,128)S(1)}, f32[2,32,1024]{2,1,0:T(8,128)S(1)}, f32[2,32,1024]{2,1,0:T(8,128)S(1)}, bf16[2,2,32,1024]{3,2,1,0:T(8,128)(2,1)S(1)}, bf16[2,2,32,1024]{3,2,1,0:T(8,128)(2,1)S(1)}) custom-call(f32[4,128,1024]{2,1,0:T(8,128)S(1)} %copy-done.1, bf16[4,128,1024]{2,1,0:T(8,128)(2,1)S(1)} %collective-permute-done.came_ref, ...), custom_call_target="tpu_custom_call" | custom-call | tf_op jit(solution)/shard_map/home/pallas_call | solution.py:34
  13.6 1.6 %collective-permute-start.2 = (bf16[2,2,32,1024]{3,2,1,0:T(8,128)(2,1)S(1)}, bf16[2,2,32,1024]{3,2,1,0:T(8,128)(2,1)S(1)}, u32[]{:S(2)}, u32[]{:S(2)}) collective-permute-start(bf16[2,2,32,1024]{3,2,1,0:T(8,128)(2,1)S(1)} %get-tuple-element.35), channel_id=1, source_target_pairs={{0,1},{1,0},{2,3},{3,2},{4,5},{5,4},{6,7},{7,6},{8,9},{9,8},{10,11... | collective-permute-start | bytes 786440 | tf_op jit(solution)/shard_map/ppermute | solution.py:210
  15.1 1.5 %collective-permute-start.3 = (bf16[2,2,32,1024]{3,2,1,0:T(8,128)(2,1)S(1)}, bf16[2,2,32,1024]{3,2,1,0:T(8,128)(2,1)S(1)}, u32[]{:S(2)}, u32[]{:S(2)}) collective-permute-start(bf16[2,2,32,1024]{3,2,1,0:T(8,128)(2,1)S(1)} %get-tuple-element.36), channel_id=1, source_target_pairs={{0,2},{1,3},{2,0},{3,1},{4,6},{5,7},{6,4},{7,5},{8,10},{9,11},{10,... | collective-permute-start | bytes 786440 | tf_op jit(solution)/shard_map/ppermute | solution.py:210
  16.6 4.2 %collective-permute-done.7.got = bf16[128,1024]{1,0:T(8,128)(2,1)S(1)} collective-permute-done((bf16[128,1024]{1,0:T(8,128)(2,1)S(1)}, bf16[128,1024]{1,0:T(8,128)(2,1)S(1)}, u32[]{:S(2)}, u32[]{:S(2)}) %collective-permute-start.7) | collective-permute-done | bytes 262176 | tf_op jit(solution)/shard_map/ppermute | solution.py:210
  20.9 0.0 collective-permute-start.8
  20.9 0.5 %collective-permute-done.2.from1_ref = bf16[2,2,32,1024]{3,2,1,0:T(8,128)(2,1)S(1)} collective-permute-done((bf16[2,2,32,1024]{3,2,1,0:T(8,128)(2,1)S(1)}, bf16[2,2,32,1024]{3,2,1,0:T(8,128)(2,1)S(1)}, u32[]{:S(2)}, u32[]{:S(2)}) %collective-permute-start.2) | collective-permute-done | bytes 262176 | tf_op jit(solution)/shard_map/ppermute | solution.py:210
  21.4 1.2 %collective-permute-done.3.from2_ref = bf16[2,2,32,1024]{3,2,1,0:T(8,128)(2,1)S(1)} collective-permute-done((bf16[2,2,32,1024]{3,2,1,0:T(8,128)(2,1)S(1)}, bf16[2,2,32,1024]{3,2,1,0:T(8,128)(2,1)S(1)}, u32[]{:S(2)}, u32[]{:S(2)}) %collective-permute-start.3) | collective-permute-done | bytes 262176 | tf_op jit(solution)/shard_map/ppermute | solution.py:210
  22.6 0.1 middle.1
  22.7 0.6 %collective-permute-start.4 = (bf16[80,1024]{1,0:T(8,128)(2,1)S(1)}, bf16[80,1024]{1,0:T(8,128)(2,1)S(1)}, u32[]{:S(2)}, u32[]{:S(2)}) collective-permute-start(bf16[80,1024]{1,0:T(8,128)(2,1)S(1)} %get-tuple-element.38), channel_id=1, source_target_pairs={{0,1},{1,0},{2,3},{3,2},{4,5},{5,4},{6,7},{7,6},{8,9},{9,8},{10,11... | collective-permute-start | bytes 491528 | tf_op jit(solution)/shard_map/ppermute | solution.py:210
  23.3 1.5 %collective-permute-start.5 = (bf16[80,1024]{1,0:T(8,128)(2,1)S(1)}, bf16[80,1024]{1,0:T(8,128)(2,1)S(1)}, u32[]{:S(2)}, u32[]{:S(2)}) collective-permute-start(bf16[80,1024]{1,0:T(8,128)(2,1)S(1)} %get-tuple-element.39), channel_id=1, source_target_pairs={{0,2},{1,3},{2,0},{3,1},{4,6},{5,7},{6,4},{7,5},{8,10},{9,11},{10,... | collective-permute-start | bytes 491528 | tf_op jit(solution)/shard_map/ppermute | solution.py:210
  24.8 0.0 collective-permute-done.6.far
  24.8 0.0 collective-permute-done.8.got_paired
  24.8 0.4 two_cross.1
  25.2 0.4 parts.1
  25.6 0.1 collective-permute-start.9
  25.7 0.5 %collective-permute-start.10 = (bf16[256,128]{1,0:T(8,128)(2,1)S(1)}, bf16[256,128]{1,0:T(8,128)(2,1)S(1)}, u32[]{:S(2)}, u32[]{:S(2)}) collective-permute-start(bf16[256,128]{1,0:T(8,128)(2,1)S(1)} %get-tuple-element.41._), channel_id=1, source_target_pairs={{0,8},{4,12},{8,0},{12,4},{16,24},{20,28},{24,16},{28,20},{1,9},{5... | collective-permute-start | bytes 196616 | tf_op jit(solution)/shard_map/ppermute | solution.py:210
  26.2 0.4 two_near.1
  26.6 3.6 %collective-permute-done.10.refs_0_.came = bf16[256,128]{1,0:T(8,128)(2,1)S(1)} collective-permute-done((bf16[256,128]{1,0:T(8,128)(2,1)S(1)}, bf16[256,128]{1,0:T(8,128)(2,1)S(1)}, u32[]{:S(2)}, u32[]{:S(2)}) %collective-permute-start.10) | collective-permute-done | bytes 65568 | tf_op jit(solution)/shard_map/ppermute | solution.py:210
  30.2 0.0 collective-permute-done.9.came_ref
  30.2 0.0 collective-permute-done.4.from1_ref
  30.2 0.0 collective-permute-done.5.from2_ref
  30.2 0.1 slab.1
  30.4 0.1 collective-permute-start.14
  30.5 0.5 %collective-permute-start.11 = (bf16[64,1024]{1,0:T(8,128)(2,1)S(1)}, bf16[64,1024]{1,0:T(8,128)(2,1)S(1)}, u32[]{:S(2)}, u32[]{:S(2)}) collective-permute-start(bf16[64,1024]{1,0:T(8,128)(2,1)S(1)} %get-tuple-element.46), channel_id=1, source_target_pairs={{0,8},{4,12},{8,0},{12,4},{16,24},{20,28},{24,16},{28,20},{1,9},{5... | collective-permute-start | bytes 393224 | tf_op jit(solution)/shard_map/ppermute | solution.py:210
  31.0 2.6 %collective-permute-start.12 = (bf16[32,1024]{1,0:T(8,128)(2,1)S(1)}, bf16[32,1024]{1,0:T(8,128)(2,1)S(1)}, u32[]{:S(2)}, u32[]{:S(2)}) collective-permute-start(bf16[32,1024]{1,0:T(8,128)(2,1)S(1)} %get-tuple-element.47), channel_id=1, source_target_pairs={{0,16},{4,20},{8,24},{12,28},{16,0},{20,4},{24,8},{28,12},{1,17},{... | collective-permute-start | bytes 196616 | tf_op jit(solution)/shard_map/ppermute | solution.py:210
  33.5 1.4 %collective-permute-start.13 = (bf16[32,1024]{1,0:T(8,128)(2,1)S(1)}, bf16[32,1024]{1,0:T(8,128)(2,1)S(1)}, u32[]{:S(2)}, u32[]{:S(2)}) collective-permute-start(bf16[32,1024]{1,0:T(8,128)(2,1)S(1)} %get-tuple-element.48), channel_id=1, source_target_pairs={{0,24},{4,28},{8,16},{12,20},{16,8},{20,12},{24,0},{28,4},{1,25},{... | collective-permute-start | bytes 196616 | tf_op jit(solution)/shard_map/ppermute | solution.py:210
  34.9 0.0 collective-permute-done.14.came
  34.9 0.1 two_place.1
  35.0 1.6 %collective-permute-start.15 = (bf16[32,1024]{1,0:T(8,128)(2,1)S(1)}, bf16[32,1024]{1,0:T(8,128)(2,1)S(1)}, u32[]{:S(2)}, u32[]{:S(2)}) collective-permute-start(bf16[32,1024]{1,0:T(8,128)(2,1)S(1)} %get-tuple-element.56), channel_id=1, source_target_pairs={{0,1},{1,0},{2,3},{3,2},{4,5},{5,4},{6,7},{7,6},{8,9},{9,8},{10,11... | collective-permute-start | bytes 196616 | tf_op jit(solution)/shard_map/ppermute | solution.py:210
  36.6 1.5 %collective-permute-start.16 = (bf16[32,1024]{1,0:T(8,128)(2,1)S(1)}, bf16[32,1024]{1,0:T(8,128)(2,1)S(1)}, u32[]{:S(2)}, u32[]{:S(2)}) collective-permute-start(bf16[32,1024]{1,0:T(8,128)(2,1)S(1)} %get-tuple-element.57), channel_id=1, source_target_pairs={{0,2},{1,3},{2,0},{3,1},{4,6},{5,7},{6,4},{7,5},{8,10},{9,11},{10,... | collective-permute-start | bytes 196616 | tf_op jit(solution)/shard_map/ppermute | solution.py:210
  38.1 0.0 collective-permute-done.12.refs_2_
  38.1 0.7 %collective-permute-start.17 = (bf16[32,1024]{1,0:T(8,128)(2,1)S(1)}, bf16[32,1024]{1,0:T(8,128)(2,1)S(1)}, u32[]{:S(2)}, u32[]{:S(2)}) collective-permute-start(bf16[32,1024]{1,0:T(8,128)(2,1)S(1)} %get-tuple-element.58), channel_id=1, source_target_pairs={{0,3},{1,2},{2,1},{3,0},{4,7},{5,6},{6,5},{7,4},{8,11},{9,10},{10,... | collective-permute-start | bytes 196616 | tf_op jit(solution)/shard_map/ppermute | solution.py:210
  38.8 1.2 %collective-permute-done.13.refs_3_ = bf16[32,1024]{1,0:T(8,128)(2,1)S(1)} collective-permute-done((bf16[32,1024]{1,0:T(8,128)(2,1)S(1)}, bf16[32,1024]{1,0:T(8,128)(2,1)S(1)}, u32[]{:S(2)}, u32[]{:S(2)}) %collective-permute-start.13) | collective-permute-done | bytes 65568 | tf_op jit(solution)/shard_map/ppermute | solution.py:210
  40.0 0.0 collective-permute-done.11.refs_1_
  40.0 1.5 %collective-permute-done.16.refs_6_ = bf16[32,1024]{1,0:T(8,128)(2,1)S(1)} collective-permute-done((bf16[32,1024]{1,0:T(8,128)(2,1)S(1)}, bf16[32,1024]{1,0:T(8,128)(2,1)S(1)}, u32[]{:S(2)}, u32[]{:S(2)}) %collective-permute-start.16) | collective-permute-done | bytes 65568 | tf_op jit(solution)/shard_map/ppermute | solution.py:210
  41.5 1.7 %collective-permute-done.17.refs_7_ = bf16[32,1024]{1,0:T(8,128)(2,1)S(1)} collective-permute-done((bf16[32,1024]{1,0:T(8,128)(2,1)S(1)}, bf16[32,1024]{1,0:T(8,128)(2,1)S(1)}, u32[]{:S(2)}, u32[]{:S(2)}) %collective-permute-start.17) | collective-permute-done | bytes 65568 | tf_op jit(solution)/shard_map/ppermute | solution.py:210
  43.3 0.8 %last.1 = (f32[32,1024]{1,0:T(8,128)}, f32[32,1024]{1,0:T(8,128)}, f32[4,32,256]{2,1,0:T(8,128)}) custom-call(f32[32,1024]{1,0:T(8,128)S(1)} %get-tuple-element.44.mine, f32[32,1024]{1,0:T(8,128)S(1)} %get-tuple-element.45._.refs_0_, bf16[64,1024]{1,0:T(8,128)(2,1)S(1)} %collective-permute-done.11.refs_1_, ...), custom_call_target="tpu_custom_call" | custom-call | tf_op jit(solution)/shard_map/last/pallas_call | solution.py:34
  (7 shorter events, 0.0 us)
Async XLA Ops:
  0.6 1.6 %copy-start = (f32[4,128,1024]{2,1,0:T(8,128)S(1)}, f32[4,128,1024]{2,1,0:T(8,128)}, u32[]{:S(2)}) copy-start(f32[4,128,1024]{2,1,0:T(8,128)} %x_ref.5) | copy-start | bytes 6291460
  2.2 2.4 %copy-start.2 = (f32[1024,256]{1,0:T(8,128)S(1)}, f32[1024,256]{1,0:T(8,128)}, u32[]{:S(2)}) copy-start(f32[1024,256]{1,0:T(8,128)} %f_ref.1) | copy-start | bytes 3145732
  2.2 2.4 %copy-start.3 = (bf16[128,256]{1,0:T(8,128)(2,1)S(1)}, bf16[128,256]{1,0:T(8,128)(2,1)}, u32[]{:S(2)}) copy-start(bf16[128,256]{1,0:T(8,128)(2,1)} %two_ref.3) | copy-start | bytes 196612
  4.1 7.3 %copy-start.1 = (f32[4,128,1024]{2,1,0:T(8,128)S(1)}, f32[4,128,1024]{2,1,0:T(8,128)}, u32[]{:S(2)}) copy-start(f32[4,128,1024]{2,1,0:T(8,128)} %x_ref.5) | copy-start | bytes 6291460
  4.1 7.3 %collective-permute-start = (bf16[4,128,1024]{2,1,0:T(8,128)(2,1)S(1)}, bf16[4,128,1024]{2,1,0:T(8,128)(2,1)S(1)}, u32[]{:S(2)}, u32[]{:S(2)}) collective-permute-start(bf16[4,128,1024]{2,1,0:T(8,128)(2,1)S(1)} %away.1._), channel_id=1, source_target_pairs={{0,4},{4,0},{8,12},{12,8},{16,20},{20,16},{24,28},{28,24},{1,5},{5... | collective-permute-start | bytes 3145736 | tf_op jit(solution)/shard_map/ppermute | solution.py:210
  5.6 5.8 %collective-permute-start.1 = (bf16[128,1024]{1,0:T(8,128)(2,1)S(1)}, bf16[128,1024]{1,0:T(8,128)(2,1)S(1)}, u32[]{:S(2)}, u32[]{:S(2)}) collective-permute-start(bf16[128,1024]{1,0:T(8,128)(2,1)S(1)} %get-tuple-element.31.u), channel_id=1, source_target_pairs={{0,4},{4,0},{8,12},{12,8},{16,20},{20,16},{24,28},{28,24},{1,5},{5... | collective-permute-start | bytes 786440 | tf_op jit(solution)/shard_map/ppermute | solution.py:210
  5.8 15.1 %collective-permute-start.7 = (bf16[128,1024]{1,0:T(8,128)(2,1)S(1)}, bf16[128,1024]{1,0:T(8,128)(2,1)S(1)}, u32[]{:S(2)}, u32[]{:S(2)}) collective-permute-start(bf16[128,1024]{1,0:T(8,128)(2,1)S(1)} %get-tuple-element.31.u), channel_id=1, source_target_pairs={{0,8},{4,12},{8,0},{12,4},{16,24},{20,28},{24,16},{28,20},{1,9},{5... | collective-permute-start | bytes 786440 | tf_op jit(solution)/shard_map/ppermute | solution.py:210
  8.8 16.0 %collective-permute-start.6 = (bf16[144,1024]{1,0:T(8,128)(2,1)S(1)}, bf16[144,1024]{1,0:T(8,128)(2,1)S(1)}, u32[]{:S(2)}, u32[]{:S(2)}) collective-permute-start(bf16[144,1024]{1,0:T(8,128)(2,1)S(1)} %get-tuple-element.40), channel_id=1, source_target_pairs={{0,16},{4,20},{8,24},{12,28},{16,0},{20,4},{24,8},{28,12},{1,17},{... | collective-permute-start | bytes 884744 | tf_op jit(solution)/shard_map/ppermute | solution.py:210
  13.6 7.8 %collective-permute-start.2 = (bf16[2,2,32,1024]{3,2,1,0:T(8,128)(2,1)S(1)}, bf16[2,2,32,1024]{3,2,1,0:T(8,128)(2,1)S(1)}, u32[]{:S(2)}, u32[]{:S(2)}) collective-permute-start(bf16[2,2,32,1024]{3,2,1,0:T(8,128)(2,1)S(1)} %get-tuple-element.35), channel_id=1, source_target_pairs={{0,1},{1,0},{2,3},{3,2},{4,5},{5,4},{6,7},{7,6},{8,9},{9,8},{10,11... | collective-permute-start | bytes 786440 | tf_op jit(solution)/shard_map/ppermute | solution.py:210
  15.1 7.5 %collective-permute-start.3 = (bf16[2,2,32,1024]{3,2,1,0:T(8,128)(2,1)S(1)}, bf16[2,2,32,1024]{3,2,1,0:T(8,128)(2,1)S(1)}, u32[]{:S(2)}, u32[]{:S(2)}) collective-permute-start(bf16[2,2,32,1024]{3,2,1,0:T(8,128)(2,1)S(1)} %get-tuple-element.36), channel_id=1, source_target_pairs={{0,2},{1,3},{2,0},{3,1},{4,6},{5,7},{6,4},{7,5},{8,10},{9,11},{10,... | collective-permute-start | bytes 786440 | tf_op jit(solution)/shard_map/ppermute | solution.py:210
  20.9 3.9 %collective-permute-start.8 = (bf16[128,1024]{1,0:T(8,128)(2,1)S(1)}, bf16[128,1024]{1,0:T(8,128)(2,1)S(1)}, u32[]{:S(2)}, u32[]{:S(2)}) collective-permute-start(bf16[128,1024]{1,0:T(8,128)(2,1)S(1)} %collective-permute-done.7.got), channel_id=1, source_target_pairs={{0,4},{4,0},{8,12},{12,8},{16,20},{20,16},{24,28},{28,24},{1,5},{5... | collective-permute-start | bytes 786440 | tf_op jit(solution)/shard_map/ppermute | solution.py:210
  22.7 7.5 %collective-permute-start.4 = (bf16[80,1024]{1,0:T(8,128)(2,1)S(1)}, bf16[80,1024]{1,0:T(8,128)(2,1)S(1)}, u32[]{:S(2)}, u32[]{:S(2)}) collective-permute-start(bf16[80,1024]{1,0:T(8,128)(2,1)S(1)} %get-tuple-element.38), channel_id=1, source_target_pairs={{0,1},{1,0},{2,3},{3,2},{4,5},{5,4},{6,7},{7,6},{8,9},{9,8},{10,11... | collective-permute-start | bytes 491528 | tf_op jit(solution)/shard_map/ppermute | solution.py:210
  23.3 6.9 %collective-permute-start.5 = (bf16[80,1024]{1,0:T(8,128)(2,1)S(1)}, bf16[80,1024]{1,0:T(8,128)(2,1)S(1)}, u32[]{:S(2)}, u32[]{:S(2)}) collective-permute-start(bf16[80,1024]{1,0:T(8,128)(2,1)S(1)} %get-tuple-element.39), channel_id=1, source_target_pairs={{0,2},{1,3},{2,0},{3,1},{4,6},{5,7},{6,4},{7,5},{8,10},{9,11},{10,... | collective-permute-start | bytes 491528 | tf_op jit(solution)/shard_map/ppermute | solution.py:210
  25.6 4.6 %collective-permute-start.9 = (bf16[64,1024]{1,0:T(8,128)(2,1)S(1)}, bf16[64,1024]{1,0:T(8,128)(2,1)S(1)}, u32[]{:S(2)}, u32[]{:S(2)}) collective-permute-start(bf16[64,1024]{1,0:T(8,128)(2,1)S(1)} %get-tuple-element.43), channel_id=1, source_target_pairs={{0,4},{4,0},{8,12},{12,8},{16,20},{20,16},{24,28},{28,24},{1,5},{5... | collective-permute-start | bytes 393224 | tf_op jit(solution)/shard_map/ppermute | solution.py:210
  25.7 4.5 %collective-permute-start.10 = (bf16[256,128]{1,0:T(8,128)(2,1)S(1)}, bf16[256,128]{1,0:T(8,128)(2,1)S(1)}, u32[]{:S(2)}, u32[]{:S(2)}) collective-permute-start(bf16[256,128]{1,0:T(8,128)(2,1)S(1)} %get-tuple-element.41._), channel_id=1, source_target_pairs={{0,8},{4,12},{8,0},{12,4},{16,24},{20,28},{24,16},{28,20},{1,9},{5... | collective-permute-start | bytes 196616 | tf_op jit(solution)/shard_map/ppermute | solution.py:210
  30.4 4.5 %collective-permute-start.14 = (bf16[64,1024]{1,0:T(8,128)(2,1)S(1)}, bf16[64,1024]{1,0:T(8,128)(2,1)S(1)}, u32[]{:S(2)}, u32[]{:S(2)}) collective-permute-start(bf16[64,1024]{1,0:T(8,128)(2,1)S(1)} %get-tuple-element.54), channel_id=1, source_target_pairs={{0,4},{4,0},{8,12},{12,8},{16,20},{20,16},{24,28},{28,24},{1,5},{5... | collective-permute-start | bytes 393224 | tf_op jit(solution)/shard_map/ppermute | solution.py:210
  30.5 9.5 %collective-permute-start.11 = (bf16[64,1024]{1,0:T(8,128)(2,1)S(1)}, bf16[64,1024]{1,0:T(8,128)(2,1)S(1)}, u32[]{:S(2)}, u32[]{:S(2)}) collective-permute-start(bf16[64,1024]{1,0:T(8,128)(2,1)S(1)} %get-tuple-element.46), channel_id=1, source_target_pairs={{0,8},{4,12},{8,0},{12,4},{16,24},{20,28},{24,16},{28,20},{1,9},{5... | collective-permute-start | bytes 393224 | tf_op jit(solution)/shard_map/ppermute | solution.py:210
  31.0 7.1 %collective-permute-start.12 = (bf16[32,1024]{1,0:T(8,128)(2,1)S(1)}, bf16[32,1024]{1,0:T(8,128)(2,1)S(1)}, u32[]{:S(2)}, u32[]{:S(2)}) collective-permute-start(bf16[32,1024]{1,0:T(8,128)(2,1)S(1)} %get-tuple-element.47), channel_id=1, source_target_pairs={{0,16},{4,20},{8,24},{12,28},{16,0},{20,4},{24,8},{28,12},{1,17},{... | collective-permute-start | bytes 196616 | tf_op jit(solution)/shard_map/ppermute | solution.py:210
  33.5 6.4 %collective-permute-start.13 = (bf16[32,1024]{1,0:T(8,128)(2,1)S(1)}, bf16[32,1024]{1,0:T(8,128)(2,1)S(1)}, u32[]{:S(2)}, u32[]{:S(2)}) collective-permute-start(bf16[32,1024]{1,0:T(8,128)(2,1)S(1)} %get-tuple-element.48), channel_id=1, source_target_pairs={{0,24},{4,28},{8,16},{12,20},{16,8},{20,12},{24,0},{28,4},{1,25},{... | collective-permute-start | bytes 196616 | tf_op jit(solution)/shard_map/ppermute | solution.py:210
  35.0 5.0 %collective-permute-start.15 = (bf16[32,1024]{1,0:T(8,128)(2,1)S(1)}, bf16[32,1024]{1,0:T(8,128)(2,1)S(1)}, u32[]{:S(2)}, u32[]{:S(2)}) collective-permute-start(bf16[32,1024]{1,0:T(8,128)(2,1)S(1)} %get-tuple-element.56), channel_id=1, source_target_pairs={{0,1},{1,0},{2,3},{3,2},{4,5},{5,4},{6,7},{7,6},{8,9},{9,8},{10,11... | collective-permute-start | bytes 196616 | tf_op jit(solution)/shard_map/ppermute | solution.py:210
  36.6 5.0 %collective-permute-start.16 = (bf16[32,1024]{1,0:T(8,128)(2,1)S(1)}, bf16[32,1024]{1,0:T(8,128)(2,1)S(1)}, u32[]{:S(2)}, u32[]{:S(2)}) collective-permute-start(bf16[32,1024]{1,0:T(8,128)(2,1)S(1)} %get-tuple-element.57), channel_id=1, source_target_pairs={{0,2},{1,3},{2,0},{3,1},{4,6},{5,7},{6,4},{7,5},{8,10},{9,11},{10,... | collective-permute-start | bytes 196616 | tf_op jit(solution)/shard_map/ppermute | solution.py:210
  38.1 5.2 %collective-permute-start.17 = (bf16[32,1024]{1,0:T(8,128)(2,1)S(1)}, bf16[32,1024]{1,0:T(8,128)(2,1)S(1)}, u32[]{:S(2)}, u32[]{:S(2)}) collective-permute-start(bf16[32,1024]{1,0:T(8,128)(2,1)S(1)} %get-tuple-element.58), channel_id=1, source_target_pairs={{0,3},{1,2},{2,1},{3,0},{4,7},{5,6},{6,5},{7,4},{8,11},{9,10},{10,... | collective-permute-start | bytes 196616 | tf_op jit(solution)/shard_map/ppermute | solution.py:210

commit v7 on v6

--- a/solution.py
+++ b/solution.py
@@ -127,7 +127,9 @@
     for t, out in enumerate(outs):
         out[:height] = rows_ref[position()[1] ^ t].astype(out.dtype)
     part_ref[...] = mine_ref[:part] + came_ref[:part].astype(F32)
-    outs[1][height:] = (mine_ref[part:] + came_ref[part:].astype(F32)).astype(BF16)
+    high, low = halves(mine_ref[part:] + came_ref[part:].astype(F32))
+    outs[1][height : height + part] = high
+    outs[1][height + part :] = low
 
 
 def near_kernel(u, paired, got, mine_ref, other_ref):
@@ -200,10 +202,12 @@
         for part in parts[i * count + 1 : (i + 1) * count]:
             total = total + part[: total.shape[0]].astype(F32)
         outs[i][...] = total * scale
-    slices, _, rank = outs[2].shape
+    slices, part, rank = outs[2].shape
+    height = parts[0].shape[0]
     for k in range(slices):
         at = slice(k * rank, (k + 1) * rank)
-        outs[2][k] = mine[:, at] + parts[1][parts[0].shape[0] :, at].astype(F32)
+        came = parts[1][height : height + part, at].astype(F32) + parts[1][height + part :, at].astype(F32)
+        outs[2][k] = mine[:, at] + came
 
 
 def xor_permute(x, axis, bits):
@@ -314,7 +318,7 @@
         slab_kernel,
         "slab",
         [
-            ((height + (part if t == 1 else 0), width), F32 if t == 0 else BF16)
+            ((height + (2 * part if t == 1 else 0), width), F32 if t == 0 else BF16)
             for t in range(count_z)
         ]
         + [((part, columns), F32)],
@@ -352,7 +356,7 @@
         scratch=[pltpu.VMEM((owned, count_ja * owned), F32)],
     )
     rows = list(rows)
-    for t in reversed(range(1, count_ka)):
+    for t in range(1, count_ka):
         rows[t] = xor_permute(rows[t], "ka", t)
     return call(
         functools.partial(last_kernel, (norm_one, norm_two), count_z),

time: 44.2 us -> 44.2 us (level)
  starting transfers between devices: 20.4 us -> 21.4 us
  waiting for transfers between devices: 13.9 us -> 12.9 us
    ppermute x18, starting transfers between devices: 20.4 us -> 21.4 us  [xor_permute(): lax.ppermute(x, axis, [(i, i ^ bits) for i in range(lax.axis_size(axis))])]
    ppermute x18, waiting for transfers between devices: 13.9 us -> 12.9 us  [xor_permute(): lax.ppermute(x, axis, [(i, i ^ bits) for i in range(lax.axis_size(axis))])]
where the time goes in v7:
time: 44.2 us; the launch traced here: 44.1 us
  starting transfers between devices  21.4 us (48%)
  waiting for transfers between devices  12.9 us (29%)
  Pallas kernels  7.38 us (17%)
  local copies, waits for them, and re-layouts  1.6 us (4%)
  between operations  0.76 us (2%)
    ppermute x18, starting transfers between devices, xor_permute(): lax.ppermute(x, axis, [(i, i ^ bits) for i in range(lax.axis_size(axis))])  21.4 us
    ppermute x18, waiting for transfers between devices, xor_permute(): lax.ppermute(x, axis, [(i, i ^ bits) for i in range(lax.axis_size(axis))])  12.9 us
    pallas_call x11, Pallas kernels, call(): pl.pallas_call(kernel, out_shape=[jax.ShapeDtypeStruct(s, d) for s, d in...  7.38 us
    unnamed x8, local copies, waits for them, and re-layouts  1.6 us
  transfers between devices with their start and end apart: 18, of which 7 were waited for; matrix products, arithmetic and copies ran while one was open for 0% of the time, Pallas kernels for 10%

profile of v7, /device:TPU:0, one launch (start us, length us, event | category | flops | bytes accessed | tf_op | source)
XLA Modules:
  0.0 44.1 jit_solution(15685582009869448513)
XLA Ops:
  0.6 0.0 copy-start
  0.6 1.6 %copy-done = f32[4,128,1024]{2,1,0:T(8,128)S(1)} copy-done((f32[4,128,1024]{2,1,0:T(8,128)S(1)}, f32[4,128,1024]{2,1,0:T(8,128)}, u32[]{:S(2)}) %copy-start) | copy-done | bytes 2097176
  2.2 1.9 %away.1._ = bf16[4,128,1024]{2,1,0:T(8,128)(2,1)S(1)} custom-call(f32[4,128,1024]{2,1,0:T(8,128)S(1)} %copy-done), custom_call_target="tpu_custom_call" | custom-call | tf_op jit(solution)/shard_map/away/pallas_call | solution.py:34
  4.1 0.0 copy-start.1
  4.1 0.5 %collective-permute-start = (bf16[4,128,1024]{2,1,0:T(8,128)(2,1)S(1)}, bf16[4,128,1024]{2,1,0:T(8,128)(2,1)S(1)}, u32[]{:S(2)}, u32[]{:S(2)}) collective-permute-start(bf16[4,128,1024]{2,1,0:T(8,128)(2,1)S(1)} %away.1._), channel_id=1, source_target_pairs={{0,4},{4,0},{8,12},{12,8},{16,20},{20,16},{24,28},{28,24},{1,5},{5... | collective-permute-start | bytes 3145736 | tf_op jit(solution)/shard_map/ppermute | solution.py:214
  4.6 1.0 %core.1 = (bf16[128,1024]{1,0:T(8,128)(2,1)S(1)}, bf16[144,1024]{1,0:T(8,128)(2,1)S(1)}) custom-call(f32[4,128,1024]{2,1,0:T(8,128)S(1)} %copy-done, f32[1024,256]{1,0:T(8,128)S(1)} %copy-done.2, bf16[128,256]{1,0:T(8,128)(2,1)S(1)} %copy-done.3, bf16[4,128,1024]{2,1,0:T(8,128)(2,1)S(1)} %away.1._), custom_call_target="tpu_custom_call" | custom-call | tf_op jit(solution)/shard_map/core/pallas_call | solution.py:34
  5.6 0.1 collective-permute-start.1
  5.8 3.0 %collective-permute-start.7 = (bf16[128,1024]{1,0:T(8,128)(2,1)S(1)}, bf16[128,1024]{1,0:T(8,128)(2,1)S(1)}, u32[]{:S(2)}, u32[]{:S(2)}) collective-permute-start(bf16[128,1024]{1,0:T(8,128)(2,1)S(1)} %get-tuple-element.31.u), channel_id=1, source_target_pairs={{0,8},{4,12},{8,0},{12,4},{16,24},{20,28},{24,16},{28,20},{1,9},{5... | collective-permute-start | bytes 786440 | tf_op jit(solution)/shard_map/ppermute | solution.py:214
  8.8 2.6 %collective-permute-start.6 = (bf16[144,1024]{1,0:T(8,128)(2,1)S(1)}, bf16[144,1024]{1,0:T(8,128)(2,1)S(1)}, u32[]{:S(2)}, u32[]{:S(2)}) collective-permute-start(bf16[144,1024]{1,0:T(8,128)(2,1)S(1)} %get-tuple-element.40), channel_id=1, source_target_pairs={{0,16},{4,20},{8,24},{12,28},{16,0},{20,4},{24,8},{28,12},{1,17},{... | collective-permute-start | bytes 884744 | tf_op jit(solution)/shard_map/ppermute | solution.py:214
  11.4 0.0 collective-permute-done.1._.paired
  11.4 0.0 collective-permute-done.came_ref
  11.4 2.1 %home.1 = (f32[4,32,1024]{2,1,0:T(8,128)S(1)}, f32[2,32,1024]{2,1,0:T(8,128)S(1)}, f32[2,32,1024]{2,1,0:T(8,128)S(1)}, bf16[2,2,32,1024]{3,2,1,0:T(8,128)(2,1)S(1)}, bf16[2,2,32,1024]{3,2,1,0:T(8,128)(2,1)S(1)}) custom-call(f32[4,128,1024]{2,1,0:T(8,128)S(1)} %copy-done.1, bf16[4,128,1024]{2,1,0:T(8,128)(2,1)S(1)} %collective-permute-done.came_ref, ...), custom_call_target="tpu_custom_call" | custom-call | tf_op jit(solution)/shard_map/home/pallas_call | solution.py:34
  13.6 1.6 %collective-permute-start.2 = (bf16[2,2,32,1024]{3,2,1,0:T(8,128)(2,1)S(1)}, bf16[2,2,32,1024]{3,2,1,0:T(8,128)(2,1)S(1)}, u32[]{:S(2)}, u32[]{:S(2)}) collective-permute-start(bf16[2,2,32,1024]{3,2,1,0:T(8,128)(2,1)S(1)} %get-tuple-element.35), channel_id=1, source_target_pairs={{0,1},{1,0},{2,3},{3,2},{4,5},{5,4},{6,7},{7,6},{8,9},{9,8},{10,11... | collective-permute-start | bytes 786440 | tf_op jit(solution)/shard_map/ppermute | solution.py:214
  15.1 1.5 %collective-permute-start.3 = (bf16[2,2,32,1024]{3,2,1,0:T(8,128)(2,1)S(1)}, bf16[2,2,32,1024]{3,2,1,0:T(8,128)(2,1)S(1)}, u32[]{:S(2)}, u32[]{:S(2)}) collective-permute-start(bf16[2,2,32,1024]{3,2,1,0:T(8,128)(2,1)S(1)} %get-tuple-element.36), channel_id=1, source_target_pairs={{0,2},{1,3},{2,0},{3,1},{4,6},{5,7},{6,4},{7,5},{8,10},{9,11},{10,... | collective-permute-start | bytes 786440 | tf_op jit(solution)/shard_map/ppermute | solution.py:214
  16.6 4.2 %collective-permute-done.7.got = bf16[128,1024]{1,0:T(8,128)(2,1)S(1)} collective-permute-done((bf16[128,1024]{1,0:T(8,128)(2,1)S(1)}, bf16[128,1024]{1,0:T(8,128)(2,1)S(1)}, u32[]{:S(2)}, u32[]{:S(2)}) %collective-permute-start.7) | collective-permute-done | bytes 262176 | tf_op jit(solution)/shard_map/ppermute | solution.py:214
  20.9 0.0 collective-permute-start.8
  20.9 0.5 %collective-permute-done.2.from1_ref = bf16[2,2,32,1024]{3,2,1,0:T(8,128)(2,1)S(1)} collective-permute-done((bf16[2,2,32,1024]{3,2,1,0:T(8,128)(2,1)S(1)}, bf16[2,2,32,1024]{3,2,1,0:T(8,128)(2,1)S(1)}, u32[]{:S(2)}, u32[]{:S(2)}) %collective-permute-start.2) | collective-permute-done | bytes 262176 | tf_op jit(solution)/shard_map/ppermute | solution.py:214
  21.4 1.2 %collective-permute-done.3.from2_ref = bf16[2,2,32,1024]{3,2,1,0:T(8,128)(2,1)S(1)} collective-permute-done((bf16[2,2,32,1024]{3,2,1,0:T(8,128)(2,1)S(1)}, bf16[2,2,32,1024]{3,2,1,0:T(8,128)(2,1)S(1)}, u32[]{:S(2)}, u32[]{:S(2)}) %collective-permute-start.3) | collective-permute-done | bytes 262176 | tf_op jit(solution)/shard_map/ppermute | solution.py:214
  22.6 0.1 middle.1
  22.7 0.6 %collective-permute-start.4 = (bf16[80,1024]{1,0:T(8,128)(2,1)S(1)}, bf16[80,1024]{1,0:T(8,128)(2,1)S(1)}, u32[]{:S(2)}, u32[]{:S(2)}) collective-permute-start(bf16[80,1024]{1,0:T(8,128)(2,1)S(1)} %get-tuple-element.38), channel_id=1, source_target_pairs={{0,1},{1,0},{2,3},{3,2},{4,5},{5,4},{6,7},{7,6},{8,9},{9,8},{10,11... | collective-permute-start | bytes 491528 | tf_op jit(solution)/shard_map/ppermute | solution.py:214
  23.3 1.5 %collective-permute-start.5 = (bf16[80,1024]{1,0:T(8,128)(2,1)S(1)}, bf16[80,1024]{1,0:T(8,128)(2,1)S(1)}, u32[]{:S(2)}, u32[]{:S(2)}) collective-permute-start(bf16[80,1024]{1,0:T(8,128)(2,1)S(1)} %get-tuple-element.39), channel_id=1, source_target_pairs={{0,2},{1,3},{2,0},{3,1},{4,6},{5,7},{6,4},{7,5},{8,10},{9,11},{10,... | collective-permute-start | bytes 491528 | tf_op jit(solution)/shard_map/ppermute | solution.py:214
  24.8 0.0 collective-permute-done.6.far
  24.8 0.0 collective-permute-done.8.got_paired
  24.8 0.4 two_cross.1
  25.2 0.4 parts.1
  25.6 0.1 collective-permute-start.9
  25.7 0.5 %collective-permute-start.10 = (bf16[256,128]{1,0:T(8,128)(2,1)S(1)}, bf16[256,128]{1,0:T(8,128)(2,1)S(1)}, u32[]{:S(2)}, u32[]{:S(2)}) collective-permute-start(bf16[256,128]{1,0:T(8,128)(2,1)S(1)} %get-tuple-element.41._), channel_id=1, source_target_pairs={{0,8},{4,12},{8,0},{12,4},{16,24},{20,28},{24,16},{28,20},{1,9},{5... | collective-permute-start | bytes 196616 | tf_op jit(solution)/shard_map/ppermute | solution.py:214
  26.2 0.4 two_near.1
  26.6 3.6 %collective-permute-done.10.refs_0_.came = bf16[256,128]{1,0:T(8,128)(2,1)S(1)} collective-permute-done((bf16[256,128]{1,0:T(8,128)(2,1)S(1)}, bf16[256,128]{1,0:T(8,128)(2,1)S(1)}, u32[]{:S(2)}, u32[]{:S(2)}) %collective-permute-start.10) | collective-permute-done | bytes 65568 | tf_op jit(solution)/shard_map/ppermute | solution.py:214
  30.2 0.0 collective-permute-done.9.came_ref
  30.2 0.0 collective-permute-done.4.from1_ref
  30.2 0.0 collective-permute-done.5.from2_ref
  30.2 0.1 slab.1
  30.4 0.1 collective-permute-start.14
  30.5 0.5 %collective-permute-start.11 = (bf16[96,1024]{1,0:T(8,128)(2,1)S(1)}, bf16[96,1024]{1,0:T(8,128)(2,1)S(1)}, u32[]{:S(2)}, u32[]{:S(2)}) collective-permute-start(bf16[96,1024]{1,0:T(8,128)(2,1)S(1)} %get-tuple-element.46), channel_id=1, source_target_pairs={{0,8},{4,12},{8,0},{12,4},{16,24},{20,28},{24,16},{28,20},{1,9},{5... | collective-permute-start | bytes 589832 | tf_op jit(solution)/shard_map/ppermute | solution.py:214
  31.0 2.6 %collective-permute-start.12 = (bf16[32,1024]{1,0:T(8,128)(2,1)S(1)}, bf16[32,1024]{1,0:T(8,128)(2,1)S(1)}, u32[]{:S(2)}, u32[]{:S(2)}) collective-permute-start(bf16[32,1024]{1,0:T(8,128)(2,1)S(1)} %get-tuple-element.47), channel_id=1, source_target_pairs={{0,16},{4,20},{8,24},{12,28},{16,0},{20,4},{24,8},{28,12},{1,17},{... | collective-permute-start | bytes 196616 | tf_op jit(solution)/shard_map/ppermute | solution.py:214
  33.6 1.4 %collective-permute-start.13 = (bf16[32,1024]{1,0:T(8,128)(2,1)S(1)}, bf16[32,1024]{1,0:T(8,128)(2,1)S(1)}, u32[]{:S(2)}, u32[]{:S(2)}) collective-permute-start(bf16[32,1024]{1,0:T(8,128)(2,1)S(1)} %get-tuple-element.48), channel_id=1, source_target_pairs={{0,24},{4,28},{8,16},{12,20},{16,8},{20,12},{24,0},{28,4},{1,25},{... | collective-permute-start | bytes 196616 | tf_op jit(solution)/shard_map/ppermute | solution.py:214
  34.9 0.0 collective-permute-done.14.came
  34.9 0.1 two_place.1
  35.0 1.6 %collective-permute-start.15 = (bf16[32,1024]{1,0:T(8,128)(2,1)S(1)}, bf16[32,1024]{1,0:T(8,128)(2,1)S(1)}, u32[]{:S(2)}, u32[]{:S(2)}) collective-permute-start(bf16[32,1024]{1,0:T(8,128)(2,1)S(1)} %get-tuple-element.56), channel_id=1, source_target_pairs={{0,1},{1,0},{2,3},{3,2},{4,5},{5,4},{6,7},{7,6},{8,9},{9,8},{10,11... | collective-permute-start | bytes 196616 | tf_op jit(solution)/shard_map/ppermute | solution.py:214
  36.6 1.5 %collective-permute-start.16 = (bf16[32,1024]{1,0:T(8,128)(2,1)S(1)}, bf16[32,1024]{1,0:T(8,128)(2,1)S(1)}, u32[]{:S(2)}, u32[]{:S(2)}) collective-permute-start(bf16[32,1024]{1,0:T(8,128)(2,1)S(1)} %get-tuple-element.57), channel_id=1, source_target_pairs={{0,2},{1,3},{2,0},{3,1},{4,6},{5,7},{6,4},{7,5},{8,10},{9,11},{10,... | collective-permute-start | bytes 196616 | tf_op jit(solution)/shard_map/ppermute | solution.py:214
  38.1 0.0 collective-permute-done.12.refs_2_
  38.1 1.8 %collective-permute-start.17 = (bf16[32,1024]{1,0:T(8,128)(2,1)S(1)}, bf16[32,1024]{1,0:T(8,128)(2,1)S(1)}, u32[]{:S(2)}, u32[]{:S(2)}) collective-permute-start(bf16[32,1024]{1,0:T(8,128)(2,1)S(1)} %get-tuple-element.58), channel_id=1, source_target_pairs={{0,3},{1,2},{2,1},{3,0},{4,7},{5,6},{6,5},{7,4},{8,11},{9,10},{10,... | collective-permute-start | bytes 196616 | tf_op jit(solution)/shard_map/ppermute | solution.py:214
  39.9 1.4 %collective-permute-done.13.refs_3_ = bf16[32,1024]{1,0:T(8,128)(2,1)S(1)} collective-permute-done((bf16[32,1024]{1,0:T(8,128)(2,1)S(1)}, bf16[32,1024]{1,0:T(8,128)(2,1)S(1)}, u32[]{:S(2)}, u32[]{:S(2)}) %collective-permute-start.13) | collective-permute-done | bytes 65568 | tf_op jit(solution)/shard_map/ppermute | solution.py:214
  41.3 0.2 collective-permute-done.16.refs_6_
  41.6 1.7 %collective-permute-done.17.refs_7_ = bf16[32,1024]{1,0:T(8,128)(2,1)S(1)} collective-permute-done((bf16[32,1024]{1,0:T(8,128)(2,1)S(1)}, bf16[32,1024]{1,0:T(8,128)(2,1)S(1)}, u32[]{:S(2)}, u32[]{:S(2)}) %collective-permute-start.17) | collective-permute-done | bytes 65568 | tf_op jit(solution)/shard_map/ppermute | solution.py:214
  43.3 0.0 collective-permute-done.11.refs_1_
  43.3 0.8 %last.1 = (f32[32,1024]{1,0:T(8,128)}, f32[32,1024]{1,0:T(8,128)}, f32[4,32,256]{2,1,0:T(8,128)}) custom-call(f32[32,1024]{1,0:T(8,128)S(1)} %get-tuple-element.44.mine, f32[32,1024]{1,0:T(8,128)S(1)} %get-tuple-element.45._.refs_0_, bf16[96,1024]{1,0:T(8,128)(2,1)S(1)} %collective-permute-done.11.refs_1_, ...), custom_call_target="tpu_custom_call" | custom-call | tf_op jit(solution)/shard_map/last/pallas_call | solution.py:34
  (7 shorter events, 0.0 us)
Async XLA Ops:
  0.6 1.6 %copy-start = (f32[4,128,1024]{2,1,0:T(8,128)S(1)}, f32[4,128,1024]{2,1,0:T(8,128)}, u32[]{:S(2)}) copy-start(f32[4,128,1024]{2,1,0:T(8,128)} %x_ref.5) | copy-start | bytes 6291460
  2.2 2.4 %copy-start.2 = (f32[1024,256]{1,0:T(8,128)S(1)}, f32[1024,256]{1,0:T(8,128)}, u32[]{:S(2)}) copy-start(f32[1024,256]{1,0:T(8,128)} %f_ref.1) | copy-start | bytes 3145732
  2.2 2.4 %copy-start.3 = (bf16[128,256]{1,0:T(8,128)(2,1)S(1)}, bf16[128,256]{1,0:T(8,128)(2,1)}, u32[]{:S(2)}) copy-start(bf16[128,256]{1,0:T(8,128)(2,1)} %two_ref.3) | copy-start | bytes 196612
  4.1 7.3 %copy-start.1 = (f32[4,128,1024]{2,1,0:T(8,128)S(1)}, f32[4,128,1024]{2,1,0:T(8,128)}, u32[]{:S(2)}) copy-start(f32[4,128,1024]{2,1,0:T(8,128)} %x_ref.5) | copy-start | bytes 6291460
  4.1 7.3 %collective-permute-start = (bf16[4,128,1024]{2,1,0:T(8,128)(2,1)S(1)}, bf16[4,128,1024]{2,1,0:T(8,128)(2,1)S(1)}, u32[]{:S(2)}, u32[]{:S(2)}) collective-permute-start(bf16[4,128,1024]{2,1,0:T(8,128)(2,1)S(1)} %away.1._), channel_id=1, source_target_pairs={{0,4},{4,0},{8,12},{12,8},{16,20},{20,16},{24,28},{28,24},{1,5},{5... | collective-permute-start | bytes 3145736 | tf_op jit(solution)/shard_map/ppermute | solution.py:214
  5.6 5.8 %collective-permute-start.1 = (bf16[128,1024]{1,0:T(8,128)(2,1)S(1)}, bf16[128,1024]{1,0:T(8,128)(2,1)S(1)}, u32[]{:S(2)}, u32[]{:S(2)}) collective-permute-start(bf16[128,1024]{1,0:T(8,128)(2,1)S(1)} %get-tuple-element.31.u), channel_id=1, source_target_pairs={{0,4},{4,0},{8,12},{12,8},{16,20},{20,16},{24,28},{28,24},{1,5},{5... | collective-permute-start | bytes 786440 | tf_op jit(solution)/shard_map/ppermute | solution.py:214
  5.8 15.1 %collective-permute-start.7 = (bf16[128,1024]{1,0:T(8,128)(2,1)S(1)}, bf16[128,1024]{1,0:T(8,128)(2,1)S(1)}, u32[]{:S(2)}, u32[]{:S(2)}) collective-permute-start(bf16[128,1024]{1,0:T(8,128)(2,1)S(1)} %get-tuple-element.31.u), channel_id=1, source_target_pairs={{0,8},{4,12},{8,0},{12,4},{16,24},{20,28},{24,16},{28,20},{1,9},{5... | collective-permute-start | bytes 786440 | tf_op jit(solution)/shard_map/ppermute | solution.py:214
  8.8 16.0 %collective-permute-start.6 = (bf16[144,1024]{1,0:T(8,128)(2,1)S(1)}, bf16[144,1024]{1,0:T(8,128)(2,1)S(1)}, u32[]{:S(2)}, u32[]{:S(2)}) collective-permute-start(bf16[144,1024]{1,0:T(8,128)(2,1)S(1)} %get-tuple-element.40), channel_id=1, source_target_pairs={{0,16},{4,20},{8,24},{12,28},{16,0},{20,4},{24,8},{28,12},{1,17},{... | collective-permute-start | bytes 884744 | tf_op jit(solution)/shard_map/ppermute | solution.py:214
  13.6 7.8 %collective-permute-start.2 = (bf16[2,2,32,1024]{3,2,1,0:T(8,128)(2,1)S(1)}, bf16[2,2,32,1024]{3,2,1,0:T(8,128)(2,1)S(1)}, u32[]{:S(2)}, u32[]{:S(2)}) collective-permute-start(bf16[2,2,32,1024]{3,2,1,0:T(8,128)(2,1)S(1)} %get-tuple-element.35), channel_id=1, source_target_pairs={{0,1},{1,0},{2,3},{3,2},{4,5},{5,4},{6,7},{7,6},{8,9},{9,8},{10,11... | collective-permute-start | bytes 786440 | tf_op jit(solution)/shard_map/ppermute | solution.py:214
  15.1 7.5 %collective-permute-start.3 = (bf16[2,2,32,1024]{3,2,1,0:T(8,128)(2,1)S(1)}, bf16[2,2,32,1024]{3,2,1,0:T(8,128)(2,1)S(1)}, u32[]{:S(2)}, u32[]{:S(2)}) collective-permute-start(bf16[2,2,32,1024]{3,2,1,0:T(8,128)(2,1)S(1)} %get-tuple-element.36), channel_id=1, source_target_pairs={{0,2},{1,3},{2,0},{3,1},{4,6},{5,7},{6,4},{7,5},{8,10},{9,11},{10,... | collective-permute-start | bytes 786440 | tf_op jit(solution)/shard_map/ppermute | solution.py:214
  20.9 3.9 %collective-permute-start.8 = (bf16[128,1024]{1,0:T(8,128)(2,1)S(1)}, bf16[128,1024]{1,0:T(8,128)(2,1)S(1)}, u32[]{:S(2)}, u32[]{:S(2)}) collective-permute-start(bf16[128,1024]{1,0:T(8,128)(2,1)S(1)} %collective-permute-done.7.got), channel_id=1, source_target_pairs={{0,4},{4,0},{8,12},{12,8},{16,20},{20,16},{24,28},{28,24},{1,5},{5... | collective-permute-start | bytes 786440 | tf_op jit(solution)/shard_map/ppermute | solution.py:214
  22.7 7.5 %collective-permute-start.4 = (bf16[80,1024]{1,0:T(8,128)(2,1)S(1)}, bf16[80,1024]{1,0:T(8,128)(2,1)S(1)}, u32[]{:S(2)}, u32[]{:S(2)}) collective-permute-start(bf16[80,1024]{1,0:T(8,128)(2,1)S(1)} %get-tuple-element.38), channel_id=1, source_target_pairs={{0,1},{1,0},{2,3},{3,2},{4,5},{5,4},{6,7},{7,6},{8,9},{9,8},{10,11... | collective-permute-start | bytes 491528 | tf_op jit(solution)/shard_map/ppermute | solution.py:214
  23.3 6.9 %collective-permute-start.5 = (bf16[80,1024]{1,0:T(8,128)(2,1)S(1)}, bf16[80,1024]{1,0:T(8,128)(2,1)S(1)}, u32[]{:S(2)}, u32[]{:S(2)}) collective-permute-start(bf16[80,1024]{1,0:T(8,128)(2,1)S(1)} %get-tuple-element.39), channel_id=1, source_target_pairs={{0,2},{1,3},{2,0},{3,1},{4,6},{5,7},{6,4},{7,5},{8,10},{9,11},{10,... | collective-permute-start | bytes 491528 | tf_op jit(solution)/shard_map/ppermute | solution.py:214
  25.6 4.6 %collective-permute-start.9 = (bf16[64,1024]{1,0:T(8,128)(2,1)S(1)}, bf16[64,1024]{1,0:T(8,128)(2,1)S(1)}, u32[]{:S(2)}, u32[]{:S(2)}) collective-permute-start(bf16[64,1024]{1,0:T(8,128)(2,1)S(1)} %get-tuple-element.43), channel_id=1, source_target_pairs={{0,4},{4,0},{8,12},{12,8},{16,20},{20,16},{24,28},{28,24},{1,5},{5... | collective-permute-start | bytes 393224 | tf_op jit(solution)/shard_map/ppermute | solution.py:214
  25.7 4.5 %collective-permute-start.10 = (bf16[256,128]{1,0:T(8,128)(2,1)S(1)}, bf16[256,128]{1,0:T(8,128)(2,1)S(1)}, u32[]{:S(2)}, u32[]{:S(2)}) collective-permute-start(bf16[256,128]{1,0:T(8,128)(2,1)S(1)} %get-tuple-element.41._), channel_id=1, source_target_pairs={{0,8},{4,12},{8,0},{12,4},{16,24},{20,28},{24,16},{28,20},{1,9},{5... | collective-permute-start | bytes 196616 | tf_op jit(solution)/shard_map/ppermute | solution.py:214
  30.4 4.5 %collective-permute-start.14 = (bf16[64,1024]{1,0:T(8,128)(2,1)S(1)}, bf16[64,1024]{1,0:T(8,128)(2,1)S(1)}, u32[]{:S(2)}, u32[]{:S(2)}) collective-permute-start(bf16[64,1024]{1,0:T(8,128)(2,1)S(1)} %get-tuple-element.54), channel_id=1, source_target_pairs={{0,4},{4,0},{8,12},{12,8},{16,20},{20,16},{24,28},{28,24},{1,5},{5... | collective-permute-start | bytes 393224 | tf_op jit(solution)/shard_map/ppermute | solution.py:214
  30.5 12.8 %collective-permute-start.11 = (bf16[96,1024]{1,0:T(8,128)(2,1)S(1)}, bf16[96,1024]{1,0:T(8,128)(2,1)S(1)}, u32[]{:S(2)}, u32[]{:S(2)}) collective-permute-start(bf16[96,1024]{1,0:T(8,128)(2,1)S(1)} %get-tuple-element.46), channel_id=1, source_target_pairs={{0,8},{4,12},{8,0},{12,4},{16,24},{20,28},{24,16},{28,20},{1,9},{5... | collective-permute-start | bytes 589832 | tf_op jit(solution)/shard_map/ppermute | solution.py:214
  31.0 7.1 %collective-permute-start.12 = (bf16[32,1024]{1,0:T(8,128)(2,1)S(1)}, bf16[32,1024]{1,0:T(8,128)(2,1)S(1)}, u32[]{:S(2)}, u32[]{:S(2)}) collective-permute-start(bf16[32,1024]{1,0:T(8,128)(2,1)S(1)} %get-tuple-element.47), channel_id=1, source_target_pairs={{0,16},{4,20},{8,24},{12,28},{16,0},{20,4},{24,8},{28,12},{1,17},{... | collective-permute-start | bytes 196616 | tf_op jit(solution)/shard_map/ppermute | solution.py:214
  33.6 7.7 %collective-permute-start.13 = (bf16[32,1024]{1,0:T(8,128)(2,1)S(1)}, bf16[32,1024]{1,0:T(8,128)(2,1)S(1)}, u32[]{:S(2)}, u32[]{:S(2)}) collective-permute-start(bf16[32,1024]{1,0:T(8,128)(2,1)S(1)} %get-tuple-element.48), channel_id=1, source_target_pairs={{0,24},{4,28},{8,16},{12,20},{16,8},{20,12},{24,0},{28,4},{1,25},{... | collective-permute-start | bytes 196616 | tf_op jit(solution)/shard_map/ppermute | solution.py:214
  35.0 6.3 %collective-permute-start.15 = (bf16[32,1024]{1,0:T(8,128)(2,1)S(1)}, bf16[32,1024]{1,0:T(8,128)(2,1)S(1)}, u32[]{:S(2)}, u32[]{:S(2)}) collective-permute-start(bf16[32,1024]{1,0:T(8,128)(2,1)S(1)} %get-tuple-element.56), channel_id=1, source_target_pairs={{0,1},{1,0},{2,3},{3,2},{4,5},{5,4},{6,7},{7,6},{8,9},{9,8},{10,11... | collective-permute-start | bytes 196616 | tf_op jit(solution)/shard_map/ppermute | solution.py:214
  36.6 5.0 %collective-permute-start.16 = (bf16[32,1024]{1,0:T(8,128)(2,1)S(1)}, bf16[32,1024]{1,0:T(8,128)(2,1)S(1)}, u32[]{:S(2)}, u32[]{:S(2)}) collective-permute-start(bf16[32,1024]{1,0:T(8,128)(2,1)S(1)} %get-tuple-element.57), channel_id=1, source_target_pairs={{0,2},{1,3},{2,0},{3,1},{4,6},{5,7},{6,4},{7,5},{8,10},{9,11},{10,... | collective-permute-start | bytes 196616 | tf_op jit(solution)/shard_map/ppermute | solution.py:214
  38.1 5.2 %collective-permute-start.17 = (bf16[32,1024]{1,0:T(8,128)(2,1)S(1)}, bf16[32,1024]{1,0:T(8,128)(2,1)S(1)}, u32[]{:S(2)}, u32[]{:S(2)}) collective-permute-start(bf16[32,1024]{1,0:T(8,128)(2,1)S(1)} %get-tuple-element.58), channel_id=1, source_target_pairs={{0,3},{1,2},{2,1},{3,0},{4,7},{5,6},{6,5},{7,4},{8,11},{9,10},{10,... | collective-permute-start | bytes 196616 | tf_op jit(solution)/shard_map/ppermute | solution.py:214

commit v8 on v7

--- a/solution.py
+++ b/solution.py
@@ -117,7 +117,7 @@
 
 
 def slab_kernel(sum_ref, from1_ref, from2_ref, mine_ref, came_ref, *refs):
-    *outs, part_ref, rows_ref = refs[1:]
+    *outs, part_ref, rows_ref = refs
     half, height = sum_ref.shape[0] // 2, sum_ref.shape[1]
     count = half * height
     part = part_ref.shape[0]
@@ -179,7 +179,7 @@
 
 
 def place_kernel(mine, came, *outs):
-    *outs, rows_ref = outs
+    _, *outs, rows_ref = outs
     owned, wide = mine.shape
     half = owned // 2
     for t in range(wide // owned):
@@ -195,19 +195,28 @@
         out[...] = rows_ref[pl.ds(at, height)].astype(out.dtype)
 
 
-def last_kernel(scales, count, mine, *refs):
-    parts, outs = refs[: 2 * count], refs[2 * count :]
-    for i, scale in enumerate(scales):
-        total = parts[i * count][...]
-        for part in parts[i * count + 1 : (i + 1) * count]:
-            total = total + part[: total.shape[0]].astype(F32)
-        outs[i][...] = total * scale
-    slices, part, rank = outs[2].shape
-    height = parts[0].shape[0]
+def one_kernel(scale, mine, *refs):
+    *parts, one_ref, reduced_ref, done_ref = refs
+    done_ref[...] = jnp.zeros_like(done_ref)
+    second = parts[1]
+    total = parts[0][...]
+    height = total.shape[0]
+    for part in parts[1:]:
+        total = total + part[:height].astype(F32)
+    one_ref[...] = total * scale
+    slices, part, rank = reduced_ref.shape
     for k in range(slices):
         at = slice(k * rank, (k + 1) * rank)
-        came = parts[1][height : height + part, at].astype(F32) + parts[1][height + part :, at].astype(F32)
-        outs[2][k] = mine[:, at] + came
+        came = second[height : height + part, at].astype(F32) + second[height + part :, at].astype(F32)
+        reduced_ref[k] = mine[:, at] + came
+
+
+def two_kernel(scale, count, *refs):
+    parts, out_ref = refs[:count], refs[-1]
+    total = parts[0][...]
+    for part in parts[1:]:
+        total = total + part[...].astype(F32)
+    out_ref[...] = total * scale
 
 
 def xor_permute(x, axis, bits):
@@ -322,13 +331,12 @@
             for t in range(count_z)
         ]
         + [((part, columns), F32)],
-        [VMEM] * 5 + [ANY],
+        [VMEM] * 5,
         total,
         from1,
         from2,
         mine_part,
         xor_permute(other_part, "ja", 1),
-        crossed,
         scratch=[pltpu.VMEM(shape, F32)],
     )
     sums = list(sums)
@@ -350,23 +358,33 @@
         place_kernel,
         "two_place",
         [(final, F32 if t == 0 else BF16) for t in range(count_ka)],
-        [VMEM] * 2,
+        [VMEM] * 2 + [ANY],
         mine,
         other,
+        sums[1],
         scratch=[pltpu.VMEM((owned, count_ja * owned), F32)],
     )
     rows = list(rows)
     for t in range(1, count_ka):
         rows[t] = xor_permute(rows[t], "ka", t)
-    return call(
-        functools.partial(last_kernel, (norm_one, norm_two), count_z),
-        "last",
-        [((height, width), F32), (final, F32), ((slices, part, rank_one), F32)],
-        [VMEM] * (1 + count_z + count_ka),
+    gram_one, reduced, done = call(
+        functools.partial(one_kernel, norm_one),
+        "one",
+        [((height, width), F32), ((slices, part, rank_one), F32), ((8, 128), F32)],
+        [VMEM] * (1 + count_z),
         mine_part,
         *sums,
+        flops=0,
+    )
+    (gram_two,) = call(
+        functools.partial(two_kernel, norm_two, count_ka),
+        "two",
+        [(final, F32)],
+        [VMEM] * count_ka + [ANY],
         *rows,
-    )
+        done,
+    )
+    return gram_one, gram_two, reduced
 
 
 def plain_shards(tensor, factor_one, factor_two):

time: 44.2 us -> 43.9 us (level)
  starting transfers between devices: 21.4 us -> 19.6 us
  waiting for transfers between devices: 12.9 us -> 13.7 us
  Pallas kernels: 7.38 us -> 8.02 us
    ppermute x18, starting transfers between devices: 21.4 us -> 19.6 us  [xor_permute(): lax.ppermute(x, axis, [(i, i ^ bits) for i in range(lax.axis_size(axis))])]
    ppermute x18, waiting for transfers between devices: 12.9 us -> 13.7 us  [xor_permute(): lax.ppermute(x, axis, [(i, i ^ bits) for i in range(lax.axis_size(axis))])]
    pallas_call x11 -> x12, Pallas kernels: 7.38 us -> 8.02 us  [call(): pl.pallas_call(kernel, out_shape=[jax.ShapeDtypeStruct(s, d) for s, d in...]
  transfers between devices with their start and end apart: 18 -> 18, of which waited for: 7 -> 10; matrix products, arithmetic and copies ran while one was open for 0% -> 0% of each run, Pallas kernels for 10% -> 12%
where the time goes in v8:
time: 43.9 us; the launch traced here: 43.7 us
  starting transfers between devices  19.6 us (45%)
  waiting for transfers between devices  13.7 us (31%)
  Pallas kernels  8.02 us (18%)
  local copies, waits for them, and re-layouts  1.6 us (4%)
  between operations  0.76 us (2%)
    ppermute x18, starting transfers between devices, xor_permute(): lax.ppermute(x, axis, [(i, i ^ bits) for i in range(lax.axis_size(axis))])  19.6 us
    ppermute x18, waiting for transfers between devices, xor_permute(): lax.ppermute(x, axis, [(i, i ^ bits) for i in range(lax.axis_size(axis))])  13.7 us
    pallas_call x12, Pallas kernels, call(): pl.pallas_call(kernel, out_shape=[jax.ShapeDtypeStruct(s, d) for s, d in...  8.02 us
    unnamed x8, local copies, waits for them, and re-layouts  1.6 us
  transfers between devices with their start and end apart: 18, of which 10 were waited for; matrix products, arithmetic and copies ran while one was open for 0% of the time, Pallas kernels for 12%

profile of v8, /device:TPU:0, one launch (start us, length us, event | category | flops | bytes accessed | tf_op | source)
XLA Modules:
  0.0 43.7 jit_solution(1914180832522427688)
XLA Ops:
  0.6 0.0 copy-start
  0.6 1.6 %copy-done = f32[4,128,1024]{2,1,0:T(8,128)S(1)} copy-done((f32[4,128,1024]{2,1,0:T(8,128)S(1)}, f32[4,128,1024]{2,1,0:T(8,128)}, u32[]{:S(2)}) %copy-start) | copy-done | bytes 2097176
  2.2 1.9 %away.1._ = bf16[4,128,1024]{2,1,0:T(8,128)(2,1)S(1)} custom-call(f32[4,128,1024]{2,1,0:T(8,128)S(1)} %copy-done), custom_call_target="tpu_custom_call" | custom-call | tf_op jit(solution)/shard_map/away/pallas_call | solution.py:34
  4.1 0.0 copy-start.1
  4.1 0.5 %collective-permute-start = (bf16[4,128,1024]{2,1,0:T(8,128)(2,1)S(1)}, bf16[4,128,1024]{2,1,0:T(8,128)(2,1)S(1)}, u32[]{:S(2)}, u32[]{:S(2)}) collective-permute-start(bf16[4,128,1024]{2,1,0:T(8,128)(2,1)S(1)} %away.1._), channel_id=1, source_target_pairs={{0,4},{4,0},{8,12},{12,8},{16,20},{20,16},{24,28},{28,24},{1,5},{5... | collective-permute-start | bytes 3145736 | tf_op jit(solution)/shard_map/ppermute | solution.py:223
  4.6 1.0 %core.1 = (bf16[128,1024]{1,0:T(8,128)(2,1)S(1)}, bf16[144,1024]{1,0:T(8,128)(2,1)S(1)}) custom-call(f32[4,128,1024]{2,1,0:T(8,128)S(1)} %copy-done, f32[1024,256]{1,0:T(8,128)S(1)} %copy-done.2, bf16[128,256]{1,0:T(8,128)(2,1)S(1)} %copy-done.3, bf16[4,128,1024]{2,1,0:T(8,128)(2,1)S(1)} %away.1._), custom_call_target="tpu_custom_call" | custom-call | tf_op jit(solution)/shard_map/core/pallas_call | solution.py:34
  5.6 0.1 collective-permute-start.1
  5.8 3.0 %collective-permute-start.7 = (bf16[128,1024]{1,0:T(8,128)(2,1)S(1)}, bf16[128,1024]{1,0:T(8,128)(2,1)S(1)}, u32[]{:S(2)}, u32[]{:S(2)}) collective-permute-start(bf16[128,1024]{1,0:T(8,128)(2,1)S(1)} %get-tuple-element.34.u), channel_id=1, source_target_pairs={{0,8},{4,12},{8,0},{12,4},{16,24},{20,28},{24,16},{28,20},{1,9},{5... | collective-permute-start | bytes 786440 | tf_op jit(solution)/shard_map/ppermute | solution.py:223
  8.8 2.6 %collective-permute-start.6 = (bf16[144,1024]{1,0:T(8,128)(2,1)S(1)}, bf16[144,1024]{1,0:T(8,128)(2,1)S(1)}, u32[]{:S(2)}, u32[]{:S(2)}) collective-permute-start(bf16[144,1024]{1,0:T(8,128)(2,1)S(1)} %get-tuple-element.43), channel_id=1, source_target_pairs={{0,16},{4,20},{8,24},{12,28},{16,0},{20,4},{24,8},{28,12},{1,17},{... | collective-permute-start | bytes 884744 | tf_op jit(solution)/shard_map/ppermute | solution.py:223
  11.4 0.0 collective-permute-done.1._.paired
  11.4 0.0 collective-permute-done.came_ref
  11.4 2.1 %home.1 = (f32[4,32,1024]{2,1,0:T(8,128)S(1)}, f32[2,32,1024]{2,1,0:T(8,128)S(1)}, f32[2,32,1024]{2,1,0:T(8,128)S(1)}, bf16[2,2,32,1024]{3,2,1,0:T(8,128)(2,1)S(1)}, bf16[2,2,32,1024]{3,2,1,0:T(8,128)(2,1)S(1)}) custom-call(f32[4,128,1024]{2,1,0:T(8,128)S(1)} %copy-done.1, bf16[4,128,1024]{2,1,0:T(8,128)(2,1)S(1)} %collective-permute-done.came_ref, ...), custom_call_target="tpu_custom_call" | custom-call | tf_op jit(solution)/shard_map/home/pallas_call | solution.py:34
  13.6 1.6 %collective-permute-start.2 = (bf16[2,2,32,1024]{3,2,1,0:T(8,128)(2,1)S(1)}, bf16[2,2,32,1024]{3,2,1,0:T(8,128)(2,1)S(1)}, u32[]{:S(2)}, u32[]{:S(2)}) collective-permute-start(bf16[2,2,32,1024]{3,2,1,0:T(8,128)(2,1)S(1)} %get-tuple-element.38), channel_id=1, source_target_pairs={{0,1},{1,0},{2,3},{3,2},{4,5},{5,4},{6,7},{7,6},{8,9},{9,8},{10,11... | collective-permute-start | bytes 786440 | tf_op jit(solution)/shard_map/ppermute | solution.py:223
  15.1 1.5 %collective-permute-start.3 = (bf16[2,2,32,1024]{3,2,1,0:T(8,128)(2,1)S(1)}, bf16[2,2,32,1024]{3,2,1,0:T(8,128)(2,1)S(1)}, u32[]{:S(2)}, u32[]{:S(2)}) collective-permute-start(bf16[2,2,32,1024]{3,2,1,0:T(8,128)(2,1)S(1)} %get-tuple-element.39), channel_id=1, source_target_pairs={{0,2},{1,3},{2,0},{3,1},{4,6},{5,7},{6,4},{7,5},{8,10},{9,11},{10,... | collective-permute-start | bytes 786440 | tf_op jit(solution)/shard_map/ppermute | solution.py:223
  16.6 4.2 %collective-permute-done.7.got = bf16[128,1024]{1,0:T(8,128)(2,1)S(1)} collective-permute-done((bf16[128,1024]{1,0:T(8,128)(2,1)S(1)}, bf16[128,1024]{1,0:T(8,128)(2,1)S(1)}, u32[]{:S(2)}, u32[]{:S(2)}) %collective-permute-start.7) | collective-permute-done | bytes 262176 | tf_op jit(solution)/shard_map/ppermute | solution.py:223
  20.9 0.0 collective-permute-start.8
  20.9 0.5 %collective-permute-done.2.from1_ref = bf16[2,2,32,1024]{3,2,1,0:T(8,128)(2,1)S(1)} collective-permute-done((bf16[2,2,32,1024]{3,2,1,0:T(8,128)(2,1)S(1)}, bf16[2,2,32,1024]{3,2,1,0:T(8,128)(2,1)S(1)}, u32[]{:S(2)}, u32[]{:S(2)}) %collective-permute-start.2) | collective-permute-done | bytes 262176 | tf_op jit(solution)/shard_map/ppermute | solution.py:223
  21.4 1.2 %collective-permute-done.3.from2_ref = bf16[2,2,32,1024]{3,2,1,0:T(8,128)(2,1)S(1)} collective-permute-done((bf16[2,2,32,1024]{3,2,1,0:T(8,128)(2,1)S(1)}, bf16[2,2,32,1024]{3,2,1,0:T(8,128)(2,1)S(1)}, u32[]{:S(2)}, u32[]{:S(2)}) %collective-permute-start.3) | collective-permute-done | bytes 262176 | tf_op jit(solution)/shard_map/ppermute | solution.py:223
  22.6 0.1 middle.1
  22.7 0.6 %collective-permute-start.4 = (bf16[80,1024]{1,0:T(8,128)(2,1)S(1)}, bf16[80,1024]{1,0:T(8,128)(2,1)S(1)}, u32[]{:S(2)}, u32[]{:S(2)}) collective-permute-start(bf16[80,1024]{1,0:T(8,128)(2,1)S(1)} %get-tuple-element.41), channel_id=1, source_target_pairs={{0,1},{1,0},{2,3},{3,2},{4,5},{5,4},{6,7},{7,6},{8,9},{9,8},{10,11... | collective-permute-start | bytes 491528 | tf_op jit(solution)/shard_map/ppermute | solution.py:223
  23.3 1.5 %collective-permute-start.5 = (bf16[80,1024]{1,0:T(8,128)(2,1)S(1)}, bf16[80,1024]{1,0:T(8,128)(2,1)S(1)}, u32[]{:S(2)}, u32[]{:S(2)}) collective-permute-start(bf16[80,1024]{1,0:T(8,128)(2,1)S(1)} %get-tuple-element.42), channel_id=1, source_target_pairs={{0,2},{1,3},{2,0},{3,1},{4,6},{5,7},{6,4},{7,5},{8,10},{9,11},{10,... | collective-permute-start | bytes 491528 | tf_op jit(solution)/shard_map/ppermute | solution.py:223
  24.8 0.0 collective-permute-done.6.far
  24.8 0.0 collective-permute-done.8.got_paired
  24.8 0.4 two_cross.1
  25.2 0.4 parts.1
  25.6 0.1 collective-permute-start.9
  25.7 0.5 %collective-permute-start.13 = (bf16[256,128]{1,0:T(8,128)(2,1)S(1)}, bf16[256,128]{1,0:T(8,128)(2,1)S(1)}, u32[]{:S(2)}, u32[]{:S(2)}) collective-permute-start(bf16[256,128]{1,0:T(8,128)(2,1)S(1)} %get-tuple-element.44._), channel_id=1, source_target_pairs={{0,8},{4,12},{8,0},{12,4},{16,24},{20,28},{24,16},{28,20},{1,9},{5... | collective-permute-start | bytes 196616 | tf_op jit(solution)/shard_map/ppermute | solution.py:223
  26.2 0.8 %collective-permute-done.9.came_ref = bf16[64,1024]{1,0:T(8,128)(2,1)S(1)} collective-permute-done((bf16[64,1024]{1,0:T(8,128)(2,1)S(1)}, bf16[64,1024]{1,0:T(8,128)(2,1)S(1)}, u32[]{:S(2)}, u32[]{:S(2)}) %collective-permute-start.9) | collective-permute-done | bytes 131104 | tf_op jit(solution)/shard_map/ppermute | solution.py:223
  27.0 1.0 %collective-permute-done.4.from1_ref = bf16[80,1024]{1,0:T(8,128)(2,1)S(1)} collective-permute-done((bf16[80,1024]{1,0:T(8,128)(2,1)S(1)}, bf16[80,1024]{1,0:T(8,128)(2,1)S(1)}, u32[]{:S(2)}, u32[]{:S(2)}) %collective-permute-start.4) | collective-permute-done | bytes 163872 | tf_op jit(solution)/shard_map/ppermute | solution.py:223
  28.1 1.0 %collective-permute-done.5.from2_ref = bf16[80,1024]{1,0:T(8,128)(2,1)S(1)} collective-permute-done((bf16[80,1024]{1,0:T(8,128)(2,1)S(1)}, bf16[80,1024]{1,0:T(8,128)(2,1)S(1)}, u32[]{:S(2)}, u32[]{:S(2)}) %collective-permute-start.5) | collective-permute-done | bytes 163872 | tf_op jit(solution)/shard_map/ppermute | solution.py:223
  29.0 0.1 slab.1
  29.1 0.1 collective-permute-start.10
  29.2 0.4 two_near.1
  29.7 0.5 %collective-permute-done.13.came = bf16[256,128]{1,0:T(8,128)(2,1)S(1)} collective-permute-done((bf16[256,128]{1,0:T(8,128)(2,1)S(1)}, bf16[256,128]{1,0:T(8,128)(2,1)S(1)}, u32[]{:S(2)}, u32[]{:S(2)}) %collective-permute-start.13) | collective-permute-done | bytes 65568 | tf_op jit(solution)/shard_map/ppermute | solution.py:223
  30.2 0.1 collective-permute-start.14
  30.3 2.6 %collective-permute-start.11 = (bf16[32,1024]{1,0:T(8,128)(2,1)S(1)}, bf16[32,1024]{1,0:T(8,128)(2,1)S(1)}, u32[]{:S(2)}, u32[]{:S(2)}) collective-permute-start(bf16[32,1024]{1,0:T(8,128)(2,1)S(1)} %get-tuple-element.50), channel_id=1, source_target_pairs={{0,16},{4,20},{8,24},{12,28},{16,0},{20,4},{24,8},{28,12},{1,17},{... | collective-permute-start | bytes 196616 | tf_op jit(solution)/shard_map/ppermute | solution.py:223
  32.9 1.3 %collective-permute-start.12 = (bf16[32,1024]{1,0:T(8,128)(2,1)S(1)}, bf16[32,1024]{1,0:T(8,128)(2,1)S(1)}, u32[]{:S(2)}, u32[]{:S(2)}) collective-permute-start(bf16[32,1024]{1,0:T(8,128)(2,1)S(1)} %get-tuple-element.51), channel_id=1, source_target_pairs={{0,24},{4,28},{8,16},{12,20},{16,8},{20,12},{24,0},{28,4},{1,25},{... | collective-permute-start | bytes 196616 | tf_op jit(solution)/shard_map/ppermute | solution.py:223
  34.2 1.8 %collective-permute-done.10.refs_1_.outs_0_ = bf16[96,1024]{1,0:T(8,128)(2,1)S(1)} collective-permute-done((bf16[96,1024]{1,0:T(8,128)(2,1)S(1)}, bf16[96,1024]{1,0:T(8,128)(2,1)S(1)}, u32[]{:S(2)}, u32[]{:S(2)}) %collective-permute-start.10) | collective-permute-done | bytes 196640 | tf_op jit(solution)/shard_map/ppermute | solution.py:223
  36.1 0.1 two_place.1
  36.2 0.1 collective-permute-start.15
  36.2 1.6 %collective-permute-start.16 = (bf16[32,1024]{1,0:T(8,128)(2,1)S(1)}, bf16[32,1024]{1,0:T(8,128)(2,1)S(1)}, u32[]{:S(2)}, u32[]{:S(2)}) collective-permute-start(bf16[32,1024]{1,0:T(8,128)(2,1)S(1)} %get-tuple-element.61), channel_id=1, source_target_pairs={{0,2},{1,3},{2,0},{3,1},{4,6},{5,7},{6,4},{7,5},{8,10},{9,11},{10,... | collective-permute-start | bytes 196616 | tf_op jit(solution)/shard_map/ppermute | solution.py:223
  37.8 1.9 %collective-permute-start.17 = (bf16[32,1024]{1,0:T(8,128)(2,1)S(1)}, bf16[32,1024]{1,0:T(8,128)(2,1)S(1)}, u32[]{:S(2)}, u32[]{:S(2)}) collective-permute-start(bf16[32,1024]{1,0:T(8,128)(2,1)S(1)} %get-tuple-element.62), channel_id=1, source_target_pairs={{0,3},{1,2},{2,1},{3,0},{4,7},{5,6},{6,5},{7,4},{8,11},{9,10},{10,... | collective-permute-start | bytes 196616 | tf_op jit(solution)/shard_map/ppermute | solution.py:223
  39.7 0.0 collective-permute-done.12.refs_3_
  39.7 0.7 %one.1 = (f32[32,1024]{1,0:T(8,128)}, f32[4,32,256]{2,1,0:T(8,128)}, f32[8,128]{1,0:T(8,128)S(1)}) custom-call(f32[32,1024]{1,0:T(8,128)S(1)} %get-tuple-element.47.mine, f32[32,1024]{1,0:T(8,128)S(1)} %get-tuple-element.48.refs_0_._, bf16[96,1024]{1,0:T(8,128)(2,1)S(1)} %collective-permute-done.10.refs_1_.outs_0_, ...), custom_call_target="tpu_custom_call" | custom-call | tf_op jit(solution)/shard_map/one/pallas_call | solution.py:34
  40.5 0.0 collective-permute-done.15.refs_1_
  40.5 0.7 %collective-permute-done.16.refs_2_ = bf16[32,1024]{1,0:T(8,128)(2,1)S(1)} collective-permute-done((bf16[32,1024]{1,0:T(8,128)(2,1)S(1)}, bf16[32,1024]{1,0:T(8,128)(2,1)S(1)}, u32[]{:S(2)}, u32[]{:S(2)}) %collective-permute-start.16) | collective-permute-done | bytes 65568 | tf_op jit(solution)/shard_map/ppermute | solution.py:223
  41.2 1.8 %collective-permute-done.17.refs_3_ = bf16[32,1024]{1,0:T(8,128)(2,1)S(1)} collective-permute-done((bf16[32,1024]{1,0:T(8,128)(2,1)S(1)}, bf16[32,1024]{1,0:T(8,128)(2,1)S(1)}, u32[]{:S(2)}, u32[]{:S(2)}) %collective-permute-start.17) | collective-permute-done | bytes 65568 | tf_op jit(solution)/shard_map/ppermute | solution.py:223
  43.0 0.7 %two.1 = f32[32,1024]{1,0:T(8,128)} custom-call(f32[32,1024]{1,0:T(8,128)S(1)} %get-tuple-element.59.refs_0_, bf16[32,1024]{1,0:T(8,128)(2,1)S(1)} %collective-permute-done.15.refs_1_, bf16[32,1024]{1,0:T(8,128)(2,1)S(1)} %collective-permute-done.16.refs_2_, bf16[32,1024]{1,0:T(8,128)(2,1)S(1)} %collective-permute-done.17.refs_3_, ...), custom_call_target="tpu_custom_call" | custom-call | tf_op jit(solution)/shard_map/two/pallas_call | solution.py:34
  (8 shorter events, 0.0 us)
Async XLA Ops:
  0.6 1.6 %copy-start = (f32[4,128,1024]{2,1,0:T(8,128)S(1)}, f32[4,128,1024]{2,1,0:T(8,128)}, u32[]{:S(2)}) copy-start(f32[4,128,1024]{2,1,0:T(8,128)} %x_ref.5) | copy-start | bytes 6291460
  2.2 2.4 %copy-start.2 = (f32[1024,256]{1,0:T(8,128)S(1)}, f32[1024,256]{1,0:T(8,128)}, u32[]{:S(2)}) copy-start(f32[1024,256]{1,0:T(8,128)} %f_ref.1) | copy-start | bytes 3145732
  2.2 2.4 %copy-start.3 = (bf16[128,256]{1,0:T(8,128)(2,1)S(1)}, bf16[128,256]{1,0:T(8,128)(2,1)}, u32[]{:S(2)}) copy-start(bf16[128,256]{1,0:T(8,128)(2,1)} %two_ref.3) | copy-start | bytes 196612
  4.1 7.3 %copy-start.1 = (f32[4,128,1024]{2,1,0:T(8,128)S(1)}, f32[4,128,1024]{2,1,0:T(8,128)}, u32[]{:S(2)}) copy-start(f32[4,128,1024]{2,1,0:T(8,128)} %x_ref.5) | copy-start | bytes 6291460
  4.1 7.3 %collective-permute-start = (bf16[4,128,1024]{2,1,0:T(8,128)(2,1)S(1)}, bf16[4,128,1024]{2,1,0:T(8,128)(2,1)S(1)}, u32[]{:S(2)}, u32[]{:S(2)}) collective-permute-start(bf16[4,128,1024]{2,1,0:T(8,128)(2,1)S(1)} %away.1._), channel_id=1, source_target_pairs={{0,4},{4,0},{8,12},{12,8},{16,20},{20,16},{24,28},{28,24},{1,5},{5... | collective-permute-start | bytes 3145736 | tf_op jit(solution)/shard_map/ppermute | solution.py:223
  5.6 5.8 %collective-permute-start.1 = (bf16[128,1024]{1,0:T(8,128)(2,1)S(1)}, bf16[128,1024]{1,0:T(8,128)(2,1)S(1)}, u32[]{:S(2)}, u32[]{:S(2)}) collective-permute-start(bf16[128,1024]{1,0:T(8,128)(2,1)S(1)} %get-tuple-element.34.u), channel_id=1, source_target_pairs={{0,4},{4,0},{8,12},{12,8},{16,20},{20,16},{24,28},{28,24},{1,5},{5... | collective-permute-start | bytes 786440 | tf_op jit(solution)/shard_map/ppermute | solution.py:223
  5.8 15.1 %collective-permute-start.7 = (bf16[128,1024]{1,0:T(8,128)(2,1)S(1)}, bf16[128,1024]{1,0:T(8,128)(2,1)S(1)}, u32[]{:S(2)}, u32[]{:S(2)}) collective-permute-start(bf16[128,1024]{1,0:T(8,128)(2,1)S(1)} %get-tuple-element.34.u), channel_id=1, source_target_pairs={{0,8},{4,12},{8,0},{12,4},{16,24},{20,28},{24,16},{28,20},{1,9},{5... | collective-permute-start | bytes 786440 | tf_op jit(solution)/shard_map/ppermute | solution.py:223
  8.8 16.0 %collective-permute-start.6 = (bf16[144,1024]{1,0:T(8,128)(2,1)S(1)}, bf16[144,1024]{1,0:T(8,128)(2,1)S(1)}, u32[]{:S(2)}, u32[]{:S(2)}) collective-permute-start(bf16[144,1024]{1,0:T(8,128)(2,1)S(1)} %get-tuple-element.43), channel_id=1, source_target_pairs={{0,16},{4,20},{8,24},{12,28},{16,0},{20,4},{24,8},{28,12},{1,17},{... | collective-permute-start | bytes 884744 | tf_op jit(solution)/shard_map/ppermute | solution.py:223
  13.6 7.8 %collective-permute-start.2 = (bf16[2,2,32,1024]{3,2,1,0:T(8,128)(2,1)S(1)}, bf16[2,2,32,1024]{3,2,1,0:T(8,128)(2,1)S(1)}, u32[]{:S(2)}, u32[]{:S(2)}) collective-permute-start(bf16[2,2,32,1024]{3,2,1,0:T(8,128)(2,1)S(1)} %get-tuple-element.38), channel_id=1, source_target_pairs={{0,1},{1,0},{2,3},{3,2},{4,5},{5,4},{6,7},{7,6},{8,9},{9,8},{10,11... | collective-permute-start | bytes 786440 | tf_op jit(solution)/shard_map/ppermute | solution.py:223
  15.1 7.5 %collective-permute-start.3 = (bf16[2,2,32,1024]{3,2,1,0:T(8,128)(2,1)S(1)}, bf16[2,2,32,1024]{3,2,1,0:T(8,128)(2,1)S(1)}, u32[]{:S(2)}, u32[]{:S(2)}) collective-permute-start(bf16[2,2,32,1024]{3,2,1,0:T(8,128)(2,1)S(1)} %get-tuple-element.39), channel_id=1, source_target_pairs={{0,2},{1,3},{2,0},{3,1},{4,6},{5,7},{6,4},{7,5},{8,10},{9,11},{10,... | collective-permute-start | bytes 786440 | tf_op jit(solution)/shard_map/ppermute | solution.py:223
  20.9 3.9 %collective-permute-start.8 = (bf16[128,1024]{1,0:T(8,128)(2,1)S(1)}, bf16[128,1024]{1,0:T(8,128)(2,1)S(1)}, u32[]{:S(2)}, u32[]{:S(2)}) collective-permute-start(bf16[128,1024]{1,0:T(8,128)(2,1)S(1)} %collective-permute-done.7.got), channel_id=1, source_target_pairs={{0,4},{4,0},{8,12},{12,8},{16,20},{20,16},{24,28},{28,24},{1,5},{5... | collective-permute-start | bytes 786440 | tf_op jit(solution)/shard_map/ppermute | solution.py:223
  22.7 5.4 %collective-permute-start.4 = (bf16[80,1024]{1,0:T(8,128)(2,1)S(1)}, bf16[80,1024]{1,0:T(8,128)(2,1)S(1)}, u32[]{:S(2)}, u32[]{:S(2)}) collective-permute-start(bf16[80,1024]{1,0:T(8,128)(2,1)S(1)} %get-tuple-element.41), channel_id=1, source_target_pairs={{0,1},{1,0},{2,3},{3,2},{4,5},{5,4},{6,7},{7,6},{8,9},{9,8},{10,11... | collective-permute-start | bytes 491528 | tf_op jit(solution)/shard_map/ppermute | solution.py:223
  23.3 5.7 %collective-permute-start.5 = (bf16[80,1024]{1,0:T(8,128)(2,1)S(1)}, bf16[80,1024]{1,0:T(8,128)(2,1)S(1)}, u32[]{:S(2)}, u32[]{:S(2)}) collective-permute-start(bf16[80,1024]{1,0:T(8,128)(2,1)S(1)} %get-tuple-element.42), channel_id=1, source_target_pairs={{0,2},{1,3},{2,0},{3,1},{4,6},{5,7},{6,4},{7,5},{8,10},{9,11},{10,... | collective-permute-start | bytes 491528 | tf_op jit(solution)/shard_map/ppermute | solution.py:223
  25.6 1.4 %collective-permute-start.9 = (bf16[64,1024]{1,0:T(8,128)(2,1)S(1)}, bf16[64,1024]{1,0:T(8,128)(2,1)S(1)}, u32[]{:S(2)}, u32[]{:S(2)}) collective-permute-start(bf16[64,1024]{1,0:T(8,128)(2,1)S(1)} %get-tuple-element.46), channel_id=1, source_target_pairs={{0,4},{4,0},{8,12},{12,8},{16,20},{20,16},{24,28},{28,24},{1,5},{5... | collective-permute-start | bytes 393224 | tf_op jit(solution)/shard_map/ppermute | solution.py:223
  25.7 4.5 %collective-permute-start.13 = (bf16[256,128]{1,0:T(8,128)(2,1)S(1)}, bf16[256,128]{1,0:T(8,128)(2,1)S(1)}, u32[]{:S(2)}, u32[]{:S(2)}) collective-permute-start(bf16[256,128]{1,0:T(8,128)(2,1)S(1)} %get-tuple-element.44._), channel_id=1, source_target_pairs={{0,8},{4,12},{8,0},{12,4},{16,24},{20,28},{24,16},{28,20},{1,9},{5... | collective-permute-start | bytes 196616 | tf_op jit(solution)/shard_map/ppermute | solution.py:223
  29.1 6.9 %collective-permute-start.10 = (bf16[96,1024]{1,0:T(8,128)(2,1)S(1)}, bf16[96,1024]{1,0:T(8,128)(2,1)S(1)}, u32[]{:S(2)}, u32[]{:S(2)}) collective-permute-start(bf16[96,1024]{1,0:T(8,128)(2,1)S(1)} %get-tuple-element.49), channel_id=1, source_target_pairs={{0,8},{4,12},{8,0},{12,4},{16,24},{20,28},{24,16},{28,20},{1,9},{5... | collective-permute-start | bytes 589832 | tf_op jit(solution)/shard_map/ppermute | solution.py:223
  30.2 4.0 %collective-permute-start.14 = (bf16[64,1024]{1,0:T(8,128)(2,1)S(1)}, bf16[64,1024]{1,0:T(8,128)(2,1)S(1)}, u32[]{:S(2)}, u32[]{:S(2)}) collective-permute-start(bf16[64,1024]{1,0:T(8,128)(2,1)S(1)} %get-tuple-element.58), channel_id=1, source_target_pairs={{0,4},{4,0},{8,12},{12,8},{16,20},{20,16},{24,28},{28,24},{1,5},{5... | collective-permute-start | bytes 393224 | tf_op jit(solution)/shard_map/ppermute | solution.py:223
  30.3 9.4 %collective-permute-start.11 = (bf16[32,1024]{1,0:T(8,128)(2,1)S(1)}, bf16[32,1024]{1,0:T(8,128)(2,1)S(1)}, u32[]{:S(2)}, u32[]{:S(2)}) collective-permute-start(bf16[32,1024]{1,0:T(8,128)(2,1)S(1)} %get-tuple-element.50), channel_id=1, source_target_pairs={{0,16},{4,20},{8,24},{12,28},{16,0},{20,4},{24,8},{28,12},{1,17},{... | collective-permute-start | bytes 196616 | tf_op jit(solution)/shard_map/ppermute | solution.py:223
  32.9 6.8 %collective-permute-start.12 = (bf16[32,1024]{1,0:T(8,128)(2,1)S(1)}, bf16[32,1024]{1,0:T(8,128)(2,1)S(1)}, u32[]{:S(2)}, u32[]{:S(2)}) collective-permute-start(bf16[32,1024]{1,0:T(8,128)(2,1)S(1)} %get-tuple-element.51), channel_id=1, source_target_pairs={{0,24},{4,28},{8,16},{12,20},{16,8},{20,12},{24,0},{28,4},{1,25},{... | collective-permute-start | bytes 196616 | tf_op jit(solution)/shard_map/ppermute | solution.py:223
  36.2 4.3 %collective-permute-start.15 = (bf16[32,1024]{1,0:T(8,128)(2,1)S(1)}, bf16[32,1024]{1,0:T(8,128)(2,1)S(1)}, u32[]{:S(2)}, u32[]{:S(2)}) collective-permute-start(bf16[32,1024]{1,0:T(8,128)(2,1)S(1)} %get-tuple-element.60), channel_id=1, source_target_pairs={{0,1},{1,0},{2,3},{3,2},{4,5},{5,4},{6,7},{7,6},{8,9},{9,8},{10,11... | collective-permute-start | bytes 196616 | tf_op jit(solution)/shard_map/ppermute | solution.py:223
  36.2 5.0 %collective-permute-start.16 = (bf16[32,1024]{1,0:T(8,128)(2,1)S(1)}, bf16[32,1024]{1,0:T(8,128)(2,1)S(1)}, u32[]{:S(2)}, u32[]{:S(2)}) collective-permute-start(bf16[32,1024]{1,0:T(8,128)(2,1)S(1)} %get-tuple-element.61), channel_id=1, source_target_pairs={{0,2},{1,3},{2,0},{3,1},{4,6},{5,7},{6,4},{7,5},{8,10},{9,11},{10,... | collective-permute-start | bytes 196616 | tf_op jit(solution)/shard_map/ppermute | solution.py:223
  37.8 5.2 %collective-permute-start.17 = (bf16[32,1024]{1,0:T(8,128)(2,1)S(1)}, bf16[32,1024]{1,0:T(8,128)(2,1)S(1)}, u32[]{:S(2)}, u32[]{:S(2)}) collective-permute-start(bf16[32,1024]{1,0:T(8,128)(2,1)S(1)} %get-tuple-element.62), channel_id=1, source_target_pairs={{0,3},{1,2},{2,1},{3,0},{4,7},{5,6},{6,5},{7,4},{8,11},{9,10},{10,... | collective-permute-start | bytes 196616 | tf_op jit(solution)/shard_map/ppermute | solution.py:223

commit v9 on v8

--- a/solution.py
+++ b/solution.py
@@ -127,9 +127,8 @@
     for t, out in enumerate(outs):
         out[:height] = rows_ref[position()[1] ^ t].astype(out.dtype)
     part_ref[...] = mine_ref[:part] + came_ref[:part].astype(F32)
-    high, low = halves(mine_ref[part:] + came_ref[part:].astype(F32))
-    outs[1][height : height + part] = high
-    outs[1][height + part :] = low
+    outs[1][height : height + part] = (mine_ref[part:] + came_ref[part:].astype(F32)).astype(BF16)
+    outs[1][height + part :] = jnp.zeros((part // 2, outs[1].shape[1]), BF16)
 
 
 def near_kernel(u, paired, got, mine_ref, other_ref):
@@ -207,7 +206,7 @@
     slices, part, rank = reduced_ref.shape
     for k in range(slices):
         at = slice(k * rank, (k + 1) * rank)
-        came = second[height : height + part, at].astype(F32) + second[height + part :, at].astype(F32)
+        came = second[height : height + part, at].astype(F32)
         reduced_ref[k] = mine[:, at] + came
 
 
@@ -327,7 +326,7 @@
         slab_kernel,
         "slab",
         [
-            ((height + (2 * part if t == 1 else 0), width), F32 if t == 0 else BF16)
+            ((height + (part + part // 2 if t == 1 else 0), width), F32 if t == 0 else BF16)
             for t in range(count_z)
         ]
         + [((part, columns), F32)],

time: 43.9 us -> 43.4 us (0.989)
  waiting for transfers between devices: 13.7 us -> 13.2 us
    ppermute x18, waiting for transfers between devices: 13.7 us -> 13.2 us  [xor_permute(): lax.ppermute(x, axis, [(i, i ^ bits) for i in range(lax.axis_size(axis))])]
  transfers between devices with their start and end apart: 18 -> 18, of which waited for: 10 -> 11; matrix products, arithmetic and copies ran while one was open for 0% -> 0% of each run, Pallas kernels for 12% -> 13%
where the time goes in v9:
time: 43.4 us; the launch traced here: 43.2 us
  starting transfers between devices  19.6 us (45%)
  waiting for transfers between devices  13.2 us (30%)
  Pallas kernels  8.01 us (18%)
  local copies, waits for them, and re-layouts  1.6 us (4%)
  between operations  0.76 us (2%)
    ppermute x18, starting transfers between devices, xor_permute(): lax.ppermute(x, axis, [(i, i ^ bits) for i in range(lax.axis_size(axis))])  19.6 us
    ppermute x18, waiting for transfers between devices, xor_permute(): lax.ppermute(x, axis, [(i, i ^ bits) for i in range(lax.axis_size(axis))])  13.2 us
    pallas_call x12, Pallas kernels, call(): pl.pallas_call(kernel, out_shape=[jax.ShapeDtypeStruct(s, d) for s, d in...  8.01 us
    unnamed x8, local copies, waits for them, and re-layouts  1.6 us
  transfers between devices with their start and end apart: 18, of which 11 were waited for; matrix products, arithmetic and copies ran while one was open for 0% of the time, Pallas kernels for 13%

profile of v9, /device:TPU:0, one launch (start us, length us, event | category | flops | bytes accessed | tf_op | source)
XLA Modules:
  0.0 43.2 jit_solution(411398719493780700)
XLA Ops:
  0.6 0.0 copy-start
  0.6 1.6 %copy-done = f32[4,128,1024]{2,1,0:T(8,128)S(1)} copy-done((f32[4,128,1024]{2,1,0:T(8,128)S(1)}, f32[4,128,1024]{2,1,0:T(8,128)}, u32[]{:S(2)}) %copy-start) | copy-done | bytes 2097176
  2.2 1.9 %away.1._ = bf16[4,128,1024]{2,1,0:T(8,128)(2,1)S(1)} custom-call(f32[4,128,1024]{2,1,0:T(8,128)S(1)} %copy-done), custom_call_target="tpu_custom_call" | custom-call | tf_op jit(solution)/shard_map/away/pallas_call | solution.py:34
  4.1 0.0 copy-start.1
  4.1 0.5 %collective-permute-start = (bf16[4,128,1024]{2,1,0:T(8,128)(2,1)S(1)}, bf16[4,128,1024]{2,1,0:T(8,128)(2,1)S(1)}, u32[]{:S(2)}, u32[]{:S(2)}) collective-permute-start(bf16[4,128,1024]{2,1,0:T(8,128)(2,1)S(1)} %away.1._), channel_id=1, source_target_pairs={{0,4},{4,0},{8,12},{12,8},{16,20},{20,16},{24,28},{28,24},{1,5},{5... | collective-permute-start | bytes 3145736 | tf_op jit(solution)/shard_map/ppermute | solution.py:222
  4.6 1.0 %core.1 = (bf16[128,1024]{1,0:T(8,128)(2,1)S(1)}, bf16[144,1024]{1,0:T(8,128)(2,1)S(1)}) custom-call(f32[4,128,1024]{2,1,0:T(8,128)S(1)} %copy-done, f32[1024,256]{1,0:T(8,128)S(1)} %copy-done.2, bf16[128,256]{1,0:T(8,128)(2,1)S(1)} %copy-done.3, bf16[4,128,1024]{2,1,0:T(8,128)(2,1)S(1)} %away.1._), custom_call_target="tpu_custom_call" | custom-call | tf_op jit(solution)/shard_map/core/pallas_call | solution.py:34
  5.6 0.1 collective-permute-start.1
  5.8 3.0 %collective-permute-start.7 = (bf16[128,1024]{1,0:T(8,128)(2,1)S(1)}, bf16[128,1024]{1,0:T(8,128)(2,1)S(1)}, u32[]{:S(2)}, u32[]{:S(2)}) collective-permute-start(bf16[128,1024]{1,0:T(8,128)(2,1)S(1)} %get-tuple-element.34.u), channel_id=1, source_target_pairs={{0,8},{4,12},{8,0},{12,4},{16,24},{20,28},{24,16},{28,20},{1,9},{5... | collective-permute-start | bytes 786440 | tf_op jit(solution)/shard_map/ppermute | solution.py:222
  8.8 2.6 %collective-permute-start.6 = (bf16[144,1024]{1,0:T(8,128)(2,1)S(1)}, bf16[144,1024]{1,0:T(8,128)(2,1)S(1)}, u32[]{:S(2)}, u32[]{:S(2)}) collective-permute-start(bf16[144,1024]{1,0:T(8,128)(2,1)S(1)} %get-tuple-element.43), channel_id=1, source_target_pairs={{0,16},{4,20},{8,24},{12,28},{16,0},{20,4},{24,8},{28,12},{1,17},{... | collective-permute-start | bytes 884744 | tf_op jit(solution)/shard_map/ppermute | solution.py:222
  11.4 0.0 collective-permute-done.1._.paired
  11.4 0.0 collective-permute-done.came_ref
  11.4 2.1 %home.1 = (f32[4,32,1024]{2,1,0:T(8,128)S(1)}, f32[2,32,1024]{2,1,0:T(8,128)S(1)}, f32[2,32,1024]{2,1,0:T(8,128)S(1)}, bf16[2,2,32,1024]{3,2,1,0:T(8,128)(2,1)S(1)}, bf16[2,2,32,1024]{3,2,1,0:T(8,128)(2,1)S(1)}) custom-call(f32[4,128,1024]{2,1,0:T(8,128)S(1)} %copy-done.1, bf16[4,128,1024]{2,1,0:T(8,128)(2,1)S(1)} %collective-permute-done.came_ref, ...), custom_call_target="tpu_custom_call" | custom-call | tf_op jit(solution)/shard_map/home/pallas_call | solution.py:34
  13.6 1.6 %collective-permute-start.2 = (bf16[2,2,32,1024]{3,2,1,0:T(8,128)(2,1)S(1)}, bf16[2,2,32,1024]{3,2,1,0:T(8,128)(2,1)S(1)}, u32[]{:S(2)}, u32[]{:S(2)}) collective-permute-start(bf16[2,2,32,1024]{3,2,1,0:T(8,128)(2,1)S(1)} %get-tuple-element.38), channel_id=1, source_target_pairs={{0,1},{1,0},{2,3},{3,2},{4,5},{5,4},{6,7},{7,6},{8,9},{9,8},{10,11... | collective-permute-start | bytes 786440 | tf_op jit(solution)/shard_map/ppermute | solution.py:222
  15.1 1.5 %collective-permute-start.3 = (bf16[2,2,32,1024]{3,2,1,0:T(8,128)(2,1)S(1)}, bf16[2,2,32,1024]{3,2,1,0:T(8,128)(2,1)S(1)}, u32[]{:S(2)}, u32[]{:S(2)}) collective-permute-start(bf16[2,2,32,1024]{3,2,1,0:T(8,128)(2,1)S(1)} %get-tuple-element.39), channel_id=1, source_target_pairs={{0,2},{1,3},{2,0},{3,1},{4,6},{5,7},{6,4},{7,5},{8,10},{9,11},{10,... | collective-permute-start | bytes 786440 | tf_op jit(solution)/shard_map/ppermute | solution.py:222
  16.6 4.2 %collective-permute-done.7.got = bf16[128,1024]{1,0:T(8,128)(2,1)S(1)} collective-permute-done((bf16[128,1024]{1,0:T(8,128)(2,1)S(1)}, bf16[128,1024]{1,0:T(8,128)(2,1)S(1)}, u32[]{:S(2)}, u32[]{:S(2)}) %collective-permute-start.7) | collective-permute-done | bytes 262176 | tf_op jit(solution)/shard_map/ppermute | solution.py:222
  20.9 0.0 collective-permute-start.8
  20.9 0.5 %collective-permute-done.2.from1_ref = bf16[2,2,32,1024]{3,2,1,0:T(8,128)(2,1)S(1)} collective-permute-done((bf16[2,2,32,1024]{3,2,1,0:T(8,128)(2,1)S(1)}, bf16[2,2,32,1024]{3,2,1,0:T(8,128)(2,1)S(1)}, u32[]{:S(2)}, u32[]{:S(2)}) %collective-permute-start.2) | collective-permute-done | bytes 262176 | tf_op jit(solution)/shard_map/ppermute | solution.py:222
  21.4 1.2 %collective-permute-done.3.from2_ref = bf16[2,2,32,1024]{3,2,1,0:T(8,128)(2,1)S(1)} collective-permute-done((bf16[2,2,32,1024]{3,2,1,0:T(8,128)(2,1)S(1)}, bf16[2,2,32,1024]{3,2,1,0:T(8,128)(2,1)S(1)}, u32[]{:S(2)}, u32[]{:S(2)}) %collective-permute-start.3) | collective-permute-done | bytes 262176 | tf_op jit(solution)/shard_map/ppermute | solution.py:222
  22.6 0.1 middle.1
  22.7 0.6 %collective-permute-start.4 = (bf16[80,1024]{1,0:T(8,128)(2,1)S(1)}, bf16[80,1024]{1,0:T(8,128)(2,1)S(1)}, u32[]{:S(2)}, u32[]{:S(2)}) collective-permute-start(bf16[80,1024]{1,0:T(8,128)(2,1)S(1)} %get-tuple-element.41), channel_id=1, source_target_pairs={{0,1},{1,0},{2,3},{3,2},{4,5},{5,4},{6,7},{7,6},{8,9},{9,8},{10,11... | collective-permute-start | bytes 491528 | tf_op jit(solution)/shard_map/ppermute | solution.py:222
  23.3 1.5 %collective-permute-start.5 = (bf16[80,1024]{1,0:T(8,128)(2,1)S(1)}, bf16[80,1024]{1,0:T(8,128)(2,1)S(1)}, u32[]{:S(2)}, u32[]{:S(2)}) collective-permute-start(bf16[80,1024]{1,0:T(8,128)(2,1)S(1)} %get-tuple-element.42), channel_id=1, source_target_pairs={{0,2},{1,3},{2,0},{3,1},{4,6},{5,7},{6,4},{7,5},{8,10},{9,11},{10,... | collective-permute-start | bytes 491528 | tf_op jit(solution)/shard_map/ppermute | solution.py:222
  24.8 0.0 collective-permute-done.6.far
  24.8 0.4 two_cross.1
  25.2 0.4 parts.1
  25.6 0.1 collective-permute-start.9
  25.7 0.5 %collective-permute-start.13 = (bf16[256,128]{1,0:T(8,128)(2,1)S(1)}, bf16[256,128]{1,0:T(8,128)(2,1)S(1)}, u32[]{:S(2)}, u32[]{:S(2)}) collective-permute-start(bf16[256,128]{1,0:T(8,128)(2,1)S(1)} %get-tuple-element.44._), channel_id=1, source_target_pairs={{0,8},{4,12},{8,0},{12,4},{16,24},{20,28},{24,16},{28,20},{1,9},{5... | collective-permute-start | bytes 196616 | tf_op jit(solution)/shard_map/ppermute | solution.py:222
  26.2 0.8 %collective-permute-done.9.came_ref = bf16[64,1024]{1,0:T(8,128)(2,1)S(1)} collective-permute-done((bf16[64,1024]{1,0:T(8,128)(2,1)S(1)}, bf16[64,1024]{1,0:T(8,128)(2,1)S(1)}, u32[]{:S(2)}, u32[]{:S(2)}) %collective-permute-start.9) | collective-permute-done | bytes 131104 | tf_op jit(solution)/shard_map/ppermute | solution.py:222
  27.0 1.0 %collective-permute-done.4.from1_ref = bf16[80,1024]{1,0:T(8,128)(2,1)S(1)} collective-permute-done((bf16[80,1024]{1,0:T(8,128)(2,1)S(1)}, bf16[80,1024]{1,0:T(8,128)(2,1)S(1)}, u32[]{:S(2)}, u32[]{:S(2)}) %collective-permute-start.4) | collective-permute-done | bytes 163872 | tf_op jit(solution)/shard_map/ppermute | solution.py:222
  28.1 1.0 %collective-permute-done.5.from2_ref = bf16[80,1024]{1,0:T(8,128)(2,1)S(1)} collective-permute-done((bf16[80,1024]{1,0:T(8,128)(2,1)S(1)}, bf16[80,1024]{1,0:T(8,128)(2,1)S(1)}, u32[]{:S(2)}, u32[]{:S(2)}) %collective-permute-start.5) | collective-permute-done | bytes 163872 | tf_op jit(solution)/shard_map/ppermute | solution.py:222
  29.0 0.1 slab.1
  29.1 0.1 collective-permute-start.10
  29.2 0.4 two_near.1
  29.6 0.6 %collective-permute-done.13.came = bf16[256,128]{1,0:T(8,128)(2,1)S(1)} collective-permute-done((bf16[256,128]{1,0:T(8,128)(2,1)S(1)}, bf16[256,128]{1,0:T(8,128)(2,1)S(1)}, u32[]{:S(2)}, u32[]{:S(2)}) %collective-permute-start.13) | collective-permute-done | bytes 65568 | tf_op jit(solution)/shard_map/ppermute | solution.py:222
  30.2 0.1 collective-permute-start.14
  30.3 2.6 %collective-permute-start.11 = (bf16[32,1024]{1,0:T(8,128)(2,1)S(1)}, bf16[32,1024]{1,0:T(8,128)(2,1)S(1)}, u32[]{:S(2)}, u32[]{:S(2)}) collective-permute-start(bf16[32,1024]{1,0:T(8,128)(2,1)S(1)} %get-tuple-element.50), channel_id=1, source_target_pairs={{0,16},{4,20},{8,24},{12,28},{16,0},{20,4},{24,8},{28,12},{1,17},{... | collective-permute-start | bytes 196616 | tf_op jit(solution)/shard_map/ppermute | solution.py:222
  32.9 1.3 %collective-permute-start.12 = (bf16[32,1024]{1,0:T(8,128)(2,1)S(1)}, bf16[32,1024]{1,0:T(8,128)(2,1)S(1)}, u32[]{:S(2)}, u32[]{:S(2)}) collective-permute-start(bf16[32,1024]{1,0:T(8,128)(2,1)S(1)} %get-tuple-element.51), channel_id=1, source_target_pairs={{0,24},{4,28},{8,16},{12,20},{16,8},{20,12},{24,0},{28,4},{1,25},{... | collective-permute-start | bytes 196616 | tf_op jit(solution)/shard_map/ppermute | solution.py:222
  34.2 1.4 %collective-permute-done.10.refs_1_.outs_0_ = bf16[80,1024]{1,0:T(8,128)(2,1)S(1)} collective-permute-done((bf16[80,1024]{1,0:T(8,128)(2,1)S(1)}, bf16[80,1024]{1,0:T(8,128)(2,1)S(1)}, u32[]{:S(2)}, u32[]{:S(2)}) %collective-permute-start.10) | collective-permute-done | bytes 163872 | tf_op jit(solution)/shard_map/ppermute | solution.py:222
  35.6 0.1 two_place.1
  35.7 0.1 collective-permute-start.15
  35.8 1.6 %collective-permute-start.16 = (bf16[32,1024]{1,0:T(8,128)(2,1)S(1)}, bf16[32,1024]{1,0:T(8,128)(2,1)S(1)}, u32[]{:S(2)}, u32[]{:S(2)}) collective-permute-start(bf16[32,1024]{1,0:T(8,128)(2,1)S(1)} %get-tuple-element.61), channel_id=1, source_target_pairs={{0,2},{1,3},{2,0},{3,1},{4,6},{5,7},{6,4},{7,5},{8,10},{9,11},{10,... | collective-permute-start | bytes 196616 | tf_op jit(solution)/shard_map/ppermute | solution.py:222
  37.4 1.9 %collective-permute-start.17 = (bf16[32,1024]{1,0:T(8,128)(2,1)S(1)}, bf16[32,1024]{1,0:T(8,128)(2,1)S(1)}, u32[]{:S(2)}, u32[]{:S(2)}) collective-permute-start(bf16[32,1024]{1,0:T(8,128)(2,1)S(1)} %get-tuple-element.62), channel_id=1, source_target_pairs={{0,3},{1,2},{2,1},{3,0},{4,7},{5,6},{6,5},{7,4},{8,11},{9,10},{10,... | collective-permute-start | bytes 196616 | tf_op jit(solution)/shard_map/ppermute | solution.py:222
  39.3 0.0 collective-permute-done.11.refs_2_
  39.3 0.0 collective-permute-done.12.refs_3_
  39.3 0.7 %one.1 = (f32[32,1024]{1,0:T(8,128)}, f32[4,32,256]{2,1,0:T(8,128)}, f32[8,128]{1,0:T(8,128)S(1)}) custom-call(f32[32,1024]{1,0:T(8,128)S(1)} %get-tuple-element.47.mine, f32[32,1024]{1,0:T(8,128)S(1)} %get-tuple-element.48.refs_0_._, bf16[80,1024]{1,0:T(8,128)(2,1)S(1)} %collective-permute-done.10.refs_1_.outs_0_, ...), custom_call_target="tpu_custom_call" | custom-call | tf_op jit(solution)/shard_map/one/pallas_call | solution.py:34
  40.0 0.2 collective-permute-done.15.refs_1_
  40.2 0.6 %collective-permute-done.16.refs_2_ = bf16[32,1024]{1,0:T(8,128)(2,1)S(1)} collective-permute-done((bf16[32,1024]{1,0:T(8,128)(2,1)S(1)}, bf16[32,1024]{1,0:T(8,128)(2,1)S(1)}, u32[]{:S(2)}, u32[]{:S(2)}) %collective-permute-start.16) | collective-permute-done | bytes 65568 | tf_op jit(solution)/shard_map/ppermute | solution.py:222
  40.8 1.7 %collective-permute-done.17.refs_3_ = bf16[32,1024]{1,0:T(8,128)(2,1)S(1)} collective-permute-done((bf16[32,1024]{1,0:T(8,128)(2,1)S(1)}, bf16[32,1024]{1,0:T(8,128)(2,1)S(1)}, u32[]{:S(2)}, u32[]{:S(2)}) %collective-permute-start.17) | collective-permute-done | bytes 65568 | tf_op jit(solution)/shard_map/ppermute | solution.py:222
  42.5 0.7 %two.1 = f32[32,1024]{1,0:T(8,128)} custom-call(f32[32,1024]{1,0:T(8,128)S(1)} %get-tuple-element.59.refs_0_, bf16[32,1024]{1,0:T(8,128)(2,1)S(1)} %collective-permute-done.15.refs_1_, bf16[32,1024]{1,0:T(8,128)(2,1)S(1)} %collective-permute-done.16.refs_2_, bf16[32,1024]{1,0:T(8,128)(2,1)S(1)} %collective-permute-done.17.refs_3_, ...), custom_call_target="tpu_custom_call" | custom-call | tf_op jit(solution)/shard_map/two/pallas_call | solution.py:34
  (8 shorter events, 0.0 us)
Async XLA Ops:
  0.6 1.6 %copy-start = (f32[4,128,1024]{2,1,0:T(8,128)S(1)}, f32[4,128,1024]{2,1,0:T(8,128)}, u32[]{:S(2)}) copy-start(f32[4,128,1024]{2,1,0:T(8,128)} %x_ref.5) | copy-start | bytes 6291460
  2.2 2.4 %copy-start.2 = (f32[1024,256]{1,0:T(8,128)S(1)}, f32[1024,256]{1,0:T(8,128)}, u32[]{:S(2)}) copy-start(f32[1024,256]{1,0:T(8,128)} %f_ref.1) | copy-start | bytes 3145732
  2.2 2.4 %copy-start.3 = (bf16[128,256]{1,0:T(8,128)(2,1)S(1)}, bf16[128,256]{1,0:T(8,128)(2,1)}, u32[]{:S(2)}) copy-start(bf16[128,256]{1,0:T(8,128)(2,1)} %two_ref.3) | copy-start | bytes 196612
  4.1 7.3 %copy-start.1 = (f32[4,128,1024]{2,1,0:T(8,128)S(1)}, f32[4,128,1024]{2,1,0:T(8,128)}, u32[]{:S(2)}) copy-start(f32[4,128,1024]{2,1,0:T(8,128)} %x_ref.5) | copy-start | bytes 6291460
  4.1 7.3 %collective-permute-start = (bf16[4,128,1024]{2,1,0:T(8,128)(2,1)S(1)}, bf16[4,128,1024]{2,1,0:T(8,128)(2,1)S(1)}, u32[]{:S(2)}, u32[]{:S(2)}) collective-permute-start(bf16[4,128,1024]{2,1,0:T(8,128)(2,1)S(1)} %away.1._), channel_id=1, source_target_pairs={{0,4},{4,0},{8,12},{12,8},{16,20},{20,16},{24,28},{28,24},{1,5},{5... | collective-permute-start | bytes 3145736 | tf_op jit(solution)/shard_map/ppermute | solution.py:222
  5.6 5.8 %collective-permute-start.1 = (bf16[128,1024]{1,0:T(8,128)(2,1)S(1)}, bf16[128,1024]{1,0:T(8,128)(2,1)S(1)}, u32[]{:S(2)}, u32[]{:S(2)}) collective-permute-start(bf16[128,1024]{1,0:T(8,128)(2,1)S(1)} %get-tuple-element.34.u), channel_id=1, source_target_pairs={{0,4},{4,0},{8,12},{12,8},{16,20},{20,16},{24,28},{28,24},{1,5},{5... | collective-permute-start | bytes 786440 | tf_op jit(solution)/shard_map/ppermute | solution.py:222
  5.8 15.1 %collective-permute-start.7 = (bf16[128,1024]{1,0:T(8,128)(2,1)S(1)}, bf16[128,1024]{1,0:T(8,128)(2,1)S(1)}, u32[]{:S(2)}, u32[]{:S(2)}) collective-permute-start(bf16[128,1024]{1,0:T(8,128)(2,1)S(1)} %get-tuple-element.34.u), channel_id=1, source_target_pairs={{0,8},{4,12},{8,0},{12,4},{16,24},{20,28},{24,16},{28,20},{1,9},{5... | collective-permute-start | bytes 786440 | tf_op jit(solution)/shard_map/ppermute | solution.py:222
  8.8 16.0 %collective-permute-start.6 = (bf16[144,1024]{1,0:T(8,128)(2,1)S(1)}, bf16[144,1024]{1,0:T(8,128)(2,1)S(1)}, u32[]{:S(2)}, u32[]{:S(2)}) collective-permute-start(bf16[144,1024]{1,0:T(8,128)(2,1)S(1)} %get-tuple-element.43), channel_id=1, source_target_pairs={{0,16},{4,20},{8,24},{12,28},{16,0},{20,4},{24,8},{28,12},{1,17},{... | collective-permute-start | bytes 884744 | tf_op jit(solution)/shard_map/ppermute | solution.py:222
  13.6 7.8 %collective-permute-start.2 = (bf16[2,2,32,1024]{3,2,1,0:T(8,128)(2,1)S(1)}, bf16[2,2,32,1024]{3,2,1,0:T(8,128)(2,1)S(1)}, u32[]{:S(2)}, u32[]{:S(2)}) collective-permute-start(bf16[2,2,32,1024]{3,2,1,0:T(8,128)(2,1)S(1)} %get-tuple-element.38), channel_id=1, source_target_pairs={{0,1},{1,0},{2,3},{3,2},{4,5},{5,4},{6,7},{7,6},{8,9},{9,8},{10,11... | collective-permute-start | bytes 786440 | tf_op jit(solution)/shard_map/ppermute | solution.py:222
  15.1 7.5 %collective-permute-start.3 = (bf16[2,2,32,1024]{3,2,1,0:T(8,128)(2,1)S(1)}, bf16[2,2,32,1024]{3,2,1,0:T(8,128)(2,1)S(1)}, u32[]{:S(2)}, u32[]{:S(2)}) collective-permute-start(bf16[2,2,32,1024]{3,2,1,0:T(8,128)(2,1)S(1)} %get-tuple-element.39), channel_id=1, source_target_pairs={{0,2},{1,3},{2,0},{3,1},{4,6},{5,7},{6,4},{7,5},{8,10},{9,11},{10,... | collective-permute-start | bytes 786440 | tf_op jit(solution)/shard_map/ppermute | solution.py:222
  20.9 3.9 %collective-permute-start.8 = (bf16[128,1024]{1,0:T(8,128)(2,1)S(1)}, bf16[128,1024]{1,0:T(8,128)(2,1)S(1)}, u32[]{:S(2)}, u32[]{:S(2)}) collective-permute-start(bf16[128,1024]{1,0:T(8,128)(2,1)S(1)} %collective-permute-done.7.got), channel_id=1, source_target_pairs={{0,4},{4,0},{8,12},{12,8},{16,20},{20,16},{24,28},{28,24},{1,5},{5... | collective-permute-start | bytes 786440 | tf_op jit(solution)/shard_map/ppermute | solution.py:222
  22.7 5.4 %collective-permute-start.4 = (bf16[80,1024]{1,0:T(8,128)(2,1)S(1)}, bf16[80,1024]{1,0:T(8,128)(2,1)S(1)}, u32[]{:S(2)}, u32[]{:S(2)}) collective-permute-start(bf16[80,1024]{1,0:T(8,128)(2,1)S(1)} %get-tuple-element.41), channel_id=1, source_target_pairs={{0,1},{1,0},{2,3},{3,2},{4,5},{5,4},{6,7},{7,6},{8,9},{9,8},{10,11... | collective-permute-start | bytes 491528 | tf_op jit(solution)/shard_map/ppermute | solution.py:222
  23.3 5.7 %collective-permute-start.5 = (bf16[80,1024]{1,0:T(8,128)(2,1)S(1)}, bf16[80,1024]{1,0:T(8,128)(2,1)S(1)}, u32[]{:S(2)}, u32[]{:S(2)}) collective-permute-start(bf16[80,1024]{1,0:T(8,128)(2,1)S(1)} %get-tuple-element.42), channel_id=1, source_target_pairs={{0,2},{1,3},{2,0},{3,1},{4,6},{5,7},{6,4},{7,5},{8,10},{9,11},{10,... | collective-permute-start | bytes 491528 | tf_op jit(solution)/shard_map/ppermute | solution.py:222
  25.6 1.4 %collective-permute-start.9 = (bf16[64,1024]{1,0:T(8,128)(2,1)S(1)}, bf16[64,1024]{1,0:T(8,128)(2,1)S(1)}, u32[]{:S(2)}, u32[]{:S(2)}) collective-permute-start(bf16[64,1024]{1,0:T(8,128)(2,1)S(1)} %get-tuple-element.46), channel_id=1, source_target_pairs={{0,4},{4,0},{8,12},{12,8},{16,20},{20,16},{24,28},{28,24},{1,5},{5... | collective-permute-start | bytes 393224 | tf_op jit(solution)/shard_map/ppermute | solution.py:222
  25.7 4.5 %collective-permute-start.13 = (bf16[256,128]{1,0:T(8,128)(2,1)S(1)}, bf16[256,128]{1,0:T(8,128)(2,1)S(1)}, u32[]{:S(2)}, u32[]{:S(2)}) collective-permute-start(bf16[256,128]{1,0:T(8,128)(2,1)S(1)} %get-tuple-element.44._), channel_id=1, source_target_pairs={{0,8},{4,12},{8,0},{12,4},{16,24},{20,28},{24,16},{28,20},{1,9},{5... | collective-permute-start | bytes 196616 | tf_op jit(solution)/shard_map/ppermute | solution.py:222
  29.1 6.5 %collective-permute-start.10 = (bf16[80,1024]{1,0:T(8,128)(2,1)S(1)}, bf16[80,1024]{1,0:T(8,128)(2,1)S(1)}, u32[]{:S(2)}, u32[]{:S(2)}) collective-permute-start(bf16[80,1024]{1,0:T(8,128)(2,1)S(1)} %get-tuple-element.49), channel_id=1, source_target_pairs={{0,8},{4,12},{8,0},{12,4},{16,24},{20,28},{24,16},{28,20},{1,9},{5... | collective-permute-start | bytes 491528 | tf_op jit(solution)/shard_map/ppermute | solution.py:222
  30.2 4.0 %collective-permute-start.14 = (bf16[64,1024]{1,0:T(8,128)(2,1)S(1)}, bf16[64,1024]{1,0:T(8,128)(2,1)S(1)}, u32[]{:S(2)}, u32[]{:S(2)}) collective-permute-start(bf16[64,1024]{1,0:T(8,128)(2,1)S(1)} %get-tuple-element.58), channel_id=1, source_target_pairs={{0,4},{4,0},{8,12},{12,8},{16,20},{20,16},{24,28},{28,24},{1,5},{5... | collective-permute-start | bytes 393224 | tf_op jit(solution)/shard_map/ppermute | solution.py:222
  30.3 8.9 %collective-permute-start.11 = (bf16[32,1024]{1,0:T(8,128)(2,1)S(1)}, bf16[32,1024]{1,0:T(8,128)(2,1)S(1)}, u32[]{:S(2)}, u32[]{:S(2)}) collective-permute-start(bf16[32,1024]{1,0:T(8,128)(2,1)S(1)} %get-tuple-element.50), channel_id=1, source_target_pairs={{0,16},{4,20},{8,24},{12,28},{16,0},{20,4},{24,8},{28,12},{1,17},{... | collective-permute-start | bytes 196616 | tf_op jit(solution)/shard_map/ppermute | solution.py:222
  32.9 6.4 %collective-permute-start.12 = (bf16[32,1024]{1,0:T(8,128)(2,1)S(1)}, bf16[32,1024]{1,0:T(8,128)(2,1)S(1)}, u32[]{:S(2)}, u32[]{:S(2)}) collective-permute-start(bf16[32,1024]{1,0:T(8,128)(2,1)S(1)} %get-tuple-element.51), channel_id=1, source_target_pairs={{0,24},{4,28},{8,16},{12,20},{16,8},{20,12},{24,0},{28,4},{1,25},{... | collective-permute-start | bytes 196616 | tf_op jit(solution)/shard_map/ppermute | solution.py:222
  35.7 4.5 %collective-permute-start.15 = (bf16[32,1024]{1,0:T(8,128)(2,1)S(1)}, bf16[32,1024]{1,0:T(8,128)(2,1)S(1)}, u32[]{:S(2)}, u32[]{:S(2)}) collective-permute-start(bf16[32,1024]{1,0:T(8,128)(2,1)S(1)} %get-tuple-element.60), channel_id=1, source_target_pairs={{0,1},{1,0},{2,3},{3,2},{4,5},{5,4},{6,7},{7,6},{8,9},{9,8},{10,11... | collective-permute-start | bytes 196616 | tf_op jit(solution)/shard_map/ppermute | solution.py:222
  35.8 5.0 %collective-permute-start.16 = (bf16[32,1024]{1,0:T(8,128)(2,1)S(1)}, bf16[32,1024]{1,0:T(8,128)(2,1)S(1)}, u32[]{:S(2)}, u32[]{:S(2)}) collective-permute-start(bf16[32,1024]{1,0:T(8,128)(2,1)S(1)} %get-tuple-element.61), channel_id=1, source_target_pairs={{0,2},{1,3},{2,0},{3,1},{4,6},{5,7},{6,4},{7,5},{8,10},{9,11},{10,... | collective-permute-start | bytes 196616 | tf_op jit(solution)/shard_map/ppermute | solution.py:222
  37.4 5.2 %collective-permute-start.17 = (bf16[32,1024]{1,0:T(8,128)(2,1)S(1)}, bf16[32,1024]{1,0:T(8,128)(2,1)S(1)}, u32[]{:S(2)}, u32[]{:S(2)}) collective-permute-start(bf16[32,1024]{1,0:T(8,128)(2,1)S(1)} %get-tuple-element.62), channel_id=1, source_target_pairs={{0,3},{1,2},{2,1},{3,0},{4,7},{5,6},{6,5},{7,4},{8,11},{9,10},{10,... | collective-permute-start | bytes 196616 | tf_op jit(solution)/shard_map/ppermute | solution.py:222

commit v10 on v9

--- a/solution.py
+++ b/solution.py
@@ -364,7 +364,7 @@
         scratch=[pltpu.VMEM((owned, count_ja * owned), F32)],
     )
     rows = list(rows)
-    for t in range(1, count_ka):
+    for t in reversed(range(1, count_ka)):
         rows[t] = xor_permute(rows[t], "ka", t)
     gram_one, reduced, done = call(
         functools.partial(one_kernel, norm_one),

time: 43.4 us -> 43.4 us (level)
  no operation moved by 1% of the time
where the time goes in v10:
time: 43.4 us; the launch traced here: 43.2 us
  starting transfers between devices  19.6 us (45%)
  waiting for transfers between devices  13.2 us (30%)
  Pallas kernels  8.01 us (18%)
  local copies, waits for them, and re-layouts  1.6 us (4%)
  between operations  0.76 us (2%)
    ppermute x18, starting transfers between devices, xor_permute(): lax.ppermute(x, axis, [(i, i ^ bits) for i in range(lax.axis_size(axis))])  19.6 us
    ppermute x18, waiting for transfers between devices, xor_permute(): lax.ppermute(x, axis, [(i, i ^ bits) for i in range(lax.axis_size(axis))])  13.2 us
    pallas_call x12, Pallas kernels, call(): pl.pallas_call(kernel, out_shape=[jax.ShapeDtypeStruct(s, d) for s, d in...  8.01 us
    unnamed x8, local copies, waits for them, and re-layouts  1.6 us
  transfers between devices with their start and end apart: 18, of which 11 were waited for; matrix products, arithmetic and copies ran while one was open for 0% of the time, Pallas kernels for 13%

profile of v10, /device:TPU:0, one launch (start us, length us, event | category | flops | bytes accessed | tf_op | source)
XLA Modules:
  0.0 43.2 jit_solution(411398719493780700)
XLA Ops:
  0.6 0.0 copy-start
  0.6 1.6 %copy-done = f32[4,128,1024]{2,1,0:T(8,128)S(1)} copy-done((f32[4,128,1024]{2,1,0:T(8,128)S(1)}, f32[4,128,1024]{2,1,0:T(8,128)}, u32[]{:S(2)}) %copy-start) | copy-done | bytes 2097176
  2.2 1.9 %away.1._ = bf16[4,128,1024]{2,1,0:T(8,128)(2,1)S(1)} custom-call(f32[4,128,1024]{2,1,0:T(8,128)S(1)} %copy-done), custom_call_target="tpu_custom_call" | custom-call | tf_op jit(solution)/shard_map/away/pallas_call | solution.py:34
  4.1 0.0 copy-start.1
  4.1 0.5 %collective-permute-start = (bf16[4,128,1024]{2,1,0:T(8,128)(2,1)S(1)}, bf16[4,128,1024]{2,1,0:T(8,128)(2,1)S(1)}, u32[]{:S(2)}, u32[]{:S(2)}) collective-permute-start(bf16[4,128,1024]{2,1,0:T(8,128)(2,1)S(1)} %away.1._), channel_id=1, source_target_pairs={{0,4},{4,0},{8,12},{12,8},{16,20},{20,16},{24,28},{28,24},{1,5},{5... | collective-permute-start | bytes 3145736 | tf_op jit(solution)/shard_map/ppermute | solution.py:222
  4.6 1.0 %core.1 = (bf16[128,1024]{1,0:T(8,128)(2,1)S(1)}, bf16[144,1024]{1,0:T(8,128)(2,1)S(1)}) custom-call(f32[4,128,1024]{2,1,0:T(8,128)S(1)} %copy-done, f32[1024,256]{1,0:T(8,128)S(1)} %copy-done.2, bf16[128,256]{1,0:T(8,128)(2,1)S(1)} %copy-done.3, bf16[4,128,1024]{2,1,0:T(8,128)(2,1)S(1)} %away.1._), custom_call_target="tpu_custom_call" | custom-call | tf_op jit(solution)/shard_map/core/pallas_call | solution.py:34
  5.6 0.1 collective-permute-start.1
  5.8 3.0 %collective-permute-start.7 = (bf16[128,1024]{1,0:T(8,128)(2,1)S(1)}, bf16[128,1024]{1,0:T(8,128)(2,1)S(1)}, u32[]{:S(2)}, u32[]{:S(2)}) collective-permute-start(bf16[128,1024]{1,0:T(8,128)(2,1)S(1)} %get-tuple-element.34.u), channel_id=1, source_target_pairs={{0,8},{4,12},{8,0},{12,4},{16,24},{20,28},{24,16},{28,20},{1,9},{5... | collective-permute-start | bytes 786440 | tf_op jit(solution)/shard_map/ppermute | solution.py:222
  8.8 2.6 %collective-permute-start.6 = (bf16[144,1024]{1,0:T(8,128)(2,1)S(1)}, bf16[144,1024]{1,0:T(8,128)(2,1)S(1)}, u32[]{:S(2)}, u32[]{:S(2)}) collective-permute-start(bf16[144,1024]{1,0:T(8,128)(2,1)S(1)} %get-tuple-element.43), channel_id=1, source_target_pairs={{0,16},{4,20},{8,24},{12,28},{16,0},{20,4},{24,8},{28,12},{1,17},{... | collective-permute-start | bytes 884744 | tf_op jit(solution)/shard_map/ppermute | solution.py:222
  11.4 0.0 collective-permute-done.1._.paired
  11.4 0.0 collective-permute-done.came_ref
  11.4 2.1 %home.1 = (f32[4,32,1024]{2,1,0:T(8,128)S(1)}, f32[2,32,1024]{2,1,0:T(8,128)S(1)}, f32[2,32,1024]{2,1,0:T(8,128)S(1)}, bf16[2,2,32,1024]{3,2,1,0:T(8,128)(2,1)S(1)}, bf16[2,2,32,1024]{3,2,1,0:T(8,128)(2,1)S(1)}) custom-call(f32[4,128,1024]{2,1,0:T(8,128)S(1)} %copy-done.1, bf16[4,128,1024]{2,1,0:T(8,128)(2,1)S(1)} %collective-permute-done.came_ref, ...), custom_call_target="tpu_custom_call" | custom-call | tf_op jit(solution)/shard_map/home/pallas_call | solution.py:34
  13.6 1.6 %collective-permute-start.2 = (bf16[2,2,32,1024]{3,2,1,0:T(8,128)(2,1)S(1)}, bf16[2,2,32,1024]{3,2,1,0:T(8,128)(2,1)S(1)}, u32[]{:S(2)}, u32[]{:S(2)}) collective-permute-start(bf16[2,2,32,1024]{3,2,1,0:T(8,128)(2,1)S(1)} %get-tuple-element.38), channel_id=1, source_target_pairs={{0,1},{1,0},{2,3},{3,2},{4,5},{5,4},{6,7},{7,6},{8,9},{9,8},{10,11... | collective-permute-start | bytes 786440 | tf_op jit(solution)/shard_map/ppermute | solution.py:222
  15.1 1.5 %collective-permute-start.3 = (bf16[2,2,32,1024]{3,2,1,0:T(8,128)(2,1)S(1)}, bf16[2,2,32,1024]{3,2,1,0:T(8,128)(2,1)S(1)}, u32[]{:S(2)}, u32[]{:S(2)}) collective-permute-start(bf16[2,2,32,1024]{3,2,1,0:T(8,128)(2,1)S(1)} %get-tuple-element.39), channel_id=1, source_target_pairs={{0,2},{1,3},{2,0},{3,1},{4,6},{5,7},{6,4},{7,5},{8,10},{9,11},{10,... | collective-permute-start | bytes 786440 | tf_op jit(solution)/shard_map/ppermute | solution.py:222
  16.6 4.2 %collective-permute-done.7.got = bf16[128,1024]{1,0:T(8,128)(2,1)S(1)} collective-permute-done((bf16[128,1024]{1,0:T(8,128)(2,1)S(1)}, bf16[128,1024]{1,0:T(8,128)(2,1)S(1)}, u32[]{:S(2)}, u32[]{:S(2)}) %collective-permute-start.7) | collective-permute-done | bytes 262176 | tf_op jit(solution)/shard_map/ppermute | solution.py:222
  20.9 0.0 collective-permute-start.8
  20.9 0.5 %collective-permute-done.2.from1_ref = bf16[2,2,32,1024]{3,2,1,0:T(8,128)(2,1)S(1)} collective-permute-done((bf16[2,2,32,1024]{3,2,1,0:T(8,128)(2,1)S(1)}, bf16[2,2,32,1024]{3,2,1,0:T(8,128)(2,1)S(1)}, u32[]{:S(2)}, u32[]{:S(2)}) %collective-permute-start.2) | collective-permute-done | bytes 262176 | tf_op jit(solution)/shard_map/ppermute | solution.py:222
  21.4 1.2 %collective-permute-done.3.from2_ref = bf16[2,2,32,1024]{3,2,1,0:T(8,128)(2,1)S(1)} collective-permute-done((bf16[2,2,32,1024]{3,2,1,0:T(8,128)(2,1)S(1)}, bf16[2,2,32,1024]{3,2,1,0:T(8,128)(2,1)S(1)}, u32[]{:S(2)}, u32[]{:S(2)}) %collective-permute-start.3) | collective-permute-done | bytes 262176 | tf_op jit(solution)/shard_map/ppermute | solution.py:222
  22.6 0.1 middle.1
  22.7 0.6 %collective-permute-start.4 = (bf16[80,1024]{1,0:T(8,128)(2,1)S(1)}, bf16[80,1024]{1,0:T(8,128)(2,1)S(1)}, u32[]{:S(2)}, u32[]{:S(2)}) collective-permute-start(bf16[80,1024]{1,0:T(8,128)(2,1)S(1)} %get-tuple-element.41), channel_id=1, source_target_pairs={{0,1},{1,0},{2,3},{3,2},{4,5},{5,4},{6,7},{7,6},{8,9},{9,8},{10,11... | collective-permute-start | bytes 491528 | tf_op jit(solution)/shard_map/ppermute | solution.py:222
  23.3 1.5 %collective-permute-start.5 = (bf16[80,1024]{1,0:T(8,128)(2,1)S(1)}, bf16[80,1024]{1,0:T(8,128)(2,1)S(1)}, u32[]{:S(2)}, u32[]{:S(2)}) collective-permute-start(bf16[80,1024]{1,0:T(8,128)(2,1)S(1)} %get-tuple-element.42), channel_id=1, source_target_pairs={{0,2},{1,3},{2,0},{3,1},{4,6},{5,7},{6,4},{7,5},{8,10},{9,11},{10,... | collective-permute-start | bytes 491528 | tf_op jit(solution)/shard_map/ppermute | solution.py:222
  24.8 0.0 collective-permute-done.6.far
  24.8 0.4 two_cross.1
  25.2 0.4 parts.1
  25.6 0.1 collective-permute-start.9
  25.7 0.5 %collective-permute-start.13 = (bf16[256,128]{1,0:T(8,128)(2,1)S(1)}, bf16[256,128]{1,0:T(8,128)(2,1)S(1)}, u32[]{:S(2)}, u32[]{:S(2)}) collective-permute-start(bf16[256,128]{1,0:T(8,128)(2,1)S(1)} %get-tuple-element.44._), channel_id=1, source_target_pairs={{0,8},{4,12},{8,0},{12,4},{16,24},{20,28},{24,16},{28,20},{1,9},{5... | collective-permute-start | bytes 196616 | tf_op jit(solution)/shard_map/ppermute | solution.py:222
  26.2 0.8 %collective-permute-done.9.came_ref = bf16[64,1024]{1,0:T(8,128)(2,1)S(1)} collective-permute-done((bf16[64,1024]{1,0:T(8,128)(2,1)S(1)}, bf16[64,1024]{1,0:T(8,128)(2,1)S(1)}, u32[]{:S(2)}, u32[]{:S(2)}) %collective-permute-start.9) | collective-permute-done | bytes 131104 | tf_op jit(solution)/shard_map/ppermute | solution.py:222
  27.0 1.0 %collective-permute-done.4.from1_ref = bf16[80,1024]{1,0:T(8,128)(2,1)S(1)} collective-permute-done((bf16[80,1024]{1,0:T(8,128)(2,1)S(1)}, bf16[80,1024]{1,0:T(8,128)(2,1)S(1)}, u32[]{:S(2)}, u32[]{:S(2)}) %collective-permute-start.4) | collective-permute-done | bytes 163872 | tf_op jit(solution)/shard_map/ppermute | solution.py:222
  28.1 1.0 %collective-permute-done.5.from2_ref = bf16[80,1024]{1,0:T(8,128)(2,1)S(1)} collective-permute-done((bf16[80,1024]{1,0:T(8,128)(2,1)S(1)}, bf16[80,1024]{1,0:T(8,128)(2,1)S(1)}, u32[]{:S(2)}, u32[]{:S(2)}) %collective-permute-start.5) | collective-permute-done | bytes 163872 | tf_op jit(solution)/shard_map/ppermute | solution.py:222
  29.0 0.1 slab.1
  29.1 0.1 collective-permute-start.10
  29.2 0.4 two_near.1
  29.6 0.6 %collective-permute-done.13.came = bf16[256,128]{1,0:T(8,128)(2,1)S(1)} collective-permute-done((bf16[256,128]{1,0:T(8,128)(2,1)S(1)}, bf16[256,128]{1,0:T(8,128)(2,1)S(1)}, u32[]{:S(2)}, u32[]{:S(2)}) %collective-permute-start.13) | collective-permute-done | bytes 65568 | tf_op jit(solution)/shard_map/ppermute | solution.py:222
  30.2 0.1 collective-permute-start.14
  30.3 2.6 %collective-permute-start.11 = (bf16[32,1024]{1,0:T(8,128)(2,1)S(1)}, bf16[32,1024]{1,0:T(8,128)(2,1)S(1)}, u32[]{:S(2)}, u32[]{:S(2)}) collective-permute-start(bf16[32,1024]{1,0:T(8,128)(2,1)S(1)} %get-tuple-element.50), channel_id=1, source_target_pairs={{0,16},{4,20},{8,24},{12,28},{16,0},{20,4},{24,8},{28,12},{1,17},{... | collective-permute-start | bytes 196616 | tf_op jit(solution)/shard_map/ppermute | solution.py:222
  32.9 1.3 %collective-permute-start.12 = (bf16[32,1024]{1,0:T(8,128)(2,1)S(1)}, bf16[32,1024]{1,0:T(8,128)(2,1)S(1)}, u32[]{:S(2)}, u32[]{:S(2)}) collective-permute-start(bf16[32,1024]{1,0:T(8,128)(2,1)S(1)} %get-tuple-element.51), channel_id=1, source_target_pairs={{0,24},{4,28},{8,16},{12,20},{16,8},{20,12},{24,0},{28,4},{1,25},{... | collective-permute-start | bytes 196616 | tf_op jit(solution)/shard_map/ppermute | solution.py:222
  34.2 1.4 %collective-permute-done.10.refs_1_.outs_0_ = bf16[80,1024]{1,0:T(8,128)(2,1)S(1)} collective-permute-done((bf16[80,1024]{1,0:T(8,128)(2,1)S(1)}, bf16[80,1024]{1,0:T(8,128)(2,1)S(1)}, u32[]{:S(2)}, u32[]{:S(2)}) %collective-permute-start.10) | collective-permute-done | bytes 163872 | tf_op jit(solution)/shard_map/ppermute | solution.py:222
  35.6 0.1 two_place.1
  35.7 0.1 collective-permute-start.15
  35.8 1.6 %collective-permute-start.16 = (bf16[32,1024]{1,0:T(8,128)(2,1)S(1)}, bf16[32,1024]{1,0:T(8,128)(2,1)S(1)}, u32[]{:S(2)}, u32[]{:S(2)}) collective-permute-start(bf16[32,1024]{1,0:T(8,128)(2,1)S(1)} %get-tuple-element.61), channel_id=1, source_target_pairs={{0,2},{1,3},{2,0},{3,1},{4,6},{5,7},{6,4},{7,5},{8,10},{9,11},{10,... | collective-permute-start | bytes 196616 | tf_op jit(solution)/shard_map/ppermute | solution.py:222
  37.4 1.9 %collective-permute-start.17 = (bf16[32,1024]{1,0:T(8,128)(2,1)S(1)}, bf16[32,1024]{1,0:T(8,128)(2,1)S(1)}, u32[]{:S(2)}, u32[]{:S(2)}) collective-permute-start(bf16[32,1024]{1,0:T(8,128)(2,1)S(1)} %get-tuple-element.62), channel_id=1, source_target_pairs={{0,3},{1,2},{2,1},{3,0},{4,7},{5,6},{6,5},{7,4},{8,11},{9,10},{10,... | collective-permute-start | bytes 196616 | tf_op jit(solution)/shard_map/ppermute | solution.py:222
  39.3 0.0 collective-permute-done.11.refs_2_
  39.3 0.0 collective-permute-done.12.refs_3_
  39.3 0.7 %one.1 = (f32[32,1024]{1,0:T(8,128)}, f32[4,32,256]{2,1,0:T(8,128)}, f32[8,128]{1,0:T(8,128)S(1)}) custom-call(f32[32,1024]{1,0:T(8,128)S(1)} %get-tuple-element.47.mine, f32[32,1024]{1,0:T(8,128)S(1)} %get-tuple-element.48.refs_0_._, bf16[80,1024]{1,0:T(8,128)(2,1)S(1)} %collective-permute-done.10.refs_1_.outs_0_, ...), custom_call_target="tpu_custom_call" | custom-call | tf_op jit(solution)/shard_map/one/pallas_call | solution.py:34
  40.0 0.2 collective-permute-done.15.refs_1_
  40.2 0.6 %collective-permute-done.16.refs_2_ = bf16[32,1024]{1,0:T(8,128)(2,1)S(1)} collective-permute-done((bf16[32,1024]{1,0:T(8,128)(2,1)S(1)}, bf16[32,1024]{1,0:T(8,128)(2,1)S(1)}, u32[]{:S(2)}, u32[]{:S(2)}) %collective-permute-start.16) | collective-permute-done | bytes 65568 | tf_op jit(solution)/shard_map/ppermute | solution.py:222
  40.8 1.7 %collective-permute-done.17.refs_3_ = bf16[32,1024]{1,0:T(8,128)(2,1)S(1)} collective-permute-done((bf16[32,1024]{1,0:T(8,128)(2,1)S(1)}, bf16[32,1024]{1,0:T(8,128)(2,1)S(1)}, u32[]{:S(2)}, u32[]{:S(2)}) %collective-permute-start.17) | collective-permute-done | bytes 65568 | tf_op jit(solution)/shard_map/ppermute | solution.py:222
  42.5 0.7 %two.1 = f32[32,1024]{1,0:T(8,128)} custom-call(f32[32,1024]{1,0:T(8,128)S(1)} %get-tuple-element.59.refs_0_, bf16[32,1024]{1,0:T(8,128)(2,1)S(1)} %collective-permute-done.15.refs_1_, bf16[32,1024]{1,0:T(8,128)(2,1)S(1)} %collective-permute-done.16.refs_2_, bf16[32,1024]{1,0:T(8,128)(2,1)S(1)} %collective-permute-done.17.refs_3_, ...), custom_call_target="tpu_custom_call" | custom-call | tf_op jit(solution)/shard_map/two/pallas_call | solution.py:34
  (8 shorter events, 0.0 us)
Async XLA Ops:
  0.6 1.6 %copy-start = (f32[4,128,1024]{2,1,0:T(8,128)S(1)}, f32[4,128,1024]{2,1,0:T(8,128)}, u32[]{:S(2)}) copy-start(f32[4,128,1024]{2,1,0:T(8,128)} %x_ref.5) | copy-start | bytes 6291460
  2.2 2.4 %copy-start.2 = (f32[1024,256]{1,0:T(8,128)S(1)}, f32[1024,256]{1,0:T(8,128)}, u32[]{:S(2)}) copy-start(f32[1024,256]{1,0:T(8,128)} %f_ref.1) | copy-start | bytes 3145732
  2.2 2.4 %copy-start.3 = (bf16[128,256]{1,0:T(8,128)(2,1)S(1)}, bf16[128,256]{1,0:T(8,128)(2,1)}, u32[]{:S(2)}) copy-start(bf16[128,256]{1,0:T(8,128)(2,1)} %two_ref.3) | copy-start | bytes 196612
  4.1 7.3 %copy-start.1 = (f32[4,128,1024]{2,1,0:T(8,128)S(1)}, f32[4,128,1024]{2,1,0:T(8,128)}, u32[]{:S(2)}) copy-start(f32[4,128,1024]{2,1,0:T(8,128)} %x_ref.5) | copy-start | bytes 6291460
  4.1 7.3 %collective-permute-start = (bf16[4,128,1024]{2,1,0:T(8,128)(2,1)S(1)}, bf16[4,128,1024]{2,1,0:T(8,128)(2,1)S(1)}, u32[]{:S(2)}, u32[]{:S(2)}) collective-permute-start(bf16[4,128,1024]{2,1,0:T(8,128)(2,1)S(1)} %away.1._), channel_id=1, source_target_pairs={{0,4},{4,0},{8,12},{12,8},{16,20},{20,16},{24,28},{28,24},{1,5},{5... | collective-permute-start | bytes 3145736 | tf_op jit(solution)/shard_map/ppermute | solution.py:222
  5.6 5.8 %collective-permute-start.1 = (bf16[128,1024]{1,0:T(8,128)(2,1)S(1)}, bf16[128,1024]{1,0:T(8,128)(2,1)S(1)}, u32[]{:S(2)}, u32[]{:S(2)}) collective-permute-start(bf16[128,1024]{1,0:T(8,128)(2,1)S(1)} %get-tuple-element.34.u), channel_id=1, source_target_pairs={{0,4},{4,0},{8,12},{12,8},{16,20},{20,16},{24,28},{28,24},{1,5},{5... | collective-permute-start | bytes 786440 | tf_op jit(solution)/shard_map/ppermute | solution.py:222
  5.8 15.1 %collective-permute-start.7 = (bf16[128,1024]{1,0:T(8,128)(2,1)S(1)}, bf16[128,1024]{1,0:T(8,128)(2,1)S(1)}, u32[]{:S(2)}, u32[]{:S(2)}) collective-permute-start(bf16[128,1024]{1,0:T(8,128)(2,1)S(1)} %get-tuple-element.34.u), channel_id=1, source_target_pairs={{0,8},{4,12},{8,0},{12,4},{16,24},{20,28},{24,16},{28,20},{1,9},{5... | collective-permute-start | bytes 786440 | tf_op jit(solution)/shard_map/ppermute | solution.py:222
  8.8 16.0 %collective-permute-start.6 = (bf16[144,1024]{1,0:T(8,128)(2,1)S(1)}, bf16[144,1024]{1,0:T(8,128)(2,1)S(1)}, u32[]{:S(2)}, u32[]{:S(2)}) collective-permute-start(bf16[144,1024]{1,0:T(8,128)(2,1)S(1)} %get-tuple-element.43), channel_id=1, source_target_pairs={{0,16},{4,20},{8,24},{12,28},{16,0},{20,4},{24,8},{28,12},{1,17},{... | collective-permute-start | bytes 884744 | tf_op jit(solution)/shard_map/ppermute | solution.py:222
  13.6 7.8 %collective-permute-start.2 = (bf16[2,2,32,1024]{3,2,1,0:T(8,128)(2,1)S(1)}, bf16[2,2,32,1024]{3,2,1,0:T(8,128)(2,1)S(1)}, u32[]{:S(2)}, u32[]{:S(2)}) collective-permute-start(bf16[2,2,32,1024]{3,2,1,0:T(8,128)(2,1)S(1)} %get-tuple-element.38), channel_id=1, source_target_pairs={{0,1},{1,0},{2,3},{3,2},{4,5},{5,4},{6,7},{7,6},{8,9},{9,8},{10,11... | collective-permute-start | bytes 786440 | tf_op jit(solution)/shard_map/ppermute | solution.py:222
  15.1 7.5 %collective-permute-start.3 = (bf16[2,2,32,1024]{3,2,1,0:T(8,128)(2,1)S(1)}, bf16[2,2,32,1024]{3,2,1,0:T(8,128)(2,1)S(1)}, u32[]{:S(2)}, u32[]{:S(2)}) collective-permute-start(bf16[2,2,32,1024]{3,2,1,0:T(8,128)(2,1)S(1)} %get-tuple-element.39), channel_id=1, source_target_pairs={{0,2},{1,3},{2,0},{3,1},{4,6},{5,7},{6,4},{7,5},{8,10},{9,11},{10,... | collective-permute-start | bytes 786440 | tf_op jit(solution)/shard_map/ppermute | solution.py:222
  20.9 3.9 %collective-permute-start.8 = (bf16[128,1024]{1,0:T(8,128)(2,1)S(1)}, bf16[128,1024]{1,0:T(8,128)(2,1)S(1)}, u32[]{:S(2)}, u32[]{:S(2)}) collective-permute-start(bf16[128,1024]{1,0:T(8,128)(2,1)S(1)} %collective-permute-done.7.got), channel_id=1, source_target_pairs={{0,4},{4,0},{8,12},{12,8},{16,20},{20,16},{24,28},{28,24},{1,5},{5... | collective-permute-start | bytes 786440 | tf_op jit(solution)/shard_map/ppermute | solution.py:222
  22.7 5.4 %collective-permute-start.4 = (bf16[80,1024]{1,0:T(8,128)(2,1)S(1)}, bf16[80,1024]{1,0:T(8,128)(2,1)S(1)}, u32[]{:S(2)}, u32[]{:S(2)}) collective-permute-start(bf16[80,1024]{1,0:T(8,128)(2,1)S(1)} %get-tuple-element.41), channel_id=1, source_target_pairs={{0,1},{1,0},{2,3},{3,2},{4,5},{5,4},{6,7},{7,6},{8,9},{9,8},{10,11... | collective-permute-start | bytes 491528 | tf_op jit(solution)/shard_map/ppermute | solution.py:222
  23.3 5.7 %collective-permute-start.5 = (bf16[80,1024]{1,0:T(8,128)(2,1)S(1)}, bf16[80,1024]{1,0:T(8,128)(2,1)S(1)}, u32[]{:S(2)}, u32[]{:S(2)}) collective-permute-start(bf16[80,1024]{1,0:T(8,128)(2,1)S(1)} %get-tuple-element.42), channel_id=1, source_target_pairs={{0,2},{1,3},{2,0},{3,1},{4,6},{5,7},{6,4},{7,5},{8,10},{9,11},{10,... | collective-permute-start | bytes 491528 | tf_op jit(solution)/shard_map/ppermute | solution.py:222
  25.6 1.4 %collective-permute-start.9 = (bf16[64,1024]{1,0:T(8,128)(2,1)S(1)}, bf16[64,1024]{1,0:T(8,128)(2,1)S(1)}, u32[]{:S(2)}, u32[]{:S(2)}) collective-permute-start(bf16[64,1024]{1,0:T(8,128)(2,1)S(1)} %get-tuple-element.46), channel_id=1, source_target_pairs={{0,4},{4,0},{8,12},{12,8},{16,20},{20,16},{24,28},{28,24},{1,5},{5... | collective-permute-start | bytes 393224 | tf_op jit(solution)/shard_map/ppermute | solution.py:222
  25.7 4.5 %collective-permute-start.13 = (bf16[256,128]{1,0:T(8,128)(2,1)S(1)}, bf16[256,128]{1,0:T(8,128)(2,1)S(1)}, u32[]{:S(2)}, u32[]{:S(2)}) collective-permute-start(bf16[256,128]{1,0:T(8,128)(2,1)S(1)} %get-tuple-element.44._), channel_id=1, source_target_pairs={{0,8},{4,12},{8,0},{12,4},{16,24},{20,28},{24,16},{28,20},{1,9},{5... | collective-permute-start | bytes 196616 | tf_op jit(solution)/shard_map/ppermute | solution.py:222
  29.1 6.5 %collective-permute-start.10 = (bf16[80,1024]{1,0:T(8,128)(2,1)S(1)}, bf16[80,1024]{1,0:T(8,128)(2,1)S(1)}, u32[]{:S(2)}, u32[]{:S(2)}) collective-permute-start(bf16[80,1024]{1,0:T(8,128)(2,1)S(1)} %get-tuple-element.49), channel_id=1, source_target_pairs={{0,8},{4,12},{8,0},{12,4},{16,24},{20,28},{24,16},{28,20},{1,9},{5... | collective-permute-start | bytes 491528 | tf_op jit(solution)/shard_map/ppermute | solution.py:222
  30.2 4.0 %collective-permute-start.14 = (bf16[64,1024]{1,0:T(8,128)(2,1)S(1)}, bf16[64,1024]{1,0:T(8,128)(2,1)S(1)}, u32[]{:S(2)}, u32[]{:S(2)}) collective-permute-start(bf16[64,1024]{1,0:T(8,128)(2,1)S(1)} %get-tuple-element.58), channel_id=1, source_target_pairs={{0,4},{4,0},{8,12},{12,8},{16,20},{20,16},{24,28},{28,24},{1,5},{5... | collective-permute-start | bytes 393224 | tf_op jit(solution)/shard_map/ppermute | solution.py:222
  30.3 8.9 %collective-permute-start.11 = (bf16[32,1024]{1,0:T(8,128)(2,1)S(1)}, bf16[32,1024]{1,0:T(8,128)(2,1)S(1)}, u32[]{:S(2)}, u32[]{:S(2)}) collective-permute-start(bf16[32,1024]{1,0:T(8,128)(2,1)S(1)} %get-tuple-element.50), channel_id=1, source_target_pairs={{0,16},{4,20},{8,24},{12,28},{16,0},{20,4},{24,8},{28,12},{1,17},{... | collective-permute-start | bytes 196616 | tf_op jit(solution)/shard_map/ppermute | solution.py:222
  32.9 6.4 %collective-permute-start.12 = (bf16[32,1024]{1,0:T(8,128)(2,1)S(1)}, bf16[32,1024]{1,0:T(8,128)(2,1)S(1)}, u32[]{:S(2)}, u32[]{:S(2)}) collective-permute-start(bf16[32,1024]{1,0:T(8,128)(2,1)S(1)} %get-tuple-element.51), channel_id=1, source_target_pairs={{0,24},{4,28},{8,16},{12,20},{16,8},{20,12},{24,0},{28,4},{1,25},{... | collective-permute-start | bytes 196616 | tf_op jit(solution)/shard_map/ppermute | solution.py:222
  35.7 4.5 %collective-permute-start.15 = (bf16[32,1024]{1,0:T(8,128)(2,1)S(1)}, bf16[32,1024]{1,0:T(8,128)(2,1)S(1)}, u32[]{:S(2)}, u32[]{:S(2)}) collective-permute-start(bf16[32,1024]{1,0:T(8,128)(2,1)S(1)} %get-tuple-element.60), channel_id=1, source_target_pairs={{0,1},{1,0},{2,3},{3,2},{4,5},{5,4},{6,7},{7,6},{8,9},{9,8},{10,11... | collective-permute-start | bytes 196616 | tf_op jit(solution)/shard_map/ppermute | solution.py:222
  35.8 5.0 %collective-permute-start.16 = (bf16[32,1024]{1,0:T(8,128)(2,1)S(1)}, bf16[32,1024]{1,0:T(8,128)(2,1)S(1)}, u32[]{:S(2)}, u32[]{:S(2)}) collective-permute-start(bf16[32,1024]{1,0:T(8,128)(2,1)S(1)} %get-tuple-element.61), channel_id=1, source_target_pairs={{0,2},{1,3},{2,0},{3,1},{4,6},{5,7},{6,4},{7,5},{8,10},{9,11},{10,... | collective-permute-start | bytes 196616 | tf_op jit(solution)/shard_map/ppermute | solution.py:222
  37.4 5.2 %collective-permute-start.17 = (bf16[32,1024]{1,0:T(8,128)(2,1)S(1)}, bf16[32,1024]{1,0:T(8,128)(2,1)S(1)}, u32[]{:S(2)}, u32[]{:S(2)}) collective-permute-start(bf16[32,1024]{1,0:T(8,128)(2,1)S(1)} %get-tuple-element.62), channel_id=1, source_target_pairs={{0,3},{1,2},{2,1},{3,0},{4,7},{5,6},{6,5},{7,4},{8,11},{9,10},{10,... | collective-permute-start | bytes 196616 | tf_op jit(solution)/shard_map/ppermute | solution.py:222
